TPU v7x, 32 devices: a whole 2x2x4 slice. The times are simulated.
32 devices in a mesh: ctx: 8 (over z, x), heads: 4 (over y, core).
Axes of the slice: x: 2, y: 2, z: 4, core: 2. Of those that a mesh axis runs over, the one named last changes fastest.
Arguments:
- q_raw: bfloat16 [2048, 8192], P('ctx', 'heads'), may hold values from -60 to 60
- k_raw: bfloat16 [2048, 1024], P('ctx', 'heads'), may hold values from -60 to 60
- values: bfloat16 [2048, 1024], P('ctx', 'heads'), may hold values from -6 to 6
- saved_out: bfloat16 [2048, 8192], P('ctx', 'heads'), may hold values from -6 to 6
- out_grad: bfloat16 [2048, 8192], P('ctx', 'heads'), may hold values from -60 to 60
- q_gain: float32 [128], replicated, may hold values from 0.25 to 1.75
- k_gain: float32 [128], replicated, may hold values from 0.25 to 1.75
- ancestors: int32 [32, 32], P('ctx'), may hold values from -1 to 31, as said below
Outputs:
- dq_raw: bfloat16 [2048, 8192], P('ctx', 'heads')
- dk_raw: bfloat16 [2048, 1024], P('ctx', 'heads')
- dv: bfloat16 [2048, 1024], P('ctx', 'heads')
- q_gain_grad: float32 [128], replicated
- k_gain_grad: float32 [128], replicated
Inputs may be any that keep to these rules, and one draw needn't show every extreme that they name: `ancestors`: the forest is 1 trees of 32 blocks each; in tree order, tree k holds blocks (k * 32 + 256 / 64 + b) mod 32 for b = 0 to 31. Row b lists, in tree order, every block on the path from its tree's first block to b, ending with b itself, then -1s. The first 16 blocks of a tree form its prompt, each the child of the block before it; every other block's parent is a block earlier in its tree, from the prompt's last block on.
All inputs are finite; a program needn't handle non-finite values.
Results may differ from a plain program's by a relative error of at most 0.0069.
Values may be sent and summed in bfloat16 or wider, within the bound.
No kernel may reach another device: no remote copies, remote signals or barrier semaphores. Data moves between devices by JAX's collectives and lax.ppermute only.
A program may use at most 64 MiB of HBM per device.

v0:
```python
import math

import jax
import jax.numpy as jnp
from jax import lax
from jax.sharding import PartitionSpec as P

TREE_DEV = 8


ROPE_BASE = 1000000.0
EPS = 1e-06


def passed_along(value, axis, steps):
    count = lax.axis_size(axis)
    pairs = [(source, (source + steps) % count) for source in range(count)]
    return lax.ppermute(value, axis, pairs)


def rope_tables(positions, head_dim):
    half_dim = head_dim // 2
    frequency = jnp.exp(
        jnp.arange(half_dim, dtype=jnp.float32) * (-2.0 * math.log(ROPE_BASE) / head_dim)
    )
    angles = positions.astype(jnp.float32)[:, None] * frequency[None, :]
    return (jnp.cos(angles), jnp.sin(angles))


def norm_rope(inputs, gain_vec, cos_table, sin_table):
    recip_rms = lax.rsqrt(jnp.mean(inputs * inputs, -1, keepdims=True) + EPS)
    scaled = inputs * recip_rms * gain_vec
    half_dim = inputs.shape[-1] // 2
    cos_part = cos_table[:, None, :]
    sin_part = sin_table[:, None, :]
    front_half = scaled[..., :half_dim]
    back_half = scaled[..., half_dim:]
    return jnp.concatenate(
        [
            front_half * cos_part - back_half * sin_part,
            back_half * cos_part + front_half * sin_part,
        ],
        -1,
    )


def norm_rope_back(inputs, gain_vec, cos_table, sin_table, upstream):
    half_dim = inputs.shape[-1] // 2
    cos_part = cos_table[:, None, :]
    sin_part = sin_table[:, None, :]
    front_half = upstream[..., :half_dim]
    back_half = upstream[..., half_dim:]
    unrotated = jnp.concatenate(
        [
            front_half * cos_part + back_half * sin_part,
            back_half * cos_part - front_half * sin_part,
        ],
        -1,
    )
    recip_rms = lax.rsqrt(jnp.mean(inputs * inputs, -1, keepdims=True) + EPS)
    normed = inputs * recip_rms
    gain_term = jnp.sum(unrotated * normed, axis=(0, 1))
    gain_grad = unrotated * gain_vec
    input_grad = recip_rms * (gain_grad - normed * jnp.mean(gain_grad * normed, -1, keepdims=True))
    return (input_grad, gain_term)


def on_device(q_raw, k_raw, values, saved_out, out_grad, q_gain, k_gain, ancestors):
    tokens_here = q_raw.shape[0]
    head_dim = q_gain.shape[0]
    kv_local = k_raw.shape[1] // head_dim
    group_size = q_raw.shape[1] // (kv_local * head_dim)
    block_count = ancestors.shape[0]
    block_len = tokens_here // block_count
    cycle_size = lax.axis_size("ctx")
    my_index = lax.axis_index("ctx")
    hop_count = TREE_DEV - 1
    inv_root = 1.0 / math.sqrt(head_dim)
    offsets = jnp.arange(block_len, dtype=jnp.int32)
    depth_count = jnp.sum((ancestors >= 0).astype(jnp.int32), 1)
    positions = (((depth_count - 1) * block_len)[:, None] + offsets[None, :]).reshape(tokens_here)
    cos_table, sin_table = rope_tables(positions, head_dim)
    q_float = q_raw.astype(jnp.float32).reshape(tokens_here, kv_local * group_size, head_dim)
    k_float = k_raw.astype(jnp.float32).reshape(tokens_here, kv_local, head_dim)
    q_rot = norm_rope(q_float, q_gain, cos_table, sin_table).astype(jnp.bfloat16)
    q_rot = q_rot.reshape(tokens_here, kv_local, group_size, head_dim)
    k_rot = norm_rope(k_float, k_gain, cos_table, sin_table).astype(jnp.bfloat16)
    v_heads = values.reshape(tokens_here, kv_local, head_dim)
    grad_heads = out_grad.reshape(tokens_here, kv_local, group_size, head_dim)
    out_heads = saved_out.reshape(tokens_here, kv_local, group_size, head_dim)
    row_delta = jnp.einsum(
        "ikgd,ikgd->kgi", grad_heads, out_heads, preferred_element_type=jnp.float32
    )
    key_value = jnp.stack((k_rot, v_heads), 1)
    local_tok = jnp.arange(tokens_here, dtype=jnp.int32)

    def visible(source):
        key_blocks = source * block_count + jnp.arange(block_count, dtype=jnp.int32)
        block_vis = jnp.any(ancestors[:, :, None] == key_blocks[None, None, :], axis=1)
        token_vis = jnp.repeat(jnp.repeat(block_vis, block_len, 0), block_len, 1)
        causal = (local_tok[None, :] <= local_tok[:, None]) | (source != my_index)
        return (token_vis & causal, jnp.any(block_vis))

    def scores_of(key_rot):
        return (
            jnp.einsum("ikgd,jkd->kgij", q_rot, key_rot, preferred_element_type=jnp.float32)
            * inv_root
        )

    def add_mass(exp_mass, key_rot, allowed):
        expo = jnp.where(allowed[None, None], jnp.exp(scores_of(key_rot)), 0.0)
        return exp_mass + jnp.sum(expo, -1)

    def accumulate(exp_mass, key_rot, allowed):
        return add_mass(exp_mass, key_rot, allowed)

    own_allowed, own_touched = visible(my_index)
    exp_mass = add_mass(
        jnp.zeros((kv_local, group_size, tokens_here), jnp.float32), k_rot, own_allowed
    )

    def forward_step(hop_index, loop_state):
        mass_now, moving = loop_state
        moving = passed_along(moving, "ctx", 1)
        allowed, touched = visible((my_index - hop_index) % cycle_size)
        return (accumulate(mass_now, moving, allowed), moving)

    exp_mass, _ = lax.fori_loop(1, hop_count + 1, forward_step, (exp_mass, k_rot))
    log_mass = jnp.log(exp_mass)

    def grad_terms(key_rot, val_rot, allowed):
        weights = jnp.where(
            allowed[None, None], jnp.exp(scores_of(key_rot) - log_mass[..., None]), 0.0
        )
        weights_low = weights.astype(jnp.bfloat16)
        grad_prob = jnp.einsum(
            "ikgd,jkd->kgij", grad_heads, val_rot, preferred_element_type=jnp.float32
        )
        dscore = (weights * (grad_prob - row_delta[..., None]) * inv_root).astype(jnp.bfloat16)
        dq_part = jnp.einsum("kgij,jkd->ikgd", dscore, key_rot, preferred_element_type=jnp.float32)
        dk_part = jnp.einsum("kgij,ikgd->jkd", dscore, q_rot, preferred_element_type=jnp.float32)
        dv_part = jnp.einsum(
            "kgij,ikgd->jkd", weights_low, grad_heads, preferred_element_type=jnp.float32
        )
        return (dq_part, jnp.stack((dk_part, dv_part), 1))

    def pair_terms(moving, allowed):
        return grad_terms(moving[:, 0], moving[:, 1], allowed)

    dq_acc, own_part = grad_terms(k_rot, v_heads, own_allowed)
    key_grads = own_part

    def back_step(hop_index, loop_state):
        dq_now, grads_now, moving = loop_state
        moving = passed_along(moving, "ctx", 1)
        source = (my_index - hop_index) % cycle_size
        allowed, touched = visible(source)
        dq_part, kv_part = pair_terms(moving, allowed)
        grads_now = passed_along(grads_now, "ctx", 1) + kv_part
        return (dq_now + dq_part, grads_now, moving)

    dq_acc, key_grads, _ = lax.fori_loop(
        1, hop_count + 1, back_step, (dq_acc, key_grads, key_value)
    )
    key_grads = passed_along(key_grads, "ctx", -hop_count)
    dq_rot = dq_acc.reshape(tokens_here, kv_local * group_size, head_dim)
    dq_input, q_gain_part = norm_rope_back(q_float, q_gain, cos_table, sin_table, dq_rot)
    dk_input, k_gain_part = norm_rope_back(k_float, k_gain, cos_table, sin_table, key_grads[:, 0])
    q_gain_grad, k_gain_grad = lax.psum((q_gain_part, k_gain_part), ("ctx", "heads"))
    dq_raw = dq_input.astype(jnp.bfloat16).reshape(tokens_here, kv_local * group_size * head_dim)
    dk_raw = dk_input.astype(jnp.bfloat16).reshape(tokens_here, kv_local * head_dim)
    dv = key_grads[:, 1].astype(jnp.bfloat16).reshape(tokens_here, kv_local * head_dim)
    return (dq_raw, dk_raw, dv, q_gain_grad, k_gain_grad)


def solution(mesh):
    in_specs = (
        P("ctx", "heads"),
        P("ctx", "heads"),
        P("ctx", "heads"),
        P("ctx", "heads"),
        P("ctx", "heads"),
        P(),
        P(),
        P("ctx", None),
    )
    out_specs = (P("ctx", "heads"), P("ctx", "heads"), P("ctx", "heads"), P(), P())
    return jax.shard_map(
        on_device, mesh=mesh, in_specs=in_specs, out_specs=out_specs, check_vma=False
    )
```

profile of v0, /device:TPU:0, one launch (start us, length us, event | category | flops | bytes accessed | tf_op | source)
XLA Modules:
  0.0 292.3 jit_solution(15943373342938131396)
XLA Ops:
  2.8 1.5 convert_bitcast_fusion
  11.5 2.9 fusion.29
  14.4 63.4 %while.38 = (s32[]{:T(128)}, f32[2,8,256]{2,1,0:T(8,128)S(1)}, bf16[256,2,128]{2,0,1:T(8,128)(2,1)S(1)}, s32[4,32]{1,0:T(4,128)S(1)}, s32[]{:T(128)}, /*index=5*...) while((s32[]{:T(128)}, f32[2,8,256]{2,1,0:T(8,128)S(1)}, ...), condition=%wide.region_8.9_spmd.clone, body=%wide.region_5.8_spmd.clone.sunk | while | flops 271778816 | bytes 2167688 | solution.py:128
  14.4 2.9 %collective-permute-start = (bf16[256,2,128]{2,0,1:T(8,128)(2,1)S(1)}, bf16[256,2,128]{2,0,1:T(8,128)(2,1)S(1)}, u32[]{:S(2)}, u32[]{:S(2)}) collective-permute-start(bf16[256,2,128]{2,0,1:T(8,128)(2,1)S(1)} %get-tuple-element.709), channel_id=1, source_target_pairs={{0,4},{4,8},{8,12},{12,16},{16,20},{20,24},{24,28},{28,0},{1,5},{5... | collective-permute-start | bytes 393224 | tf_op jit(solution)/shard_map/while/body/eval_jaxpr/ppermute | solution.py:18
  17.9 6.0 %collective-permute-done = bf16[256,2,128]{2,0,1:T(8,128)(2,1)S(1)} collective-permute-done((bf16[256,2,128]{2,0,1:T(8,128)(2,1)S(1)}, bf16[256,2,128]{2,0,1:T(8,128)(2,1)S(1)}, u32[]{:S(2)}, u32[]{:S(2)}) %collective-permute-start) | collective-permute-done | bytes 131104 | tf_op jit(solution)/shard_map/while/body/eval_jaxpr/ppermute | solution.py:18
  25.6 7.1 %collective-permute-done = bf16[256,2,128]{2,0,1:T(8,128)(2,1)S(1)} collective-permute-done((bf16[256,2,128]{2,0,1:T(8,128)(2,1)S(1)}, bf16[256,2,128]{2,0,1:T(8,128)(2,1)S(1)}, u32[]{:S(2)}, u32[]{:S(2)}) %collective-permute-start) | collective-permute-done | bytes 131104 | tf_op jit(solution)/shard_map/while/body/eval_jaxpr/ppermute | solution.py:18
  34.4 7.1 %collective-permute-done = bf16[256,2,128]{2,0,1:T(8,128)(2,1)S(1)} collective-permute-done((bf16[256,2,128]{2,0,1:T(8,128)(2,1)S(1)}, bf16[256,2,128]{2,0,1:T(8,128)(2,1)S(1)}, u32[]{:S(2)}, u32[]{:S(2)}) %collective-permute-start) | collective-permute-done | bytes 131104 | tf_op jit(solution)/shard_map/while/body/eval_jaxpr/ppermute | solution.py:18
  43.2 7.1 %collective-permute-done = bf16[256,2,128]{2,0,1:T(8,128)(2,1)S(1)} collective-permute-done((bf16[256,2,128]{2,0,1:T(8,128)(2,1)S(1)}, bf16[256,2,128]{2,0,1:T(8,128)(2,1)S(1)}, u32[]{:S(2)}, u32[]{:S(2)}) %collective-permute-start) | collective-permute-done | bytes 131104 | tf_op jit(solution)/shard_map/while/body/eval_jaxpr/ppermute | solution.py:18
  52.0 7.1 %collective-permute-done = bf16[256,2,128]{2,0,1:T(8,128)(2,1)S(1)} collective-permute-done((bf16[256,2,128]{2,0,1:T(8,128)(2,1)S(1)}, bf16[256,2,128]{2,0,1:T(8,128)(2,1)S(1)}, u32[]{:S(2)}, u32[]{:S(2)}) %collective-permute-start) | collective-permute-done | bytes 131104 | tf_op jit(solution)/shard_map/while/body/eval_jaxpr/ppermute | solution.py:18
  60.8 7.1 %collective-permute-done = bf16[256,2,128]{2,0,1:T(8,128)(2,1)S(1)} collective-permute-done((bf16[256,2,128]{2,0,1:T(8,128)(2,1)S(1)}, bf16[256,2,128]{2,0,1:T(8,128)(2,1)S(1)}, u32[]{:S(2)}, u32[]{:S(2)}) %collective-permute-start) | collective-permute-done | bytes 131104 | tf_op jit(solution)/shard_map/while/body/eval_jaxpr/ppermute | solution.py:18
  69.6 7.1 %collective-permute-done = bf16[256,2,128]{2,0,1:T(8,128)(2,1)S(1)} collective-permute-done((bf16[256,2,128]{2,0,1:T(8,128)(2,1)S(1)}, bf16[256,2,128]{2,0,1:T(8,128)(2,1)S(1)}, u32[]{:S(2)}, u32[]{:S(2)}) %collective-permute-start) | collective-permute-done | bytes 131104 | tf_op jit(solution)/shard_map/while/body/eval_jaxpr/ppermute | solution.py:18
  78.9 1.9 copy.122
  83.5 3.3 %fusion.40 = f32[256,1,2,128]{0,3,2,1:T(8,128)S(1)} fusion(bf16[256,2,8,128]{0,3,2,1:T(8,128)(2,1)S(1)} %bitcast.262, f32[2,256,256,8]{2,1,3,0:T(8,128)} %get-tuple-element.597, f32[2,8,256]{2,1,0:T(8,128)S(1)} %copy-done.24, pred[256,256]{0,1:T(8,128)(4,1)S(1)} %copy-done.21), kind=kOutput, calls=%fused_computation.66 | convolution fusion | flops 272629760 | bytes 5586944 | tf_op jit(solution)/shard_map/kgij,ikgd->jkd/dot_general | solution.py:142
  86.9 1.5 fusion.27
  89.3 1.8 convolution_bitcast_fusion.1
  94.2 1.9 copy.98
  96.1 1.7 copy.97
  97.8 1.7 pad_maximum_fusion.3
  99.5 129.3 %while.39 = (s32[]{:T(128)}, f32[256,2,8,128]{3,0,2,1:T(8,128)S(1)}, f32[256,2,2,128]{3,0,2,1:T(8,128)}, bf16[256,2,2,128]{3,0,2,1:T(8,128)(2,1)}, s32[4,32]{1,0...) while((s32[]{:T(128)}, ...), condition=%wide.region_11.12_spmd.clone, body=%wide.region_9.11_spmd.clone.sunk | while | flops 1354695680 | bytes 37999652 | solution.py:162
  101.2 7.6 %collective-permute-done.1 = bf16[256,2,2,128]{3,0,2,1:T(8,128)(2,1)S(1)} collective-permute-done((bf16[256,2,2,128]{3,0,2,1:T(8,128)(2,1)}, bf16[256,2,2,128]{3,0,2,1:T(8,128)(2,1)S(1)}, u32[]{:S(2)}, u32[]{:S(2)}) %collective-permute-start.1) | collective-permute-done | bytes 262176 | tf_op jit(solution)/shard_map/while/body/eval_jaxpr/ppermute | solution.py:18
  110.0 1.5 fusion.95
  111.5 1.4 bitcast_add_fusion.2
  115.4 1.9 maximum_add_fusion.2
  119.0 7.6 %collective-permute-done.1 = bf16[256,2,2,128]{3,0,2,1:T(8,128)(2,1)S(1)} collective-permute-done((bf16[256,2,2,128]{3,0,2,1:T(8,128)(2,1)}, bf16[256,2,2,128]{3,0,2,1:T(8,128)(2,1)S(1)}, u32[]{:S(2)}, u32[]{:S(2)}) %collective-permute-start.1) | collective-permute-done | bytes 262176 | tf_op jit(solution)/shard_map/while/body/eval_jaxpr/ppermute | solution.py:18
  127.8 1.5 fusion.95
  129.3 1.4 bitcast_add_fusion.2
  133.3 1.9 maximum_add_fusion.2
  137.0 7.6 %collective-permute-done.1 = bf16[256,2,2,128]{3,0,2,1:T(8,128)(2,1)S(1)} collective-permute-done((bf16[256,2,2,128]{3,0,2,1:T(8,128)(2,1)}, bf16[256,2,2,128]{3,0,2,1:T(8,128)(2,1)S(1)}, u32[]{:S(2)}, u32[]{:S(2)}) %collective-permute-start.1) | collective-permute-done | bytes 262176 | tf_op jit(solution)/shard_map/while/body/eval_jaxpr/ppermute | solution.py:18
  145.8 1.5 fusion.95
  151.6 1.9 maximum_add_fusion.2
  155.2 7.6 %collective-permute-done.1 = bf16[256,2,2,128]{3,0,2,1:T(8,128)(2,1)S(1)} collective-permute-done((bf16[256,2,2,128]{3,0,2,1:T(8,128)(2,1)}, bf16[256,2,2,128]{3,0,2,1:T(8,128)(2,1)S(1)}, u32[]{:S(2)}, u32[]{:S(2)}) %collective-permute-start.1) | collective-permute-done | bytes 262176 | tf_op jit(solution)/shard_map/while/body/eval_jaxpr/ppermute | solution.py:18
  164.0 1.5 fusion.95
  165.5 1.4 bitcast_add_fusion.2
  170.1 1.9 maximum_add_fusion.2
  173.7 7.6 %collective-permute-done.1 = bf16[256,2,2,128]{3,0,2,1:T(8,128)(2,1)S(1)} collective-permute-done((bf16[256,2,2,128]{3,0,2,1:T(8,128)(2,1)}, bf16[256,2,2,128]{3,0,2,1:T(8,128)(2,1)S(1)}, u32[]{:S(2)}, u32[]{:S(2)}) %collective-permute-start.1) | collective-permute-done | bytes 262176 | tf_op jit(solution)/shard_map/while/body/eval_jaxpr/ppermute | solution.py:18
  182.5 1.5 fusion.95
  188.8 1.9 maximum_add_fusion.2
  192.4 7.6 %collective-permute-done.1 = bf16[256,2,2,128]{3,0,2,1:T(8,128)(2,1)S(1)} collective-permute-done((bf16[256,2,2,128]{3,0,2,1:T(8,128)(2,1)}, bf16[256,2,2,128]{3,0,2,1:T(8,128)(2,1)S(1)}, u32[]{:S(2)}, u32[]{:S(2)}) %collective-permute-start.1) | collective-permute-done | bytes 262176 | tf_op jit(solution)/shard_map/while/body/eval_jaxpr/ppermute | solution.py:18
  201.2 1.5 fusion.95
  207.7 1.9 maximum_add_fusion.2
  211.4 7.6 %collective-permute-done.1 = bf16[256,2,2,128]{3,0,2,1:T(8,128)(2,1)S(1)} collective-permute-done((bf16[256,2,2,128]{3,0,2,1:T(8,128)(2,1)}, bf16[256,2,2,128]{3,0,2,1:T(8,128)(2,1)S(1)}, u32[]{:S(2)}, u32[]{:S(2)}) %collective-permute-start.1) | collective-permute-done | bytes 262176 | tf_op jit(solution)/shard_map/while/body/eval_jaxpr/ppermute | solution.py:18
  220.2 1.5 fusion.95
  225.5 1.5 collective-permute-done.2
  226.9 1.9 maximum_add_fusion.2
  230.4 2.5 multiply_add_fusion
  233.0 2.1 multiply_reduce_fusion.1
  236.3 3.8 %fusion.36 = (f32[2048]{0:T(1024)S(1)}, bf16[256,2048]{1,0:T(8,128)(2,1)}) fusion(bf16[256,2048]{1,0:T(8,128)(2,1)S(1)} %copy-done.3, f32[32,8,16,128]{3,2,1,0:T(8,128)S(1)} %bitcast.265, f32[32,8,16,128]{3,2,1,0:T(8,128)S(1)} %bitcast.267, f32[32,8,16,128]{3,2,1,0:T(8,128)S(1)} %bitcast.266, f32[2048]{0:T(1024)S(1)} %broadcast_bitcast_fusion), kind=kLoop, calls=%fused_computation.53 | loop fusion | flops 4716544 | bytes 8404992 | tf_op jit(solution)/shard_map/reduce_sum | solution.py:62
  243.5 48.7 %all-reduce = (f32[128]{0:T(128)}, f32[128]{0:T(128)}) all-reduce(f32[128]{0:T(128)S(1)} %bitcast_reduce_fusion, f32[128]{0:T(128)S(1)} %bitcast_reduce_fusion.1), channel_id=1, replica_groups=mesh['ctx'=8,'heads'=4] {'ctx','heads'}, use_global_device_ids=true, to_apply=%region_16.17 | all-reduce | flops 256 | bytes 2048 | tf_op jit(solution)/shard_map/psum | solution.py:169
  (320 shorter events, 80.9 us)
Async XLA Ops:
  1.7 3.0 %copy-start.10 = (bf16[256,256]{0,1:T(8,128)(2,1)}, bf16[256,256]{0,1:T(8,128)(2,1)S(1)}, u32[]{:S(2)}) copy-start(bf16[256,256]{0,1:T(8,128)(2,1)S(1)} %copy.82) | copy-start | bytes 393220
  1.8 5.1 %copy-start.6 = (f32[256,2,128]{2,0,1:T(8,128)}, f32[256,2,128]{2,0,1:T(8,128)S(1)}, u32[]{:S(2)}) copy-start(f32[256,2,128]{2,0,1:T(8,128)S(1)} %copy.83) | copy-start | bytes 786436
  4.7 2.2 copy-start
  4.7 1.3 copy-start.26
  7.3 2.6 copy-start.12
  11.5 2.9 copy-start.19
  14.4 64.0 %copy-start.14 = (bf16[256,2048]{1,0:T(8,128)(2,1)S(1)}, bf16[256,2048]{1,0:T(8,128)(2,1)}, u32[]{:S(2)}) copy-start(bf16[256,2048]{1,0:T(8,128)(2,1)} %param.16) | copy-start | bytes 3145732
  14.4 9.5 %collective-permute-start = (bf16[256,2,128]{2,0,1:T(8,128)(2,1)S(1)}, bf16[256,2,128]{2,0,1:T(8,128)(2,1)S(1)}, u32[]{:S(2)}, u32[]{:S(2)}) collective-permute-start(bf16[256,2,128]{2,0,1:T(8,128)(2,1)S(1)} %get-tuple-element.709), channel_id=1, source_target_pairs={{0,4},{4,8},{8,12},{12,16},{16,20},{20,24},{24,28},{28,0},{1,5},{5... | collective-permute-start | bytes 393224 | tf_op jit(solution)/shard_map/while/body/eval_jaxpr/ppermute | solution.py:18
  25.0 7.7 %collective-permute-start = (bf16[256,2,128]{2,0,1:T(8,128)(2,1)S(1)}, bf16[256,2,128]{2,0,1:T(8,128)(2,1)S(1)}, u32[]{:S(2)}, u32[]{:S(2)}) collective-permute-start(bf16[256,2,128]{2,0,1:T(8,128)(2,1)S(1)} %get-tuple-element.709), channel_id=1, source_target_pairs={{0,4},{4,8},{8,12},{12,16},{16,20},{20,24},{24,28},{28,0},{1,5},{5... | collective-permute-start | bytes 393224 | tf_op jit(solution)/shard_map/while/body/eval_jaxpr/ppermute | solution.py:18
  33.8 7.7 %collective-permute-start = (bf16[256,2,128]{2,0,1:T(8,128)(2,1)S(1)}, bf16[256,2,128]{2,0,1:T(8,128)(2,1)S(1)}, u32[]{:S(2)}, u32[]{:S(2)}) collective-permute-start(bf16[256,2,128]{2,0,1:T(8,128)(2,1)S(1)} %get-tuple-element.709), channel_id=1, source_target_pairs={{0,4},{4,8},{8,12},{12,16},{16,20},{20,24},{24,28},{28,0},{1,5},{5... | collective-permute-start | bytes 393224 | tf_op jit(solution)/shard_map/while/body/eval_jaxpr/ppermute | solution.py:18
  42.6 7.7 %collective-permute-start = (bf16[256,2,128]{2,0,1:T(8,128)(2,1)S(1)}, bf16[256,2,128]{2,0,1:T(8,128)(2,1)S(1)}, u32[]{:S(2)}, u32[]{:S(2)}) collective-permute-start(bf16[256,2,128]{2,0,1:T(8,128)(2,1)S(1)} %get-tuple-element.709), channel_id=1, source_target_pairs={{0,4},{4,8},{8,12},{12,16},{16,20},{20,24},{24,28},{28,0},{1,5},{5... | collective-permute-start | bytes 393224 | tf_op jit(solution)/shard_map/while/body/eval_jaxpr/ppermute | solution.py:18
  51.4 7.7 %collective-permute-start = (bf16[256,2,128]{2,0,1:T(8,128)(2,1)S(1)}, bf16[256,2,128]{2,0,1:T(8,128)(2,1)S(1)}, u32[]{:S(2)}, u32[]{:S(2)}) collective-permute-start(bf16[256,2,128]{2,0,1:T(8,128)(2,1)S(1)} %get-tuple-element.709), channel_id=1, source_target_pairs={{0,4},{4,8},{8,12},{12,16},{16,20},{20,24},{24,28},{28,0},{1,5},{5... | collective-permute-start | bytes 393224 | tf_op jit(solution)/shard_map/while/body/eval_jaxpr/ppermute | solution.py:18
  60.2 7.7 %collective-permute-start = (bf16[256,2,128]{2,0,1:T(8,128)(2,1)S(1)}, bf16[256,2,128]{2,0,1:T(8,128)(2,1)S(1)}, u32[]{:S(2)}, u32[]{:S(2)}) collective-permute-start(bf16[256,2,128]{2,0,1:T(8,128)(2,1)S(1)} %get-tuple-element.709), channel_id=1, source_target_pairs={{0,4},{4,8},{8,12},{12,16},{16,20},{20,24},{24,28},{28,0},{1,5},{5... | collective-permute-start | bytes 393224 | tf_op jit(solution)/shard_map/while/body/eval_jaxpr/ppermute | solution.py:18
  69.0 7.7 %collective-permute-start = (bf16[256,2,128]{2,0,1:T(8,128)(2,1)S(1)}, bf16[256,2,128]{2,0,1:T(8,128)(2,1)S(1)}, u32[]{:S(2)}, u32[]{:S(2)}) collective-permute-start(bf16[256,2,128]{2,0,1:T(8,128)(2,1)S(1)} %get-tuple-element.709), channel_id=1, source_target_pairs={{0,4},{4,8},{8,12},{12,16},{16,20},{20,24},{24,28},{28,0},{1,5},{5... | collective-permute-start | bytes 393224 | tf_op jit(solution)/shard_map/while/body/eval_jaxpr/ppermute | solution.py:18
  78.9 1.9 copy-start.15
  80.8 1.6 copy-start.2
  81.0 2.3 copy-start.17
  81.1 2.4 copy-start.21
  81.1 2.4 copy-start.24
  83.4 3.4 %copy-start.22 = (f32[2,8,256]{2,1,0:T(8,128)}, f32[2,8,256]{2,1,0:T(8,128)S(1)}, u32[]{:S(2)}) copy-start(f32[2,8,256]{2,1,0:T(8,128)S(1)} %copy.123) | copy-start | bytes 49156
  83.5 3.5 %copy-start.30 = (f32[2,256,256,8]{2,1,3,0:T(8,128)S(1)}, f32[2,256,256,8]{2,1,3,0:T(8,128)}, u32[]{:S(2)}) copy-start(f32[2,256,256,8]{2,1,3,0:T(8,128)} %get-tuple-element.597) | copy-start | bytes 12582916
  94.2 3.6 %copy-start.13 = (bf16[256,2,64]{2,0,1:T(8,128)(2,1)S(1)}, bf16[256,2,64]{2,0,1:T(8,128)(2,1)}, u32[]{:S(2)}) copy-start(bf16[256,2,64]{2,0,1:T(8,128)(2,1)} %copy-done.12) | copy-start | bytes 196612
  99.5 9.3 %collective-permute-start.1 = (bf16[256,2,2,128]{3,0,2,1:T(8,128)(2,1)}, bf16[256,2,2,128]{3,0,2,1:T(8,128)(2,1)S(1)}, u32[]{:S(2)}, u32[]{:S(2)}) collective-permute-start(bf16[256,2,2,128]{3,0,2,1:T(8,128)(2,1)} %get-tuple-element.747), channel_id=1, source_target_pairs={{0,4},{4,8},{8,12},{12,16},{16,20},{20,24},{24,28},{28,0},{1,5},{5... | collective-permute-start | bytes 786440 | tf_op jit(solution)/shard_map/while/body/eval_jaxpr/ppermute | solution.py:18
  99.5 15.8 %collective-permute-start.2 = (f32[256,2,2,128]{3,0,2,1:T(8,128)}, f32[256,2,2,128]{3,0,2,1:T(8,128)}, u32[]{:S(2)}, u32[]{:S(2)}) collective-permute-start(f32[256,2,2,128]{3,0,2,1:T(8,128)} %get-tuple-element.746), channel_id=1, source_target_pairs={{0,4},{4,8},{8,12},{12,16},{16,20},{20,24},{24,28},{28,0},{1,5},{5... | collective-permute-start | bytes 1572872 | tf_op jit(solution)/shard_map/while/body/eval_jaxpr/ppermute | solution.py:18
  108.8 1.2 copy-start.25
  117.3 9.3 %collective-permute-start.1 = (bf16[256,2,2,128]{3,0,2,1:T(8,128)(2,1)}, bf16[256,2,2,128]{3,0,2,1:T(8,128)(2,1)S(1)}, u32[]{:S(2)}, u32[]{:S(2)}) collective-permute-start(bf16[256,2,2,128]{3,0,2,1:T(8,128)(2,1)} %get-tuple-element.747), channel_id=1, source_target_pairs={{0,4},{4,8},{8,12},{12,16},{16,20},{20,24},{24,28},{28,0},{1,5},{5... | collective-permute-start | bytes 786440 | tf_op jit(solution)/shard_map/while/body/eval_jaxpr/ppermute | solution.py:18
  117.3 16.1 %collective-permute-start.2 = (f32[256,2,2,128]{3,0,2,1:T(8,128)}, f32[256,2,2,128]{3,0,2,1:T(8,128)}, u32[]{:S(2)}, u32[]{:S(2)}) collective-permute-start(f32[256,2,2,128]{3,0,2,1:T(8,128)} %get-tuple-element.746), channel_id=1, source_target_pairs={{0,4},{4,8},{8,12},{12,16},{16,20},{20,24},{24,28},{28,0},{1,5},{5... | collective-permute-start | bytes 1572872 | tf_op jit(solution)/shard_map/while/body/eval_jaxpr/ppermute | solution.py:18
  126.5 1.2 copy-start.25
  135.3 9.3 %collective-permute-start.1 = (bf16[256,2,2,128]{3,0,2,1:T(8,128)(2,1)}, bf16[256,2,2,128]{3,0,2,1:T(8,128)(2,1)S(1)}, u32[]{:S(2)}, u32[]{:S(2)}) collective-permute-start(bf16[256,2,2,128]{3,0,2,1:T(8,128)(2,1)} %get-tuple-element.747), channel_id=1, source_target_pairs={{0,4},{4,8},{8,12},{12,16},{16,20},{20,24},{24,28},{28,0},{1,5},{5... | collective-permute-start | bytes 786440 | tf_op jit(solution)/shard_map/while/body/eval_jaxpr/ppermute | solution.py:18
  135.3 16.3 %collective-permute-start.2 = (f32[256,2,2,128]{3,0,2,1:T(8,128)}, f32[256,2,2,128]{3,0,2,1:T(8,128)}, u32[]{:S(2)}, u32[]{:S(2)}) collective-permute-start(f32[256,2,2,128]{3,0,2,1:T(8,128)} %get-tuple-element.746), channel_id=1, source_target_pairs={{0,4},{4,8},{8,12},{12,16},{16,20},{20,24},{24,28},{28,0},{1,5},{5... | collective-permute-start | bytes 1572872 | tf_op jit(solution)/shard_map/while/body/eval_jaxpr/ppermute | solution.py:18
  153.5 9.3 %collective-permute-start.1 = (bf16[256,2,2,128]{3,0,2,1:T(8,128)(2,1)}, bf16[256,2,2,128]{3,0,2,1:T(8,128)(2,1)S(1)}, u32[]{:S(2)}, u32[]{:S(2)}) collective-permute-start(bf16[256,2,2,128]{3,0,2,1:T(8,128)(2,1)} %get-tuple-element.747), channel_id=1, source_target_pairs={{0,4},{4,8},{8,12},{12,16},{16,20},{20,24},{24,28},{28,0},{1,5},{5... | collective-permute-start | bytes 786440 | tf_op jit(solution)/shard_map/while/body/eval_jaxpr/ppermute | solution.py:18
  153.5 16.6 %collective-permute-start.2 = (f32[256,2,2,128]{3,0,2,1:T(8,128)}, f32[256,2,2,128]{3,0,2,1:T(8,128)}, u32[]{:S(2)}, u32[]{:S(2)}) collective-permute-start(f32[256,2,2,128]{3,0,2,1:T(8,128)} %get-tuple-element.746), channel_id=1, source_target_pairs={{0,4},{4,8},{8,12},{12,16},{16,20},{20,24},{24,28},{28,0},{1,5},{5... | collective-permute-start | bytes 1572872 | tf_op jit(solution)/shard_map/while/body/eval_jaxpr/ppermute | solution.py:18
  162.8 1.2 copy-start.25
  172.0 9.3 %collective-permute-start.1 = (bf16[256,2,2,128]{3,0,2,1:T(8,128)(2,1)}, bf16[256,2,2,128]{3,0,2,1:T(8,128)(2,1)S(1)}, u32[]{:S(2)}, u32[]{:S(2)}) collective-permute-start(bf16[256,2,2,128]{3,0,2,1:T(8,128)(2,1)} %get-tuple-element.747), channel_id=1, source_target_pairs={{0,4},{4,8},{8,12},{12,16},{16,20},{20,24},{24,28},{28,0},{1,5},{5... | collective-permute-start | bytes 786440 | tf_op jit(solution)/shard_map/while/body/eval_jaxpr/ppermute | solution.py:18
  172.0 16.8 %collective-permute-start.2 = (f32[256,2,2,128]{3,0,2,1:T(8,128)}, f32[256,2,2,128]{3,0,2,1:T(8,128)}, u32[]{:S(2)}, u32[]{:S(2)}) collective-permute-start(f32[256,2,2,128]{3,0,2,1:T(8,128)} %get-tuple-element.746), channel_id=1, source_target_pairs={{0,4},{4,8},{8,12},{12,16},{16,20},{20,24},{24,28},{28,0},{1,5},{5... | collective-permute-start | bytes 1572872 | tf_op jit(solution)/shard_map/while/body/eval_jaxpr/ppermute | solution.py:18
  181.3 1.2 copy-start.25
  190.7 9.3 %collective-permute-start.1 = (bf16[256,2,2,128]{3,0,2,1:T(8,128)(2,1)}, bf16[256,2,2,128]{3,0,2,1:T(8,128)(2,1)S(1)}, u32[]{:S(2)}, u32[]{:S(2)}) collective-permute-start(bf16[256,2,2,128]{3,0,2,1:T(8,128)(2,1)} %get-tuple-element.747), channel_id=1, source_target_pairs={{0,4},{4,8},{8,12},{12,16},{16,20},{20,24},{24,28},{28,0},{1,5},{5... | collective-permute-start | bytes 786440 | tf_op jit(solution)/shard_map/while/body/eval_jaxpr/ppermute | solution.py:18
  190.7 17.1 %collective-permute-start.2 = (f32[256,2,2,128]{3,0,2,1:T(8,128)}, f32[256,2,2,128]{3,0,2,1:T(8,128)}, u32[]{:S(2)}, u32[]{:S(2)}) collective-permute-start(f32[256,2,2,128]{3,0,2,1:T(8,128)} %get-tuple-element.746), channel_id=1, source_target_pairs={{0,4},{4,8},{8,12},{12,16},{16,20},{20,24},{24,28},{28,0},{1,5},{5... | collective-permute-start | bytes 1572872 | tf_op jit(solution)/shard_map/while/body/eval_jaxpr/ppermute | solution.py:18
  209.7 9.3 %collective-permute-start.1 = (bf16[256,2,2,128]{3,0,2,1:T(8,128)(2,1)}, bf16[256,2,2,128]{3,0,2,1:T(8,128)(2,1)S(1)}, u32[]{:S(2)}, u32[]{:S(2)}) collective-permute-start(bf16[256,2,2,128]{3,0,2,1:T(8,128)(2,1)} %get-tuple-element.747), channel_id=1, source_target_pairs={{0,4},{4,8},{8,12},{12,16},{16,20},{20,24},{24,28},{28,0},{1,5},{5... | collective-permute-start | bytes 786440 | tf_op jit(solution)/shard_map/while/body/eval_jaxpr/ppermute | solution.py:18
  209.7 17.3 %collective-permute-start.2 = (f32[256,2,2,128]{3,0,2,1:T(8,128)}, f32[256,2,2,128]{3,0,2,1:T(8,128)}, u32[]{:S(2)}, u32[]{:S(2)}) collective-permute-start(f32[256,2,2,128]{3,0,2,1:T(8,128)} %get-tuple-element.746), channel_id=1, source_target_pairs={{0,4},{4,8},{8,12},{12,16},{16,20},{20,24},{24,28},{28,0},{1,5},{5... | collective-permute-start | bytes 1572872 | tf_op jit(solution)/shard_map/while/body/eval_jaxpr/ppermute | solution.py:18
  228.9 12.1 %collective-permute-start.3 = (f32[256,2,2,128]{3,0,2,1:T(8,128)}, f32[256,2,2,128]{3,0,2,1:T(8,128)S(1)}, u32[]{:S(2)}, u32[]{:S(2)}) collective-permute-start(f32[256,2,2,128]{3,0,2,1:T(8,128)} %get-tuple-element.450), channel_id=1, source_target_pairs={{0,4},{4,8},{8,12},{12,16},{16,20},{20,24},{24,28},{28,0},{1,5},{5... | collective-permute-start | bytes 1572872 | tf_op jit(solution)/shard_map/ppermute | solution.py:18
  230.4 2.5 copy-start.1
  230.4 2.5 copy-start.9
  230.4 2.5 copy-start.27
  235.1 1.2 copy-start.3
  236.3 3.8 %copy-start.29 = (f32[128]{0:T(128)S(1)}, f32[128]{0:T(128)}, u32[]{:S(2)}) copy-start(f32[128]{0:T(128)} %param.18) | copy-start | bytes 1540
  236.3 4.8 %copy-start.7 = (f32[256,2,128]{2,0,1:T(8,128)S(1)}, f32[256,2,128]{2,0,1:T(8,128)}, u32[]{:S(2)}) copy-start(f32[256,2,128]{2,0,1:T(8,128)} %copy-done.6) | copy-start | bytes 786436
  240.1 1.5 copy-start.11
  (23 other events, 26.0 us)
where the time goes:
time: 293 us; the launch traced here: 292 us
  waiting for transfers between devices  107 us (37%)
  matrix products  54.6 us (19%)
  blocking collectives  48.7 us (17%)
  other arithmetic  39.4 us (13%)
  local copies, waits for them, and re-layouts  36.7 us (13%)
  starting transfers between devices  3.33 us (1%)
    ppermute x22, waiting for transfers between devices, passed_along(): return lax.ppermute(value, axis, pairs)  107 us
    psum x1, blocking collectives, on_device(): lax.psum((q_gain_part, k_gain_part), ('ctx', 'heads'))  48.7 us
    dot_general x15, matrix products, scores_of(): jnp.einsum('ikgd,jkd->kgij', q_rot, key_rot, preferred_element_type=jnp.f...  15.1 us
    unnamed x68, local copies, waits for them, and re-layouts  13.4 us
    add x7, other arithmetic, back_step(): grads_now = passed_along(grads_now, 'ctx', 1) + kv_part  13.3 us
    dot_general x8, matrix products, grad_terms(): jnp.einsum('ikgd,jkd->kgij', grad_heads, val_rot, preferred_element_type=...  12.1 us
    dot_general x8, matrix products, grad_terms(): jnp.einsum('kgij,jkd->ikgd', dscore, key_rot, preferred_element_type=jnp....  11.6 us
    dot_general x8, matrix products, grad_terms(): jnp.einsum('kgij,ikgd->jkd', weights_low, grad_heads, preferred_element_t...  10 us
  transfers between devices with their start and end apart: 22, of which 21 were waited for; matrix products, arithmetic and copies ran while one was open for 23% of the time, Pallas kernels for 0%

commit v1 on v0

v1 whole, which is shorter than its diff:
```python
import math

import jax
import jax.numpy as jnp
import numpy as np
from jax import lax
from jax.experimental import pallas as pl
from jax.experimental.pallas import tpu as pltpu
from jax.sharding import PartitionSpec as P

ROPE_BASE = 1000000.0
EPS = 1e-06
LOG2_E = 1.4426950408889634
HIDDEN = -100000.0
VMEM_LIMIT = 48 * 1024 * 1024
F32 = jnp.float32
BF16 = jnp.bfloat16


def rope_rows(count, head_dim):
    half = head_dim // 2
    frequency = np.exp(
        np.arange(half, dtype=np.float32) * np.float32(-2.0 * math.log(ROPE_BASE) / head_dim)
    ).astype(np.float32)
    angles = np.arange(count, dtype=np.float32)[:, None] * frequency[None, :]
    cos = np.cos(angles.astype(np.float64)).astype(np.float32)
    sin = np.sin(angles.astype(np.float64)).astype(np.float32)
    return np.concatenate([cos, cos], 1), np.concatenate([-sin, sin], 1)


def turned(rows, cos, sin):
    return rows * cos + pltpu.roll(rows, rows.shape[-1] // 2, 1) * sin


def turned_back(rows, cos, sin):
    return rows * cos - pltpu.roll(rows, rows.shape[-1] // 2, 1) * sin


def inverse_rms(rows):
    return lax.rsqrt(jnp.mean(rows * rows, -1, keepdims=True) + EPS)


def own_tables(depth_ref, cos_ref, sin_ref, blocks, block_len):
    starts = [pl.multiple_of(depth_ref[a] * block_len, block_len) for a in range(blocks)]
    cos = jnp.concatenate([cos_ref[pl.ds(s, block_len), :] for s in starts], 0)
    sin = jnp.concatenate([sin_ref[pl.ds(s, block_len), :] for s in starts], 0)
    return cos, sin


def dot_nt(lhs, rhs):
    return lax.dot_general(lhs, rhs, (((1,), (1,)), ((), ())), preferred_element_type=F32)


def dot_nn(lhs, rhs):
    return lax.dot_general(lhs, rhs, (((1,), (0,)), ((), ())), preferred_element_type=F32)


def prep_kernel(blocks, block_len, depth_ref, cos_ref, sin_ref, gain_ref, q_ref, grad_ref, out_ref,
                q_rot_ref, grad_heads_ref, delta_ref):
    heads = q_rot_ref.shape[0]
    head_dim = q_rot_ref.shape[2]
    cos, sin = own_tables(depth_ref, cos_ref, sin_ref, blocks, block_len)
    gain = gain_ref[...]
    for head in range(heads):
        cols = pl.ds(head * head_dim, head_dim)
        rows = q_ref[:, cols].astype(F32)
        scaled = rows * inverse_rms(rows) * gain
        q_rot_ref[head] = turned(scaled, cos, sin).astype(BF16)
        grad = grad_ref[:, cols]
        grad_heads_ref[head] = grad
        product = grad.astype(F32) * out_ref[:, cols].astype(F32)
        delta_ref[head] = jnp.sum(jnp.transpose(product), 0, keepdims=True)


def main_kernel(blocks, block_len, tree_dev, first_pos, inv_root,
                anc_ref, place_ref, cos_ref, sin_ref, gain_ref, k_ref, v_ref, q_ref, grad_ref, delta_ref,
                dq_ref, dk_ref, dv_ref, gain_part_ref,
                slot_blk, slot_bits, slot_depth, keys, keys_t, vals, normed, expo, mass, w_all, ds_all):
    group = q_ref.shape[0]
    tokens = q_ref.shape[1]
    head_dim = q_ref.shape[2]
    slots = tree_dev * blocks
    place = place_ref[0]

    for i in range(slots):
        slot_blk[i] = 0
        slot_bits[i] = 0
        slot_depth[i] = 0

    def merge(b, carry):
        count, steps = carry[0], carry[1:]
        bits = jnp.int32(0)
        depth = jnp.int32(0)
        later = []
        for a in range(blocks):
            hit = anc_ref[a, jnp.minimum(steps[a], slots - 1)] == b
            bits = bits | jnp.where(hit, 1 << a, 0)
            depth = jnp.where(hit, steps[a], depth)
            later.append(steps[a] + jnp.where(hit, 1, 0))
        own = b - place * blocks
        slot = jnp.where(own >= 0, own, jnp.minimum(count, slots - 1))
        slot_blk[slot] = b
        slot_bits[slot] = bits
        slot_depth[slot] = depth
        count = count + jnp.where((own < 0) & (bits != 0), 1, 0)
        return (count, *later)

    zero = jnp.int32(0)
    count = lax.fori_loop(0, (place + 1) * blocks, merge, (jnp.int32(blocks), *([zero] * blocks)))[0]
    chunks = (count + blocks - 1) // blocks

    lane = lax.broadcasted_iota(jnp.int32, (1, head_dim), 1)
    row_block = lax.broadcasted_iota(jnp.int32, (tokens, head_dim), 0) // block_len
    row_tag = (row_block == lax.broadcasted_iota(jnp.int32, (tokens, head_dim), 1)).astype(BF16)
    gain = gain_ref[...]

    def where_of(slot):
        b = slot_blk[slot]
        position = lax.rem(b // blocks + first_pos, tree_dev)
        return position, pl.ds(pl.multiple_of(lax.rem(b, blocks) * block_len, block_len), block_len)

    def tables_of(slot):
        at = pl.ds(pl.multiple_of(slot_depth[slot] * block_len, block_len), block_len)
        return cos_ref[at, :], sin_ref[at, :]

    def load_chunk(c):
        for j in range(blocks):
            slot = c * blocks + j
            position, rows = where_of(slot)
            raw = k_ref[position, rows, :].astype(F32)
            unit = raw * inverse_rms(raw)
            cos, sin = tables_of(slot)
            rotated = turned(unit * gain, cos, sin).astype(BF16)
            here = pl.ds(j * block_len, block_len)
            normed[c, here, :] = unit
            keys[c, here, 0:head_dim] = rotated
            bits = jnp.where(slot < count, slot_bits[slot], 0)
            shown = jnp.zeros((1, head_dim), F32)
            for a in range(blocks):
                seen = lax.rem(lax.shift_right_logical(bits, a), 2)
                shown = jnp.where((lane == a) & (seen == 0), HIDDEN, shown)
            keys[c, here, head_dim:] = jnp.broadcast_to(shown, (block_len, head_dim)).astype(BF16)
            vals[c, here, :] = v_ref[position, rows, :]
        keys_t[c] = jnp.transpose(keys[c, :, 0:head_dim].astype(F32)).astype(BF16)

    def masses(c, causal):
        load_chunk(c)
        for g in range(group):
            tagged = jnp.concatenate([q_ref[g], row_tag], 1)
            e = jnp.exp2(dot_nt(keys[c], tagged) * (inv_root * LOG2_E))
            if causal is not None:
                e = jnp.where(causal, e, 0.0)
            expo[c, g] = e
            part = jnp.sum(e.reshape(tokens // 8, 8, tokens), 0)
            if causal is not None:
                mass[g] = part
            else:
                mass[g] = mass[g] + part

    key_row = lax.broadcasted_iota(jnp.int32, (tokens, tokens), 0)
    query_col = lax.broadcasted_iota(jnp.int32, (tokens, tokens), 1)
    masses(0, key_row <= query_col)

    @pl.loop(1, chunks)
    def _(c):
        masses(c, None)

    for g in range(group):
        total = jnp.sum(mass[g], 0, keepdims=True)
        mass[g] = jnp.broadcast_to(1.0 / total, (8, tokens))
        dq_ref[g] = jnp.zeros((head_dim, tokens), F32)
    dk_ref[...] = jnp.zeros(dk_ref.shape, dk_ref.dtype)
    dv_ref[...] = jnp.zeros(dv_ref.shape, dv_ref.dtype)
    gain_part_ref[...] = jnp.zeros(gain_part_ref.shape, F32)

    @pl.loop(0, chunks)
    def _(c):
        for g in range(group):
            grad_prob = dot_nt(vals[c], grad_ref[g])
            weights = expo[c, g] * mass[g, 0:1, :]
            dscore = (weights * (grad_prob - delta_ref[g])).astype(BF16)
            w_all[:, pl.ds(g * tokens, tokens)] = weights.astype(BF16)
            ds_all[:, pl.ds(g * tokens, tokens)] = dscore
            dq_ref[g] = dq_ref[g] + dot_nn(keys_t[c], dscore)
        dv = dot_nn(w_all[...], grad_ref[...].reshape(group * tokens, head_dim))
        dk = dot_nn(ds_all[...], q_ref[...].reshape(group * tokens, head_dim)) * inv_root
        gain_part = jnp.zeros((1, head_dim), F32)
        for j in range(blocks):
            slot = c * blocks + j

            @pl.when(slot < count)
            def _():
                position, rows = where_of(slot)
                here = slice(j * block_len, (j + 1) * block_len)
                dk_ref[position, rows, :] = dk[here].astype(dk_ref.dtype)
                dv_ref[position, rows, :] = dv[here].astype(dv_ref.dtype)
                cos, sin = tables_of(slot)
                term = turned_back(dk[here], cos, sin) * normed[c, here, :]
                gain_part_ref[0] = gain_part_ref[0] + jnp.sum(term.reshape(block_len // 8, 8, head_dim), 0)


def query_kernel(blocks, block_len, inv_root, depth_ref, cos_ref, sin_ref, gain_ref, q_ref, dq_ref, out_ref, part_ref):
    heads, head_dim, tokens = dq_ref.shape
    cos, sin = own_tables(depth_ref, cos_ref, sin_ref, blocks, block_len)
    gain = gain_ref[...]
    part = jnp.zeros((8, head_dim), F32)
    for head in range(heads):
        cols = pl.ds(head * head_dim, head_dim)
        rows = q_ref[:, cols].astype(F32)
        recip = inverse_rms(rows)
        normed = rows * recip
        scaled_grad = turned_back(jnp.transpose(dq_ref[head]), cos, sin) * inv_root
        term = scaled_grad * normed
        part = part + jnp.sum(term.reshape(tokens // 8, 8, head_dim), 0)
        inner = jnp.mean(term * gain, -1, keepdims=True)
        out_ref[:, cols] = (recip * (scaled_grad * gain - normed * inner)).astype(BF16)
    part_ref[...] = part


def key_kernel(blocks, block_len, depth_ref, cos_ref, sin_ref, gain_ref, k_ref, dk_ref, dv_ref, dk_out_ref, dv_out_ref):
    head_dim = gain_ref.shape[1]
    cos, sin = own_tables(depth_ref, cos_ref, sin_ref, blocks, block_len)
    gain = gain_ref[...]
    for head in range(k_ref.shape[1] // head_dim):
        cols = pl.ds(head * head_dim, head_dim)
        rows = k_ref[:, cols].astype(F32)
        recip = inverse_rms(rows)
        normed = rows * recip
        grad = turned_back(dk_ref[:, cols].astype(F32), cos, sin) * gain
        inner = jnp.mean(grad * normed, -1, keepdims=True)
        dk_out_ref[:, cols] = (recip * (grad - normed * inner)).astype(BF16)
    dv_out_ref[...] = dv_ref[...].astype(BF16)


def on_device(q_raw, k_raw, values, saved_out, out_grad, q_gain, k_gain, ancestors):
    tokens = q_raw.shape[0]
    head_dim = q_gain.shape[0]
    kv_heads = k_raw.shape[1] // head_dim
    heads = q_raw.shape[1] // head_dim
    group = heads // kv_heads
    blocks = ancestors.shape[0]
    tree_blocks = ancestors.shape[1]
    block_len = tokens // blocks
    tree_dev = tree_blocks // blocks
    cycle = lax.axis_size("ctx")
    inv_root = 1.0 / math.sqrt(head_dim)
    place = (lax.axis_index("ctx") - 1 + cycle) % cycle % tree_dev
    if cycle == tree_dev:
        groups, first_pos = None, 1
    else:
        groups = [
            [(tree * tree_dev + 1 + step) % cycle for step in range(tree_dev)]
            for tree in range(cycle // tree_dev)
        ]
        first_pos = 0

    depth = jnp.sum((ancestors >= 0).astype(jnp.int32), 1) - 1
    total_blocks = blocks * cycle
    in_tree = jnp.where(
        ancestors >= 0, (ancestors - blocks + total_blocks) % total_blocks % tree_blocks, -1
    )
    place = place.reshape(1).astype(jnp.int32)
    cos_np, sin_np = rope_rows(tree_blocks * block_len, head_dim)
    cos, sin = jnp.asarray(cos_np), jnp.asarray(sin_np)
    q_gain_row, k_gain_row = q_gain.reshape(1, head_dim), k_gain.reshape(1, head_dim)

    k_all = lax.all_gather(k_raw, "ctx", axis_index_groups=groups)
    v_all = lax.all_gather(values, "ctx", axis_index_groups=groups)

    params = pltpu.CompilerParams(vmem_limit_bytes=VMEM_LIMIT)
    smem = pl.BlockSpec(memory_space=pltpu.SMEM)
    vmem = pl.BlockSpec(memory_space=pltpu.VMEM)
    sds = jax.ShapeDtypeStruct

    q_rot, grad_heads, delta = pl.pallas_call(
        lambda *refs: prep_kernel(blocks, block_len, *refs),
        out_shape=(
            sds((heads, tokens, head_dim), BF16),
            sds((heads, tokens, head_dim), BF16),
            sds((heads, 1, tokens), F32),
        ),
        in_specs=[smem] + [vmem] * 6,
        out_specs=(vmem, vmem, vmem),
        compiler_params=params,
        name="prep",
    )(depth, cos, sin, q_gain_row, q_raw, out_grad, saved_out)

    slots = tree_blocks
    keys_here = pl.BlockSpec((tree_dev, tokens, head_dim), lambda h: (0, 0, h))
    rows_here = pl.BlockSpec((group, tokens, head_dim), lambda h: (h, 0, 0))
    whole = lambda *shape: pl.BlockSpec(shape, lambda h: (0,) * len(shape))
    dq_t, dk_part, dv_part, k_gain_part = pl.pallas_call(
        lambda *refs: main_kernel(blocks, block_len, tree_dev, first_pos, inv_root, *refs),
        grid=(kv_heads,),
        out_shape=(
            sds((heads, head_dim, tokens), F32),
            sds((tree_dev, tokens, kv_heads * head_dim), BF16),
            sds((tree_dev, tokens, kv_heads * head_dim), BF16),
            sds((kv_heads, 8, head_dim), F32),
        ),
        in_specs=[
            smem,
            smem,
            whole(tree_blocks * block_len, head_dim),
            whole(tree_blocks * block_len, head_dim),
            whole(1, head_dim),
            keys_here,
            keys_here,
            rows_here,
            rows_here,
            pl.BlockSpec((group, 1, tokens), lambda h: (h, 0, 0)),
        ],
        out_specs=(
            pl.BlockSpec((group, head_dim, tokens), lambda h: (h, 0, 0)),
            keys_here,
            keys_here,
            pl.BlockSpec((1, 8, head_dim), lambda h: (h, 0, 0)),
        ),
        scratch_shapes=[
            pltpu.SMEM((slots,), jnp.int32),
            pltpu.SMEM((slots,), jnp.int32),
            pltpu.SMEM((slots,), jnp.int32),
            pltpu.VMEM((tree_dev, tokens, 2 * head_dim), BF16),
            pltpu.VMEM((tree_dev, head_dim, tokens), BF16),
            pltpu.VMEM((tree_dev, tokens, head_dim), BF16),
            pltpu.VMEM((tree_dev, tokens, head_dim), F32),
            pltpu.VMEM((tree_dev, group, tokens, tokens), F32),
            pltpu.VMEM((group, 8, tokens), F32),
            pltpu.VMEM((tokens, group * tokens), BF16),
            pltpu.VMEM((tokens, group * tokens), BF16),
        ],
        compiler_params=params,
        name="attend",
    )(in_tree, place, cos, sin, k_gain_row, k_all, v_all, q_rot, grad_heads, delta)

    dk_sum = lax.psum_scatter(dk_part, "ctx", scatter_dimension=0, axis_index_groups=groups)
    dv_sum = lax.psum_scatter(dv_part, "ctx", scatter_dimension=0, axis_index_groups=groups)

    dq_raw, q_gain_part = pl.pallas_call(
        lambda *refs: query_kernel(blocks, block_len, inv_root, *refs),
        out_shape=(sds((tokens, heads * head_dim), BF16), sds((8, head_dim), F32)),
        in_specs=[smem] + [vmem] * 5,
        out_specs=(vmem, vmem),
        compiler_params=params,
        name="query_back",
    )(depth, cos, sin, q_gain_row, q_raw, dq_t)

    gains = jnp.stack([jnp.sum(q_gain_part, 0), jnp.sum(k_gain_part, (0, 1))])
    gains = lax.psum(gains, ("ctx", "heads"))

    dk_raw, dv = pl.pallas_call(
        lambda *refs: key_kernel(blocks, block_len, *refs),
        out_shape=(sds(k_raw.shape, BF16), sds(k_raw.shape, BF16)),
        in_specs=[smem] + [vmem] * 6,
        out_specs=(vmem, vmem),
        compiler_params=params,
        name="key_back",
    )(depth, cos, sin, k_gain_row, k_raw, dk_sum, dv_sum)
    return (dq_raw, dk_raw, dv, gains[0], gains[1])


def solution(mesh):
    split = P("ctx", "heads")
    return jax.shard_map(
        on_device,
        mesh=mesh,
        in_specs=(split, split, split, split, split, P(), P(), P("ctx", None)),
        out_specs=(split, split, split, P(), P()),
        check_vma=False,
    )
```

time: 293 us -> 293 us (level)
  Pallas kernels: 0 us -> 71.4 us
  matrix products: 54.6 us -> 0 us
  waiting for transfers between devices: 107 us -> 158 us
  other arithmetic: 39.4 us -> 0.86 us
  local copies, waits for them, and re-layouts: 36.7 us -> 14 us
  between operations: 1.21 us -> 13.8 us
  blocking collectives: 48.7 us -> 37.1 us
  starting transfers between devices: 3.33 us -> 0.16 us
    ppermute x22 -> x0, waiting for transfers between devices: 107 us -> none  [passed_along(): return lax.ppermute(value, axis, pairs)]
    reduce_scatter x0 -> x2, waiting for transfers between devices: none -> 82.1 us  [the longest x1 66.2 us: on_device(): lax.psum_scatter(dv_part, 'ctx', scatter_dimension=0, axis_index_groups=g...]
    all_gather x0 -> x2, waiting for transfers between devices: none -> 73.7 us  [the longest x1 41.1 us: on_device(): k_all = lax.all_gather(k_raw, 'ctx', axis_index_groups=groups)]
    pallas_call x0 -> x4, Pallas kernels: none -> 71.4 us  [the longest x1 60.8 us: on_device(): pl.pallas_call(lambda *refs: main_kernel(blocks, block_len, tree_dev, fir...]
    dot_general x47 -> x0, matrix products: 54.6 us -> none  [the longest x15 15.1 us: scores_of(): jnp.einsum('ikgd,jkd->kgij', q_rot, key_rot, preferred_element_type=jnp.f...]
    add x31 -> x0, other arithmetic: 16.1 us -> none  [the longest x7 13.3 us: back_step(): grads_now = passed_along(grads_now, 'ctx', 1) + kv_part]
    psum x1, blocking collectives: 48.7 us -> 37.1 us  [on_device(): gains = lax.psum(gains, ('ctx', 'heads'))]
    while x56 -> x0, local copies, waits for them, and re-layouts: 8.61 us -> none
  transfers between devices with their start and end apart: 22 -> 4, of which waited for: 21 -> 4; matrix products, arithmetic and copies ran while one was open for 23% -> 0% of each run, Pallas kernels for 0% -> 3%
where the time goes in v1:
time: 293 us; the launch traced here: 295 us
  waiting for transfers between devices  158 us (54%)
  Pallas kernels  71.4 us (24%)
  blocking collectives  37.1 us (13%)
  local copies, waits for them, and re-layouts  14 us (5%)
  between operations  13.8 us (5%)
    reduce_scatter x1, waiting for transfers between devices, on_device(): lax.psum_scatter(dv_part, 'ctx', scatter_dimension=0, axis_index_groups=g...  66.2 us
    pallas_call x1, Pallas kernels, on_device(): pl.pallas_call(lambda *refs: main_kernel(blocks, block_len, tree_dev, fir...  60.8 us
    all_gather x1, waiting for transfers between devices, on_device(): k_all = lax.all_gather(k_raw, 'ctx', axis_index_groups=groups)  41.1 us
    psum x1, blocking collectives, on_device(): gains = lax.psum(gains, ('ctx', 'heads'))  37.1 us
    all_gather x1, waiting for transfers between devices, on_device(): v_all = lax.all_gather(values, 'ctx', axis_index_groups=groups)  32.6 us
    reduce_scatter x1, waiting for transfers between devices, on_device(): lax.psum_scatter(dk_part, 'ctx', scatter_dimension=0, axis_index_groups=g...  15.9 us
    unnamed x36, local copies, waits for them, and re-layouts  13.5 us
  transfers between devices with their start and end apart: 4, of which 4 were waited for; matrix products, arithmetic and copies ran while one was open for 0% of the time, Pallas kernels for 3%

profile of v1, /device:TPU:0, one launch (start us, length us, event | category | flops | bytes accessed | tf_op | source)
XLA Modules:
  0.0 295.2 jit_solution(11249638936943321982)
XLA Ops:
  7.2 0.0 all-gather.7.cloned.1.call-start
  7.2 0.7 all-gather.7.cloned.1.call-update
  7.9 0.0 all-gather.5.cloned.1.call-start
  7.9 0.7 all-gather.5.cloned.1.call-update
  8.6 0.0 reduce-scatter.3.cloned.1.call-start
  8.7 0.8 fusion.2
  9.5 0.0 copy-start
  9.6 1.2 copy-done
  10.8 0.0 copy-start.2
  10.8 1.2 copy-done.2
  12.0 1.2 copy-done.4
  13.2 0.0 copy-start.15
  13.2 0.7 copy-done.15
  13.9 0.0 copy-start.1
  13.9 0.0 copy-start.3
  13.9 0.0 copy-start.17
  13.9 4.5 %prep.1 = (bf16[16,256,128]{2,1,0:T(8,128)(2,1)S(1)}, bf16[16,256,128]{2,1,0:T(8,128)(2,1)S(1)}, f32[16,1,256]{2,1,0:T(1,128)S(1)}) custom-call(s32[4]{0:T(128)S(1)} %broadcast_add_fusion.refs_0_, f32[2048,128]{1,0:T(8,128)S(1)} %copy-done.2, f32[2048,128]{1,0:T(8,128)S(1)} %copy-done, f32[1,128]{1,0:T(1,128)S(1)} %bitcast.16, ...), custom_call_target="tpu_custom_call" | custom-call | tf_op jit(solution)/shard_map/prep/pallas_call | solution.py:275
  18.4 0.0 copy-start.8
  18.4 1.0 copy-done.8
  19.4 0.0 copy-start.9
  19.4 1.0 copy-done.9
  20.4 32.6 %all-gather.7.cloned.1.call-done = bf16[2048,256]{1,0:T(8,128)(2,1)} async-done(((bf16[256,256]{1,0:T(8,128)(2,1)}), bf16[2048,256]{1,0:T(8,128)(2,1)}) %all-gather.7.cloned.1.call-update) | async-done | bytes 1048592 | tf_op jit(solution)/shard_map/all_gather | solution.py:268
  53.0 41.1 %all-gather.5.cloned.1.call-done = bf16[2048,256]{1,0:T(8,128)(2,1)} async-done(((bf16[256,256]{1,0:T(8,128)(2,1)}), bf16[2048,256]{1,0:T(8,128)(2,1)}) %all-gather.5.cloned.1.call-update) | async-done | bytes 1048592 | tf_op jit(solution)/shard_map/all_gather | solution.py:267
  94.1 0.0 copy-done.1
  94.1 0.0 copy-done.3
  94.1 0.0 copy-done.17
  94.1 0.0 copy-start.7
  94.1 1.2 copy-done.7
  95.3 60.8 %attend.1 = (f32[16,128,256]{2,1,0:T(8,128)}, bf16[8,256,256]{2,1,0:T(8,128)(2,1)S(1)}, bf16[8,256,256]{2,1,0:T(8,128)(2,1)S(1)}, f32[2,8,128]{2,1,0:T(8,128)S(1)}) custom-call(s32[4,32]{1,0:T(4,128)S(1)} %get-tuple-element.27.refs_0_, s32[1]{0:T(128)} %bitcast.1.refs_1_, f32[2048,128]{1,0:T(8,128)S(1)} %copy-done.3, f32[2048,128]{1,0:T(8,128)S(1)} %copy-done.1, ...), custom_call_target="tpu_custom_call" | custom-call | tf_op jit(solution)/shard_map/attend/pallas_call | solution.py:292
  156.1 0.0 copy-start.10
  156.1 1.0 copy-done.10
  157.0 0.0 copy-start.11
  157.0 1.0 copy-done.11
  158.0 0.0 reduce-scatter.3.cloned.1.call-update
  158.1 0.0 reduce-scatter.5.cloned.1.call-start
  158.1 0.5 reduce-scatter.5.cloned.1.call-update
  158.6 0.6 copy-done.5
  159.3 0.0 copy-done.16
  159.3 1.6 copy-done.6
  160.9 4.6 %query_back.1 = (bf16[256,2048]{1,0:T(8,128)(2,1)}, f32[8,128]{1,0:T(8,128)S(1)}) custom-call(s32[4]{0:T(128)S(1)} %broadcast_add_fusion.refs_0_, f32[2048,128]{1,0:T(8,128)S(1)} %copy-done.3, f32[2048,128]{1,0:T(8,128)S(1)} %copy-done.1, f32[1,128]{1,0:T(1,128)S(1)} %bitcast.17, bf16[256,2048]{1,0:T(8,128)(2,1)S(1)} %copy-done.5, f32[16,128,256]{2,1,0:T(8,128)S(1)} %copy-done.6), custom_call_target="tpu_custom_call" | custom-call | tf_op jit(solution)/shard_map/query_back/pallas_call | solution.py:339
  165.5 37.1 %psum.7 = f32[2,128]{1,0:T(2,128)S(1)} all-reduce(f32[2,128]{1,0:T(2,128)S(1)} %pad_maximum_fusion), channel_id=1, replica_groups=mesh['ctx'=8,'heads'=4] {'ctx','heads'}, use_global_device_ids=true, to_apply=%region_5.6 | all-reduce | flops 256 | bytes 2048 | tf_op jit(solution)/shard_map/psum | solution.py:349
  202.6 0.5 slice_bitcast_fusion
  203.1 15.9 %reduce-scatter.3.cloned.1.call-done = bf16[1,256,256]{2,1,0:T(8,128)(2,1)} async-done(((bf16[8,256,256]{2,1,0:T(8,128)(2,1)}), bf16[1,256,256]{2,1,0:T(8,128)(2,1)}) %reduce-scatter.3.cloned.1.call-update) | async-done | bytes 131088 | tf_op jit(solution)/shard_map/reduce_scatter | solution.py:336
  219.0 66.2 %reduce-scatter.5.cloned.1.call-done = bf16[1,256,256]{2,1,0:T(8,128)(2,1)} async-done(((bf16[8,256,256]{2,1,0:T(8,128)(2,1)}), bf16[1,256,256]{2,1,0:T(8,128)(2,1)}) %reduce-scatter.5.cloned.1.call-update) | async-done | bytes 131088 | tf_op jit(solution)/shard_map/reduce_scatter | solution.py:337
  285.2 0.0 copy-done.12
  285.2 0.9 copy-done.13
  286.1 0.9 copy-done.14
  287.0 1.6 key_back.1
  (11 shorter events, 0.1 us)
Async XLA Ops:
  7.2 45.8 %all-gather.7.cloned.1.call-start = ((), (), s32[]{:S(2)}) async-start(), calls=%async_computation.5 | async-start | bytes 1179648 | tf_op jit(solution)/shard_map/all_gather | solution.py:268
  7.9 86.2 %all-gather.5.cloned.1.call-start = ((), (), s32[]{:S(2)}) async-start(), calls=%async_computation.4 | async-start | bytes 1179648 | tf_op jit(solution)/shard_map/all_gather | solution.py:267
  8.6 210.4 %reduce-scatter.3.cloned.1.call-start = ((), (), s32[]{:S(2)}) async-start(), calls=%async_computation.2 | async-start | bytes 1179648 | tf_op jit(solution)/shard_map/reduce_scatter | solution.py:336
  9.5 1.2 copy-start
  10.8 1.2 copy-start.2
  12.0 1.2 copy-start.4
  13.2 0.7 copy-start.15
  13.9 80.2 %copy-start.1 = (f32[2048,128]{1,0:T(8,128)S(1)}, f32[2048,128]{1,0:T(8,128)}, u32[]{:S(2)}) copy-start(f32[2048,128]{1,0:T(8,128)} %constant.63.clone.refs_2_.refs_3_) | copy-start | bytes 3145732
  13.9 80.2 %copy-start.3 = (f32[2048,128]{1,0:T(8,128)S(1)}, f32[2048,128]{1,0:T(8,128)}, u32[]{:S(2)}) copy-start(f32[2048,128]{1,0:T(8,128)} %constant.62.clone.refs_1_.refs_2_) | copy-start | bytes 3145732
  13.9 80.2 %copy-start.17 = (f32[128]{0:T(128)S(1)}, f32[128]{0:T(128)}, u32[]{:S(2)}) copy-start(f32[128]{0:T(128)} %param.16) | copy-start | bytes 1540
  18.4 1.0 copy-start.8
  19.4 1.0 copy-start.9
  94.1 1.2 copy-start.7
  156.1 1.0 copy-start.10
  157.0 1.0 copy-start.11
  158.0 1.2 copy-start.5
  158.0 1.2 copy-start.16
  158.1 127.2 %reduce-scatter.5.cloned.1.call-start = ((), (), s32[]{:S(2)}) async-start(), calls=%async_computation.3 | async-start | bytes 1179648 | tf_op jit(solution)/shard_map/reduce_scatter | solution.py:337
  159.3 1.6 copy-start.6
  160.9 124.4 %copy-start.12 = (bf16[256,256]{1,0:T(8,128)(2,1)S(1)}, bf16[256,256]{1,0:T(8,128)(2,1)}, u32[]{:S(2)}) copy-start(bf16[256,256]{1,0:T(8,128)(2,1)} %refs_4_.5) | copy-start | bytes 393220
  285.2 0.9 copy-start.13
  286.1 0.9 copy-start.14
Sparse Core Ops, SparseCore 0:
  10.1 42.8 all-gather.6
  55.1 38.8 all-gather.4
  158.2 60.8 reduce-scatter.2
  222.7 62.5 reduce-scatter.4

commit v2 on v1

v2 whole, which is shorter than its diff:
```python
import math

import jax
import jax.numpy as jnp
import numpy as np
from jax import lax
from jax.experimental import pallas as pl
from jax.experimental.pallas import tpu as pltpu
from jax.sharding import PartitionSpec as P

ROPE_BASE = 1000000.0
EPS = 1e-06
LOG2_E = 1.4426950408889634
HIDDEN = -100000.0
VMEM_LIMIT = 48 * 1024 * 1024
GATHER_RELAYED = (True, False)
COLLECT_RELAYED = (False, True)
F32 = jnp.float32
BF16 = jnp.bfloat16


def rope_rows(count, head_dim):
    half = head_dim // 2
    frequency = np.exp(
        np.arange(half, dtype=np.float32) * np.float32(-2.0 * math.log(ROPE_BASE) / head_dim)
    ).astype(np.float32)
    angles = np.arange(count, dtype=np.float32)[:, None] * frequency[None, :]
    cos = np.cos(angles.astype(np.float64)).astype(np.float32)
    sin = np.sin(angles.astype(np.float64)).astype(np.float32)
    return np.concatenate([cos, cos], 1), np.concatenate([-sin, sin], 1)


def turned(rows, cos, sin):
    return rows * cos + pltpu.roll(rows, rows.shape[-1] // 2, 1) * sin


def turned_back(rows, cos, sin):
    return rows * cos - pltpu.roll(rows, rows.shape[-1] // 2, 1) * sin


def inverse_rms(rows):
    return lax.rsqrt(jnp.mean(rows * rows, -1, keepdims=True) + EPS)


def own_tables(depth_ref, cos_ref, sin_ref, blocks, block_len):
    starts = [pl.multiple_of(depth_ref[a] * block_len, block_len) for a in range(blocks)]
    cos = jnp.concatenate([cos_ref[pl.ds(s, block_len), :] for s in starts], 0)
    sin = jnp.concatenate([sin_ref[pl.ds(s, block_len), :] for s in starts], 0)
    return cos, sin


def dot_nt(lhs, rhs):
    return lax.dot_general(lhs, rhs, (((1,), (1,)), ((), ())), preferred_element_type=F32)


def dot_nn(lhs, rhs):
    return lax.dot_general(lhs, rhs, (((1,), (0,)), ((), ())), preferred_element_type=F32)


def plan_kernel(blocks, tree_dev, place_ref, anc_ref, plan_ref):
    slots = tree_dev * blocks
    place = place_ref[0]
    here = lax.rem(place + 1, tree_dev)
    for row in range(4):
        for i in range(slots):
            plan_ref[row, i] = 0

    def merge(b, carry):
        count, steps = carry[0], carry[1:]
        bits = jnp.int32(0)
        depth = jnp.int32(0)
        later = []
        for a in range(blocks):
            hit = anc_ref[a, jnp.minimum(steps[a], slots - 1)] == b
            bits = bits | jnp.where(hit, 1 << a, 0)
            depth = jnp.where(hit, steps[a], depth)
            later.append(steps[a] + jnp.where(hit, 1, 0))
        own = b - place * blocks
        slot = jnp.where(own >= 0, own, jnp.minimum(count, slots - 1))
        there = lax.rem(b // blocks + 1, tree_dev)
        odd = lax.rem(here + there, 2)
        near = here + odd * (1 - 2 * lax.rem(here, 2))
        piece = odd * (tree_dev // 2) + lax.rem(near - there + tree_dev, tree_dev) // 2
        plan_ref[0, slot] = piece
        plan_ref[1, slot] = lax.rem(b, blocks)
        plan_ref[2, slot] = depth
        plan_ref[3, slot] = bits
        count = count + jnp.where((own < 0) & (bits != 0), 1, 0)
        return (count, *later)

    zero = jnp.int32(0)
    count = lax.fori_loop(0, (place + 1) * blocks, merge, (jnp.int32(blocks), *([zero] * blocks)))[0]
    for i in range(slots):
        plan_ref[4, i] = count


def prep_kernel(blocks, block_len, depth_ref, cos_ref, sin_ref, gain_ref, q_ref, grad_ref, out_ref,
                q_ref_t, q_rot_ref, grad_t_ref, grad_heads_ref, delta_ref):
    heads, tokens, head_dim = q_rot_ref.shape
    cos, sin = own_tables(depth_ref, cos_ref, sin_ref, blocks, block_len)
    gain = gain_ref[...]
    tag_row = lax.broadcasted_iota(jnp.int32, (head_dim, tokens), 0)
    tag_col = lax.broadcasted_iota(jnp.int32, (head_dim, tokens), 1) // block_len
    tag = (tag_row == tag_col).astype(BF16)
    for head in range(heads):
        cols = pl.ds(head * head_dim, head_dim)
        rows = q_ref[:, cols].astype(F32)
        rotated = turned(rows * inverse_rms(rows) * gain, cos, sin)
        q_rot_ref[head] = rotated.astype(BF16)
        q_ref_t[head, 0:head_dim, :] = jnp.transpose(rotated).astype(BF16)
        q_ref_t[head, head_dim:, :] = tag
        grad = grad_ref[:, cols]
        grad_heads_ref[head] = grad
        grad_rows = jnp.transpose(grad.astype(F32))
        grad_t_ref[head] = grad_rows.astype(BF16)
        product = grad_rows * jnp.transpose(out_ref[:, cols].astype(F32))
        delta_ref[head] = jnp.sum(product, 0, keepdims=True)


def main_kernel(blocks, block_len, tree_dev, inv_root, *refs):
    plan_ref, cos_ref, sin_ref, gain_ref = refs[:4]
    pieces = refs[4:4 + tree_dev]
    q_t_ref, q_ref, grad_t_ref, grad_ref, delta_ref = refs[4 + tree_dev:9 + tree_dev]
    dq_ref, gain_part_ref = refs[9 + tree_dev:11 + tree_dev]
    parts = refs[11 + tree_dev:11 + 2 * tree_dev]
    raw, keys, keys_t, vals, with_cos, with_sin, expo, mass, w_all, ds_all, found, spread = refs[11 + 2 * tree_dev:]
    group, tokens, head_dim = q_ref.shape
    count = plan_ref[4, 0]
    chunks = (count + blocks - 1) // blocks
    gain = gain_ref[...]
    lane = lax.broadcasted_iota(jnp.int32, (1, head_dim), 1)
    for piece in range(tree_dev):
        raw[piece] = pieces[piece][...]

    def rows_of(start):
        return pl.ds(pl.multiple_of(start * block_len, block_len), block_len)

    @pl.loop(0, chunks)
    def _(c):
        for j in range(blocks):
            slot = c * blocks + j
            piece = plan_ref[0, slot]
            rows = rows_of(plan_ref[1, slot])
            table = rows_of(plan_ref[2, slot])
            cos, sin = cos_ref[table, :], sin_ref[table, :]
            unit = raw[piece, rows, 0:head_dim].astype(F32)
            unit = unit * inverse_rms(unit)
            here = pl.ds(j * block_len, block_len)
            with_cos[c, here, :] = unit * cos
            with_sin[c, here, :] = pltpu.roll(unit * sin, head_dim // 2, 1)
            keys[c, here, 0:head_dim] = turned(unit * gain, cos, sin).astype(BF16)
            bits = jnp.where(slot < count, plan_ref[3, slot], 0)
            shown = jnp.zeros((1, head_dim), F32)
            for a in range(blocks):
                seen = lax.rem(lax.shift_right_logical(bits, a), 2)
                shown = jnp.where((lane == a) & (seen == 0), HIDDEN, shown)
            keys[c, here, head_dim:] = jnp.broadcast_to(shown, (block_len, head_dim)).astype(BF16)
            vals[c, here, :] = raw[piece, rows, head_dim:]
        keys_t[c] = jnp.transpose(keys[c, :, 0:head_dim].astype(F32)).astype(BF16)

    def exps(c, g):
        return jnp.exp2(dot_nn(keys[c], q_t_ref[g]) * (inv_root * LOG2_E))

    def summed(e):
        return jnp.sum(e.reshape(tokens // 8, 8, tokens), 0)

    key_row = lax.broadcasted_iota(jnp.int32, (tokens, tokens), 0)
    query_col = lax.broadcasted_iota(jnp.int32, (tokens, tokens), 1)
    for g in range(group):
        e = jnp.where(key_row <= query_col, exps(0, g), 0.0)
        expo[0, g] = e
        mass[g] = summed(e)

    @pl.loop(1, chunks)
    def _(c):
        for g in range(group):
            e = exps(c, g)
            expo[c, g] = e
            mass[g] = mass[g] + summed(e)

    for g in range(group):
        total = jnp.sum(mass[g], 0, keepdims=True)
        mass[g] = jnp.broadcast_to(1.0 / total, (8, tokens))
        dq_ref[g] = jnp.zeros((head_dim, tokens), F32)
    gain_part_ref[...] = jnp.zeros(gain_part_ref.shape, F32)
    spread[...] = jnp.zeros(spread.shape, BF16)

    @pl.loop(0, chunks)
    def _(c):
        for g in range(group):
            grad_prob = dot_nn(vals[c], grad_t_ref[g])
            weights = expo[c, g] * mass[g, 0:1, :]
            dscore = (weights * (grad_prob - delta_ref[g])).astype(BF16)
            w_all[:, pl.ds(g * tokens, tokens)] = weights.astype(BF16)
            ds_all[:, pl.ds(g * tokens, tokens)] = dscore
            dq_ref[g] = dq_ref[g] + dot_nn(keys_t[c], dscore)
        dv = dot_nn(w_all[...], grad_ref[...].reshape(group * tokens, head_dim))
        dk = dot_nn(ds_all[...], q_ref[...].reshape(group * tokens, head_dim)) * inv_root
        found[c, :, 0:head_dim] = dk.astype(BF16)
        found[c, :, head_dim:] = dv.astype(BF16)
        front = jnp.sum((dk * with_cos[c]).reshape(tokens // 8, 8, head_dim), 0)
        back = jnp.sum((dk * with_sin[c]).reshape(tokens // 8, 8, head_dim), 0)
        gain_part_ref[...] = gain_part_ref[...] + front - pltpu.roll(back, head_dim // 2, 1)

    @pl.loop(0, count)
    def _(slot):
        rows = rows_of(lax.rem(slot, blocks))
        spread[plan_ref[0, slot], rows_of(plan_ref[1, slot]), :] = found[slot // blocks, rows, :]

    for piece in range(tree_dev):
        parts[piece][...] = spread[piece]


def query_kernel(blocks, block_len, inv_root, depth_ref, cos_ref, sin_ref, gain_ref, q_ref, *refs):
    dq_refs, (out_ref, part_ref) = refs[:-2], refs[-2:]
    group, head_dim, tokens = dq_refs[0].shape
    cos, sin = own_tables(depth_ref, cos_ref, sin_ref, blocks, block_len)
    gain = gain_ref[...]
    part = jnp.zeros((8, head_dim), F32)
    for head in range(group * len(dq_refs)):
        cols = pl.ds(head * head_dim, head_dim)
        rows = q_ref[:, cols].astype(F32)
        recip = inverse_rms(rows)
        normed = rows * recip
        dq = jnp.transpose(dq_refs[head // group][head % group])
        scaled_grad = turned_back(dq, cos, sin) * inv_root
        term = scaled_grad * normed
        part = part + jnp.sum(term.reshape(tokens // 8, 8, head_dim), 0)
        inner = jnp.mean(term * gain, -1, keepdims=True)
        out_ref[:, cols] = (recip * (scaled_grad * gain - normed * inner)).astype(BF16)
    part_ref[...] = part


def key_kernel(blocks, block_len, counts, depth_ref, cos_ref, sin_ref, gain_ref, k_ref, *refs):
    sums, (dk_out_ref, dv_out_ref) = refs[:-2], refs[-2:]
    head_dim = gain_ref.shape[1]
    cos, sin = own_tables(depth_ref, cos_ref, sin_ref, blocks, block_len)
    gain = gain_ref[...]
    for head, each in enumerate(counts):
        cols = pl.ds(head * head_dim, head_dim)
        rows = k_ref[:, cols].astype(F32)
        recip = inverse_rms(rows)
        normed = rows * recip
        mine = sums[sum(counts[:head]):][:each]
        both = mine[0][...].astype(F32)
        for other in mine[1:]:
            both = both + other[...].astype(F32)
        grad = turned_back(both[:, 0:head_dim], cos, sin) * gain
        inner = jnp.mean(grad * normed, -1, keepdims=True)
        dk_out_ref[:, cols] = (recip * (grad - normed * inner)).astype(BF16)
        dv_out_ref[:, cols] = both[:, head_dim:].astype(BF16)


class Tree:
    def __init__(self, size, cycle):
        self.size, self.cycle = size, cycle

    def order(self, index):
        return (index - 1) % self.size

    def send(self, value, target, wanted):
        pairs = []
        for tree in range(self.cycle // self.size):
            for index in range(self.size):
                if wanted(index):
                    ends = [(tree * self.size + 1 + self.order(i)) % self.cycle for i in (index, target(index))]
                    pairs.append(tuple(ends))
        return lax.ppermute(value, "ctx", pairs)

    def after(self, *pair):
        return self.order(pair[1] % self.size) > self.order(pair[0] % self.size)

    def gather(self, own, relayed):
        size, after = self.size, self.after
        cross = self.send(own, lambda i: i ^ 1, lambda i: after(i, i ^ 1))
        straight, crossed = [], []
        for step in range(2, size, 2):
            there = lambda i: (i + step) % size
            if relayed:
                piece = self.send(own, there, lambda i: after(i, there(i)) or after(i, there(i) ^ 1))
                straight.append(piece)
            else:
                straight.append(self.send(own, there, lambda i: after(i, there(i))))
                crossed.append(self.send(own, lambda i: there(i) ^ 1, lambda i: after(i, there(i) ^ 1)))
        if relayed:
            for step, piece in zip(range(2, size, 2), straight):
                crossed.append(self.send(piece, lambda i: i ^ 1, lambda i: after(i - step, i ^ 1)))
        return [own, *straight, cross, *crossed]

    def collect(self, parts, relayed):
        size, after = self.size, self.after
        half = size // 2
        terms = [parts[0]]
        if relayed:
            halves = []
            for step in range(2, size, 2):
                part = parts[half + step // 2]
                halves.append(self.send(part, lambda i: i ^ 1, lambda i: after((i ^ 1) - step, i)))
            terms.append(self.send(parts[half], lambda i: i ^ 1, lambda i: after(i ^ 1, i)))
            for step, other in zip(range(2, size, 2), halves):
                there = lambda i: (i - step) % size
                both = (parts[step // 2].astype(F32) + other.astype(F32)).astype(BF16)
                terms.append(self.send(both, there, lambda i: after(there(i), i) or after(there(i), i ^ 1)))
            return terms
        terms.append(self.send(parts[half], lambda i: i ^ 1, lambda i: after(i ^ 1, i)))
        for step in range(2, size, 2):
            there = lambda i: (i - step) % size
            across = lambda i: ((i ^ 1) - step) % size
            terms.append(self.send(parts[step // 2], there, lambda i: after(there(i), i)))
            terms.append(self.send(parts[half + step // 2], across, lambda i: after(across(i), i)))
        return terms


def on_device(q_raw, k_raw, values, saved_out, out_grad, q_gain, k_gain, ancestors):
    tokens = q_raw.shape[0]
    head_dim = q_gain.shape[0]
    kv_heads = k_raw.shape[1] // head_dim
    heads = q_raw.shape[1] // head_dim
    group = heads // kv_heads
    blocks = ancestors.shape[0]
    tree_blocks = ancestors.shape[1]
    block_len = tokens // blocks
    tree_dev = tree_blocks // blocks
    cycle = lax.axis_size("ctx")
    inv_root = 1.0 / math.sqrt(head_dim)
    tree = Tree(tree_dev, cycle)
    place = (lax.axis_index("ctx") - 1 + cycle) % cycle % tree_dev
    place = place.reshape(1).astype(jnp.int32)

    depth = jnp.sum((ancestors >= 0).astype(jnp.int32), 1) - 1
    total_blocks = blocks * cycle
    in_tree = jnp.where(
        ancestors >= 0, (ancestors - blocks + total_blocks) % total_blocks % tree_blocks, -1
    )
    cos_np, sin_np = rope_rows(tree_blocks * block_len, head_dim)
    cos, sin = jnp.asarray(cos_np), jnp.asarray(sin_np)
    q_gain_row, k_gain_row = q_gain.reshape(1, head_dim), k_gain.reshape(1, head_dim)

    own = []
    for h in range(kv_heads):
        cols = slice(h * head_dim, (h + 1) * head_dim)
        own.append(jnp.concatenate([k_raw[:, cols], values[:, cols]], 1))
    gathered = [tree.gather(own[h], GATHER_RELAYED[h > 0]) for h in range(kv_heads)]

    params = pltpu.CompilerParams(vmem_limit_bytes=VMEM_LIMIT)
    smem = pl.BlockSpec(memory_space=pltpu.SMEM)
    vmem = pl.BlockSpec(memory_space=pltpu.VMEM)
    sds = jax.ShapeDtypeStruct

    plan = pl.pallas_call(
        lambda *refs: plan_kernel(blocks, tree_dev, *refs),
        out_shape=sds((5, tree_blocks), jnp.int32),
        in_specs=[smem, smem],
        out_specs=smem,
        name="plan",
    )(place, in_tree)

    def prep(h):
        columns = pl.BlockSpec((tokens, group * head_dim), lambda i: (0, h))
        whole = lambda *shape: pl.BlockSpec(shape, lambda i: (0,) * len(shape))
        table = whole(tree_blocks * block_len, head_dim)
        shapes = (
            (group, 2 * head_dim, tokens),
            (group, tokens, head_dim),
            (group, head_dim, tokens),
            (group, tokens, head_dim),
            (group, 1, tokens),
        )
        return pl.pallas_call(
            lambda *refs: prep_kernel(blocks, block_len, *refs),
            grid=(1,),
            out_shape=tuple(sds(shape, F32 if shape[1] == 1 else BF16) for shape in shapes),
            in_specs=[smem, table, table, whole(1, head_dim), columns, columns, columns],
            out_specs=tuple(whole(*shape) for shape in shapes),
            compiler_params=params,
            name="prep",
        )(depth, cos, sin, q_gain_row, q_raw, out_grad, saved_out)

    def attend(pieces, queries):
        return pl.pallas_call(
            lambda *refs: main_kernel(blocks, block_len, tree_dev, inv_root, *refs),
            out_shape=(
                sds((group, head_dim, tokens), F32),
                sds((8, head_dim), F32),
                *[sds((tokens, 2 * head_dim), BF16)] * tree_dev,
            ),
            in_specs=[smem] + [vmem] * (8 + tree_dev),
            out_specs=tuple([vmem] * (2 + tree_dev)),
            scratch_shapes=[
                pltpu.VMEM((tree_dev, tokens, 2 * head_dim), BF16),
                pltpu.VMEM((tree_dev, tokens, 2 * head_dim), BF16),
                pltpu.VMEM((tree_dev, head_dim, tokens), BF16),
                pltpu.VMEM((tree_dev, tokens, head_dim), BF16),
                pltpu.VMEM((tree_dev, tokens, head_dim), F32),
                pltpu.VMEM((tree_dev, tokens, head_dim), F32),
                pltpu.VMEM((tree_dev, group, tokens, tokens), F32),
                pltpu.VMEM((group, 8, tokens), F32),
                pltpu.VMEM((tokens, group * tokens), BF16),
                pltpu.VMEM((tokens, group * tokens), BF16),
                pltpu.VMEM((tree_dev, tokens, 2 * head_dim), BF16),
                pltpu.VMEM((tree_dev, tokens, 2 * head_dim), BF16),
            ],
            compiler_params=params,
            cost_estimate=pl.CostEstimate(
                flops=10 * group * tokens * tree_dev * tokens * head_dim,
                bytes_accessed=8 * 1024 * 1024,
                transcendentals=group * tokens * tree_dev * tokens,
            ),
            name="attend",
        )(plan, cos, sin, k_gain_row, *pieces, *queries)

    queries = [prep(h) for h in range(kv_heads)]
    dq, terms, counts, k_gain_parts = [], [], [], []
    for h in range(kv_heads):
        dq_here, k_gain_part, *parts = attend(gathered[h], queries[h])
        dq.append(dq_here)
        k_gain_parts.append(k_gain_part)
        mine = tree.collect(parts, COLLECT_RELAYED[h > 0])
        terms.extend(mine)
        counts.append(len(mine))

    dq_raw, q_gain_part = pl.pallas_call(
        lambda *refs: query_kernel(blocks, block_len, inv_root, *refs),
        out_shape=(sds((tokens, heads * head_dim), BF16), sds((8, head_dim), F32)),
        in_specs=[smem] + [vmem] * (4 + kv_heads),
        out_specs=(vmem, vmem),
        compiler_params=params,
        name="query_back",
    )(depth, cos, sin, q_gain_row, q_raw, *dq)

    gains = jnp.stack([jnp.sum(q_gain_part, 0), jnp.sum(sum(k_gain_parts), 0)])
    gains = lax.psum(gains, ("ctx", "heads"))

    dk_raw, dv = pl.pallas_call(
        lambda *refs: key_kernel(blocks, block_len, counts, *refs),
        out_shape=(sds(k_raw.shape, BF16), sds(k_raw.shape, BF16)),
        in_specs=[smem] + [vmem] * (4 + len(terms)),
        out_specs=(vmem, vmem),
        compiler_params=params,
        name="key_back",
    )(depth, cos, sin, k_gain_row, k_raw, *terms)
    return (dq_raw, dk_raw, dv, gains[0], gains[1])


def solution(mesh):
    split = P("ctx", "heads")
    return jax.shard_map(
        on_device,
        mesh=mesh,
        in_specs=(split, split, split, split, split, P(), P(), P("ctx", None)),
        out_specs=(split, split, split, P(), P()),
        check_vma=False,
    )
```

time: 293 us -> 201 us (0.69); the launches traced: 295 us -> 199 us
  waiting for transfers between devices: 158 us -> 12.7 us
  starting transfers between devices: 0.16 us -> 62.7 us
  between operations: 13.8 us -> 1.14 us
  local copies, waits for them, and re-layouts: 14 us -> 8.83 us
  blocking collectives: 37.1 us -> 41.9 us
  Pallas kernels: 71.4 us -> 67.8 us
  other arithmetic: 0.86 us -> 3.87 us
    reduce_scatter x2 -> x0, waiting for transfers between devices: 82.1 us -> none  [the longest x1 66.2 us: on_device(): lax.psum_scatter(dv_part, 'ctx', scatter_dimension=0, axis_index_groups=g...]
    all_gather x2 -> x0, waiting for transfers between devices: 73.7 us -> none  [the longest x1 41.1 us: on_device(): k_all = lax.all_gather(k_raw, 'ctx', axis_index_groups=groups)]
    ppermute x0 -> x28, starting transfers between devices: none -> 62.7 us  [send(): return lax.ppermute(value, 'ctx', pairs)]
    ppermute x0 -> x28, waiting for transfers between devices: none -> 12.7 us  [send(): return lax.ppermute(value, 'ctx', pairs)]
    unnamed x36 -> x38, local copies, waits for them, and re-layouts: 13.5 us -> 7.36 us
    psum x1, blocking collectives: 37.1 us -> 41.9 us  [on_device(): gains = lax.psum(gains, ('ctx', 'heads'))]
    pallas_call x3 -> x6, Pallas kernels: 66.8 us -> 63.2 us  [the longest x2 52.5 us: attend(): pl.pallas_call(lambda *refs: main_kernel(blocks, block_len, tree_dev, inv...]
  transfers between devices with their start and end apart: 4 -> 28, of which waited for: 4 -> 6; matrix products, arithmetic and copies ran while one was open for 0% -> 2% of each run, Pallas kernels for 3% -> 20%
where the time goes in v2:
time: 201 us; the launch traced here: 199 us
  Pallas kernels  67.8 us (34%)
  starting transfers between devices  62.7 us (31%)
  blocking collectives  41.9 us (21%)
  waiting for transfers between devices  12.7 us (6%)
  local copies, waits for them, and re-layouts  8.83 us (4%)
  other arithmetic  3.87 us (2%)
    ppermute x28, starting transfers between devices, send(): return lax.ppermute(value, 'ctx', pairs)  62.7 us
    pallas_call x2, Pallas kernels, attend(): pl.pallas_call(lambda *refs: main_kernel(blocks, block_len, tree_dev, inv...  52.5 us
    psum x1, blocking collectives, on_device(): gains = lax.psum(gains, ('ctx', 'heads'))  41.9 us
    ppermute x28, waiting for transfers between devices, send(): return lax.ppermute(value, 'ctx', pairs)  12.7 us
    unnamed x38, local copies, waits for them, and re-layouts  7.36 us
    pallas_call x2, Pallas kernels, prep(): pl.pallas_call(lambda *refs: prep_kernel(blocks, block_len, *refs), grid=...  6.19 us
    pallas_call x1, Pallas kernels, on_device(): pl.pallas_call(lambda *refs: query_kernel(blocks, block_len, inv_root, *r...  4.67 us
  transfers between devices with their start and end apart: 28, of which 6 were waited for; matrix products, arithmetic and copies ran while one was open for 2% of the time, Pallas kernels for 20%

profile of v2, /device:TPU:0, one launch (start us, length us, event | category | flops | bytes accessed | tf_op | source)
XLA Modules:
  0.0 198.9 jit_solution(125614480269411369)
XLA Ops:
  0.6 1.0 fusion.3
  1.6 1.3 collective-permute-start.13
  2.9 1.3 collective-permute-start.12
  4.2 1.3 collective-permute-start.11
  5.5 1.3 collective-permute-start.10
  6.8 1.3 collective-permute-start.9
  8.8 0.7 fusion.2
  9.5 2.9 %plan.1.refs_0_ = s32[5,32]{1,0:T(8,128)} custom-call(s32[1]{0:T(128)} %bitcast.1.refs_0_, s32[4,32]{1,0:T(4,128)} %get-tuple-element.77.refs_1_), custom_call_target="tpu_custom_call" | custom-call | tf_op jit(solution)/shard_map/plan/pallas_call | solution.py:350
  12.4 3.6 %collective-permute-done.13.refs_11_ = bf16[256,256]{1,0:T(8,128)(2,1)S(1)} collective-permute-done((bf16[256,256]{1,0:T(8,128)(2,1)S(1)}, bf16[256,256]{1,0:T(8,128)(2,1)S(1)}, u32[]{:S(2)}, u32[]{:S(2)}) %collective-permute-start.13) | collective-permute-done | bytes 131104 | tf_op jit(solution)/shard_map/ppermute | solution.py:268
  16.0 1.3 collective-permute-start.8
  17.3 1.3 collective-permute-start.7
  19.3 1.2 copy-done
  20.5 1.2 copy-done.3
  21.7 1.2 copy-done.5
  22.9 3.1 %prep.3 = (bf16[8,256,256]{2,1,0:T(8,128)(2,1)S(1)}, bf16[8,256,128]{2,1,0:T(8,128)(2,1)S(1)}, bf16[8,128,256]{2,1,0:T(8,128)(2,1)S(1)}, bf16[8,256,128]{2,1,0:T(8,128)(2,1)S(1)}, f32[8,1,256]{2,1,0:T(1,128)S(1)}) custom-call(s32[4]{0:T(128)S(1)} %broadcast_add_fusion.refs_0_, f32[2048,128]{1,0:T(8,128)S(1)} %copy-done.3, f32[2048,128]{1,0:T(8,128)S(1)} %copy-done, ...), custom_call_target="tpu_custom_call" | custom-call | tf_op jit(solution)/shard_map/prep/pallas_call | solution.py:369
  26.0 1.0 copy-done.12
  27.0 1.6 collective-permute-done.7.refs_5_
  29.4 25.9 %attend.3 = (f32[8,128,256]{2,1,0:T(8,128)S(1)}, f32[8,128]{1,0:T(8,128)S(1)}, bf16[256,256]{1,0:T(8,128)(2,1)S(1)}, bf16[256,256]{1,0:T(8,128)(2,1)S(1)}, bf16[...) custom-call(s32[5,32]{1,0:T(8,128)S(1)} %copy-done.9, ...), custom_call_target="tpu_custom_call" | custom-call | flops 5368709120 | bytes 8388608 | tf_op jit(solution)/shard_map/attend/pallas_call | solution.py:380
  55.3 1.3 collective-permute-start.22
  56.6 1.3 collective-permute-start.3
  57.9 1.3 collective-permute-start.2
  59.2 1.3 collective-permute-start.1
  60.5 1.3 collective-permute-start
  61.9 3.1 %prep.2 = (bf16[8,256,256]{2,1,0:T(8,128)(2,1)S(1)}, bf16[8,256,128]{2,1,0:T(8,128)(2,1)S(1)}, bf16[8,128,256]{2,1,0:T(8,128)(2,1)S(1)}, bf16[8,256,128]{2,1,0:T(8,128)(2,1)S(1)}, f32[8,1,256]{2,1,0:T(1,128)S(1)}) custom-call(s32[4]{0:T(128)S(1)} %broadcast_add_fusion.refs_0_, f32[2048,128]{1,0:T(8,128)S(1)} %copy-done.3, f32[2048,128]{1,0:T(8,128)S(1)} %copy-done.1, ...), custom_call_target="tpu_custom_call" | custom-call | tf_op jit(solution)/shard_map/prep/pallas_call | solution.py:369
  65.0 9.7 %collective-permute-start.24 = (bf16[256,256]{1,0:T(8,128)(2,1)S(1)}, bf16[256,256]{1,0:T(8,128)(2,1)S(1)}, u32[]{:S(2)}, u32[]{:S(2)}) collective-permute-start(bf16[256,256]{1,0:T(8,128)(2,1)S(1)} %get-tuple-element.65), channel_id=1, source_target_pairs={{0,4},{16,20},{24,28},{28,24},{1,5},{17,21},{25,29},{29,25},{2,6},... | collective-permute-start | bytes 393224 | tf_op jit(solution)/shard_map/ppermute | solution.py:268
  75.4 1.8 collective-permute-done.24
  77.3 4.4 %collective-permute-start.26 = (bf16[256,256]{1,0:T(8,128)(2,1)S(1)}, bf16[256,256]{1,0:T(8,128)(2,1)S(1)}, u32[]{:S(2)}, u32[]{:S(2)}) collective-permute-start(bf16[256,256]{1,0:T(8,128)(2,1)S(1)} %get-tuple-element.67), channel_id=1, source_target_pairs={{0,4},{24,28},{1,5},{25,29},{2,6},{26,30},{3,7},{27,31}} | collective-permute-start | bytes 393224 | tf_op jit(solution)/shard_map/ppermute | solution.py:268
  82.3 1.3 collective-permute-start.21
  83.7 1.3 collective-permute-start.6
  85.0 1.3 collective-permute-start.5
  86.3 1.3 collective-permute-start.4
  88.3 9.5 %collective-permute-start.23 = (bf16[256,256]{1,0:T(8,128)(2,1)}, bf16[256,256]{1,0:T(8,128)(2,1)S(1)}, u32[]{:S(2)}, u32[]{:S(2)}) collective-permute-start(bf16[256,256]{1,0:T(8,128)(2,1)} %add_convert_fusion.2), channel_id=1, source_target_pairs={{0,24},{4,28},{12,4},{16,8},{20,12},{24,16},{28,20},{1,25},{5,29},... | collective-permute-start | bytes 393224 | tf_op jit(solution)/shard_map/ppermute | solution.py:268
  97.8 1.3 collective-permute-start.25
  99.1 1.3 collective-permute-start.27
  100.4 26.5 %attend.2 = (f32[8,128,256]{2,1,0:T(8,128)S(1)}, f32[8,128]{1,0:T(8,128)S(1)}, bf16[256,256]{1,0:T(8,128)(2,1)S(1)}, bf16[256,256]{1,0:T(8,128)(2,1)}, bf16[256,...) custom-call(s32[5,32]{1,0:T(8,128)S(1)} %copy-done.9, ...), custom_call_target="tpu_custom_call" | custom-call | flops 5368709120 | bytes 8388608 | tf_op jit(solution)/shard_map/attend/pallas_call | solution.py:380
  127.0 1.3 collective-permute-start.14
  128.3 1.5 collective-permute-start.15
  130.3 4.7 %query_back.1 = (bf16[256,2048]{1,0:T(8,128)(2,1)}, f32[8,128]{1,0:T(8,128)S(1)}) custom-call(s32[4]{0:T(128)S(1)} %broadcast_add_fusion.refs_0_, f32[2048,128]{1,0:T(8,128)S(1)} %copy-done.3, f32[2048,128]{1,0:T(8,128)S(1)} %copy-done.2, f32[1,128]{1,0:T(1,128)S(1)} %bitcast.11, bf16[256,2048]{1,0:T(8,128)(2,1)S(1)} %copy-done.6, ...), custom_call_target="tpu_custom_call" | custom-call | tf_op jit(solution)/shard_map/query_back/pallas_call | solution.py:422
  136.2 41.9 %psum.7 = f32[2,128]{1,0:T(2,128)S(1)} all-reduce(f32[2,128]{1,0:T(2,128)S(1)} %pad_maximum_fusion.2), channel_id=1, replica_groups=mesh['ctx'=8,'heads'=4] {'ctx','heads'}, use_global_device_ids=true, to_apply=%region_3.4 | all-reduce | flops 256 | bytes 2048 | tf_op jit(solution)/shard_map/psum | solution.py:432
  178.1 5.2 %collective-permute-start.16 = (bf16[256,256]{1,0:T(8,128)(2,1)}, bf16[256,256]{1,0:T(8,128)(2,1)S(1)}, u32[]{:S(2)}, u32[]{:S(2)}) collective-permute-start(bf16[256,256]{1,0:T(8,128)(2,1)} %copy-done.15), channel_id=1, source_target_pairs={{0,28},{8,4},{16,12},{20,8},{24,20},{28,16},{1,29},{9,5},{17,13},{... | collective-permute-start | bytes 393224 | tf_op jit(solution)/shard_map/ppermute | solution.py:268
  183.3 4.0 %collective-permute-start.17 = (bf16[256,256]{1,0:T(8,128)(2,1)}, bf16[256,256]{1,0:T(8,128)(2,1)S(1)}, u32[]{:S(2)}, u32[]{:S(2)}) collective-permute-start(bf16[256,256]{1,0:T(8,128)(2,1)} %copy-done.14), channel_id=1, source_target_pairs={{0,16},{20,4},{24,8},{28,12},{1,17},{21,5},{25,9},{29,13},{2,18},{... | collective-permute-start | bytes 393224 | tf_op jit(solution)/shard_map/ppermute | solution.py:268
  187.3 1.3 collective-permute-start.18
  188.6 1.3 collective-permute-start.19
  189.9 1.3 collective-permute-start.20
  191.7 2.6 %collective-permute-done.18.refs_10_ = bf16[256,256]{1,0:T(8,128)(2,1)S(1)} collective-permute-done((bf16[256,256]{1,0:T(8,128)(2,1)}, bf16[256,256]{1,0:T(8,128)(2,1)S(1)}, u32[]{:S(2)}, u32[]{:S(2)}) %collective-permute-start.18) | collective-permute-done | bytes 131104 | tf_op jit(solution)/shard_map/ppermute | solution.py:268
  194.3 1.5 collective-permute-done.19.refs_11_
  195.8 1.5 collective-permute-done.20.refs_12_
  197.3 1.7 key_back.1
  (66 shorter events, 6.5 us)
Async XLA Ops:
  1.6 14.4 %collective-permute-start.13 = (bf16[256,256]{1,0:T(8,128)(2,1)S(1)}, bf16[256,256]{1,0:T(8,128)(2,1)S(1)}, u32[]{:S(2)}, u32[]{:S(2)}) collective-permute-start(bf16[256,256]{1,0:T(8,128)(2,1)S(1)} %pad_maximum_fusion.1.refs_4_), channel_id=1, source_target_pairs={{4,24},{12,0},{5,25},{13,1},{6,26},{14,2},{7,27},{15,3}} | collective-permute-start | bytes 393224 | tf_op jit(solution)/shard_map/ppermute | solution.py:268
  2.9 14.4 %collective-permute-start.12 = (bf16[256,256]{1,0:T(8,128)(2,1)S(1)}, bf16[256,256]{1,0:T(8,128)(2,1)S(1)}, u32[]{:S(2)}, u32[]{:S(2)}) collective-permute-start(bf16[256,256]{1,0:T(8,128)(2,1)S(1)} %pad_maximum_fusion.1.refs_4_), channel_id=1, source_target_pairs={{4,16},{8,28},{12,24},{20,0},{5,17},{9,29},{13,25},{21,1},{6,18},{... | collective-permute-start | bytes 393224 | tf_op jit(solution)/shard_map/ppermute | solution.py:268
  4.2 22.8 %collective-permute-start.11 = (bf16[256,256]{1,0:T(8,128)(2,1)S(1)}, bf16[256,256]{1,0:T(8,128)(2,1)S(1)}, u32[]{:S(2)}, u32[]{:S(2)}) collective-permute-start(bf16[256,256]{1,0:T(8,128)(2,1)S(1)} %pad_maximum_fusion.1.refs_4_), channel_id=1, source_target_pairs={{4,8},{8,20},{12,16},{16,28},{20,24},{28,0},{5,9},{9,21},{13,17},{... | collective-permute-start | bytes 393224 | tf_op jit(solution)/shard_map/ppermute | solution.py:268
  5.5 21.5 %collective-permute-start.10 = (bf16[256,256]{1,0:T(8,128)(2,1)S(1)}, bf16[256,256]{1,0:T(8,128)(2,1)S(1)}, u32[]{:S(2)}, u32[]{:S(2)}) collective-permute-start(bf16[256,256]{1,0:T(8,128)(2,1)S(1)} %pad_maximum_fusion.1.refs_4_), channel_id=1, source_target_pairs={{4,0},{8,12},{16,20},{24,28},{5,1},{9,13},{17,21},{25,29},{6,2},{1... | collective-permute-start | bytes 393224 | tf_op jit(solution)/shard_map/ppermute | solution.py:268
  6.8 20.2 %collective-permute-start.9 = (bf16[256,256]{1,0:T(8,128)(2,1)S(1)}, bf16[256,256]{1,0:T(8,128)(2,1)S(1)}, u32[]{:S(2)}, u32[]{:S(2)}) collective-permute-start(bf16[256,256]{1,0:T(8,128)(2,1)S(1)} %pad_maximum_fusion.1.refs_4_), channel_id=1, source_target_pairs={{4,28},{8,0},{5,29},{9,1},{6,30},{10,2},{7,31},{11,3}} | collective-permute-start | bytes 393224 | tf_op jit(solution)/shard_map/ppermute | solution.py:268
  8.1 0.7 copy-start.16
  16.0 11.0 %collective-permute-start.8 = (bf16[256,256]{1,0:T(8,128)(2,1)S(1)}, bf16[256,256]{1,0:T(8,128)(2,1)S(1)}, u32[]{:S(2)}, u32[]{:S(2)}) collective-permute-start(bf16[256,256]{1,0:T(8,128)(2,1)S(1)} %pad_maximum_fusion.1.refs_4_), channel_id=1, source_target_pairs={{4,20},{8,24},{12,28},{16,0},{5,21},{9,25},{13,29},{17,1},{6,22},{... | collective-permute-start | bytes 393224 | tf_op jit(solution)/shard_map/ppermute | solution.py:268
  17.3 11.4 %collective-permute-start.7 = (bf16[256,256]{1,0:T(8,128)(2,1)S(1)}, bf16[256,256]{1,0:T(8,128)(2,1)S(1)}, u32[]{:S(2)}, u32[]{:S(2)}) collective-permute-start(bf16[256,256]{1,0:T(8,128)(2,1)S(1)} %pad_maximum_fusion.1.refs_4_), channel_id=1, source_target_pairs={{4,12},{8,16},{12,20},{16,24},{20,28},{24,0},{5,13},{9,17},{13,21}... | collective-permute-start | bytes 393224 | tf_op jit(solution)/shard_map/ppermute | solution.py:268
  18.6 0.7 copy-start.8
  19.3 1.2 copy-start
  20.5 1.2 copy-start.3
  21.7 1.2 copy-start.5
  26.0 1.0 copy-start.12
  28.7 0.7 copy-start.9
  28.7 0.7 copy-start.10
  29.4 32.5 %copy-start.1 = (f32[2048,128]{1,0:T(8,128)S(1)}, f32[2048,128]{1,0:T(8,128)}, u32[]{:S(2)}) copy-start(f32[2048,128]{1,0:T(8,128)} %constant.63.clone.refs_2_) | copy-start | bytes 3145732
  29.4 32.5 %copy-start.6 = (bf16[256,2048]{1,0:T(8,128)(2,1)S(1)}, bf16[256,2048]{1,0:T(8,128)(2,1)}, u32[]{:S(2)}) copy-start(bf16[256,2048]{1,0:T(8,128)(2,1)} %refs_4_.6) | copy-start | bytes 3145732
  55.3 9.7 %collective-permute-start.22 = (bf16[256,256]{1,0:T(8,128)(2,1)S(1)}, bf16[256,256]{1,0:T(8,128)(2,1)S(1)}, u32[]{:S(2)}, u32[]{:S(2)}) collective-permute-start(bf16[256,256]{1,0:T(8,128)(2,1)S(1)} %get-tuple-element.63), channel_id=1, source_target_pairs={{0,4},{8,12},{16,20},{20,16},{24,28},{28,24},{1,5},{9,13},{17,21},... | collective-permute-start | bytes 393224 | tf_op jit(solution)/shard_map/ppermute | solution.py:268
  56.6 31.6 %collective-permute-start.3 = (bf16[256,256]{1,0:T(8,128)(2,1)S(1)}, bf16[256,256]{1,0:T(8,128)(2,1)S(1)}, u32[]{:S(2)}, u32[]{:S(2)}) collective-permute-start(bf16[256,256]{1,0:T(8,128)(2,1)S(1)} %pad_maximum_fusion.refs_4_), channel_id=1, source_target_pairs={{4,0},{8,12},{16,20},{24,28},{5,1},{9,13},{17,21},{25,29},{6,2},{1... | collective-permute-start | bytes 393224 | tf_op jit(solution)/shard_map/ppermute | solution.py:268
  57.9 24.4 %collective-permute-start.2 = (bf16[256,256]{1,0:T(8,128)(2,1)S(1)}, bf16[256,256]{1,0:T(8,128)(2,1)S(1)}, u32[]{:S(2)}, u32[]{:S(2)}) collective-permute-start(bf16[256,256]{1,0:T(8,128)(2,1)S(1)} %pad_maximum_fusion.refs_4_), channel_id=1, source_target_pairs={{4,28},{8,0},{12,4},{5,29},{9,1},{13,5},{6,30},{10,2},{14,6},{7,31... | collective-permute-start | bytes 393224 | tf_op jit(solution)/shard_map/ppermute | solution.py:268
  59.2 24.4 %collective-permute-start.1 = (bf16[256,256]{1,0:T(8,128)(2,1)S(1)}, bf16[256,256]{1,0:T(8,128)(2,1)S(1)}, u32[]{:S(2)}, u32[]{:S(2)}) collective-permute-start(bf16[256,256]{1,0:T(8,128)(2,1)S(1)} %pad_maximum_fusion.refs_4_), channel_id=1, source_target_pairs={{4,20},{8,24},{12,28},{16,0},{20,4},{5,21},{9,25},{13,29},{17,1},{... | collective-permute-start | bytes 393224 | tf_op jit(solution)/shard_map/ppermute | solution.py:268
  60.5 24.4 %collective-permute-start = (bf16[256,256]{1,0:T(8,128)(2,1)S(1)}, bf16[256,256]{1,0:T(8,128)(2,1)S(1)}, u32[]{:S(2)}, u32[]{:S(2)}) collective-permute-start(bf16[256,256]{1,0:T(8,128)(2,1)S(1)} %pad_maximum_fusion.refs_4_), channel_id=1, source_target_pairs={{4,12},{8,16},{12,20},{16,24},{20,28},{24,0},{28,4},{5,13},{9,17},... | collective-permute-start | bytes 393224 | tf_op jit(solution)/shard_map/ppermute | solution.py:268
  65.0 35.5 %copy-start.11 = (bf16[8,256,256]{2,1,0:T(8,128)(2,1)}, bf16[8,256,256]{2,1,0:T(8,128)(2,1)S(1)}, u32[]{:S(2)}) copy-start(bf16[8,256,256]{2,1,0:T(8,128)(2,1)S(1)} %get-tuple-element.39.refs_12_) | copy-start | bytes 3145732
  65.0 12.3 %collective-permute-start.24 = (bf16[256,256]{1,0:T(8,128)(2,1)S(1)}, bf16[256,256]{1,0:T(8,128)(2,1)S(1)}, u32[]{:S(2)}, u32[]{:S(2)}) collective-permute-start(bf16[256,256]{1,0:T(8,128)(2,1)S(1)} %get-tuple-element.65), channel_id=1, source_target_pairs={{0,4},{16,20},{24,28},{28,24},{1,5},{17,21},{25,29},{29,25},{2,6},... | collective-permute-start | bytes 393224 | tf_op jit(solution)/shard_map/ppermute | solution.py:268
  77.3 9.0 %collective-permute-start.26 = (bf16[256,256]{1,0:T(8,128)(2,1)S(1)}, bf16[256,256]{1,0:T(8,128)(2,1)S(1)}, u32[]{:S(2)}, u32[]{:S(2)}) collective-permute-start(bf16[256,256]{1,0:T(8,128)(2,1)S(1)} %get-tuple-element.67), channel_id=1, source_target_pairs={{0,4},{24,28},{1,5},{25,29},{2,6},{26,30},{3,7},{27,31}} | collective-permute-start | bytes 393224 | tf_op jit(solution)/shard_map/ppermute | solution.py:268
  82.3 45.9 %collective-permute-start.21 = (bf16[256,256]{1,0:T(8,128)(2,1)S(1)}, bf16[256,256]{1,0:T(8,128)(2,1)S(1)}, u32[]{:S(2)}, u32[]{:S(2)}) collective-permute-start(bf16[256,256]{1,0:T(8,128)(2,1)S(1)} %get-tuple-element.61), channel_id=1, source_target_pairs={{0,4},{12,8},{20,16},{28,24},{1,5},{13,9},{21,17},{29,25},{2,6},{1... | collective-permute-start | bytes 393224 | tf_op jit(solution)/shard_map/ppermute | solution.py:268
  83.7 14.1 %collective-permute-start.6 = (bf16[256,256]{1,0:T(8,128)(2,1)S(1)}, bf16[256,256]{1,0:T(8,128)(2,1)S(1)}, u32[]{:S(2)}, u32[]{:S(2)}) collective-permute-start(bf16[256,256]{1,0:T(8,128)(2,1)S(1)} %collective-permute-done.2.refs_7_), channel_id=1, source_target_pairs={{4,0},{28,24},{5,1},{29,25},{6,2},{30,26},{7,3},{31,27}} | collective-permute-start | bytes 393224 | tf_op jit(solution)/shard_map/ppermute | solution.py:268
  85.0 14.1 %collective-permute-start.5 = (bf16[256,256]{1,0:T(8,128)(2,1)S(1)}, bf16[256,256]{1,0:T(8,128)(2,1)S(1)}, u32[]{:S(2)}, u32[]{:S(2)}) collective-permute-start(bf16[256,256]{1,0:T(8,128)(2,1)S(1)} %collective-permute-done.1.refs_6_), channel_id=1, source_target_pairs={{4,0},{20,16},{24,28},{28,24},{5,1},{21,17},{25,29},{29,25},{6,2},... | collective-permute-start | bytes 393224 | tf_op jit(solution)/shard_map/ppermute | solution.py:268
  86.3 14.1 %collective-permute-start.4 = (bf16[256,256]{1,0:T(8,128)(2,1)S(1)}, bf16[256,256]{1,0:T(8,128)(2,1)S(1)}, u32[]{:S(2)}, u32[]{:S(2)}) collective-permute-start(bf16[256,256]{1,0:T(8,128)(2,1)S(1)} %collective-permute-done.refs_5_), channel_id=1, source_target_pairs={{4,0},{12,8},{16,20},{20,16},{24,28},{28,24},{5,1},{13,9},{17,21},... | collective-permute-start | bytes 393224 | tf_op jit(solution)/shard_map/ppermute | solution.py:268
  88.3 89.9 %collective-permute-start.23 = (bf16[256,256]{1,0:T(8,128)(2,1)}, bf16[256,256]{1,0:T(8,128)(2,1)S(1)}, u32[]{:S(2)}, u32[]{:S(2)}) collective-permute-start(bf16[256,256]{1,0:T(8,128)(2,1)} %add_convert_fusion.2), channel_id=1, source_target_pairs={{0,24},{4,28},{12,4},{16,8},{20,12},{24,16},{28,20},{1,25},{5,29},... | collective-permute-start | bytes 393224 | tf_op jit(solution)/shard_map/ppermute | solution.py:268
  97.8 85.5 %collective-permute-start.25 = (bf16[256,256]{1,0:T(8,128)(2,1)}, bf16[256,256]{1,0:T(8,128)(2,1)S(1)}, u32[]{:S(2)}, u32[]{:S(2)}) collective-permute-start(bf16[256,256]{1,0:T(8,128)(2,1)} %add_convert_fusion.1), channel_id=1, source_target_pairs={{0,16},{4,20},{20,4},{24,8},{28,12},{1,17},{5,21},{21,5},{25,9},{2... | collective-permute-start | bytes 393224 | tf_op jit(solution)/shard_map/ppermute | solution.py:268
  99.1 88.1 %collective-permute-start.27 = (bf16[256,256]{1,0:T(8,128)(2,1)}, bf16[256,256]{1,0:T(8,128)(2,1)S(1)}, u32[]{:S(2)}, u32[]{:S(2)}) collective-permute-start(bf16[256,256]{1,0:T(8,128)(2,1)} %add_convert_fusion), channel_id=1, source_target_pairs={{0,8},{4,12},{28,4},{1,9},{5,13},{29,5},{2,10},{6,14},{30,6},{3,11... | collective-permute-start | bytes 393224 | tf_op jit(solution)/shard_map/ppermute | solution.py:268
  100.4 29.9 %copy-start.2 = (f32[2048,128]{1,0:T(8,128)S(1)}, f32[2048,128]{1,0:T(8,128)}, u32[]{:S(2)}) copy-start(f32[2048,128]{1,0:T(8,128)} %constant.63.clone.refs_2_) | copy-start | bytes 3145732
  127.0 8.0 %copy-start.13 = (bf16[256,256]{1,0:T(8,128)(2,1)}, bf16[256,256]{1,0:T(8,128)(2,1)S(1)}, u32[]{:S(2)}) copy-start(bf16[256,256]{1,0:T(8,128)(2,1)S(1)} %get-tuple-element.57) | copy-start | bytes 393220
  127.0 8.0 %copy-start.14 = (bf16[256,256]{1,0:T(8,128)(2,1)}, bf16[256,256]{1,0:T(8,128)(2,1)S(1)}, u32[]{:S(2)}) copy-start(bf16[256,256]{1,0:T(8,128)(2,1)S(1)} %get-tuple-element.56) | copy-start | bytes 393220
  127.0 8.0 %copy-start.15 = (bf16[256,256]{1,0:T(8,128)(2,1)}, bf16[256,256]{1,0:T(8,128)(2,1)S(1)}, u32[]{:S(2)}) copy-start(bf16[256,256]{1,0:T(8,128)(2,1)S(1)} %get-tuple-element.55) | copy-start | bytes 393220
  127.0 61.6 %collective-permute-start.14 = (bf16[256,256]{1,0:T(8,128)(2,1)}, bf16[256,256]{1,0:T(8,128)(2,1)S(1)}, u32[]{:S(2)}, u32[]{:S(2)}) collective-permute-start(bf16[256,256]{1,0:T(8,128)(2,1)} %get-tuple-element.53), channel_id=1, source_target_pairs={{0,4},{12,8},{20,16},{28,24},{1,5},{13,9},{21,17},{29,25},{2,6},{1... | collective-permute-start | bytes 393224 | tf_op jit(solution)/shard_map/ppermute | solution.py:268
  128.3 61.6 %collective-permute-start.15 = (bf16[256,256]{1,0:T(8,128)(2,1)}, bf16[256,256]{1,0:T(8,128)(2,1)S(1)}, u32[]{:S(2)}, u32[]{:S(2)}) collective-permute-start(bf16[256,256]{1,0:T(8,128)(2,1)} %get-tuple-element.54), channel_id=1, source_target_pairs={{0,24},{12,4},{16,8},{20,12},{24,16},{28,20},{1,25},{13,5},{17,9},... | collective-permute-start | bytes 393224 | tf_op jit(solution)/shard_map/ppermute | solution.py:268
  130.3 67.0 %copy-start.4 = (f32[2048,128]{1,0:T(8,128)S(1)}, f32[2048,128]{1,0:T(8,128)}, u32[]{:S(2)}) copy-start(f32[2048,128]{1,0:T(8,128)} %constant.62.clone.refs_1_) | copy-start | bytes 3145732
  130.3 67.0 %copy-start.7 = (bf16[256,256]{1,0:T(8,128)(2,1)S(1)}, bf16[256,256]{1,0:T(8,128)(2,1)}, u32[]{:S(2)}) copy-start(bf16[256,256]{1,0:T(8,128)(2,1)} %refs_4_.7) | copy-start | bytes 393220
  135.5 0.7 copy-start.17
  135.5 0.7 copy-start.18
  178.1 13.6 %collective-permute-start.16 = (bf16[256,256]{1,0:T(8,128)(2,1)}, bf16[256,256]{1,0:T(8,128)(2,1)S(1)}, u32[]{:S(2)}, u32[]{:S(2)}) collective-permute-start(bf16[256,256]{1,0:T(8,128)(2,1)} %copy-done.15), channel_id=1, source_target_pairs={{0,28},{8,4},{16,12},{20,8},{24,20},{28,16},{1,29},{9,5},{17,13},{... | collective-permute-start | bytes 393224 | tf_op jit(solution)/shard_map/ppermute | solution.py:268
  183.3 8.4 %collective-permute-start.17 = (bf16[256,256]{1,0:T(8,128)(2,1)}, bf16[256,256]{1,0:T(8,128)(2,1)S(1)}, u32[]{:S(2)}, u32[]{:S(2)}) collective-permute-start(bf16[256,256]{1,0:T(8,128)(2,1)} %copy-done.14), channel_id=1, source_target_pairs={{0,16},{20,4},{24,8},{28,12},{1,17},{21,5},{25,9},{29,13},{2,18},{... | collective-permute-start | bytes 393224 | tf_op jit(solution)/shard_map/ppermute | solution.py:268
  187.3 7.0 %collective-permute-start.18 = (bf16[256,256]{1,0:T(8,128)(2,1)}, bf16[256,256]{1,0:T(8,128)(2,1)S(1)}, u32[]{:S(2)}, u32[]{:S(2)}) collective-permute-start(bf16[256,256]{1,0:T(8,128)(2,1)} %copy-done.13), channel_id=1, source_target_pairs={{0,20},{16,4},{24,12},{28,8},{1,21},{17,5},{25,13},{29,9},{2,22},{... | collective-permute-start | bytes 393224 | tf_op jit(solution)/shard_map/ppermute | solution.py:268
  188.6 7.2 %collective-permute-start.19 = (bf16[256,256]{1,0:T(8,128)(2,1)S(1)}, bf16[256,256]{1,0:T(8,128)(2,1)S(1)}, u32[]{:S(2)}, u32[]{:S(2)}) collective-permute-start(bf16[256,256]{1,0:T(8,128)(2,1)S(1)} %get-tuple-element.58), channel_id=1, source_target_pairs={{0,8},{28,4},{1,9},{29,5},{2,10},{30,6},{3,11},{31,7}} | collective-permute-start | bytes 393224 | tf_op jit(solution)/shard_map/ppermute | solution.py:268
  189.9 7.4 %collective-permute-start.20 = (bf16[256,256]{1,0:T(8,128)(2,1)S(1)}, bf16[256,256]{1,0:T(8,128)(2,1)S(1)}, u32[]{:S(2)}, u32[]{:S(2)}) collective-permute-start(bf16[256,256]{1,0:T(8,128)(2,1)S(1)} %get-tuple-element.59), channel_id=1, source_target_pairs={{0,12},{24,4},{1,13},{25,5},{2,14},{26,6},{3,15},{27,7}} | collective-permute-start | bytes 393224 | tf_op jit(solution)/shard_map/ppermute | solution.py:268

commit v3 on v2

v3 whole, which is shorter than its diff:
```python
import math

import jax
import jax.numpy as jnp
import numpy as np
from jax import lax
from jax.experimental import pallas as pl
from jax.experimental.pallas import tpu as pltpu
from jax.sharding import PartitionSpec as P

ROPE_BASE = 1000000.0
EPS = 1e-06
HIDDEN = -100000.0
VMEM_LIMIT = 56 * 1024 * 1024
F32 = jnp.float32
BF16 = jnp.bfloat16


def rope_rows(starts, head_dim):
    half = head_dim // 2
    frequency = np.exp(
        np.arange(half, dtype=np.float32) * np.float32(-2.0 * math.log(ROPE_BASE) / head_dim)
    ).astype(np.float32)
    angles = np.asarray(starts, np.float32)[:, None] * frequency[None, :]
    cos = np.cos(angles.astype(np.float64)).astype(np.float32)
    sin = np.sin(angles.astype(np.float64)).astype(np.float32)
    return np.concatenate([cos, cos], 1), np.concatenate([-sin, sin], 1)


def block_tables(depth, tables):
    start_cos, start_sin, offset_cos, offset_sin = tables
    cos, sin = start_cos[pl.ds(depth, 1), :], start_sin[pl.ds(depth, 1), :]
    both_cos = cos * offset_cos[...] - sin * offset_sin[...]
    both_sin = sin * offset_cos[...] + cos * offset_sin[...]
    return both_cos, both_sin


def turned(rows, cos, sin):
    return rows * cos + pltpu.roll(rows, rows.shape[-1] // 2, 1) * sin


def turned_back(rows, cos, sin):
    return rows * cos - pltpu.roll(rows, rows.shape[-1] // 2, 1) * sin


def inverse_rms(rows):
    return lax.rsqrt(jnp.mean(rows * rows, -1, keepdims=True) + EPS)


def own_tables(depth_ref, tables, blocks):
    parts = [block_tables(depth_ref[a], tables) for a in range(blocks)]
    return jnp.concatenate([p[0] for p in parts], 0), jnp.concatenate([p[1] for p in parts], 0)


def dot_nn(lhs, rhs):
    return lax.dot_general(lhs, rhs, (((1,), (0,)), ((), ())), preferred_element_type=F32)


def plan_kernel(blocks, tree_dev, place_ref, anc_ref, plan_ref):
    slots = tree_dev * blocks
    place = place_ref[0]
    here = lax.rem(place + 1, tree_dev)
    for row in range(4):
        for i in range(slots):
            plan_ref[row, i] = 0

    def merge(b, carry):
        count, steps = carry[0], carry[1:]
        bits = jnp.int32(0)
        depth = jnp.int32(0)
        later = []
        for a in range(blocks):
            hit = anc_ref[a, jnp.minimum(steps[a], slots - 1)] == b
            bits = bits | jnp.where(hit, 1 << a, 0)
            depth = jnp.where(hit, steps[a], depth)
            later.append(steps[a] + jnp.where(hit, 1, 0))
        own = b - place * blocks
        slot = jnp.where(own >= 0, own, jnp.minimum(count, slots - 1))
        there = lax.rem(b // blocks + 1, tree_dev)
        odd = lax.rem(here + there, 2)
        near = here + odd * (1 - 2 * lax.rem(here, 2))
        piece = odd * (tree_dev // 2) + lax.rem(near - there + tree_dev, tree_dev) // 2
        plan_ref[0, slot] = piece
        plan_ref[1, slot] = lax.rem(b, blocks)
        plan_ref[2, slot] = depth
        plan_ref[3, slot] = bits
        count = count + jnp.where((own < 0) & (bits != 0), 1, 0)
        return (count, *later)

    zero = jnp.int32(0)
    count = lax.fori_loop(0, (place + 1) * blocks, merge, (jnp.int32(blocks), *([zero] * blocks)))[0]
    for i in range(slots):
        plan_ref[4, i] = count


def prep_kernel(blocks, block_len, kv_heads, depth_ref, t0, t1, t2, t3, gain_ref, q_ref, grad_ref, out_ref, *outs):
    tokens = q_ref.shape[0]
    head_dim = gain_ref.shape[1]
    cos, sin = own_tables(depth_ref, (t0, t1, t2, t3), blocks)
    gain = gain_ref[...]
    group = q_ref.shape[1] // head_dim // kv_heads
    for head in range(group * kv_heads):
        g = head % group
        q_t_ref, q_rot_ref, grad_t_ref, grad_heads_ref, delta_ref = outs[5 * (head // group):][:5]
        cols = pl.ds(head * head_dim, head_dim)
        here = pl.ds(g * tokens, tokens)
        rows = q_ref[:, cols].astype(F32)
        rotated = turned(rows * inverse_rms(rows) * gain, cos, sin)
        q_rot_ref[here, :] = rotated.astype(BF16)
        q_t_ref[:, here] = jnp.transpose(rotated).astype(BF16)
        grad = grad_ref[:, cols]
        grad_heads_ref[here, :] = grad
        grad_rows = jnp.transpose(grad.astype(F32))
        grad_t_ref[:, here] = grad_rows.astype(BF16)
        product = grad_rows * jnp.transpose(out_ref[:, cols].astype(F32))
        delta_ref[:, here] = jnp.sum(product, 0, keepdims=True)


def main_kernel(blocks, block_len, tree_dev, inv_root, head, whole_dots, *refs):
    plan_ref, gain_ref = refs[:2]
    tables = refs[2:6]
    pieces = refs[6:6 + tree_dev]
    q_t_ref, q_ref, grad_t_ref, grad_ref, delta_ref = refs[6 + tree_dev:11 + tree_dev]
    half = tree_dev // 2
    dq_ref, gain_part_ref = refs[11 + tree_dev:13 + tree_dev]
    straight = refs[13 + tree_dev:13 + tree_dev + half]
    crossed, raw, keys, keys_t, vals, shown, with_cos, with_sin, expo, mass, w_all, ds_all, found, spread, wide = refs[
        13 + tree_dev + half:]
    head_dim = gain_ref.shape[1]
    tokens = raw.shape[1]
    group = q_ref.shape[0] // tokens
    count = plan_ref[4, 0]
    chunks = (count + blocks - 1) // blocks
    gain = gain_ref[...]
    kv_heads = pieces[0].shape[1] // (2 * head_dim)
    for piece in range(tree_dev):
        raw[piece, :, 0:head_dim] = pieces[piece][:, head * head_dim:(head + 1) * head_dim]
        raw[piece, :, head_dim:] = pieces[piece][:, (kv_heads + head) * head_dim:(kv_heads + head + 1) * head_dim]
    query_block = lax.broadcasted_iota(jnp.int32, (1, tokens), 1) // block_len

    def rows_of(start):
        return pl.ds(pl.multiple_of(start * block_len, block_len), block_len)

    @pl.loop(0, chunks)
    def _(c):
        for j in range(blocks):
            slot = c * blocks + j
            piece = plan_ref[0, slot]
            rows = rows_of(plan_ref[1, slot])
            cos, sin = block_tables(plan_ref[2, slot], tables)
            unit = raw[piece, rows, 0:head_dim].astype(F32)
            unit = unit * inverse_rms(unit)
            here = pl.ds(j * block_len, block_len)
            with_cos[c, here, :] = unit * cos
            with_sin[c, here, :] = pltpu.roll(unit * sin, head_dim // 2, 1)
            keys[c, here, :] = turned(unit * gain, cos, sin).astype(BF16)
            bits = jnp.where(slot < count, plan_ref[3, slot], 0)
            row = jnp.zeros((1, tokens), F32)
            for a in range(blocks):
                seen = lax.rem(lax.shift_right_logical(bits, a), 2)
                row = jnp.where((query_block == a) & (seen == 0), HIDDEN, row)
            shown[c, j:j + 1, :] = row
            vals[c, here, :] = raw[piece, rows, head_dim:]
        keys_t[c] = jnp.transpose(keys[c].astype(F32)).astype(BF16)

    def exps(c, g, scores):
        parts = []
        for j in range(blocks):
            here = slice(j * block_len, (j + 1) * block_len)
            parts.append(jnp.exp(scores[here] * inv_root + shown[c, j:j + 1, :]))
        return jnp.concatenate(parts, 0)

    def summed(e):
        return jnp.sum(e.reshape(tokens // 8, 8, tokens), 0)

    key_row = lax.broadcasted_iota(jnp.int32, (tokens, tokens), 0)
    query_col = lax.broadcasted_iota(jnp.int32, (tokens, tokens), 1)

    def cols_of(g):
        return pl.ds(g * tokens, tokens)

    def masses(c, first):
        if whole_dots:
            wide[...] = dot_nn(keys[c], q_t_ref[...])
        for g in range(group):
            scores = wide[:, cols_of(g)] if whole_dots else dot_nn(keys[c], q_t_ref[:, cols_of(g)])
            e = exps(c, g, scores)
            if first:
                e = jnp.where(key_row <= query_col, e, 0.0)
            expo[c, g] = e
            mass[g] = summed(e) if first else mass[g] + summed(e)

    masses(0, True)

    @pl.loop(1, chunks)
    def _(c):
        masses(c, False)

    for g in range(group):
        total = jnp.sum(mass[g], 0, keepdims=True)
        mass[g] = jnp.broadcast_to(1.0 / total, (8, tokens))
    dq_ref[...] = jnp.zeros(dq_ref.shape, F32)
    gain_part_ref[...] = jnp.zeros(gain_part_ref.shape, F32)
    spread[...] = jnp.zeros(spread.shape, BF16)

    @pl.loop(0, chunks)
    def _(c):
        dk = jnp.zeros((tokens, head_dim), F32)
        dv = jnp.zeros((tokens, head_dim), F32)
        if whole_dots:
            wide[...] = dot_nn(vals[c], grad_t_ref[...])
        for g in range(group):
            cols = cols_of(g)
            grad_prob = wide[:, cols] if whole_dots else dot_nn(vals[c], grad_t_ref[:, cols])
            weights = expo[c, g] * mass[g, 0:1, :]
            dscore = (weights * (grad_prob - delta_ref[:, cols])).astype(BF16)
            weights = weights.astype(BF16)
            if whole_dots:
                w_all[:, cols] = weights
                ds_all[:, cols] = dscore
            else:
                dv = dv + dot_nn(weights, grad_ref[cols, :])
                dk = dk + dot_nn(dscore, q_ref[cols, :])
                dq_ref[:, cols] = dq_ref[:, cols] + dot_nn(keys_t[c], dscore)
        if whole_dots:
            dv = dot_nn(w_all[...], grad_ref[...])
            dk = dot_nn(ds_all[...], q_ref[...])
            dq_ref[...] = dq_ref[...] + dot_nn(keys_t[c], ds_all[...])
        dk = dk * inv_root
        found[c, :, 0:head_dim] = dk.astype(BF16)
        found[c, :, head_dim:] = dv.astype(BF16)
        front = jnp.sum((dk * with_cos[c]).reshape(tokens // 8, 8, head_dim), 0)
        back = jnp.sum((dk * with_sin[c]).reshape(tokens // 8, 8, head_dim), 0)
        gain_part_ref[...] = gain_part_ref[...] + front - pltpu.roll(back, head_dim // 2, 1)

    @pl.loop(0, count)
    def _(slot):
        rows = rows_of(lax.rem(slot, blocks))
        spread[plan_ref[0, slot], rows_of(plan_ref[1, slot]), :] = found[slot // blocks, rows, :]

    for piece in range(half):
        straight[piece][...] = spread[piece]
        crossed[piece] = spread[half + piece]


def merge_kernel(*refs):
    parts, crossed_ref, outs = refs[:len(refs) // 2], refs[len(refs) // 2], refs[len(refs) // 2 + 1:]
    outs[0][...] = (parts[0][...].astype(F32) + crossed_ref[0].astype(F32))
    for i in range(1, len(parts)):
        outs[i][...] = (parts[i][...].astype(F32) + crossed_ref[i].astype(F32)).astype(BF16)


def query_kernel(blocks, inv_root, depth_ref, t0, t1, t2, t3, gain_ref, q_ref, *refs):
    dq_refs, (out_ref, part_ref) = refs[:-2], refs[-2:]
    tokens = q_ref.shape[0]
    head_dim = gain_ref.shape[1]
    group = dq_refs[0].shape[1] // tokens
    cos, sin = own_tables(depth_ref, (t0, t1, t2, t3), blocks)
    gain = gain_ref[...]
    part = jnp.zeros((8, head_dim), F32)
    for head in range(group * len(dq_refs)):
        cols = pl.ds(head * head_dim, head_dim)
        rows = q_ref[:, cols].astype(F32)
        recip = inverse_rms(rows)
        normed = rows * recip
        dq = jnp.transpose(dq_refs[head // group][:, pl.ds(head % group * tokens, tokens)])
        scaled_grad = turned_back(dq, cos, sin) * inv_root
        term = scaled_grad * normed
        part = part + jnp.sum(term.reshape(tokens // 8, 8, head_dim), 0)
        inner = jnp.mean(term * gain, -1, keepdims=True)
        out_ref[:, cols] = (recip * (scaled_grad * gain - normed * inner)).astype(BF16)
    part_ref[...] = part


def key_kernel(blocks, counts, depth_ref, t0, t1, t2, t3, gain_ref, k_ref, *refs):
    sums, (dk_out_ref, dv_out_ref) = refs[:-2], refs[-2:]
    head_dim = gain_ref.shape[1]
    cos, sin = own_tables(depth_ref, (t0, t1, t2, t3), blocks)
    gain = gain_ref[...]
    for head, each in enumerate(counts):
        cols = pl.ds(head * head_dim, head_dim)
        rows = k_ref[:, cols].astype(F32)
        recip = inverse_rms(rows)
        normed = rows * recip
        mine = sums[sum(counts[:head]):][:each]
        both = mine[0][...].astype(F32)
        for other in mine[1:]:
            both = both + other[...].astype(F32)
        grad = turned_back(both[:, 0:head_dim], cos, sin) * gain
        inner = jnp.mean(grad * normed, -1, keepdims=True)
        dk_out_ref[:, cols] = (recip * (grad - normed * inner)).astype(BF16)
        dv_out_ref[:, cols] = both[:, head_dim:].astype(BF16)


class Tree:
    def __init__(self, size, cycle):
        self.size, self.cycle = size, cycle

    def order(self, index):
        return (index - 1) % self.size

    def send(self, value, target, wanted):
        pairs = []
        for tree in range(self.cycle // self.size):
            for index in range(self.size):
                if wanted(index):
                    ends = [(tree * self.size + 1 + self.order(i)) % self.cycle for i in (index, target(index))]
                    pairs.append(tuple(ends))
        return lax.ppermute(value, "ctx", pairs)

    def after(self, *pair):
        return self.order(pair[1] % self.size) > self.order(pair[0] % self.size)

    def gather(self, own):
        size, after = self.size, self.after
        cross = self.send(own, lambda i: i ^ 1, lambda i: after(i, i ^ 1))
        straight, crossed = [], []
        for step in range(2, size, 2):
            there = lambda i: (i + step) % size
            straight.append(self.send(own, there, lambda i: after(i, there(i)) or after(i, there(i) ^ 1)))
        for step, piece in zip(range(2, size, 2), straight):
            crossed.append(self.send(piece, lambda i: i ^ 1, lambda i: after(i - step, i ^ 1)))
        return [own, *straight, cross, *crossed]

    def across(self, crossed):
        steps = range(0, self.size, 2)
        return self.send(crossed, lambda i: i ^ 1, lambda i: any(self.after((i ^ 1) - step, i) for step in steps))

    def back(self, merged):
        size, after = self.size, self.after
        terms = []
        for step, both in zip(range(2, size, 2), merged):
            there = lambda i: (i - step) % size
            terms.append(self.send(both, there, lambda i: after(there(i), i) or after(there(i), i ^ 1)))
        return terms


def total_over(value, axis):
    size = lax.axis_size(axis)
    if size & (size - 1):
        return lax.psum(value, axis)
    bit = 1
    while bit < size:
        value = value + lax.ppermute(value, axis, [(i, i ^ bit) for i in range(size)])
        bit *= 2
    return value


def on_device(q_raw, k_raw, values, saved_out, out_grad, q_gain, k_gain, ancestors):
    tokens = q_raw.shape[0]
    head_dim = q_gain.shape[0]
    kv_heads = k_raw.shape[1] // head_dim
    heads = q_raw.shape[1] // head_dim
    group = heads // kv_heads
    blocks = ancestors.shape[0]
    tree_blocks = ancestors.shape[1]
    block_len = tokens // blocks
    tree_dev = tree_blocks // blocks
    cycle = lax.axis_size("ctx")
    inv_root = 1.0 / math.sqrt(head_dim)
    tree = Tree(tree_dev, cycle)
    place = (lax.axis_index("ctx") - 1 + cycle) % cycle % tree_dev
    place = place.reshape(1).astype(jnp.int32)

    depth = jnp.sum((ancestors >= 0).astype(jnp.int32), 1) - 1
    total_blocks = blocks * cycle
    in_tree = jnp.where(
        ancestors >= 0, (ancestors - blocks + total_blocks) % total_blocks % tree_blocks, -1
    )
    tables = [
        jnp.asarray(table)
        for starts in (range(0, tree_blocks * block_len, block_len), range(block_len))
        for table in rope_rows(starts, head_dim)
    ]
    q_gain_row, k_gain_row = q_gain.reshape(1, head_dim), k_gain.reshape(1, head_dim)

    pieces = tree.gather(jnp.concatenate([k_raw, values], 1))

    params = pltpu.CompilerParams(vmem_limit_bytes=VMEM_LIMIT)
    smem = pl.BlockSpec(memory_space=pltpu.SMEM)
    vmem = pl.BlockSpec(memory_space=pltpu.VMEM)
    sds = jax.ShapeDtypeStruct

    plan = pl.pallas_call(
        lambda *refs: plan_kernel(blocks, tree_dev, *refs),
        out_shape=sds((5, tree_blocks), jnp.int32),
        in_specs=[smem, smem],
        out_specs=smem,
        name="plan",
    )(place, in_tree)

    rows = group * tokens
    queries = pl.pallas_call(
        lambda *refs: prep_kernel(blocks, block_len, kv_heads, *refs),
        out_shape=tuple(
            [
                sds((head_dim, rows), BF16),
                sds((rows, head_dim), BF16),
                sds((head_dim, rows), BF16),
                sds((rows, head_dim), BF16),
                sds((1, rows), F32),
            ]
            * kv_heads
        ),
        in_specs=[smem] + [vmem] * 8,
        out_specs=tuple([vmem] * (5 * kv_heads)),
        compiler_params=params,
        name="prep",
    )(depth, *tables, q_gain_row, q_raw, out_grad, saved_out)

    half = tree_dev // 2

    def attend(h):
        return pl.pallas_call(
            lambda *refs: main_kernel(blocks, block_len, tree_dev, inv_root, h, h > 0, *refs),
            out_shape=(
                sds((head_dim, rows), F32),
                sds((8, head_dim), F32),
                *[sds((tokens, 2 * head_dim), BF16)] * half,
                sds((half, tokens, 2 * head_dim), BF16),
            ),
            in_specs=[smem] + [vmem] * (10 + tree_dev),
            out_specs=tuple([vmem] * (3 + half)),
            scratch_shapes=[
                pltpu.VMEM((tree_dev, tokens, 2 * head_dim), BF16),
                pltpu.VMEM((tree_dev, tokens, head_dim), BF16),
                pltpu.VMEM((tree_dev, head_dim, tokens), BF16),
                pltpu.VMEM((tree_dev, tokens, head_dim), BF16),
                pltpu.VMEM((tree_dev, 8 * ((blocks + 7) // 8), tokens), F32),
                pltpu.VMEM((tree_dev, tokens, head_dim), F32),
                pltpu.VMEM((tree_dev, tokens, head_dim), F32),
                pltpu.VMEM((tree_dev, group, tokens, tokens), F32),
                pltpu.VMEM((group, 8, tokens), F32),
                pltpu.VMEM((tokens, rows), BF16),
                pltpu.VMEM((tokens, rows), BF16),
                pltpu.VMEM((tree_dev, tokens, 2 * head_dim), BF16),
                pltpu.VMEM((tree_dev, tokens, 2 * head_dim), BF16),
                pltpu.VMEM((tokens, rows), F32),
            ],
            compiler_params=params,
            cost_estimate=pl.CostEstimate(
                flops=10 * group * tokens * tree_dev * tokens * head_dim,
                bytes_accessed=8 * 1024 * 1024,
                transcendentals=group * tokens * tree_dev * tokens,
            ),
            name="attend",
        )(plan, k_gain_row, *tables, *pieces, *queries[5 * h:5 * h + 5])

    dq, terms, counts, k_gain_parts = [], [], [], []
    for h in range(kv_heads):
        dq_here, k_gain_part, *parts, crossed = attend(h)
        dq.append(dq_here)
        k_gain_parts.append(k_gain_part)
        own, *merged = pl.pallas_call(
            merge_kernel,
            out_shape=tuple(
                sds((tokens, 2 * head_dim), F32 if i == 0 else BF16) for i in range(half)
            ),
            in_specs=[vmem] * (half + 1),
            out_specs=tuple([vmem] * half),
            compiler_params=params,
            name="merge",
        )(*parts, tree.across(crossed))
        mine = [own, *tree.back(merged)]
        terms.extend(mine)
        counts.append(len(mine))

    dq_raw, q_gain_part = pl.pallas_call(
        lambda *refs: query_kernel(blocks, inv_root, *refs),
        out_shape=(sds((tokens, heads * head_dim), BF16), sds((8, head_dim), F32)),
        in_specs=[smem] + [vmem] * (6 + kv_heads),
        out_specs=(vmem, vmem),
        compiler_params=params,
        name="query_back",
    )(depth, *tables, q_gain_row, q_raw, *dq)

    gains = jnp.stack([jnp.sum(q_gain_part, 0), jnp.sum(sum(k_gain_parts), 0)])
    gains = total_over(total_over(gains, "heads"), "ctx")

    dk_raw, dv = pl.pallas_call(
        lambda *refs: key_kernel(blocks, counts, *refs),
        out_shape=(sds(k_raw.shape, BF16), sds(k_raw.shape, BF16)),
        in_specs=[smem] + [vmem] * (6 + len(terms)),
        out_specs=(vmem, vmem),
        compiler_params=params,
        name="key_back",
    )(depth, *tables, k_gain_row, k_raw, *terms)
    return (dq_raw, dk_raw, dv, gains[0], gains[1])


def solution(mesh):
    split = P("ctx", "heads")
    return jax.shard_map(
        on_device,
        mesh=mesh,
        in_specs=(split, split, split, split, split, P(), P(), P("ctx", None)),
        out_specs=(split, split, split, P(), P()),
        check_vma=False,
    )
```

time: 201 us -> 144 us (0.72)
  the two profiles are of different devices: /device:TPU:0 before, /device:TPU:2 now
where the time goes in v3:
time: 144 us; the launch traced here: 142 us
  starting transfers between devices  66.1 us (46%)
  waiting for transfers between devices  34.7 us (24%)
  Pallas kernels  33.9 us (24%)
  local copies, waits for them, and re-layouts  4.48 us (3%)
  other arithmetic  2.01 us (1%)
    ppermute x15, starting transfers between devices, send(): return lax.ppermute(value, 'ctx', pairs)  63.9 us
    ppermute x15, waiting for transfers between devices, send(): return lax.ppermute(value, 'ctx', pairs)  22 us
    ppermute x5, waiting for transfers between devices, total_over(): lax.ppermute(value, axis, [(i, i ^ bit) for i in range(size)])  12.7 us
    pallas_call x2, Pallas kernels, attend(): pl.pallas_call(lambda *refs: main_kernel(blocks, block_len, tree_dev, inv...  12.7 us
    pallas_call x1, Pallas kernels, on_device(): pl.pallas_call(lambda *refs: prep_kernel(blocks, block_len, kv_heads, *re...  6.77 us
    pallas_call x1, Pallas kernels, on_device(): pl.pallas_call(lambda *refs: query_kernel(blocks, inv_root, *refs), out_s...  6.02 us
    pallas_call x2, Pallas kernels, on_device(): pl.pallas_call(merge_kernel, out_shape=tuple((sds((tokens, 2 * head_dim),...  4.37 us
    unnamed x41, local copies, waits for them, and re-layouts  3.95 us
  transfers between devices with their start and end apart: 20, of which 9 were waited for; matrix products, arithmetic and copies ran while one was open for 2% of the time, Pallas kernels for 17%

profile of v3, /device:TPU:2, one launch (start us, length us, event | category | flops | bytes accessed | tf_op | source)
XLA Modules:
  0.0 142.3 jit_solution(4591374052504339544)
XLA Ops:
  0.6 1.0 constant_dynamic-update-slice_fusion.1
  1.6 0.0 copy-done.2
  1.6 0.0 copy-start.12
  1.6 5.5 %collective-permute-start.2 = (bf16[256,512]{1,0:T(8,128)(2,1)S(1)}, bf16[256,512]{1,0:T(8,128)(2,1)S(1)}, u32[]{:S(2)}, u32[]{:S(2)}) collective-permute-start(bf16[256,512]{1,0:T(8,128)(2,1)S(1)} %constant_dynamic-update-slice_fusion.refs_6_), channel_id=1, source_target_pairs={{4,28},{8,0},{12,4},{5,29},{9,1},{13,5},{6,30},{10,2},{14,6},{7,31... | collective-permute-start | bytes 786440 | tf_op jit(solution)/shard_map/ppermute | solution.py:309
  7.2 1.9 %collective-permute-start.1 = (bf16[256,512]{1,0:T(8,128)(2,1)S(1)}, bf16[256,512]{1,0:T(8,128)(2,1)S(1)}, u32[]{:S(2)}, u32[]{:S(2)}) collective-permute-start(bf16[256,512]{1,0:T(8,128)(2,1)S(1)} %constant_dynamic-update-slice_fusion.refs_6_), channel_id=1, source_target_pairs={{4,20},{8,24},{12,28},{16,0},{20,4},{5,21},{9,25},{13,29},{17,1},{... | collective-permute-start | bytes 786440 | tf_op jit(solution)/shard_map/ppermute | solution.py:309
  9.1 1.9 %collective-permute-start = (bf16[256,512]{1,0:T(8,128)(2,1)S(1)}, bf16[256,512]{1,0:T(8,128)(2,1)S(1)}, u32[]{:S(2)}, u32[]{:S(2)}) collective-permute-start(bf16[256,512]{1,0:T(8,128)(2,1)S(1)} %constant_dynamic-update-slice_fusion.refs_6_), channel_id=1, source_target_pairs={{4,12},{8,16},{12,20},{16,24},{20,28},{24,0},{28,4},{5,13},{9,17},... | collective-permute-start | bytes 786440 | tf_op jit(solution)/shard_map/ppermute | solution.py:309
  11.0 1.3 collective-permute-start.3
  12.3 1.6 %collective-permute-done.2.refs_9_ = bf16[256,512]{1,0:T(8,128)(2,1)S(1)} collective-permute-done((bf16[256,512]{1,0:T(8,128)(2,1)S(1)}, bf16[256,512]{1,0:T(8,128)(2,1)S(1)}, u32[]{:S(2)}, u32[]{:S(2)}) %collective-permute-start.2) | collective-permute-done | bytes 262176 | tf_op jit(solution)/shard_map/ppermute | solution.py:309
  13.9 10.6 %collective-permute-start.6 = (bf16[256,512]{1,0:T(8,128)(2,1)S(1)}, bf16[256,512]{1,0:T(8,128)(2,1)S(1)}, u32[]{:S(2)}, u32[]{:S(2)}) collective-permute-start(bf16[256,512]{1,0:T(8,128)(2,1)S(1)} %collective-permute-done.2.refs_9_), channel_id=1, source_target_pairs={{4,0},{28,24},{5,1},{29,25},{6,2},{30,26},{7,3},{31,27}} | collective-permute-start | bytes 786440 | tf_op jit(solution)/shard_map/ppermute | solution.py:309
  24.5 1.3 collective-permute-start.5
  25.8 0.0 collective-permute-done.refs_7_
  25.8 1.3 collective-permute-start.4
  27.2 0.7 fusion.2
  27.9 1.6 %plan.1.refs_0_ = s32[5,32]{1,0:T(8,128)} custom-call(s32[1]{0:T(128)} %bitcast.1.refs_0_, s32[4,32]{1,0:T(4,128)} %get-tuple-element.77.refs_1_), custom_call_target="tpu_custom_call" | custom-call | tf_op jit(solution)/shard_map/plan/pallas_call | solution.py:384
  29.5 0.5 broadcast_add_fusion.refs_0_
  30.0 6.8 %prep.1 = (bf16[128,2048]{1,0:T(8,128)(2,1)}, bf16[2048,128]{1,0:T(8,128)(2,1)}, bf16[128,2048]{1,0:T(8,128)(2,1)}, bf16[2048,128]{1,0:T(8,128)(2,1)}, f32[1,204...) custom-call(s32[4]{0:T(128)} %broadcast_add_fusion.refs_0_, ...), custom_call_target="tpu_custom_call" | custom-call | tf_op jit(solution)/shard_map/prep/pallas_call | solution.py:393
  36.8 0.0 collective-permute-done.3.refs_10_
  36.9 3.8 %collective-permute-done.4.refs_11_ = bf16[256,512]{1,0:T(8,128)(2,1)S(1)} collective-permute-done((bf16[256,512]{1,0:T(8,128)(2,1)S(1)}, bf16[256,512]{1,0:T(8,128)(2,1)S(1)}, u32[]{:S(2)}, u32[]{:S(2)}) %collective-permute-start.4) | collective-permute-done | bytes 262176 | tf_op jit(solution)/shard_map/ppermute | solution.py:309
  40.7 0.7 copy-done.19
  41.4 6.7 %attend.2 = (f32[128,2048]{1,0:T(8,128)}, f32[8,128]{1,0:T(8,128)}, bf16[256,256]{1,0:T(8,128)(2,1)}, bf16[256,256]{1,0:T(8,128)(2,1)}, bf16[256,256]{1,0:T(8,12...) custom-call(s32[5,32]{1,0:T(8,128)} %plan.1.refs_0_, f32[1,128]{1,0:T(1,128)} %bitcast.17, ...), custom_call_target="tpu_custom_call" | custom-call | flops 5368709120 | bytes 8388608 | tf_op jit(solution)/shard_map/attend/pallas_call | solution.py:414
  48.2 1.3 collective-permute-start.7
  49.4 6.0 %attend.3 = (f32[128,2048]{1,0:T(8,128)}, f32[8,128]{1,0:T(8,128)}, bf16[256,256]{1,0:T(8,128)(2,1)}, bf16[256,256]{1,0:T(8,128)(2,1)}, bf16[256,256]{1,0:T(8,12...) custom-call(s32[5,32]{1,0:T(8,128)} %plan.1.refs_0_, f32[1,128]{1,0:T(1,128)} %bitcast.18, ...), custom_call_target="tpu_custom_call" | custom-call | flops 5368709120 | bytes 8388608 | tf_op jit(solution)/shard_map/attend/pallas_call | solution.py:414
  55.4 1.5 %collective-permute-start.11 = (bf16[4,256,256]{2,1,0:T(8,128)(2,1)}, bf16[4,256,256]{2,1,0:T(8,128)(2,1)S(1)}, u32[]{:S(2)}, u32[]{:S(2)}) collective-permute-start(bf16[4,256,256]{2,1,0:T(8,128)(2,1)} %get-tuple-element.67), channel_id=1, source_target_pairs={{0,4},{8,12},{12,8},{16,20},{20,16},{24,28},{28,24},{1,5},{9,13},{... | collective-permute-start | bytes 1572872 | tf_op jit(solution)/shard_map/ppermute | solution.py:309
  56.9 6.0 %query_back.1 = (bf16[256,2048]{1,0:T(8,128)(2,1)}, f32[8,128]{1,0:T(8,128)}) custom-call(s32[4]{0:T(128)} %broadcast_add_fusion.refs_0_, f32[32,128]{1,0:T(8,128)} %constant.66.clone.refs_1_.refs_2_, f32[32,128]{1,0:T(8,128)} %constant.67.clone.refs_2_.refs_3_, f32[64,128]{1,0:T(8,128)} %constant.68.clone.refs_3_.refs_4_, ...), custom_call_target="tpu_custom_call" | custom-call | tf_op jit(solution)/shard_map/query_back/pallas_call | solution.py:468
  62.9 0.7 reduce_sum.28
  63.6 0.1 collective-permute-start.15
  63.7 1.1 collective-permute-done.15
  64.8 2.0 %collective-permute-start.16 = (f32[2,128]{1,0:T(2,128)S(1)}, f32[2,128]{1,0:T(2,128)S(1)}, u32[]{:S(2)}, u32[]{:S(2)}) collective-permute-start(f32[2,128]{1,0:T(2,128)S(1)} %fusion.3), channel_id=1, source_target_pairs={{0,2},{1,3},{2,0},{3,1},{4,6},{5,7},{6,4},{7,5},{8,10},{9,11},{10,... | collective-permute-start | bytes 3080 | tf_op jit(solution)/shard_map/ppermute | solution.py:344
  66.9 10.2 %collective-permute-done.7.refs_4_ = bf16[4,256,256]{2,1,0:T(8,128)(2,1)S(1)} collective-permute-done((bf16[4,256,256]{2,1,0:T(8,128)(2,1)}, bf16[4,256,256]{2,1,0:T(8,128)(2,1)S(1)}, u32[]{:S(2)}, u32[]{:S(2)}) %collective-permute-start.7) | collective-permute-done | bytes 524320 | tf_op jit(solution)/shard_map/ppermute | solution.py:309
  77.1 0.8 copy-done.1
  77.9 2.2 %merge.2 = (f32[256,256]{1,0:T(8,128)}, bf16[256,256]{1,0:T(8,128)(2,1)}, bf16[256,256]{1,0:T(8,128)(2,1)}, bf16[256,256]{1,0:T(8,128)(2,1)}) custom-call(bf16[256,256]{1,0:T(8,128)(2,1)} %get-tuple-element.54.refs_0_, bf16[256,256]{1,0:T(8,128)(2,1)} %get-tuple-element.55.refs_1_, bf16[256,256]{1,0:T(8,128)(2,1)} %get-tuple-element.56.refs_2_, ...), custom_call_target="tpu_custom_call" | custom-call | tf_op jit(solution)/shard_map/merge/pallas_call | solution.py:454
  80.1 23.9 %collective-permute-start.8 = (bf16[256,256]{1,0:T(8,128)(2,1)}, bf16[256,256]{1,0:T(8,128)(2,1)S(1)}, u32[]{:S(2)}, u32[]{:S(2)}) collective-permute-start(bf16[256,256]{1,0:T(8,128)(2,1)} %get-tuple-element.60), channel_id=1, source_target_pairs={{0,24},{4,28},{12,4},{16,8},{20,12},{24,16},{28,20},{1,25},{5,29},... | collective-permute-start | bytes 393224 | tf_op jit(solution)/shard_map/ppermute | solution.py:309
  104.0 0.1 collective-permute-start.17
  104.1 3.6 %collective-permute-done.17 = f32[2,128]{1,0:T(2,128)S(1)} collective-permute-done((f32[2,128]{1,0:T(2,128)S(1)}, f32[2,128]{1,0:T(2,128)S(1)}, u32[]{:S(2)}, u32[]{:S(2)}) %collective-permute-start.17) | collective-permute-done | bytes 1056 | tf_op jit(solution)/shard_map/ppermute | solution.py:344
  107.7 3.6 %collective-permute-done.18 = f32[2,128]{1,0:T(2,128)S(1)} collective-permute-done((f32[2,128]{1,0:T(2,128)S(1)}, f32[2,128]{1,0:T(2,128)S(1)}, u32[]{:S(2)}, u32[]{:S(2)}) %collective-permute-start.18) | collective-permute-done | bytes 1056 | tf_op jit(solution)/shard_map/ppermute | solution.py:344
  111.3 4.5 %collective-permute-done.19 = f32[2,128]{1,0:T(2,128)S(1)} collective-permute-done((f32[2,128]{1,0:T(2,128)S(1)}, f32[2,128]{1,0:T(2,128)S(1)}, u32[]{:S(2)}, u32[]{:S(2)}) %collective-permute-start.19) | collective-permute-done | bytes 1056 | tf_op jit(solution)/shard_map/ppermute | solution.py:344
  115.7 1.9 %collective-permute-start.9 = (bf16[256,256]{1,0:T(8,128)(2,1)}, bf16[256,256]{1,0:T(8,128)(2,1)S(1)}, u32[]{:S(2)}, u32[]{:S(2)}) collective-permute-start(bf16[256,256]{1,0:T(8,128)(2,1)} %get-tuple-element.61), channel_id=1, source_target_pairs={{0,16},{4,20},{20,4},{24,8},{28,12},{1,17},{5,21},{21,5},{25,9},{2... | collective-permute-start | bytes 393224 | tf_op jit(solution)/shard_map/ppermute | solution.py:309
  117.6 1.9 %collective-permute-start.10 = (bf16[256,256]{1,0:T(8,128)(2,1)}, bf16[256,256]{1,0:T(8,128)(2,1)S(1)}, u32[]{:S(2)}, u32[]{:S(2)}) collective-permute-start(bf16[256,256]{1,0:T(8,128)(2,1)} %get-tuple-element.62), channel_id=1, source_target_pairs={{0,8},{4,12},{28,4},{1,9},{5,13},{29,5},{2,10},{6,14},{30,6},{3,11... | collective-permute-start | bytes 393224 | tf_op jit(solution)/shard_map/ppermute | solution.py:309
  119.6 0.8 copy-done
  120.4 2.2 %merge.3 = (f32[256,256]{1,0:T(8,128)}, bf16[256,256]{1,0:T(8,128)(2,1)}, bf16[256,256]{1,0:T(8,128)(2,1)}, bf16[256,256]{1,0:T(8,128)(2,1)}) custom-call(bf16[256,256]{1,0:T(8,128)(2,1)} %get-tuple-element.63.refs_0_, bf16[256,256]{1,0:T(8,128)(2,1)} %get-tuple-element.64.refs_1_, bf16[256,256]{1,0:T(8,128)(2,1)} %get-tuple-element.65.refs_2_, ...), custom_call_target="tpu_custom_call" | custom-call | tf_op jit(solution)/shard_map/merge/pallas_call | solution.py:454
  122.6 5.7 %collective-permute-start.12 = (bf16[256,256]{1,0:T(8,128)(2,1)}, bf16[256,256]{1,0:T(8,128)(2,1)S(1)}, u32[]{:S(2)}, u32[]{:S(2)}) collective-permute-start(bf16[256,256]{1,0:T(8,128)(2,1)} %get-tuple-element.69), channel_id=1, source_target_pairs={{0,24},{4,28},{12,4},{16,8},{20,12},{24,16},{28,20},{1,25},{5,29},... | collective-permute-start | bytes 393224 | tf_op jit(solution)/shard_map/ppermute | solution.py:309
  128.3 1.9 %collective-permute-start.13 = (bf16[256,256]{1,0:T(8,128)(2,1)}, bf16[256,256]{1,0:T(8,128)(2,1)S(1)}, u32[]{:S(2)}, u32[]{:S(2)}) collective-permute-start(bf16[256,256]{1,0:T(8,128)(2,1)} %get-tuple-element.70), channel_id=1, source_target_pairs={{0,16},{4,20},{20,4},{24,8},{28,12},{1,17},{5,21},{21,5},{25,9},{2... | collective-permute-start | bytes 393224 | tf_op jit(solution)/shard_map/ppermute | solution.py:309
  130.2 1.9 %collective-permute-start.14 = (bf16[256,256]{1,0:T(8,128)(2,1)}, bf16[256,256]{1,0:T(8,128)(2,1)S(1)}, u32[]{:S(2)}, u32[]{:S(2)}) collective-permute-start(bf16[256,256]{1,0:T(8,128)(2,1)} %get-tuple-element.71), channel_id=1, source_target_pairs={{0,8},{4,12},{28,4},{1,9},{5,13},{29,5},{2,10},{6,14},{30,6},{3,11... | collective-permute-start | bytes 393224 | tf_op jit(solution)/shard_map/ppermute | solution.py:309
  132.2 0.5 slice_bitcast_fusion
  132.7 3.8 %collective-permute-done.13.refs_13_ = bf16[256,256]{1,0:T(8,128)(2,1)S(1)} collective-permute-done((bf16[256,256]{1,0:T(8,128)(2,1)}, bf16[256,256]{1,0:T(8,128)(2,1)S(1)}, u32[]{:S(2)}, u32[]{:S(2)}) %collective-permute-start.13) | collective-permute-done | bytes 131104 | tf_op jit(solution)/shard_map/ppermute | solution.py:309
  136.5 2.6 %collective-permute-done.14.refs_14_ = bf16[256,256]{1,0:T(8,128)(2,1)S(1)} collective-permute-done((bf16[256,256]{1,0:T(8,128)(2,1)}, bf16[256,256]{1,0:T(8,128)(2,1)S(1)}, u32[]{:S(2)}, u32[]{:S(2)}) %collective-permute-start.14) | collective-permute-done | bytes 131104 | tf_op jit(solution)/shard_map/ppermute | solution.py:309
  139.1 0.6 copy-done.8
  139.8 2.5 %key_back.1 = (bf16[256,256]{1,0:T(8,128)(2,1)}, bf16[256,256]{1,0:T(8,128)(2,1)}) custom-call(s32[4]{0:T(128)} %broadcast_add_fusion.refs_0_, f32[32,128]{1,0:T(8,128)} %constant.66.clone.refs_1_.refs_2_, f32[32,128]{1,0:T(8,128)} %constant.67.clone.refs_2_.refs_3_, f32[64,128]{1,0:T(8,128)} %constant.68.clone.refs_3_.refs_4_, ...), custom_call_target="tpu_custom_call" | custom-call | tf_op jit(solution)/shard_map/key_back/pallas_call | solution.py:480
  (53 shorter events, 0.2 us)
Async XLA Ops:
  0.6 1.0 copy-start.2
  1.6 25.6 %copy-start.12 = (s32[4,32]{1,0:T(4,128)S(1)}, s32[4,32]{1,0:T(4,128)}, u32[]{:S(2)}) copy-start(s32[4,32]{1,0:T(4,128)} %param.19) | copy-start | bytes 1540
  1.6 35.1 %copy-start.9 = (bf16[256,512]{1,0:T(8,128)(2,1)}, bf16[256,512]{1,0:T(8,128)(2,1)S(1)}, u32[]{:S(2)}) copy-start(bf16[256,512]{1,0:T(8,128)(2,1)S(1)} %constant_dynamic-update-slice_fusion.refs_6_) | copy-start | bytes 786436
  1.6 12.2 %collective-permute-start.2 = (bf16[256,512]{1,0:T(8,128)(2,1)S(1)}, bf16[256,512]{1,0:T(8,128)(2,1)S(1)}, u32[]{:S(2)}, u32[]{:S(2)}) collective-permute-start(bf16[256,512]{1,0:T(8,128)(2,1)S(1)} %constant_dynamic-update-slice_fusion.refs_6_), channel_id=1, source_target_pairs={{4,28},{8,0},{12,4},{5,29},{9,1},{13,5},{6,30},{10,2},{14,6},{7,31... | collective-permute-start | bytes 786440 | tf_op jit(solution)/shard_map/ppermute | solution.py:309
  7.2 17.3 %collective-permute-start.1 = (bf16[256,512]{1,0:T(8,128)(2,1)S(1)}, bf16[256,512]{1,0:T(8,128)(2,1)S(1)}, u32[]{:S(2)}, u32[]{:S(2)}) collective-permute-start(bf16[256,512]{1,0:T(8,128)(2,1)S(1)} %constant_dynamic-update-slice_fusion.refs_6_), channel_id=1, source_target_pairs={{4,20},{8,24},{12,28},{16,0},{20,4},{5,21},{9,25},{13,29},{17,1},{... | collective-permute-start | bytes 786440 | tf_op jit(solution)/shard_map/ppermute | solution.py:309
  9.1 16.7 %collective-permute-start = (bf16[256,512]{1,0:T(8,128)(2,1)S(1)}, bf16[256,512]{1,0:T(8,128)(2,1)S(1)}, u32[]{:S(2)}, u32[]{:S(2)}) collective-permute-start(bf16[256,512]{1,0:T(8,128)(2,1)S(1)} %constant_dynamic-update-slice_fusion.refs_6_), channel_id=1, source_target_pairs={{4,12},{8,16},{12,20},{16,24},{20,28},{24,0},{28,4},{5,13},{9,17},... | collective-permute-start | bytes 786440 | tf_op jit(solution)/shard_map/ppermute | solution.py:309
  11.0 25.8 %collective-permute-start.3 = (bf16[256,512]{1,0:T(8,128)(2,1)S(1)}, bf16[256,512]{1,0:T(8,128)(2,1)S(1)}, u32[]{:S(2)}, u32[]{:S(2)}) collective-permute-start(bf16[256,512]{1,0:T(8,128)(2,1)S(1)} %constant_dynamic-update-slice_fusion.refs_6_), channel_id=1, source_target_pairs={{4,0},{8,12},{16,20},{24,28},{5,1},{9,13},{17,21},{25,29},{6,2},{1... | collective-permute-start | bytes 786440 | tf_op jit(solution)/shard_map/ppermute | solution.py:309
  13.9 22.9 %copy-start.13 = (bf16[256,512]{1,0:T(8,128)(2,1)}, bf16[256,512]{1,0:T(8,128)(2,1)S(1)}, u32[]{:S(2)}) copy-start(bf16[256,512]{1,0:T(8,128)(2,1)S(1)} %collective-permute-done.2.refs_9_) | copy-start | bytes 786436
  13.9 22.9 %collective-permute-start.6 = (bf16[256,512]{1,0:T(8,128)(2,1)S(1)}, bf16[256,512]{1,0:T(8,128)(2,1)S(1)}, u32[]{:S(2)}, u32[]{:S(2)}) collective-permute-start(bf16[256,512]{1,0:T(8,128)(2,1)S(1)} %collective-permute-done.2.refs_9_), channel_id=1, source_target_pairs={{4,0},{28,24},{5,1},{29,25},{6,2},{30,26},{7,3},{31,27}} | collective-permute-start | bytes 786440 | tf_op jit(solution)/shard_map/ppermute | solution.py:309
  24.5 12.3 %copy-start.14 = (bf16[256,512]{1,0:T(8,128)(2,1)}, bf16[256,512]{1,0:T(8,128)(2,1)S(1)}, u32[]{:S(2)}) copy-start(bf16[256,512]{1,0:T(8,128)(2,1)S(1)} %collective-permute-done.1.refs_8_) | copy-start | bytes 786436
  24.5 12.3 %collective-permute-start.5 = (bf16[256,512]{1,0:T(8,128)(2,1)S(1)}, bf16[256,512]{1,0:T(8,128)(2,1)S(1)}, u32[]{:S(2)}, u32[]{:S(2)}) collective-permute-start(bf16[256,512]{1,0:T(8,128)(2,1)S(1)} %collective-permute-done.1.refs_8_), channel_id=1, source_target_pairs={{4,0},{20,16},{24,28},{28,24},{5,1},{21,17},{25,29},{29,25},{6,2},... | collective-permute-start | bytes 786440 | tf_op jit(solution)/shard_map/ppermute | solution.py:309
  25.8 11.0 %copy-start.15 = (bf16[256,512]{1,0:T(8,128)(2,1)}, bf16[256,512]{1,0:T(8,128)(2,1)S(1)}, u32[]{:S(2)}) copy-start(bf16[256,512]{1,0:T(8,128)(2,1)S(1)} %collective-permute-done.refs_7_) | copy-start | bytes 786436
  25.8 14.9 %collective-permute-start.4 = (bf16[256,512]{1,0:T(8,128)(2,1)S(1)}, bf16[256,512]{1,0:T(8,128)(2,1)S(1)}, u32[]{:S(2)}, u32[]{:S(2)}) collective-permute-start(bf16[256,512]{1,0:T(8,128)(2,1)S(1)} %collective-permute-done.refs_7_), channel_id=1, source_target_pairs={{4,0},{12,8},{16,20},{20,16},{24,28},{28,24},{5,1},{13,9},{17,21},... | collective-permute-start | bytes 786440 | tf_op jit(solution)/shard_map/ppermute | solution.py:309
  36.8 3.9 %copy-start.16 = (bf16[256,512]{1,0:T(8,128)(2,1)}, bf16[256,512]{1,0:T(8,128)(2,1)S(1)}, u32[]{:S(2)}) copy-start(bf16[256,512]{1,0:T(8,128)(2,1)S(1)} %collective-permute-done.3.refs_10_) | copy-start | bytes 786436
  36.8 3.9 %copy-start.17 = (bf16[256,512]{1,0:T(8,128)(2,1)}, bf16[256,512]{1,0:T(8,128)(2,1)S(1)}, u32[]{:S(2)}) copy-start(bf16[256,512]{1,0:T(8,128)(2,1)S(1)} %collective-permute-done.6.refs_13_) | copy-start | bytes 786436
  36.9 3.8 %copy-start.18 = (bf16[256,512]{1,0:T(8,128)(2,1)}, bf16[256,512]{1,0:T(8,128)(2,1)S(1)}, u32[]{:S(2)}) copy-start(bf16[256,512]{1,0:T(8,128)(2,1)S(1)} %collective-permute-done.5.refs_12_) | copy-start | bytes 786436
  40.7 0.7 copy-start.19
  48.2 29.0 %collective-permute-start.7 = (bf16[4,256,256]{2,1,0:T(8,128)(2,1)}, bf16[4,256,256]{2,1,0:T(8,128)(2,1)S(1)}, u32[]{:S(2)}, u32[]{:S(2)}) collective-permute-start(bf16[4,256,256]{2,1,0:T(8,128)(2,1)} %get-tuple-element.58), channel_id=1, source_target_pairs={{0,4},{8,12},{12,8},{16,20},{20,16},{24,28},{28,24},{1,5},{9,13},{... | collective-permute-start | bytes 1572872 | tf_op jit(solution)/shard_map/ppermute | solution.py:309
  55.4 64.2 %collective-permute-start.11 = (bf16[4,256,256]{2,1,0:T(8,128)(2,1)}, bf16[4,256,256]{2,1,0:T(8,128)(2,1)S(1)}, u32[]{:S(2)}, u32[]{:S(2)}) collective-permute-start(bf16[4,256,256]{2,1,0:T(8,128)(2,1)} %get-tuple-element.67), channel_id=1, source_target_pairs={{0,4},{8,12},{12,8},{16,20},{20,16},{24,28},{28,24},{1,5},{9,13},{... | collective-permute-start | bytes 1572872 | tf_op jit(solution)/shard_map/ppermute | solution.py:309
  62.9 0.7 copy-start.10
  62.9 0.7 copy-start.11
  63.6 1.2 collective-permute-start.15
  64.8 39.2 %collective-permute-start.16 = (f32[2,128]{1,0:T(2,128)S(1)}, f32[2,128]{1,0:T(2,128)S(1)}, u32[]{:S(2)}, u32[]{:S(2)}) collective-permute-start(f32[2,128]{1,0:T(2,128)S(1)} %fusion.3), channel_id=1, source_target_pairs={{0,2},{1,3},{2,0},{3,1},{4,6},{5,7},{6,4},{7,5},{8,10},{9,11},{10,... | collective-permute-start | bytes 3080 | tf_op jit(solution)/shard_map/ppermute | solution.py:344
  77.1 0.8 copy-start.1
  80.1 50.1 %collective-permute-start.8 = (bf16[256,256]{1,0:T(8,128)(2,1)}, bf16[256,256]{1,0:T(8,128)(2,1)S(1)}, u32[]{:S(2)}, u32[]{:S(2)}) collective-permute-start(bf16[256,256]{1,0:T(8,128)(2,1)} %get-tuple-element.60), channel_id=1, source_target_pairs={{0,24},{4,28},{12,4},{16,8},{20,12},{24,16},{28,20},{1,25},{5,29},... | collective-permute-start | bytes 393224 | tf_op jit(solution)/shard_map/ppermute | solution.py:309
  104.0 3.6 %collective-permute-start.17 = (f32[2,128]{1,0:T(2,128)S(1)}, f32[2,128]{1,0:T(2,128)S(1)}, u32[]{:S(2)}, u32[]{:S(2)}) collective-permute-start(f32[2,128]{1,0:T(2,128)S(1)} %fusion.4), channel_id=1, source_target_pairs={{0,4},{4,0},{8,12},{12,8},{16,20},{20,16},{24,28},{28,24},{1,5},{5... | collective-permute-start | bytes 3080 | tf_op jit(solution)/shard_map/ppermute | solution.py:344
  107.7 3.6 %collective-permute-start.18 = (f32[2,128]{1,0:T(2,128)S(1)}, f32[2,128]{1,0:T(2,128)S(1)}, u32[]{:S(2)}, u32[]{:S(2)}) collective-permute-start(f32[2,128]{1,0:T(2,128)S(1)} %add.64), channel_id=1, source_target_pairs={{0,8},{4,12},{8,0},{12,4},{16,24},{20,28},{24,16},{28,20},{1,9},{5... | collective-permute-start | bytes 3080 | tf_op jit(solution)/shard_map/ppermute | solution.py:344
  111.3 4.5 %collective-permute-start.19 = (f32[2,128]{1,0:T(2,128)S(1)}, f32[2,128]{1,0:T(2,128)S(1)}, u32[]{:S(2)}, u32[]{:S(2)}) collective-permute-start(f32[2,128]{1,0:T(2,128)S(1)} %add.65), channel_id=1, source_target_pairs={{0,16},{4,20},{8,24},{12,28},{16,0},{20,4},{24,8},{28,12},{1,17},{... | collective-permute-start | bytes 3080 | tf_op jit(solution)/shard_map/ppermute | solution.py:344
  115.7 16.9 %collective-permute-start.9 = (bf16[256,256]{1,0:T(8,128)(2,1)}, bf16[256,256]{1,0:T(8,128)(2,1)S(1)}, u32[]{:S(2)}, u32[]{:S(2)}) collective-permute-start(bf16[256,256]{1,0:T(8,128)(2,1)} %get-tuple-element.61), channel_id=1, source_target_pairs={{0,16},{4,20},{20,4},{24,8},{28,12},{1,17},{5,21},{21,5},{25,9},{2... | collective-permute-start | bytes 393224 | tf_op jit(solution)/shard_map/ppermute | solution.py:309
  117.6 15.0 %collective-permute-start.10 = (bf16[256,256]{1,0:T(8,128)(2,1)}, bf16[256,256]{1,0:T(8,128)(2,1)S(1)}, u32[]{:S(2)}, u32[]{:S(2)}) collective-permute-start(bf16[256,256]{1,0:T(8,128)(2,1)} %get-tuple-element.62), channel_id=1, source_target_pairs={{0,8},{4,12},{28,4},{1,9},{5,13},{29,5},{2,10},{6,14},{30,6},{3,11... | collective-permute-start | bytes 393224 | tf_op jit(solution)/shard_map/ppermute | solution.py:309
  119.6 0.8 copy-start
  122.6 10.1 %collective-permute-start.12 = (bf16[256,256]{1,0:T(8,128)(2,1)}, bf16[256,256]{1,0:T(8,128)(2,1)S(1)}, u32[]{:S(2)}, u32[]{:S(2)}) collective-permute-start(bf16[256,256]{1,0:T(8,128)(2,1)} %get-tuple-element.69), channel_id=1, source_target_pairs={{0,24},{4,28},{12,4},{16,8},{20,12},{24,16},{28,20},{1,25},{5,29},... | collective-permute-start | bytes 393224 | tf_op jit(solution)/shard_map/ppermute | solution.py:309
  128.3 8.2 %collective-permute-start.13 = (bf16[256,256]{1,0:T(8,128)(2,1)}, bf16[256,256]{1,0:T(8,128)(2,1)S(1)}, u32[]{:S(2)}, u32[]{:S(2)}) collective-permute-start(bf16[256,256]{1,0:T(8,128)(2,1)} %get-tuple-element.70), channel_id=1, source_target_pairs={{0,16},{4,20},{20,4},{24,8},{28,12},{1,17},{5,21},{21,5},{25,9},{2... | collective-permute-start | bytes 393224 | tf_op jit(solution)/shard_map/ppermute | solution.py:309
  130.2 8.9 %copy-start.3 = (bf16[256,256]{1,0:T(8,128)(2,1)}, bf16[256,256]{1,0:T(8,128)(2,1)S(1)}, u32[]{:S(2)}) copy-start(bf16[256,256]{1,0:T(8,128)(2,1)S(1)} %collective-permute-done.8.refs_8_) | copy-start | bytes 393220
  130.2 8.9 %collective-permute-start.14 = (bf16[256,256]{1,0:T(8,128)(2,1)}, bf16[256,256]{1,0:T(8,128)(2,1)S(1)}, u32[]{:S(2)}, u32[]{:S(2)}) collective-permute-start(bf16[256,256]{1,0:T(8,128)(2,1)} %get-tuple-element.71), channel_id=1, source_target_pairs={{0,8},{4,12},{28,4},{1,9},{5,13},{29,5},{2,10},{6,14},{30,6},{3,11... | collective-permute-start | bytes 393224 | tf_op jit(solution)/shard_map/ppermute | solution.py:309
  132.7 6.4 %copy-start.4 = (bf16[256,256]{1,0:T(8,128)(2,1)}, bf16[256,256]{1,0:T(8,128)(2,1)S(1)}, u32[]{:S(2)}) copy-start(bf16[256,256]{1,0:T(8,128)(2,1)S(1)} %collective-permute-done.9.refs_9_) | copy-start | bytes 393220
  132.7 6.4 %copy-start.5 = (bf16[256,256]{1,0:T(8,128)(2,1)}, bf16[256,256]{1,0:T(8,128)(2,1)S(1)}, u32[]{:S(2)}) copy-start(bf16[256,256]{1,0:T(8,128)(2,1)S(1)} %collective-permute-done.10.refs_10_) | copy-start | bytes 393220
  132.7 6.4 %copy-start.6 = (bf16[256,256]{1,0:T(8,128)(2,1)}, bf16[256,256]{1,0:T(8,128)(2,1)S(1)}, u32[]{:S(2)}) copy-start(bf16[256,256]{1,0:T(8,128)(2,1)S(1)} %collective-permute-done.12.refs_12_) | copy-start | bytes 393220
  136.5 2.6 %copy-start.7 = (bf16[256,256]{1,0:T(8,128)(2,1)}, bf16[256,256]{1,0:T(8,128)(2,1)S(1)}, u32[]{:S(2)}) copy-start(bf16[256,256]{1,0:T(8,128)(2,1)S(1)} %collective-permute-done.13.refs_13_) | copy-start | bytes 393220
  139.1 0.7 copy-start.8

commit v4 on v3

--- a/solution.py
+++ b/solution.py
@@ -59,36 +59,31 @@
 def plan_kernel(blocks, tree_dev, place_ref, anc_ref, plan_ref):
     slots = tree_dev * blocks
     place = place_ref[0]
-    here = lax.rem(place + 1, tree_dev)
+    here = jnp.where(place + 1 == tree_dev, 0, place + 1)
     for row in range(4):
         for i in range(slots):
             plan_ref[row, i] = 0
-
-    def merge(b, carry):
-        count, steps = carry[0], carry[1:]
+    count = jnp.int32(blocks)
+    steps = [jnp.int32(0)] * blocks
+    for b in range(slots):
         bits = jnp.int32(0)
         depth = jnp.int32(0)
-        later = []
         for a in range(blocks):
             hit = anc_ref[a, jnp.minimum(steps[a], slots - 1)] == b
             bits = bits | jnp.where(hit, 1 << a, 0)
             depth = jnp.where(hit, steps[a], depth)
-            later.append(steps[a] + jnp.where(hit, 1, 0))
-        own = b - place * blocks
-        slot = jnp.where(own >= 0, own, jnp.minimum(count, slots - 1))
-        there = lax.rem(b // blocks + 1, tree_dev)
-        odd = lax.rem(here + there, 2)
-        near = here + odd * (1 - 2 * lax.rem(here, 2))
-        piece = odd * (tree_dev // 2) + lax.rem(near - there + tree_dev, tree_dev) // 2
-        plan_ref[0, slot] = piece
-        plan_ref[1, slot] = lax.rem(b, blocks)
+            steps[a] = steps[a] + jnp.where(hit, 1, 0)
+        own = place == b // blocks
+        slot = jnp.where(own, b % blocks, jnp.minimum(count, slots - 1))
+        there = (b // blocks + 1) % tree_dev
+        odd = jnp.bitwise_and(here + there, 1)
+        gap = jnp.bitwise_xor(here, odd) - there
+        gap = jnp.where(gap < 0, gap + tree_dev, gap)
+        plan_ref[0, slot] = odd * (tree_dev // 2) + lax.shift_right_logical(gap, 1)
+        plan_ref[1, slot] = b % blocks
         plan_ref[2, slot] = depth
         plan_ref[3, slot] = bits
-        count = count + jnp.where((own < 0) & (bits != 0), 1, 0)
-        return (count, *later)
-
-    zero = jnp.int32(0)
-    count = lax.fori_loop(0, (place + 1) * blocks, merge, (jnp.int32(blocks), *([zero] * blocks)))[0]
+        count = count + jnp.where(own | (bits == 0), 0, 1)
     for i in range(slots):
         plan_ref[4, i] = count
 
@@ -105,18 +100,17 @@
         cols = pl.ds(head * head_dim, head_dim)
         here = pl.ds(g * tokens, tokens)
         rows = q_ref[:, cols].astype(F32)
-        rotated = turned(rows * inverse_rms(rows) * gain, cos, sin)
-        q_rot_ref[here, :] = rotated.astype(BF16)
-        q_t_ref[:, here] = jnp.transpose(rotated).astype(BF16)
+        rotated = turned(rows * inverse_rms(rows) * gain, cos, sin).astype(BF16)
+        q_rot_ref[here, :] = rotated
+        q_t_ref[:, here] = jnp.transpose(rotated)
         grad = grad_ref[:, cols]
         grad_heads_ref[here, :] = grad
-        grad_rows = jnp.transpose(grad.astype(F32))
-        grad_t_ref[:, here] = grad_rows.astype(BF16)
-        product = grad_rows * jnp.transpose(out_ref[:, cols].astype(F32))
-        delta_ref[:, here] = jnp.sum(product, 0, keepdims=True)
-
-
-def main_kernel(blocks, block_len, tree_dev, inv_root, head, whole_dots, *refs):
+        grad_t_ref[:, here] = jnp.transpose(grad)
+        product = grad.astype(F32) * out_ref[:, cols].astype(F32)
+        delta_ref[:, here] = jnp.sum(jnp.transpose(product), 0, keepdims=True)
+
+
+def main_kernel(blocks, block_len, tree_dev, inv_root, staged, *refs):
     plan_ref, gain_ref = refs[:2]
     tables = refs[2:6]
     pieces = refs[6:6 + tree_dev]
@@ -132,19 +126,16 @@
     count = plan_ref[4, 0]
     chunks = (count + blocks - 1) // blocks
     gain = gain_ref[...]
-    kv_heads = pieces[0].shape[1] // (2 * head_dim)
     for piece in range(tree_dev):
-        raw[piece, :, 0:head_dim] = pieces[piece][:, head * head_dim:(head + 1) * head_dim]
-        raw[piece, :, head_dim:] = pieces[piece][:, (kv_heads + head) * head_dim:(kv_heads + head + 1) * head_dim]
+        raw[piece] = pieces[piece][...]
     query_block = lax.broadcasted_iota(jnp.int32, (1, tokens), 1) // block_len
 
     def rows_of(start):
         return pl.ds(pl.multiple_of(start * block_len, block_len), block_len)
 
-    @pl.loop(0, chunks)
-    def _(c):
+    def load_chunk(c):
         for j in range(blocks):
-            slot = c * blocks + j
+            slot = jnp.minimum(c * blocks + j, tree_dev * blocks - 1)
             piece = plan_ref[0, slot]
             rows = rows_of(plan_ref[1, slot])
             cos, sin = block_tables(plan_ref[2, slot], tables)
@@ -154,7 +145,7 @@
             with_cos[c, here, :] = unit * cos
             with_sin[c, here, :] = pltpu.roll(unit * sin, head_dim // 2, 1)
             keys[c, here, :] = turned(unit * gain, cos, sin).astype(BF16)
-            bits = jnp.where(slot < count, plan_ref[3, slot], 0)
+            bits = jnp.where(c * blocks + j < count, plan_ref[3, slot], 0)
             row = jnp.zeros((1, tokens), F32)
             for a in range(blocks):
                 seen = lax.rem(lax.shift_right_logical(bits, a), 2)
@@ -180,21 +171,24 @@
         return pl.ds(g * tokens, tokens)
 
     def masses(c, first):
-        if whole_dots:
+        if staged:
             wide[...] = dot_nn(keys[c], q_t_ref[...])
         for g in range(group):
-            scores = wide[:, cols_of(g)] if whole_dots else dot_nn(keys[c], q_t_ref[:, cols_of(g)])
+            scores = wide[:, cols_of(g)] if staged else dot_nn(keys[c], q_t_ref[:, cols_of(g)])
             e = exps(c, g, scores)
             if first:
                 e = jnp.where(key_row <= query_col, e, 0.0)
             expo[c, g] = e
             mass[g] = summed(e) if first else mass[g] + summed(e)
 
+    load_chunk(0)
     masses(0, True)
+    load_chunk(1)
 
     @pl.loop(1, chunks)
     def _(c):
         masses(c, False)
+        load_chunk(c + 1)
 
     for g in range(group):
         total = jnp.sum(mass[g], 0, keepdims=True)
@@ -205,27 +199,17 @@
 
     @pl.loop(0, chunks)
     def _(c):
-        dk = jnp.zeros((tokens, head_dim), F32)
-        dv = jnp.zeros((tokens, head_dim), F32)
-        if whole_dots:
+        if staged:
             wide[...] = dot_nn(vals[c], grad_t_ref[...])
         for g in range(group):
             cols = cols_of(g)
-            grad_prob = wide[:, cols] if whole_dots else dot_nn(vals[c], grad_t_ref[:, cols])
+            grad_prob = wide[:, cols] if staged else dot_nn(vals[c], grad_t_ref[:, cols])
             weights = expo[c, g] * mass[g, 0:1, :]
-            dscore = (weights * (grad_prob - delta_ref[:, cols])).astype(BF16)
-            weights = weights.astype(BF16)
-            if whole_dots:
-                w_all[:, cols] = weights
-                ds_all[:, cols] = dscore
-            else:
-                dv = dv + dot_nn(weights, grad_ref[cols, :])
-                dk = dk + dot_nn(dscore, q_ref[cols, :])
-                dq_ref[:, cols] = dq_ref[:, cols] + dot_nn(keys_t[c], dscore)
-        if whole_dots:
-            dv = dot_nn(w_all[...], grad_ref[...])
-            dk = dot_nn(ds_all[...], q_ref[...])
-            dq_ref[...] = dq_ref[...] + dot_nn(keys_t[c], ds_all[...])
+            ds_all[:, cols] = (weights * (grad_prob - delta_ref[:, cols])).astype(BF16)
+            w_all[:, cols] = weights.astype(BF16)
+        dv = dot_nn(w_all[...], grad_ref[...])
+        dk = dot_nn(ds_all[...], q_ref[...])
+        dq_ref[...] = dq_ref[...] + dot_nn(keys_t[c], ds_all[...])
         dk = dk * inv_root
         found[c, :, 0:head_dim] = dk.astype(BF16)
         found[c, :, head_dim:] = dv.astype(BF16)
@@ -273,7 +257,8 @@
 
 
 def key_kernel(blocks, counts, depth_ref, t0, t1, t2, t3, gain_ref, k_ref, *refs):
-    sums, (dk_out_ref, dv_out_ref) = refs[:-2], refs[-2:]
+    sums, (gains_ref, dk_out_ref, dv_out_ref, total_ref) = refs[:-4], refs[-4:]
+    total_ref[...] = jnp.sum(gains_ref[...], 0)
     head_dim = gain_ref.shape[1]
     cos, sin = own_tables(depth_ref, (t0, t1, t2, t3), blocks)
     gain = gain_ref[...]
@@ -313,14 +298,13 @@
 
     def gather(self, own):
         size, after = self.size, self.after
-        cross = self.send(own, lambda i: i ^ 1, lambda i: after(i, i ^ 1))
-        straight, crossed = [], []
-        for step in range(2, size, 2):
-            there = lambda i: (i + step) % size
-            straight.append(self.send(own, there, lambda i: after(i, there(i)) or after(i, there(i) ^ 1)))
-        for step, piece in zip(range(2, size, 2), straight):
-            crossed.append(self.send(piece, lambda i: i ^ 1, lambda i: after(i - step, i ^ 1)))
-        return [own, *straight, cross, *crossed]
+        pieces = [own]
+        for odd in range(2):
+            for step in range(0, size, 2):
+                if odd or step:
+                    there = lambda i: (i + step) % size ^ odd
+                    pieces.append(self.send(own, there, lambda i: after(i, there(i))))
+        return pieces
 
     def across(self, crossed):
         steps = range(0, self.size, 2)
@@ -333,17 +317,6 @@
             there = lambda i: (i - step) % size
             terms.append(self.send(both, there, lambda i: after(there(i), i) or after(there(i), i ^ 1)))
         return terms
-
-
-def total_over(value, axis):
-    size = lax.axis_size(axis)
-    if size & (size - 1):
-        return lax.psum(value, axis)
-    bit = 1
-    while bit < size:
-        value = value + lax.ppermute(value, axis, [(i, i ^ bit) for i in range(size)])
-        bit *= 2
-    return value
 
 
 def on_device(q_raw, k_raw, values, saved_out, out_grad, q_gain, k_gain, ancestors):
@@ -374,7 +347,10 @@
     ]
     q_gain_row, k_gain_row = q_gain.reshape(1, head_dim), k_gain.reshape(1, head_dim)
 
-    pieces = tree.gather(jnp.concatenate([k_raw, values], 1))
+    pieces = []
+    for h in range(kv_heads):
+        cols = slice(h * head_dim, (h + 1) * head_dim)
+        pieces.append(tree.gather(jnp.concatenate([k_raw[:, cols], values[:, cols]], 1)))
 
     params = pltpu.CompilerParams(vmem_limit_bytes=VMEM_LIMIT)
     smem = pl.BlockSpec(memory_space=pltpu.SMEM)
@@ -412,7 +388,7 @@
 
     def attend(h):
         return pl.pallas_call(
-            lambda *refs: main_kernel(blocks, block_len, tree_dev, inv_root, h, h > 0, *refs),
+            lambda *refs: main_kernel(blocks, block_len, tree_dev, inv_root, h > 0, *refs),
             out_shape=(
                 sds((head_dim, rows), F32),
                 sds((8, head_dim), F32),
@@ -423,12 +399,12 @@
             out_specs=tuple([vmem] * (3 + half)),
             scratch_shapes=[
                 pltpu.VMEM((tree_dev, tokens, 2 * head_dim), BF16),
-                pltpu.VMEM((tree_dev, tokens, head_dim), BF16),
-                pltpu.VMEM((tree_dev, head_dim, tokens), BF16),
-                pltpu.VMEM((tree_dev, tokens, head_dim), BF16),
-                pltpu.VMEM((tree_dev, 8 * ((blocks + 7) // 8), tokens), F32),
-                pltpu.VMEM((tree_dev, tokens, head_dim), F32),
-                pltpu.VMEM((tree_dev, tokens, head_dim), F32),
+                pltpu.VMEM((tree_dev + 1, tokens, head_dim), BF16),
+                pltpu.VMEM((tree_dev + 1, head_dim, tokens), BF16),
+                pltpu.VMEM((tree_dev + 1, tokens, head_dim), BF16),
+                pltpu.VMEM((tree_dev + 1, 8 * ((blocks + 7) // 8), tokens), F32),
+                pltpu.VMEM((tree_dev + 1, tokens, head_dim), F32),
+                pltpu.VMEM((tree_dev + 1, tokens, head_dim), F32),
                 pltpu.VMEM((tree_dev, group, tokens, tokens), F32),
                 pltpu.VMEM((group, 8, tokens), F32),
                 pltpu.VMEM((tokens, rows), BF16),
@@ -444,7 +420,7 @@
                 transcendentals=group * tokens * tree_dev * tokens,
             ),
             name="attend",
-        )(plan, k_gain_row, *tables, *pieces, *queries[5 * h:5 * h + 5])
+        )(plan, k_gain_row, *tables, *pieces[h], *queries[5 * h:5 * h + 5])
 
     dq, terms, counts, k_gain_parts = [], [], [], []
     for h in range(kv_heads):
@@ -475,17 +451,17 @@
     )(depth, *tables, q_gain_row, q_raw, *dq)
 
     gains = jnp.stack([jnp.sum(q_gain_part, 0), jnp.sum(sum(k_gain_parts), 0)])
-    gains = total_over(total_over(gains, "heads"), "ctx")
-
-    dk_raw, dv = pl.pallas_call(
+    gains = lax.all_gather(gains, ("ctx", "heads"))
+
+    dk_raw, dv, total = pl.pallas_call(
         lambda *refs: key_kernel(blocks, counts, *refs),
-        out_shape=(sds(k_raw.shape, BF16), sds(k_raw.shape, BF16)),
-        in_specs=[smem] + [vmem] * (6 + len(terms)),
-        out_specs=(vmem, vmem),
+        out_shape=(sds(k_raw.shape, BF16), sds(k_raw.shape, BF16), sds(gains.shape[1:], F32)),
+        in_specs=[smem] + [vmem] * (7 + len(terms)),
+        out_specs=(vmem, vmem, vmem),
         compiler_params=params,
         name="key_back",
-    )(depth, *tables, k_gain_row, k_raw, *terms)
-    return (dq_raw, dk_raw, dv, gains[0], gains[1])
+    )(depth, *tables, k_gain_row, k_raw, *terms, gains)
+    return (dq_raw, dk_raw, dv, total[0], total[1])
 
 
 def solution(mesh):

time: 144 us -> 166 us (1.15)
  the two profiles are of different devices: /device:TPU:2 before, /device:TPU:0 now
where the time goes in v4:
time: 166 us
  Pallas kernels  60.6 us (37%)
  blocking collectives  46.2 us (28%)
  starting transfers between devices  45 us (27%)
  waiting for transfers between devices  5.71 us (3%)
  local copies, waits for them, and re-layouts  5.32 us (3%)
  other arithmetic  1.97 us (1%)
    all_gather x1, blocking collectives, on_device(): gains = lax.all_gather(gains, ('ctx', 'heads'))  46.2 us
    ppermute x22, starting transfers between devices, send(): return lax.ppermute(value, 'ctx', pairs)  45 us
    pallas_call x2, Pallas kernels, attend(): pl.pallas_call(lambda *refs: main_kernel(blocks, block_len, tree_dev, inv...  38.2 us
    pallas_call x1, Pallas kernels, on_device(): pl.pallas_call(lambda *refs: prep_kernel(blocks, block_len, kv_heads, *re...  7.48 us
    pallas_call x1, Pallas kernels, on_device(): pl.pallas_call(lambda *refs: query_kernel(blocks, inv_root, *refs), out_s...  6.02 us
    ppermute x22, waiting for transfers between devices, send(): return lax.ppermute(value, 'ctx', pairs)  5.71 us
    pallas_call x2, Pallas kernels, on_device(): pl.pallas_call(merge_kernel, out_shape=tuple((sds((tokens, 2 * head_dim),...  4.36 us
    unnamed x56, local copies, waits for them, and re-layouts  3.84 us
  transfers between devices with their start and end apart: 22, of which 3 were waited for; matrix products, arithmetic and copies ran while one was open for 1% of the time, Pallas kernels for 35%

profile of v4, /device:TPU:0, one launch (start us, length us, event | category | flops | bytes accessed | tf_op | source)
XLA Modules:
  0.0 166.1 jit_solution(11510839503687280806)
XLA Ops:
  0.6 1.0 fusion.3
  1.6 1.3 collective-permute-start.10
  2.9 1.3 collective-permute-start.11
  4.2 1.3 collective-permute-start.12
  5.5 1.3 collective-permute-start.13
  6.8 1.3 collective-permute-start.7
  8.1 0.7 fusion.2
  8.9 2.0 %plan.1.refs_0_ = s32[5,32]{1,0:T(8,128)} custom-call(s32[1]{0:T(128)} %bitcast.1.refs_0_, s32[4,32]{1,0:T(4,128)} %get-tuple-element.83.refs_1_), custom_call_target="tpu_custom_call" | custom-call | tf_op jit(solution)/shard_map/plan/pallas_call | solution.py:360
  10.9 1.3 collective-permute-start.8
  12.2 2.1 %collective-permute-done.11.refs_11_ = bf16[256,256]{1,0:T(8,128)(2,1)S(1)} collective-permute-done((bf16[256,256]{1,0:T(8,128)(2,1)S(1)}, bf16[256,256]{1,0:T(8,128)(2,1)S(1)}, u32[]{:S(2)}, u32[]{:S(2)}) %collective-permute-start.11) | collective-permute-done | bytes 131104 | tf_op jit(solution)/shard_map/ppermute | solution.py:294
  14.3 1.3 collective-permute-start.9
  15.6 2.2 %collective-permute-done.12.refs_12_ = bf16[256,256]{1,0:T(8,128)(2,1)S(1)} collective-permute-done((bf16[256,256]{1,0:T(8,128)(2,1)S(1)}, bf16[256,256]{1,0:T(8,128)(2,1)S(1)}, u32[]{:S(2)}, u32[]{:S(2)}) %collective-permute-start.12) | collective-permute-done | bytes 131104 | tf_op jit(solution)/shard_map/ppermute | solution.py:294
  17.8 1.3 collective-permute-start
  19.1 1.4 collective-permute-done.13.refs_13_
  20.5 1.3 collective-permute-start.1
  21.8 0.5 broadcast_add_fusion.refs_0_
  22.3 7.5 %prep.1 = (bf16[128,2048]{1,0:T(8,128)(2,1)}, bf16[2048,128]{1,0:T(8,128)(2,1)}, bf16[128,2048]{1,0:T(8,128)(2,1)}, bf16[2048,128]{1,0:T(8,128)(2,1)}, f32[1,204...) custom-call(s32[4]{0:T(128)} %broadcast_add_fusion.refs_0_, ...), custom_call_target="tpu_custom_call" | custom-call | tf_op jit(solution)/shard_map/prep/pallas_call | solution.py:369
  29.8 1.3 collective-permute-start.2
  31.2 1.3 collective-permute-start.3
  32.5 1.3 collective-permute-start.4
  33.8 1.3 collective-permute-start.5
  35.1 1.3 collective-permute-start.6
  36.5 18.5 %attend.3 = (f32[128,2048]{1,0:T(8,128)}, f32[8,128]{1,0:T(8,128)}, bf16[256,256]{1,0:T(8,128)(2,1)}, bf16[256,256]{1,0:T(8,128)(2,1)}, bf16[256,256]{1,0:T(8,12...) custom-call(s32[5,32]{1,0:T(8,128)} %plan.1.refs_0_, f32[1,128]{1,0:T(1,128)} %bitcast.15, ...), custom_call_target="tpu_custom_call" | custom-call | flops 5368709120 | bytes 8388608 | tf_op jit(solution)/shard_map/attend/pallas_call | solution.py:390
  55.0 3.4 %collective-permute-start.18 = (bf16[4,256,256]{2,1,0:T(8,128)(2,1)}, bf16[4,256,256]{2,1,0:T(8,128)(2,1)S(1)}, u32[]{:S(2)}, u32[]{:S(2)}) collective-permute-start(bf16[4,256,256]{2,1,0:T(8,128)(2,1)} %get-tuple-element.68), channel_id=1, source_target_pairs={{0,4},{8,12},{12,8},{16,20},{20,16},{24,28},{28,24},{1,5},{9,13},{... | collective-permute-start | bytes 1572872 | tf_op jit(solution)/shard_map/ppermute | solution.py:294
  58.5 0.6 copy-done.23
  59.0 0.1 copy-done.25
  59.2 19.7 %attend.2 = (f32[128,2048]{1,0:T(8,128)}, f32[8,128]{1,0:T(8,128)}, bf16[256,256]{1,0:T(8,128)(2,1)}, bf16[256,256]{1,0:T(8,128)(2,1)}, bf16[256,256]{1,0:T(8,12...) custom-call(s32[5,32]{1,0:T(8,128)} %plan.1.refs_0_, f32[1,128]{1,0:T(1,128)} %bitcast.16, ...), custom_call_target="tpu_custom_call" | custom-call | flops 5368709120 | bytes 8388608 | tf_op jit(solution)/shard_map/attend/pallas_call | solution.py:390
  78.9 1.3 collective-permute-start.14
  80.3 0.8 copy-done
  81.1 2.2 %merge.3 = (f32[256,256]{1,0:T(8,128)}, bf16[256,256]{1,0:T(8,128)(2,1)}, bf16[256,256]{1,0:T(8,128)(2,1)}, bf16[256,256]{1,0:T(8,128)(2,1)}) custom-call(bf16[256,256]{1,0:T(8,128)(2,1)} %get-tuple-element.64.refs_0_, bf16[256,256]{1,0:T(8,128)(2,1)} %get-tuple-element.65.refs_1_, bf16[256,256]{1,0:T(8,128)(2,1)} %get-tuple-element.66.refs_2_, ...), custom_call_target="tpu_custom_call" | custom-call | tf_op jit(solution)/shard_map/merge/pallas_call | solution.py:430
  83.3 11.2 %collective-permute-start.19 = (bf16[256,256]{1,0:T(8,128)(2,1)}, bf16[256,256]{1,0:T(8,128)(2,1)S(1)}, u32[]{:S(2)}, u32[]{:S(2)}) collective-permute-start(bf16[256,256]{1,0:T(8,128)(2,1)} %get-tuple-element.70), channel_id=1, source_target_pairs={{0,24},{4,28},{12,4},{16,8},{20,12},{24,16},{28,20},{1,25},{5,29},... | collective-permute-start | bytes 393224 | tf_op jit(solution)/shard_map/ppermute | solution.py:294
  94.5 1.3 collective-permute-start.20
  95.8 1.5 collective-permute-start.21
  97.3 0.8 copy-done.1
  98.1 2.2 %merge.2 = (f32[256,256]{1,0:T(8,128)}, bf16[256,256]{1,0:T(8,128)(2,1)}, bf16[256,256]{1,0:T(8,128)(2,1)}, bf16[256,256]{1,0:T(8,128)(2,1)}) custom-call(bf16[256,256]{1,0:T(8,128)(2,1)} %get-tuple-element.55.refs_0_, bf16[256,256]{1,0:T(8,128)(2,1)} %get-tuple-element.56.refs_1_, bf16[256,256]{1,0:T(8,128)(2,1)} %get-tuple-element.57.refs_2_, ...), custom_call_target="tpu_custom_call" | custom-call | tf_op jit(solution)/shard_map/merge/pallas_call | solution.py:430
  100.3 5.7 %collective-permute-start.15 = (bf16[256,256]{1,0:T(8,128)(2,1)}, bf16[256,256]{1,0:T(8,128)(2,1)S(1)}, u32[]{:S(2)}, u32[]{:S(2)}) collective-permute-start(bf16[256,256]{1,0:T(8,128)(2,1)} %get-tuple-element.61), channel_id=1, source_target_pairs={{0,24},{4,28},{12,4},{16,8},{20,12},{24,16},{28,20},{1,25},{5,29},... | collective-permute-start | bytes 393224 | tf_op jit(solution)/shard_map/ppermute | solution.py:294
  106.0 1.3 collective-permute-start.16
  107.3 1.3 collective-permute-start.17
  108.6 6.0 %query_back.1 = (bf16[256,2048]{1,0:T(8,128)(2,1)}, f32[8,128]{1,0:T(8,128)}) custom-call(s32[4]{0:T(128)} %broadcast_add_fusion.refs_0_, f32[32,128]{1,0:T(8,128)} %constant.66.clone.refs_1_.refs_2_, f32[32,128]{1,0:T(8,128)} %constant.67.clone.refs_2_.refs_3_, f32[64,128]{1,0:T(8,128)} %constant.68.clone.refs_3_.refs_4_, ...), custom_call_target="tpu_custom_call" | custom-call | tf_op jit(solution)/shard_map/query_back/pallas_call | solution.py:444
  114.6 0.7 reduce_sum.28
  115.3 46.2 %all-gather.1.refs_15_ = f32[32,2,128]{2,1,0:T(2,128)} all-gather(f32[1,2,128]{2,1,0:T(2,128)S(1)} %maximum_bitcast_fusion), channel_id=2, replica_groups=mesh['ctx'=8,'heads'=4] {'ctx','heads'}, dimensions={0}, use_global_device_ids=true | all-gather | bytes 33792 | tf_op jit(solution)/shard_map/all_gather | solution.py:454
  161.6 0.6 copy-done.5
  162.2 0.1 copy-done.6
  162.2 0.1 copy-done.7
  162.3 0.1 copy-done.9
  162.4 2.5 %key_back.1 = (bf16[256,256]{1,0:T(8,128)(2,1)}, bf16[256,256]{1,0:T(8,128)(2,1)}, f32[2,128]{1,0:T(2,128)}) custom-call(s32[4]{0:T(128)} %broadcast_add_fusion.refs_0_, f32[32,128]{1,0:T(8,128)} %constant.66.clone.refs_1_.refs_2_, f32[32,128]{1,0:T(8,128)} %constant.67.clone.refs_2_.refs_3_, f32[64,128]{1,0:T(8,128)} %constant.68.clone.refs_3_.refs_4_, ...), custom_call_target="tpu_custom_call" | custom-call | tf_op jit(solution)/shard_map/key_back/pallas_call | solution.py:456
  164.9 0.7 copy-done.13
  165.6 0.5 slice_bitcast_fusion
  (70 shorter events, 0.3 us)
Async XLA Ops:
  1.6 6.5 %copy-start.12 = (s32[4,32]{1,0:T(4,128)S(1)}, s32[4,32]{1,0:T(4,128)}, u32[]{:S(2)}) copy-start(s32[4,32]{1,0:T(4,128)} %param.19) | copy-start | bytes 1540
  1.6 12.7 %copy-start.2 = (bf16[256,256]{1,0:T(8,128)(2,1)}, bf16[256,256]{1,0:T(8,128)(2,1)S(1)}, u32[]{:S(2)}) copy-start(bf16[256,256]{1,0:T(8,128)(2,1)S(1)} %pad_maximum_fusion.1.refs_6_) | copy-start | bytes 393220
  1.6 9.3 %collective-permute-start.10 = (bf16[256,256]{1,0:T(8,128)(2,1)S(1)}, bf16[256,256]{1,0:T(8,128)(2,1)S(1)}, u32[]{:S(2)}, u32[]{:S(2)}) collective-permute-start(bf16[256,256]{1,0:T(8,128)(2,1)S(1)} %pad_maximum_fusion.1.refs_6_), channel_id=1, source_target_pairs={{4,0},{8,12},{16,20},{24,28},{5,1},{9,13},{17,21},{25,29},{6,2},{1... | collective-permute-start | bytes 393224 | tf_op jit(solution)/shard_map/ppermute | solution.py:294
  2.9 11.4 %collective-permute-start.11 = (bf16[256,256]{1,0:T(8,128)(2,1)S(1)}, bf16[256,256]{1,0:T(8,128)(2,1)S(1)}, u32[]{:S(2)}, u32[]{:S(2)}) collective-permute-start(bf16[256,256]{1,0:T(8,128)(2,1)S(1)} %pad_maximum_fusion.1.refs_6_), channel_id=1, source_target_pairs={{4,8},{8,20},{12,16},{16,28},{20,24},{28,0},{5,9},{9,21},{13,17},{... | collective-permute-start | bytes 393224 | tf_op jit(solution)/shard_map/ppermute | solution.py:294
  4.2 13.5 %collective-permute-start.12 = (bf16[256,256]{1,0:T(8,128)(2,1)S(1)}, bf16[256,256]{1,0:T(8,128)(2,1)S(1)}, u32[]{:S(2)}, u32[]{:S(2)}) collective-permute-start(bf16[256,256]{1,0:T(8,128)(2,1)S(1)} %pad_maximum_fusion.1.refs_6_), channel_id=1, source_target_pairs={{4,16},{8,28},{12,24},{20,0},{5,17},{9,29},{13,25},{21,1},{6,18},{... | collective-permute-start | bytes 393224 | tf_op jit(solution)/shard_map/ppermute | solution.py:294
  5.5 15.0 %collective-permute-start.13 = (bf16[256,256]{1,0:T(8,128)(2,1)S(1)}, bf16[256,256]{1,0:T(8,128)(2,1)S(1)}, u32[]{:S(2)}, u32[]{:S(2)}) collective-permute-start(bf16[256,256]{1,0:T(8,128)(2,1)S(1)} %pad_maximum_fusion.1.refs_6_), channel_id=1, source_target_pairs={{4,24},{12,0},{5,25},{13,1},{6,26},{14,2},{7,27},{15,3}} | collective-permute-start | bytes 393224 | tf_op jit(solution)/shard_map/ppermute | solution.py:294
  6.8 23.0 %collective-permute-start.7 = (bf16[256,256]{1,0:T(8,128)(2,1)S(1)}, bf16[256,256]{1,0:T(8,128)(2,1)S(1)}, u32[]{:S(2)}, u32[]{:S(2)}) collective-permute-start(bf16[256,256]{1,0:T(8,128)(2,1)S(1)} %pad_maximum_fusion.1.refs_6_), channel_id=1, source_target_pairs={{4,12},{8,16},{12,20},{16,24},{20,28},{24,0},{5,13},{9,17},{13,21}... | collective-permute-start | bytes 393224 | tf_op jit(solution)/shard_map/ppermute | solution.py:294
  10.9 24.2 %copy-start.3 = (bf16[256,256]{1,0:T(8,128)(2,1)}, bf16[256,256]{1,0:T(8,128)(2,1)S(1)}, u32[]{:S(2)}) copy-start(bf16[256,256]{1,0:T(8,128)(2,1)S(1)} %pad_maximum_fusion.refs_6_) | copy-start | bytes 393220
  10.9 18.8 %copy-start.14 = (bf16[256,256]{1,0:T(8,128)(2,1)}, bf16[256,256]{1,0:T(8,128)(2,1)S(1)}, u32[]{:S(2)}) copy-start(bf16[256,256]{1,0:T(8,128)(2,1)S(1)} %collective-permute-done.10.refs_10_) | copy-start | bytes 393220
  10.9 20.2 %collective-permute-start.8 = (bf16[256,256]{1,0:T(8,128)(2,1)S(1)}, bf16[256,256]{1,0:T(8,128)(2,1)S(1)}, u32[]{:S(2)}, u32[]{:S(2)}) collective-permute-start(bf16[256,256]{1,0:T(8,128)(2,1)S(1)} %pad_maximum_fusion.1.refs_6_), channel_id=1, source_target_pairs={{4,20},{8,24},{12,28},{16,0},{5,21},{9,25},{13,29},{17,1},{6,22},{... | collective-permute-start | bytes 393224 | tf_op jit(solution)/shard_map/ppermute | solution.py:294
  14.3 15.5 %copy-start.15 = (bf16[256,256]{1,0:T(8,128)(2,1)}, bf16[256,256]{1,0:T(8,128)(2,1)S(1)}, u32[]{:S(2)}) copy-start(bf16[256,256]{1,0:T(8,128)(2,1)S(1)} %collective-permute-done.11.refs_11_) | copy-start | bytes 393220
  14.3 18.1 %collective-permute-start.9 = (bf16[256,256]{1,0:T(8,128)(2,1)S(1)}, bf16[256,256]{1,0:T(8,128)(2,1)S(1)}, u32[]{:S(2)}, u32[]{:S(2)}) collective-permute-start(bf16[256,256]{1,0:T(8,128)(2,1)S(1)} %pad_maximum_fusion.1.refs_6_), channel_id=1, source_target_pairs={{4,28},{8,0},{5,29},{9,1},{6,30},{10,2},{7,31},{11,3}} | collective-permute-start | bytes 393224 | tf_op jit(solution)/shard_map/ppermute | solution.py:294
  17.8 12.0 %copy-start.16 = (bf16[256,256]{1,0:T(8,128)(2,1)}, bf16[256,256]{1,0:T(8,128)(2,1)S(1)}, u32[]{:S(2)}) copy-start(bf16[256,256]{1,0:T(8,128)(2,1)S(1)} %collective-permute-done.12.refs_12_) | copy-start | bytes 393220
  17.8 16.0 %collective-permute-start = (bf16[256,256]{1,0:T(8,128)(2,1)S(1)}, bf16[256,256]{1,0:T(8,128)(2,1)S(1)}, u32[]{:S(2)}, u32[]{:S(2)}) collective-permute-start(bf16[256,256]{1,0:T(8,128)(2,1)S(1)} %pad_maximum_fusion.refs_6_), channel_id=1, source_target_pairs={{4,12},{8,16},{12,20},{16,24},{20,28},{24,0},{5,13},{9,17},{13,21}... | collective-permute-start | bytes 393224 | tf_op jit(solution)/shard_map/ppermute | solution.py:294
  20.5 9.3 %copy-start.17 = (bf16[256,256]{1,0:T(8,128)(2,1)}, bf16[256,256]{1,0:T(8,128)(2,1)S(1)}, u32[]{:S(2)}) copy-start(bf16[256,256]{1,0:T(8,128)(2,1)S(1)} %collective-permute-done.13.refs_13_) | copy-start | bytes 393220
  20.5 14.6 %collective-permute-start.1 = (bf16[256,256]{1,0:T(8,128)(2,1)S(1)}, bf16[256,256]{1,0:T(8,128)(2,1)S(1)}, u32[]{:S(2)}, u32[]{:S(2)}) collective-permute-start(bf16[256,256]{1,0:T(8,128)(2,1)S(1)} %pad_maximum_fusion.refs_6_), channel_id=1, source_target_pairs={{4,20},{8,24},{12,28},{16,0},{5,21},{9,25},{13,29},{17,1},{6,22},{... | collective-permute-start | bytes 393224 | tf_op jit(solution)/shard_map/ppermute | solution.py:294
  29.8 6.6 %copy-start.18 = (bf16[256,256]{1,0:T(8,128)(2,1)}, bf16[256,256]{1,0:T(8,128)(2,1)S(1)}, u32[]{:S(2)}) copy-start(bf16[256,256]{1,0:T(8,128)(2,1)S(1)} %collective-permute-done.7.refs_7_) | copy-start | bytes 393220
  29.8 25.1 %collective-permute-start.2 = (bf16[256,256]{1,0:T(8,128)(2,1)S(1)}, bf16[256,256]{1,0:T(8,128)(2,1)S(1)}, u32[]{:S(2)}, u32[]{:S(2)}) collective-permute-start(bf16[256,256]{1,0:T(8,128)(2,1)S(1)} %pad_maximum_fusion.refs_6_), channel_id=1, source_target_pairs={{4,28},{8,0},{5,29},{9,1},{6,30},{10,2},{7,31},{11,3}} | collective-permute-start | bytes 393224 | tf_op jit(solution)/shard_map/ppermute | solution.py:294
  31.1 5.3 %copy-start.22 = (bf16[256,256]{1,0:T(8,128)(2,1)}, bf16[256,256]{1,0:T(8,128)(2,1)S(1)}, u32[]{:S(2)}) copy-start(bf16[256,256]{1,0:T(8,128)(2,1)S(1)} %collective-permute-done.8.refs_8_) | copy-start | bytes 393220
  31.2 27.2 %collective-permute-start.3 = (bf16[256,256]{1,0:T(8,128)(2,1)S(1)}, bf16[256,256]{1,0:T(8,128)(2,1)S(1)}, u32[]{:S(2)}, u32[]{:S(2)}) collective-permute-start(bf16[256,256]{1,0:T(8,128)(2,1)S(1)} %pad_maximum_fusion.refs_6_), channel_id=1, source_target_pairs={{4,0},{8,12},{16,20},{24,28},{5,1},{9,13},{17,21},{25,29},{6,2},{1... | collective-permute-start | bytes 393224 | tf_op jit(solution)/shard_map/ppermute | solution.py:294
  32.5 4.0 %copy-start.24 = (bf16[256,256]{1,0:T(8,128)(2,1)}, bf16[256,256]{1,0:T(8,128)(2,1)S(1)}, u32[]{:S(2)}) copy-start(bf16[256,256]{1,0:T(8,128)(2,1)S(1)} %collective-permute-done.9.refs_9_) | copy-start | bytes 393220
  32.5 25.9 %collective-permute-start.4 = (bf16[256,256]{1,0:T(8,128)(2,1)S(1)}, bf16[256,256]{1,0:T(8,128)(2,1)S(1)}, u32[]{:S(2)}, u32[]{:S(2)}) collective-permute-start(bf16[256,256]{1,0:T(8,128)(2,1)S(1)} %pad_maximum_fusion.refs_6_), channel_id=1, source_target_pairs={{4,8},{8,20},{12,16},{16,28},{20,24},{28,0},{5,9},{9,21},{13,17},{... | collective-permute-start | bytes 393224 | tf_op jit(solution)/shard_map/ppermute | solution.py:294
  33.8 21.2 %copy-start.19 = (bf16[256,256]{1,0:T(8,128)(2,1)}, bf16[256,256]{1,0:T(8,128)(2,1)S(1)}, u32[]{:S(2)}) copy-start(bf16[256,256]{1,0:T(8,128)(2,1)S(1)} %collective-permute-done.refs_7_) | copy-start | bytes 393220
  33.8 24.6 %collective-permute-start.5 = (bf16[256,256]{1,0:T(8,128)(2,1)S(1)}, bf16[256,256]{1,0:T(8,128)(2,1)S(1)}, u32[]{:S(2)}, u32[]{:S(2)}) collective-permute-start(bf16[256,256]{1,0:T(8,128)(2,1)S(1)} %pad_maximum_fusion.refs_6_), channel_id=1, source_target_pairs={{4,16},{8,28},{12,24},{20,0},{5,17},{9,29},{13,25},{21,1},{6,18},{... | collective-permute-start | bytes 393224 | tf_op jit(solution)/shard_map/ppermute | solution.py:294
  35.1 19.8 %copy-start.20 = (bf16[256,256]{1,0:T(8,128)(2,1)}, bf16[256,256]{1,0:T(8,128)(2,1)S(1)}, u32[]{:S(2)}) copy-start(bf16[256,256]{1,0:T(8,128)(2,1)S(1)} %collective-permute-done.1.refs_8_) | copy-start | bytes 393220
  35.1 23.3 %collective-permute-start.6 = (bf16[256,256]{1,0:T(8,128)(2,1)S(1)}, bf16[256,256]{1,0:T(8,128)(2,1)S(1)}, u32[]{:S(2)}, u32[]{:S(2)}) collective-permute-start(bf16[256,256]{1,0:T(8,128)(2,1)S(1)} %pad_maximum_fusion.refs_6_), channel_id=1, source_target_pairs={{4,24},{12,0},{5,25},{13,1},{6,26},{14,2},{7,27},{15,3}} | collective-permute-start | bytes 393224 | tf_op jit(solution)/shard_map/ppermute | solution.py:294
  55.0 3.5 %copy-start.21 = (bf16[256,256]{1,0:T(8,128)(2,1)}, bf16[256,256]{1,0:T(8,128)(2,1)S(1)}, u32[]{:S(2)}) copy-start(bf16[256,256]{1,0:T(8,128)(2,1)S(1)} %collective-permute-done.2.refs_9_) | copy-start | bytes 393220
  55.0 25.3 %collective-permute-start.18 = (bf16[4,256,256]{2,1,0:T(8,128)(2,1)}, bf16[4,256,256]{2,1,0:T(8,128)(2,1)S(1)}, u32[]{:S(2)}, u32[]{:S(2)}) collective-permute-start(bf16[4,256,256]{2,1,0:T(8,128)(2,1)} %get-tuple-element.68), channel_id=1, source_target_pairs={{0,4},{8,12},{12,8},{16,20},{20,16},{24,28},{28,24},{1,5},{9,13},{... | collective-permute-start | bytes 1572872 | tf_op jit(solution)/shard_map/ppermute | solution.py:294
  58.4 0.7 copy-start.25
  58.4 0.7 copy-start.26
  58.5 0.7 copy-start.27
  78.9 18.3 %collective-permute-start.14 = (bf16[4,256,256]{2,1,0:T(8,128)(2,1)}, bf16[4,256,256]{2,1,0:T(8,128)(2,1)S(1)}, u32[]{:S(2)}, u32[]{:S(2)}) collective-permute-start(bf16[4,256,256]{2,1,0:T(8,128)(2,1)} %get-tuple-element.59), channel_id=1, source_target_pairs={{0,4},{8,12},{12,8},{16,20},{20,16},{24,28},{28,24},{1,5},{9,13},{... | collective-permute-start | bytes 1572872 | tf_op jit(solution)/shard_map/ppermute | solution.py:294
  80.3 0.8 copy-start
  83.3 24.0 %collective-permute-start.19 = (bf16[256,256]{1,0:T(8,128)(2,1)}, bf16[256,256]{1,0:T(8,128)(2,1)S(1)}, u32[]{:S(2)}, u32[]{:S(2)}) collective-permute-start(bf16[256,256]{1,0:T(8,128)(2,1)} %get-tuple-element.70), channel_id=1, source_target_pairs={{0,24},{4,28},{12,4},{16,8},{20,12},{24,16},{28,20},{1,25},{5,29},... | collective-permute-start | bytes 393224 | tf_op jit(solution)/shard_map/ppermute | solution.py:294
  94.5 67.0 %collective-permute-start.20 = (bf16[256,256]{1,0:T(8,128)(2,1)}, bf16[256,256]{1,0:T(8,128)(2,1)S(1)}, u32[]{:S(2)}, u32[]{:S(2)}) collective-permute-start(bf16[256,256]{1,0:T(8,128)(2,1)} %get-tuple-element.71), channel_id=1, source_target_pairs={{0,16},{4,20},{20,4},{24,8},{28,12},{1,17},{5,21},{21,5},{25,9},{2... | collective-permute-start | bytes 393224 | tf_op jit(solution)/shard_map/ppermute | solution.py:294
  95.8 65.7 %collective-permute-start.21 = (bf16[256,256]{1,0:T(8,128)(2,1)}, bf16[256,256]{1,0:T(8,128)(2,1)S(1)}, u32[]{:S(2)}, u32[]{:S(2)}) collective-permute-start(bf16[256,256]{1,0:T(8,128)(2,1)} %get-tuple-element.72), channel_id=1, source_target_pairs={{0,8},{4,12},{28,4},{1,9},{5,13},{29,5},{2,10},{6,14},{30,6},{3,11... | collective-permute-start | bytes 393224 | tf_op jit(solution)/shard_map/ppermute | solution.py:294
  97.3 0.8 copy-start.1
  100.3 8.3 %copy-start.11 = (f32[8,128]{1,0:T(8,128)S(1)}, f32[8,128]{1,0:T(8,128)}, u32[]{:S(2)}) copy-start(f32[8,128]{1,0:T(8,128)} %get-tuple-element.74) | copy-start | bytes 12292
  100.3 8.3 %copy-start.10 = (f32[8,128]{1,0:T(8,128)S(1)}, f32[8,128]{1,0:T(8,128)}, u32[]{:S(2)}) copy-start(f32[8,128]{1,0:T(8,128)} %get-tuple-element.75) | copy-start | bytes 12292
  100.3 61.3 %collective-permute-start.15 = (bf16[256,256]{1,0:T(8,128)(2,1)}, bf16[256,256]{1,0:T(8,128)(2,1)S(1)}, u32[]{:S(2)}, u32[]{:S(2)}) collective-permute-start(bf16[256,256]{1,0:T(8,128)(2,1)} %get-tuple-element.61), channel_id=1, source_target_pairs={{0,24},{4,28},{12,4},{16,8},{20,12},{24,16},{28,20},{1,25},{5,29},... | collective-permute-start | bytes 393224 | tf_op jit(solution)/shard_map/ppermute | solution.py:294
  106.0 55.6 %collective-permute-start.16 = (bf16[256,256]{1,0:T(8,128)(2,1)}, bf16[256,256]{1,0:T(8,128)(2,1)S(1)}, u32[]{:S(2)}, u32[]{:S(2)}) collective-permute-start(bf16[256,256]{1,0:T(8,128)(2,1)} %get-tuple-element.62), channel_id=1, source_target_pairs={{0,16},{4,20},{20,4},{24,8},{28,12},{1,17},{5,21},{21,5},{25,9},{2... | collective-permute-start | bytes 393224 | tf_op jit(solution)/shard_map/ppermute | solution.py:294
  107.3 7.4 %copy-start.4 = (bf16[256,256]{1,0:T(8,128)(2,1)}, bf16[256,256]{1,0:T(8,128)(2,1)S(1)}, u32[]{:S(2)}) copy-start(bf16[256,256]{1,0:T(8,128)(2,1)S(1)} %collective-permute-done.19.refs_12_) | copy-start | bytes 393220
  107.3 54.3 %collective-permute-start.17 = (bf16[256,256]{1,0:T(8,128)(2,1)}, bf16[256,256]{1,0:T(8,128)(2,1)S(1)}, u32[]{:S(2)}, u32[]{:S(2)}) collective-permute-start(bf16[256,256]{1,0:T(8,128)(2,1)} %get-tuple-element.63), channel_id=1, source_target_pairs={{0,8},{4,12},{28,4},{1,9},{5,13},{29,5},{2,10},{6,14},{30,6},{3,11... | collective-permute-start | bytes 393224 | tf_op jit(solution)/shard_map/ppermute | solution.py:294
  161.5 0.7 copy-start.6
  161.5 0.7 copy-start.7
  161.6 0.8 copy-start.8
  161.6 0.8 copy-start.9
  164.9 0.7 copy-start.13
  (2 other events, 1.3 us)

commit v5 on v4

--- a/solution.py
+++ b/solution.py
@@ -88,37 +88,37 @@
         plan_ref[4, i] = count
 
 
-def prep_kernel(blocks, block_len, kv_heads, depth_ref, t0, t1, t2, t3, gain_ref, q_ref, grad_ref, out_ref, *outs):
+def prep_kernel(blocks, depth_ref, t0, t1, t2, t3, gain_ref, q_ref, grad_ref, out_ref,
+                q_t_ref, q_rot_ref, grad_t_ref, grad_heads_ref, delta_ref):
     tokens = q_ref.shape[0]
     head_dim = gain_ref.shape[1]
     cos, sin = own_tables(depth_ref, (t0, t1, t2, t3), blocks)
     gain = gain_ref[...]
-    group = q_ref.shape[1] // head_dim // kv_heads
-    for head in range(group * kv_heads):
-        g = head % group
-        q_t_ref, q_rot_ref, grad_t_ref, grad_heads_ref, delta_ref = outs[5 * (head // group):][:5]
-        cols = pl.ds(head * head_dim, head_dim)
-        here = pl.ds(g * tokens, tokens)
+
+    @pl.loop(0, q_ref.shape[1] // head_dim)
+    def _(head):
+        cols = pl.ds(pl.multiple_of(head * head_dim, head_dim), head_dim)
+        here = pl.ds(pl.multiple_of(head * tokens, tokens), tokens)
         rows = q_ref[:, cols].astype(F32)
         rotated = turned(rows * inverse_rms(rows) * gain, cos, sin).astype(BF16)
-        q_rot_ref[here, :] = rotated
-        q_t_ref[:, here] = jnp.transpose(rotated)
+        q_rot_ref[0, here, :] = rotated
+        q_t_ref[0, :, here] = jnp.transpose(rotated)
         grad = grad_ref[:, cols]
-        grad_heads_ref[here, :] = grad
-        grad_t_ref[:, here] = jnp.transpose(grad)
+        grad_heads_ref[0, here, :] = grad
+        grad_t_ref[0, :, here] = jnp.transpose(grad)
         product = grad.astype(F32) * out_ref[:, cols].astype(F32)
-        delta_ref[:, here] = jnp.sum(jnp.transpose(product), 0, keepdims=True)
-
-
-def main_kernel(blocks, block_len, tree_dev, inv_root, staged, *refs):
+        delta_ref[0, :, here] = jnp.sum(jnp.transpose(product), 0, keepdims=True)
+
+
+def main_kernel(blocks, block_len, tree_dev, inv_root, head, *refs):
     plan_ref, gain_ref = refs[:2]
     tables = refs[2:6]
     pieces = refs[6:6 + tree_dev]
-    q_t_ref, q_ref, grad_t_ref, grad_ref, delta_ref = refs[6 + tree_dev:11 + tree_dev]
+    q_t_ref, q_ref, grad_t_ref, grad_ref, delta_ref = [ref.at[head] for ref in refs[6 + tree_dev:11 + tree_dev]]
     half = tree_dev // 2
     dq_ref, gain_part_ref = refs[11 + tree_dev:13 + tree_dev]
     straight = refs[13 + tree_dev:13 + tree_dev + half]
-    crossed, raw, keys, keys_t, vals, shown, with_cos, with_sin, expo, mass, w_all, ds_all, found, spread, wide = refs[
+    crossed, raw, keys, keys_t, vals, shown, with_cos, with_sin, expo, mass, w_all, ds_all, found, spread = refs[
         13 + tree_dev + half:]
     head_dim = gain_ref.shape[1]
     tokens = raw.shape[1]
@@ -126,8 +126,10 @@
     count = plan_ref[4, 0]
     chunks = (count + blocks - 1) // blocks
     gain = gain_ref[...]
+    kv_heads = pieces[0].shape[1] // (2 * head_dim)
     for piece in range(tree_dev):
-        raw[piece] = pieces[piece][...]
+        raw[piece, :, 0:head_dim] = pieces[piece][:, head * head_dim:(head + 1) * head_dim]
+        raw[piece, :, head_dim:] = pieces[piece][:, (kv_heads + head) * head_dim:(kv_heads + head + 1) * head_dim]
     query_block = lax.broadcasted_iota(jnp.int32, (1, tokens), 1) // block_len
 
     def rows_of(start):
@@ -154,7 +156,7 @@
             vals[c, here, :] = raw[piece, rows, head_dim:]
         keys_t[c] = jnp.transpose(keys[c].astype(F32)).astype(BF16)
 
-    def exps(c, g, scores):
+    def exps(c, scores):
         parts = []
         for j in range(blocks):
             here = slice(j * block_len, (j + 1) * block_len)
@@ -170,41 +172,40 @@
     def cols_of(g):
         return pl.ds(g * tokens, tokens)
 
-    def masses(c, first):
-        if staged:
-            wide[...] = dot_nn(keys[c], q_t_ref[...])
+    mass[...] = jnp.zeros(mass.shape, F32)
+    load_chunk(0)
+
+    def masses(c, later):
         for g in range(group):
-            scores = wide[:, cols_of(g)] if staged else dot_nn(keys[c], q_t_ref[:, cols_of(g)])
-            e = exps(c, g, scores)
-            if first:
-                e = jnp.where(key_row <= query_col, e, 0.0)
+            e = exps(c, dot_nn(keys[c], q_t_ref[:, cols_of(g)]))
             expo[c, g] = e
-            mass[g] = summed(e) if first else mass[g] + summed(e)
-
-    load_chunk(0)
-    masses(0, True)
+            mass[later, g] = mass[later, g] + summed(e)
+
+    masses(0, 0)
     load_chunk(1)
 
     @pl.loop(1, chunks)
     def _(c):
-        masses(c, False)
+        masses(c, 1)
         load_chunk(c + 1)
 
-    for g in range(group):
-        total = jnp.sum(mass[g], 0, keepdims=True)
-        mass[g] = jnp.broadcast_to(1.0 / total, (8, tokens))
+    @pl.loop(0, group)
+    def _(g):
+        e = jnp.where(key_row <= query_col, expo[0, g], 0.0)
+        expo[0, g] = e
+        total = jnp.sum(mass[1, g] + summed(e), 0, keepdims=True)
+        mass[0, g] = jnp.broadcast_to(1.0 / total, (8, tokens))
+
     dq_ref[...] = jnp.zeros(dq_ref.shape, F32)
     gain_part_ref[...] = jnp.zeros(gain_part_ref.shape, F32)
     spread[...] = jnp.zeros(spread.shape, BF16)
 
     @pl.loop(0, chunks)
     def _(c):
-        if staged:
-            wide[...] = dot_nn(vals[c], grad_t_ref[...])
         for g in range(group):
             cols = cols_of(g)
-            grad_prob = wide[:, cols] if staged else dot_nn(vals[c], grad_t_ref[:, cols])
-            weights = expo[c, g] * mass[g, 0:1, :]
+            grad_prob = dot_nn(vals[c], grad_t_ref[:, cols])
+            weights = expo[c, g] * mass[0, g, 0:1, :]
             ds_all[:, cols] = (weights * (grad_prob - delta_ref[:, cols])).astype(BF16)
             w_all[:, cols] = weights.astype(BF16)
         dv = dot_nn(w_all[...], grad_ref[...])
@@ -234,26 +235,34 @@
         outs[i][...] = (parts[i][...].astype(F32) + crossed_ref[i].astype(F32)).astype(BF16)
 
 
-def query_kernel(blocks, inv_root, depth_ref, t0, t1, t2, t3, gain_ref, q_ref, *refs):
+def query_kernel(blocks, inv_root, shares, depth_ref, t0, t1, t2, t3, gain_ref, q_ref, *refs):
     dq_refs, (out_ref, part_ref) = refs[:-2], refs[-2:]
     tokens = q_ref.shape[0]
     head_dim = gain_ref.shape[1]
-    group = dq_refs[0].shape[1] // tokens
     cos, sin = own_tables(depth_ref, (t0, t1, t2, t3), blocks)
     gain = gain_ref[...]
-    part = jnp.zeros((8, head_dim), F32)
-    for head in range(group * len(dq_refs)):
-        cols = pl.ds(head * head_dim, head_dim)
-        rows = q_ref[:, cols].astype(F32)
-        recip = inverse_rms(rows)
-        normed = rows * recip
-        dq = jnp.transpose(dq_refs[head // group][:, pl.ds(head % group * tokens, tokens)])
-        scaled_grad = turned_back(dq, cos, sin) * inv_root
-        term = scaled_grad * normed
-        part = part + jnp.sum(term.reshape(tokens // 8, 8, head_dim), 0)
-        inner = jnp.mean(term * gain, -1, keepdims=True)
-        out_ref[:, cols] = (recip * (scaled_grad * gain - normed * inner)).astype(BF16)
-    part_ref[...] = part
+    step = pl.program_id(0)
+
+    @pl.when(step == 0)
+    def _():
+        part_ref[...] = jnp.zeros(part_ref.shape, F32)
+
+    for kv, dq_ref in enumerate(dq_refs):
+
+        @pl.when(step // shares == kv)
+        def _():
+            @pl.loop(0, q_ref.shape[1] // head_dim)
+            def _(head):
+                cols = pl.ds(pl.multiple_of(head * head_dim, head_dim), head_dim)
+                rows = q_ref[:, cols].astype(F32)
+                recip = inverse_rms(rows)
+                normed = rows * recip
+                dq = jnp.transpose(dq_ref[:, pl.ds(pl.multiple_of(head * tokens, tokens), tokens)])
+                scaled_grad = turned_back(dq, cos, sin) * inv_root
+                term = scaled_grad * normed
+                part_ref[...] = part_ref[...] + jnp.sum(term.reshape(tokens // 8, 8, head_dim), 0)
+                inner = jnp.mean(term * gain, -1, keepdims=True)
+                out_ref[:, cols] = (recip * (scaled_grad * gain - normed * inner)).astype(BF16)
 
 
 def key_kernel(blocks, counts, depth_ref, t0, t1, t2, t3, gain_ref, k_ref, *refs):
@@ -296,15 +305,20 @@
     def after(self, *pair):
         return self.order(pair[1] % self.size) > self.order(pair[0] % self.size)
 
+    def passed(self, index, step):
+        size, piece = self.size, index - step
+        needed = self.after(piece, index) or self.after(piece, index ^ 1)
+        return needed or (step + 2 < size and self.passed((index + 2) % size, step + 2))
+
     def gather(self, own):
         size, after = self.size, self.after
-        pieces = [own]
-        for odd in range(2):
-            for step in range(0, size, 2):
-                if odd or step:
-                    there = lambda i: (i + step) % size ^ odd
-                    pieces.append(self.send(own, there, lambda i: after(i, there(i))))
-        return pieces
+        cross = [self.send(own, lambda i: i ^ 1, lambda i: after(i, i ^ 1))]
+        straight = [own]
+        for step in range(2, size, 2):
+            there = lambda i: (i + 2) % size
+            straight.append(self.send(straight[-1], there, lambda i: self.passed(there(i), step)))
+            cross.append(self.send(straight[-1], lambda i: i ^ 1, lambda i: after(i - step, i ^ 1)))
+        return straight + cross
 
     def across(self, crossed):
         steps = range(0, self.size, 2)
@@ -347,10 +361,7 @@
     ]
     q_gain_row, k_gain_row = q_gain.reshape(1, head_dim), k_gain.reshape(1, head_dim)
 
-    pieces = []
-    for h in range(kv_heads):
-        cols = slice(h * head_dim, (h + 1) * head_dim)
-        pieces.append(tree.gather(jnp.concatenate([k_raw[:, cols], values[:, cols]], 1)))
+    pieces = tree.gather(jnp.concatenate([k_raw, values], 1))
 
     params = pltpu.CompilerParams(vmem_limit_bytes=VMEM_LIMIT)
     smem = pl.BlockSpec(memory_space=pltpu.SMEM)
@@ -366,20 +377,25 @@
     )(place, in_tree)
 
     rows = group * tokens
+    shares = 2
+    part_rows = rows // shares
+    whole = lambda *shape: pl.BlockSpec(shape, lambda i: (0,) * len(shape))
+    table_specs = [whole(*table.shape) for table in tables]
+    columns = pl.BlockSpec((tokens, part_rows // tokens * head_dim), lambda i: (0, i))
+    tall = pl.BlockSpec((1, part_rows, head_dim), lambda i: (i // shares, i % shares, 0))
+    flat = lambda n: pl.BlockSpec((1, n, part_rows), lambda i: (i // shares, 0, i % shares))
     queries = pl.pallas_call(
-        lambda *refs: prep_kernel(blocks, block_len, kv_heads, *refs),
-        out_shape=tuple(
-            [
-                sds((head_dim, rows), BF16),
-                sds((rows, head_dim), BF16),
-                sds((head_dim, rows), BF16),
-                sds((rows, head_dim), BF16),
-                sds((1, rows), F32),
-            ]
-            * kv_heads
+        lambda *refs: prep_kernel(blocks, *refs),
+        grid=(kv_heads * shares,),
+        out_shape=(
+            sds((kv_heads, head_dim, rows), BF16),
+            sds((kv_heads, rows, head_dim), BF16),
+            sds((kv_heads, head_dim, rows), BF16),
+            sds((kv_heads, rows, head_dim), BF16),
+            sds((kv_heads, 1, rows), F32),
         ),
-        in_specs=[smem] + [vmem] * 8,
-        out_specs=tuple([vmem] * (5 * kv_heads)),
+        in_specs=[smem, *table_specs, whole(1, head_dim), columns, columns, columns],
+        out_specs=(flat(head_dim), tall, flat(head_dim), tall, flat(1)),
         compiler_params=params,
         name="prep",
     )(depth, *tables, q_gain_row, q_raw, out_grad, saved_out)
@@ -388,7 +404,7 @@
 
     def attend(h):
         return pl.pallas_call(
-            lambda *refs: main_kernel(blocks, block_len, tree_dev, inv_root, h > 0, *refs),
+            lambda *refs: main_kernel(blocks, block_len, tree_dev, inv_root, h, *refs),
             out_shape=(
                 sds((head_dim, rows), F32),
                 sds((8, head_dim), F32),
@@ -406,12 +422,11 @@
                 pltpu.VMEM((tree_dev + 1, tokens, head_dim), F32),
                 pltpu.VMEM((tree_dev + 1, tokens, head_dim), F32),
                 pltpu.VMEM((tree_dev, group, tokens, tokens), F32),
-                pltpu.VMEM((group, 8, tokens), F32),
+                pltpu.VMEM((2, group, 8, tokens), F32),
                 pltpu.VMEM((tokens, rows), BF16),
                 pltpu.VMEM((tokens, rows), BF16),
                 pltpu.VMEM((tree_dev, tokens, 2 * head_dim), BF16),
                 pltpu.VMEM((tree_dev, tokens, 2 * head_dim), BF16),
-                pltpu.VMEM((tokens, rows), F32),
             ],
             compiler_params=params,
             cost_estimate=pl.CostEstimate(
@@ -420,7 +435,7 @@
                 transcendentals=group * tokens * tree_dev * tokens,
             ),
             name="attend",
-        )(plan, k_gain_row, *tables, *pieces[h], *queries[5 * h:5 * h + 5])
+        )(plan, k_gain_row, *tables, *pieces, *queries)
 
     dq, terms, counts, k_gain_parts = [], [], [], []
     for h in range(kv_heads):
@@ -441,17 +456,29 @@
         terms.extend(mine)
         counts.append(len(mine))
 
+    def share_of(kv):
+        return lambda i: (0, jnp.clip(i - kv * shares, 0, shares - 1))
+
     dq_raw, q_gain_part = pl.pallas_call(
-        lambda *refs: query_kernel(blocks, inv_root, *refs),
+        lambda *refs: query_kernel(blocks, inv_root, shares, *refs),
+        grid=(kv_heads * shares,),
         out_shape=(sds((tokens, heads * head_dim), BF16), sds((8, head_dim), F32)),
-        in_specs=[smem] + [vmem] * (6 + kv_heads),
-        out_specs=(vmem, vmem),
+        in_specs=[
+            smem,
+            *table_specs,
+            whole(1, head_dim),
+            columns,
+            *[pl.BlockSpec((head_dim, part_rows), share_of(kv)) for kv in range(kv_heads)],
+        ],
+        out_specs=(columns, whole(8, head_dim)),
         compiler_params=params,
         name="query_back",
     )(depth, *tables, q_gain_row, q_raw, *dq)
 
     gains = jnp.stack([jnp.sum(q_gain_part, 0), jnp.sum(sum(k_gain_parts), 0)])
-    gains = lax.all_gather(gains, ("ctx", "heads"))
+    everyone = cycle * lax.axis_size("heads")
+    gains = jnp.broadcast_to(gains[None], (everyone, *gains.shape))
+    gains = lax.all_to_all(gains, ("ctx", "heads"), 0, 0)
 
     dk_raw, dv, total = pl.pallas_call(
         lambda *refs: key_kernel(blocks, counts, *refs),

time: 166 us -> 144 us (0.87); the launches traced: 166 us -> 141 us
  blocking collectives: 46.2 us -> 18.7 us
  waiting for transfers between devices: 5.71 us -> 30.8 us
  starting transfers between devices: 45 us -> 24.8 us
  Pallas kernels: 60.6 us -> 58.3 us
    all_gather x1 -> x0, blocking collectives: 46.2 us -> none  [on_device(): gains = lax.all_gather(gains, ('ctx', 'heads'))]
    ppermute x22 -> x15, waiting for transfers between devices: 5.71 us -> 30.8 us  [send(): return lax.ppermute(value, 'ctx', pairs)]
    ppermute x22 -> x15, starting transfers between devices: 45 us -> 24.8 us  [send(): return lax.ppermute(value, 'ctx', pairs)]
    all_to_all x0 -> x1, blocking collectives: none -> 18.7 us  [on_device(): gains = lax.all_to_all(gains, ('ctx', 'heads'), 0, 0)]
    pallas_call x2, Pallas kernels: 38.2 us -> 34.4 us  [attend(): pl.pallas_call(lambda *refs: main_kernel(blocks, block_len, tree_dev, inv...]
    unnamed x56 -> x47, local copies, waits for them, and re-layouts: 3.84 us -> 4.71 us
  transfers between devices with their start and end apart: 22 -> 15, of which waited for: 3 -> 5; matrix products, arithmetic and copies ran while one was open for 1% -> 1% of each run, Pallas kernels for 35% -> 27%
where the time goes in v5:
time: 144 us; the launch traced here: 141 us
  Pallas kernels  58.3 us (40%)
  waiting for transfers between devices  30.8 us (21%)
  starting transfers between devices  24.8 us (17%)
  blocking collectives  18.7 us (13%)
  local copies, waits for them, and re-layouts  5.25 us (4%)
  other arithmetic  1.94 us (1%)
    pallas_call x2, Pallas kernels, attend(): pl.pallas_call(lambda *refs: main_kernel(blocks, block_len, tree_dev, inv...  34.4 us
    ppermute x15, waiting for transfers between devices, send(): return lax.ppermute(value, 'ctx', pairs)  30.8 us
    ppermute x15, starting transfers between devices, send(): return lax.ppermute(value, 'ctx', pairs)  24.8 us
    all_to_all x1, blocking collectives, on_device(): gains = lax.all_to_all(gains, ('ctx', 'heads'), 0, 0)  18.7 us
    pallas_call x1, Pallas kernels, on_device(): pl.pallas_call(lambda *refs: prep_kernel(blocks, *refs), grid=(kv_heads *...  7.8 us
    pallas_call x1, Pallas kernels, on_device(): pl.pallas_call(lambda *refs: query_kernel(blocks, inv_root, shares, *refs...  7.2 us
    unnamed x47, local copies, waits for them, and re-layouts  4.71 us
    pallas_call x2, Pallas kernels, on_device(): pl.pallas_call(merge_kernel, out_shape=tuple((sds((tokens, 2 * head_dim),...  4.42 us
  transfers between devices with their start and end apart: 15, of which 5 were waited for; matrix products, arithmetic and copies ran while one was open for 1% of the time, Pallas kernels for 27%

profile of v5, /device:TPU:0, one launch (start us, length us, event | category | flops | bytes accessed | tf_op | source)
XLA Modules:
  0.0 140.9 jit_solution(314481336598050612)
XLA Ops:
  0.6 1.0 constant_dynamic-update-slice_fusion.1
  1.6 0.0 copy-done.2
  1.6 0.0 copy-start.12
  1.6 1.3 collective-permute-start
  2.9 12.0 %collective-permute-done.refs_7_ = bf16[256,512]{1,0:T(8,128)(2,1)S(1)} collective-permute-done((bf16[256,512]{1,0:T(8,128)(2,1)S(1)}, bf16[256,512]{1,0:T(8,128)(2,1)S(1)}, u32[]{:S(2)}, u32[]{:S(2)}) %collective-permute-start) | collective-permute-done | bytes 262176 | tf_op jit(solution)/shard_map/ppermute | solution.py:303
  14.9 1.3 collective-permute-start.1
  16.2 9.9 %collective-permute-done.1.refs_8_ = bf16[256,512]{1,0:T(8,128)(2,1)S(1)} collective-permute-done((bf16[256,512]{1,0:T(8,128)(2,1)S(1)}, bf16[256,512]{1,0:T(8,128)(2,1)S(1)}, u32[]{:S(2)}, u32[]{:S(2)}) %collective-permute-start.1) | collective-permute-done | bytes 262176 | tf_op jit(solution)/shard_map/ppermute | solution.py:303
  26.1 1.3 collective-permute-start.2
  27.4 1.3 collective-permute-start.3
  28.7 1.3 collective-permute-start.4
  30.0 1.3 collective-permute-start.5
  31.3 5.1 %collective-permute-done.2.refs_9_ = bf16[256,512]{1,0:T(8,128)(2,1)S(1)} collective-permute-done((bf16[256,512]{1,0:T(8,128)(2,1)S(1)}, bf16[256,512]{1,0:T(8,128)(2,1)S(1)}, u32[]{:S(2)}, u32[]{:S(2)}) %collective-permute-start.2) | collective-permute-done | bytes 262176 | tf_op jit(solution)/shard_map/ppermute | solution.py:303
  36.3 1.3 collective-permute-start.6
  37.6 0.7 fusion.2
  38.4 2.0 %plan.1.refs_0_ = s32[5,32]{1,0:T(8,128)} custom-call(s32[1]{0:T(128)} %bitcast.1.refs_0_, s32[4,32]{1,0:T(4,128)} %get-tuple-element.69.refs_1_), custom_call_target="tpu_custom_call" | custom-call | tf_op jit(solution)/shard_map/plan/pallas_call | solution.py:371
  40.4 0.5 broadcast_add_fusion.refs_0_
  40.9 7.8 %prep.1 = (bf16[2,128,2048]{2,1,0:T(8,128)(2,1)}, bf16[2,2048,128]{2,1,0:T(8,128)(2,1)}, bf16[2,128,2048]{2,1,0:T(8,128)(2,1)}, bf16[2,2048,128]{2,1,0:T(8,128)(2,1)}, f32[2,1,2048]{2,1,0:T(1,128)}) custom-call(s32[4]{0:T(128)} %broadcast_add_fusion.refs_0_, f32[32,128]{1,0:T(8,128)} %constant.66.clone.refs_1_.refs_2_, ...), custom_call_target="tpu_custom_call" | custom-call | tf_op jit(solution)/shard_map/prep/pallas_call | solution.py:387
  48.8 0.0 collective-permute-done.4.refs_11_
  48.8 1.0 collective-permute-done.5.refs_12_
  49.7 2.9 %collective-permute-done.6.refs_13_ = bf16[256,512]{1,0:T(8,128)(2,1)S(1)} collective-permute-done((bf16[256,512]{1,0:T(8,128)(2,1)S(1)}, bf16[256,512]{1,0:T(8,128)(2,1)S(1)}, u32[]{:S(2)}, u32[]{:S(2)}) %collective-permute-start.6) | collective-permute-done | bytes 262176 | tf_op jit(solution)/shard_map/ppermute | solution.py:303
  52.7 0.7 copy-done.20
  53.4 17.2 %attend.3 = (f32[128,2048]{1,0:T(8,128)}, f32[8,128]{1,0:T(8,128)}, bf16[256,256]{1,0:T(8,128)(2,1)}, bf16[256,256]{1,0:T(8,128)(2,1)}, bf16[256,256]{1,0:T(8,12...) custom-call(s32[5,32]{1,0:T(8,128)} %plan.1.refs_0_, f32[1,128]{1,0:T(1,128)} %bitcast.13, ...), custom_call_target="tpu_custom_call" | custom-call | flops 5368709120 | bytes 8388608 | tf_op jit(solution)/shard_map/attend/pallas_call | solution.py:406
  70.6 1.3 collective-permute-start.11
  71.9 17.2 %attend.2 = (f32[128,2048]{1,0:T(8,128)}, f32[8,128]{1,0:T(8,128)}, bf16[256,256]{1,0:T(8,128)(2,1)}, bf16[256,256]{1,0:T(8,128)(2,1)}, bf16[256,256]{1,0:T(8,12...) custom-call(s32[5,32]{1,0:T(8,128)} %plan.1.refs_0_, f32[1,128]{1,0:T(1,128)} %bitcast.14, ...), custom_call_target="tpu_custom_call" | custom-call | flops 5368709120 | bytes 8388608 | tf_op jit(solution)/shard_map/attend/pallas_call | solution.py:406
  89.1 1.3 collective-permute-start.7
  90.4 0.0 collective-permute-done.11.refs_4_
  90.4 0.0 copy-start.1
  90.4 0.8 copy-done.1
  91.2 2.2 %merge.3 = (f32[256,256]{1,0:T(8,128)}, bf16[256,256]{1,0:T(8,128)(2,1)}, bf16[256,256]{1,0:T(8,128)(2,1)}, bf16[256,256]{1,0:T(8,128)(2,1)}) custom-call(bf16[256,256]{1,0:T(8,128)(2,1)} %get-tuple-element.54.refs_0_, bf16[256,256]{1,0:T(8,128)(2,1)} %get-tuple-element.55.refs_1_, bf16[256,256]{1,0:T(8,128)(2,1)} %get-tuple-element.56.refs_2_, ...), custom_call_target="tpu_custom_call" | custom-call | tf_op jit(solution)/shard_map/merge/pallas_call | solution.py:445
  93.4 6.7 %collective-permute-start.12 = (bf16[256,256]{1,0:T(8,128)(2,1)}, bf16[256,256]{1,0:T(8,128)(2,1)S(1)}, u32[]{:S(2)}, u32[]{:S(2)}) collective-permute-start(bf16[256,256]{1,0:T(8,128)(2,1)} %get-tuple-element.60), channel_id=1, source_target_pairs={{0,24},{4,28},{12,4},{16,8},{20,12},{24,16},{28,20},{1,25},{5,29},... | collective-permute-start | bytes 393224 | tf_op jit(solution)/shard_map/ppermute | solution.py:303
  100.1 7.2 %query_back.1 = (bf16[256,2048]{1,0:T(8,128)(2,1)}, f32[8,128]{1,0:T(8,128)}) custom-call(s32[4]{0:T(128)} %broadcast_add_fusion.refs_0_, f32[32,128]{1,0:T(8,128)} %constant.66.clone.refs_1_.refs_2_, f32[32,128]{1,0:T(8,128)} %constant.67.clone.refs_2_.refs_3_, f32[64,128]{1,0:T(8,128)} %constant.68.clone.refs_3_.refs_4_, ...), custom_call_target="tpu_custom_call" | custom-call | tf_op jit(solution)/shard_map/query_back/pallas_call | solution.py:462
  107.3 0.7 reduce_sum.28
  108.0 1.3 collective-permute-start.13
  109.3 1.3 collective-permute-start.14
  110.7 0.8 copy-done
  111.5 2.2 %merge.2 = (f32[256,256]{1,0:T(8,128)}, bf16[256,256]{1,0:T(8,128)(2,1)}, bf16[256,256]{1,0:T(8,128)(2,1)}, bf16[256,256]{1,0:T(8,128)(2,1)}) custom-call(bf16[256,256]{1,0:T(8,128)(2,1)} %get-tuple-element.45.refs_0_, bf16[256,256]{1,0:T(8,128)(2,1)} %get-tuple-element.46.refs_1_, bf16[256,256]{1,0:T(8,128)(2,1)} %get-tuple-element.47.refs_2_, ...), custom_call_target="tpu_custom_call" | custom-call | tf_op jit(solution)/shard_map/merge/pallas_call | solution.py:445
  113.7 1.3 collective-permute-start.8
  115.0 1.3 collective-permute-start.9
  116.3 1.3 collective-permute-start.10
  117.6 18.7 %all_to_all.5.refs_15_ = f32[32,2,128]{2,1,0:T(2,128)} all-to-all(f32[32,2,128]{2,1,0:T(2,128)S(1)} %broadcast_in_dim.11), channel_id=1, replica_groups=mesh['ctx'=8,'heads'=4] {'ctx','heads'}, dimensions={0} | all-to-all | bytes 65536 | tf_op jit(solution)/shard_map/all_to_all | solution.py:481
  136.4 0.6 copy-done.4
  137.0 0.1 copy-done.5
  137.0 0.0 copy-done.6
  137.1 0.0 copy-done.7
  137.1 0.1 copy-done.8
  137.2 2.5 %key_back.1 = (bf16[256,256]{1,0:T(8,128)(2,1)}, bf16[256,256]{1,0:T(8,128)(2,1)}, f32[2,128]{1,0:T(2,128)}) custom-call(s32[4]{0:T(128)} %broadcast_add_fusion.refs_0_, f32[32,128]{1,0:T(8,128)} %constant.66.clone.refs_1_.refs_2_, f32[32,128]{1,0:T(8,128)} %constant.67.clone.refs_2_.refs_3_, f32[64,128]{1,0:T(8,128)} %constant.68.clone.refs_3_.refs_4_, ...), custom_call_target="tpu_custom_call" | custom-call | tf_op jit(solution)/shard_map/key_back/pallas_call | solution.py:483
  139.7 0.7 copy-done.13
  140.4 0.5 slice_bitcast_fusion
  (46 shorter events, 0.1 us)
Async XLA Ops:
  0.6 1.0 copy-start.2
  1.6 36.0 %copy-start.12 = (s32[4,32]{1,0:T(4,128)S(1)}, s32[4,32]{1,0:T(4,128)}, u32[]{:S(2)}) copy-start(s32[4,32]{1,0:T(4,128)} %param.19) | copy-start | bytes 1540
  1.6 47.1 %copy-start.9 = (bf16[256,512]{1,0:T(8,128)(2,1)}, bf16[256,512]{1,0:T(8,128)(2,1)S(1)}, u32[]{:S(2)}) copy-start(bf16[256,512]{1,0:T(8,128)(2,1)S(1)} %constant_dynamic-update-slice_fusion.refs_6_) | copy-start | bytes 786436
  1.6 13.3 %collective-permute-start = (bf16[256,512]{1,0:T(8,128)(2,1)S(1)}, bf16[256,512]{1,0:T(8,128)(2,1)S(1)}, u32[]{:S(2)}, u32[]{:S(2)}) collective-permute-start(bf16[256,512]{1,0:T(8,128)(2,1)S(1)} %constant_dynamic-update-slice_fusion.refs_6_), channel_id=1, source_target_pairs={{4,12},{8,16},{12,20},{16,24},{20,28},{24,0},{28,4},{5,13},{9,17},... | collective-permute-start | bytes 786440 | tf_op jit(solution)/shard_map/ppermute | solution.py:303
  14.9 33.8 %copy-start.14 = (bf16[256,512]{1,0:T(8,128)(2,1)}, bf16[256,512]{1,0:T(8,128)(2,1)S(1)}, u32[]{:S(2)}) copy-start(bf16[256,512]{1,0:T(8,128)(2,1)S(1)} %collective-permute-done.refs_7_) | copy-start | bytes 786436
  14.9 11.2 %collective-permute-start.1 = (bf16[256,512]{1,0:T(8,128)(2,1)S(1)}, bf16[256,512]{1,0:T(8,128)(2,1)S(1)}, u32[]{:S(2)}, u32[]{:S(2)}) collective-permute-start(bf16[256,512]{1,0:T(8,128)(2,1)S(1)} %collective-permute-done.refs_7_), channel_id=1, source_target_pairs={{12,20},{16,24},{20,28},{24,0},{28,4},{13,21},{17,25},{21,29},{25,... | collective-permute-start | bytes 786440 | tf_op jit(solution)/shard_map/ppermute | solution.py:303
  26.1 22.6 %copy-start.15 = (bf16[256,512]{1,0:T(8,128)(2,1)}, bf16[256,512]{1,0:T(8,128)(2,1)S(1)}, u32[]{:S(2)}) copy-start(bf16[256,512]{1,0:T(8,128)(2,1)S(1)} %collective-permute-done.1.refs_8_) | copy-start | bytes 786436
  26.1 10.3 %collective-permute-start.2 = (bf16[256,512]{1,0:T(8,128)(2,1)S(1)}, bf16[256,512]{1,0:T(8,128)(2,1)S(1)}, u32[]{:S(2)}, u32[]{:S(2)}) collective-permute-start(bf16[256,512]{1,0:T(8,128)(2,1)S(1)} %collective-permute-done.1.refs_8_), channel_id=1, source_target_pairs={{20,28},{24,0},{28,4},{21,29},{25,1},{29,5},{22,30},{26,2},{30,6},... | collective-permute-start | bytes 786440 | tf_op jit(solution)/shard_map/ppermute | solution.py:303
  27.4 21.4 %collective-permute-start.3 = (bf16[256,512]{1,0:T(8,128)(2,1)S(1)}, bf16[256,512]{1,0:T(8,128)(2,1)S(1)}, u32[]{:S(2)}, u32[]{:S(2)}) collective-permute-start(bf16[256,512]{1,0:T(8,128)(2,1)S(1)} %constant_dynamic-update-slice_fusion.refs_6_), channel_id=1, source_target_pairs={{4,0},{8,12},{16,20},{24,28},{5,1},{9,13},{17,21},{25,29},{6,2},{1... | collective-permute-start | bytes 786440 | tf_op jit(solution)/shard_map/ppermute | solution.py:303
  28.7 20.1 %collective-permute-start.4 = (bf16[256,512]{1,0:T(8,128)(2,1)S(1)}, bf16[256,512]{1,0:T(8,128)(2,1)S(1)}, u32[]{:S(2)}, u32[]{:S(2)}) collective-permute-start(bf16[256,512]{1,0:T(8,128)(2,1)S(1)} %collective-permute-done.refs_7_), channel_id=1, source_target_pairs={{4,0},{12,8},{16,20},{20,16},{24,28},{28,24},{5,1},{13,9},{17,21},... | collective-permute-start | bytes 786440 | tf_op jit(solution)/shard_map/ppermute | solution.py:303
  30.0 19.8 %collective-permute-start.5 = (bf16[256,512]{1,0:T(8,128)(2,1)S(1)}, bf16[256,512]{1,0:T(8,128)(2,1)S(1)}, u32[]{:S(2)}, u32[]{:S(2)}) collective-permute-start(bf16[256,512]{1,0:T(8,128)(2,1)S(1)} %collective-permute-done.1.refs_8_), channel_id=1, source_target_pairs={{4,0},{20,16},{24,28},{28,24},{5,1},{21,17},{25,29},{29,25},{6,2},... | collective-permute-start | bytes 786440 | tf_op jit(solution)/shard_map/ppermute | solution.py:303
  36.3 12.4 %copy-start.16 = (bf16[256,512]{1,0:T(8,128)(2,1)}, bf16[256,512]{1,0:T(8,128)(2,1)S(1)}, u32[]{:S(2)}) copy-start(bf16[256,512]{1,0:T(8,128)(2,1)S(1)} %collective-permute-done.2.refs_9_) | copy-start | bytes 786436
  36.3 16.4 %collective-permute-start.6 = (bf16[256,512]{1,0:T(8,128)(2,1)S(1)}, bf16[256,512]{1,0:T(8,128)(2,1)S(1)}, u32[]{:S(2)}, u32[]{:S(2)}) collective-permute-start(bf16[256,512]{1,0:T(8,128)(2,1)S(1)} %collective-permute-done.2.refs_9_), channel_id=1, source_target_pairs={{4,0},{28,24},{5,1},{29,25},{6,2},{30,26},{7,3},{31,27}} | collective-permute-start | bytes 786440 | tf_op jit(solution)/shard_map/ppermute | solution.py:303
  48.7 3.9 %copy-start.17 = (bf16[256,512]{1,0:T(8,128)(2,1)}, bf16[256,512]{1,0:T(8,128)(2,1)S(1)}, u32[]{:S(2)}) copy-start(bf16[256,512]{1,0:T(8,128)(2,1)S(1)} %collective-permute-done.3.refs_10_) | copy-start | bytes 786436
  48.8 3.9 %copy-start.18 = (bf16[256,512]{1,0:T(8,128)(2,1)}, bf16[256,512]{1,0:T(8,128)(2,1)S(1)}, u32[]{:S(2)}) copy-start(bf16[256,512]{1,0:T(8,128)(2,1)S(1)} %collective-permute-done.4.refs_11_) | copy-start | bytes 786436
  49.7 3.0 %copy-start.19 = (bf16[256,512]{1,0:T(8,128)(2,1)}, bf16[256,512]{1,0:T(8,128)(2,1)S(1)}, u32[]{:S(2)}) copy-start(bf16[256,512]{1,0:T(8,128)(2,1)S(1)} %collective-permute-done.5.refs_12_) | copy-start | bytes 786436
  52.7 0.7 copy-start.20
  70.6 19.8 %collective-permute-start.11 = (bf16[4,256,256]{2,1,0:T(8,128)(2,1)}, bf16[4,256,256]{2,1,0:T(8,128)(2,1)S(1)}, u32[]{:S(2)}, u32[]{:S(2)}) collective-permute-start(bf16[4,256,256]{2,1,0:T(8,128)(2,1)} %get-tuple-element.58), channel_id=1, source_target_pairs={{0,4},{8,12},{12,8},{16,20},{20,16},{24,28},{28,24},{1,5},{9,13},{... | collective-permute-start | bytes 1572872 | tf_op jit(solution)/shard_map/ppermute | solution.py:303
  89.1 21.6 %collective-permute-start.7 = (bf16[4,256,256]{2,1,0:T(8,128)(2,1)}, bf16[4,256,256]{2,1,0:T(8,128)(2,1)S(1)}, u32[]{:S(2)}, u32[]{:S(2)}) collective-permute-start(bf16[4,256,256]{2,1,0:T(8,128)(2,1)} %get-tuple-element.49), channel_id=1, source_target_pairs={{0,4},{8,12},{12,8},{16,20},{20,16},{24,28},{28,24},{1,5},{9,13},{... | collective-permute-start | bytes 1572872 | tf_op jit(solution)/shard_map/ppermute | solution.py:303
  90.4 0.8 copy-start.1
  93.4 22.9 %collective-permute-start.12 = (bf16[256,256]{1,0:T(8,128)(2,1)}, bf16[256,256]{1,0:T(8,128)(2,1)S(1)}, u32[]{:S(2)}, u32[]{:S(2)}) collective-permute-start(bf16[256,256]{1,0:T(8,128)(2,1)} %get-tuple-element.60), channel_id=1, source_target_pairs={{0,24},{4,28},{12,4},{16,8},{20,12},{24,16},{28,20},{1,25},{5,29},... | collective-permute-start | bytes 393224 | tf_op jit(solution)/shard_map/ppermute | solution.py:303
  100.1 7.9 %copy-start.22 = (bf16[256,256]{1,0:T(8,128)(2,1)S(1)}, bf16[256,256]{1,0:T(8,128)(2,1)}, u32[]{:S(2)}) copy-start(bf16[256,256]{1,0:T(8,128)(2,1)} %get-tuple-element.61) | copy-start | bytes 393220
  100.1 9.3 %copy-start.21 = (bf16[256,256]{1,0:T(8,128)(2,1)S(1)}, bf16[256,256]{1,0:T(8,128)(2,1)}, u32[]{:S(2)}) copy-start(bf16[256,256]{1,0:T(8,128)(2,1)} %get-tuple-element.62) | copy-start | bytes 393220
  107.3 0.7 copy-start.10
  107.3 0.7 copy-start.11
  108.0 28.3 %collective-permute-start.13 = (bf16[256,256]{1,0:T(8,128)(2,1)S(1)}, bf16[256,256]{1,0:T(8,128)(2,1)S(1)}, u32[]{:S(2)}, u32[]{:S(2)}) collective-permute-start(bf16[256,256]{1,0:T(8,128)(2,1)S(1)} %copy-done.22), channel_id=1, source_target_pairs={{0,16},{4,20},{20,4},{24,8},{28,12},{1,17},{5,21},{21,5},{25,9},{2... | collective-permute-start | bytes 393224 | tf_op jit(solution)/shard_map/ppermute | solution.py:303
  109.3 27.0 %collective-permute-start.14 = (bf16[256,256]{1,0:T(8,128)(2,1)S(1)}, bf16[256,256]{1,0:T(8,128)(2,1)S(1)}, u32[]{:S(2)}, u32[]{:S(2)}) collective-permute-start(bf16[256,256]{1,0:T(8,128)(2,1)S(1)} %copy-done.21), channel_id=1, source_target_pairs={{0,8},{4,12},{28,4},{1,9},{5,13},{29,5},{2,10},{6,14},{30,6},{3,11... | collective-permute-start | bytes 393224 | tf_op jit(solution)/shard_map/ppermute | solution.py:303
  110.7 0.8 copy-start
  113.7 22.7 %collective-permute-start.8 = (bf16[256,256]{1,0:T(8,128)(2,1)}, bf16[256,256]{1,0:T(8,128)(2,1)S(1)}, u32[]{:S(2)}, u32[]{:S(2)}) collective-permute-start(bf16[256,256]{1,0:T(8,128)(2,1)} %get-tuple-element.51), channel_id=1, source_target_pairs={{0,24},{4,28},{12,4},{16,8},{20,12},{24,16},{28,20},{1,25},{5,29},... | collective-permute-start | bytes 393224 | tf_op jit(solution)/shard_map/ppermute | solution.py:303
  115.0 21.4 %collective-permute-start.9 = (bf16[256,256]{1,0:T(8,128)(2,1)}, bf16[256,256]{1,0:T(8,128)(2,1)S(1)}, u32[]{:S(2)}, u32[]{:S(2)}) collective-permute-start(bf16[256,256]{1,0:T(8,128)(2,1)} %get-tuple-element.52), channel_id=1, source_target_pairs={{0,16},{4,20},{20,4},{24,8},{28,12},{1,17},{5,21},{21,5},{25,9},{2... | collective-permute-start | bytes 393224 | tf_op jit(solution)/shard_map/ppermute | solution.py:303
  116.3 20.1 %copy-start.3 = (bf16[256,256]{1,0:T(8,128)(2,1)}, bf16[256,256]{1,0:T(8,128)(2,1)S(1)}, u32[]{:S(2)}) copy-start(bf16[256,256]{1,0:T(8,128)(2,1)S(1)} %collective-permute-done.12.refs_12_) | copy-start | bytes 393220
  116.3 20.1 %collective-permute-start.10 = (bf16[256,256]{1,0:T(8,128)(2,1)}, bf16[256,256]{1,0:T(8,128)(2,1)S(1)}, u32[]{:S(2)}, u32[]{:S(2)}) collective-permute-start(bf16[256,256]{1,0:T(8,128)(2,1)} %get-tuple-element.53), channel_id=1, source_target_pairs={{0,8},{4,12},{28,4},{1,9},{5,13},{29,5},{2,10},{6,14},{30,6},{3,11... | collective-permute-start | bytes 393224 | tf_op jit(solution)/shard_map/ppermute | solution.py:303
  136.3 0.7 copy-start.4
  136.3 0.7 copy-start.5
  136.4 0.7 copy-start.6
  136.4 0.7 copy-start.7
  136.4 0.8 copy-start.8
  139.7 0.7 copy-start.13

commit v6 on v4

--- a/solution.py
+++ b/solution.py
@@ -52,6 +52,27 @@
     return jnp.concatenate([p[0] for p in parts], 0), jnp.concatenate([p[1] for p in parts], 0)
 
 
+def two_parts(values):
+    high = values.astype(BF16)
+    return high, (values - high.astype(F32)).astype(BF16)
+
+
+def row_means(values):
+    size = values.shape[-1]
+    ones = jnp.ones((size, size), BF16)
+    high, low = two_parts(values)
+    return (dot_nn(high, ones) + dot_nn(low, ones)) * (1.0 / size)
+
+
+def sums_in_row(values):
+    ones = jnp.ones((8, values.shape[-1]), BF16)
+    contract = (((1,), (1,)), ((), ()))
+    high, low = two_parts(values)
+    sums = lax.dot_general(ones, high, contract, preferred_element_type=F32)
+    sums = sums + lax.dot_general(ones, low, contract, preferred_element_type=F32)
+    return sums[0:1]
+
+
 def dot_nn(lhs, rhs):
     return lax.dot_general(lhs, rhs, (((1,), (0,)), ((), ())), preferred_element_type=F32)
 
@@ -60,7 +81,7 @@
     slots = tree_dev * blocks
     place = place_ref[0]
     here = jnp.where(place + 1 == tree_dev, 0, place + 1)
-    for row in range(4):
+    for row in range(5):
         for i in range(slots):
             plan_ref[row, i] = 0
     count = jnp.int32(blocks)
@@ -83,9 +104,10 @@
         plan_ref[1, slot] = b % blocks
         plan_ref[2, slot] = depth
         plan_ref[3, slot] = bits
+        plan_ref[4, slot] = there
         count = count + jnp.where(own | (bits == 0), 0, 1)
     for i in range(slots):
-        plan_ref[4, i] = count
+        plan_ref[5, i] = count
 
 
 def prep_kernel(blocks, block_len, kv_heads, depth_ref, t0, t1, t2, t3, gain_ref, q_ref, grad_ref, out_ref, *outs):
@@ -94,40 +116,45 @@
     cos, sin = own_tables(depth_ref, (t0, t1, t2, t3), blocks)
     gain = gain_ref[...]
     group = q_ref.shape[1] // head_dim // kv_heads
-    for head in range(group * kv_heads):
-        g = head % group
-        q_t_ref, q_rot_ref, grad_t_ref, grad_heads_ref, delta_ref = outs[5 * (head // group):][:5]
-        cols = pl.ds(head * head_dim, head_dim)
-        here = pl.ds(g * tokens, tokens)
-        rows = q_ref[:, cols].astype(F32)
-        rotated = turned(rows * inverse_rms(rows) * gain, cos, sin).astype(BF16)
-        q_rot_ref[here, :] = rotated
-        q_t_ref[:, here] = jnp.transpose(rotated)
-        grad = grad_ref[:, cols]
-        grad_heads_ref[here, :] = grad
-        grad_t_ref[:, here] = jnp.transpose(grad)
-        product = grad.astype(F32) * out_ref[:, cols].astype(F32)
-        delta_ref[:, here] = jnp.sum(jnp.transpose(product), 0, keepdims=True)
-
-
-def main_kernel(blocks, block_len, tree_dev, inv_root, staged, *refs):
+    for kv in range(kv_heads):
+        q_t_ref, q_rot_ref, grad_t_ref, grad_heads_ref, delta_ref = outs[5 * kv:][:5]
+
+        @pl.loop(0, group)
+        def _(g):
+            cols = pl.ds(pl.multiple_of((kv * group + g) * head_dim, head_dim), head_dim)
+            here = pl.ds(pl.multiple_of(g * tokens, tokens), tokens)
+            rows = q_ref[:, cols].astype(F32)
+            recip = lax.rsqrt(row_means(rows * rows) + EPS)
+            rotated = turned(rows * recip * gain, cos, sin).astype(BF16)
+            q_rot_ref[here, :] = rotated
+            q_t_ref[:, here] = jnp.transpose(rotated)
+            grad = grad_ref[:, cols]
+            grad_heads_ref[here, :] = grad
+            grad_t_ref[:, here] = jnp.transpose(grad)
+            delta_ref[:, here] = sums_in_row(grad.astype(F32) * out_ref[:, cols].astype(F32))
+
+
+def main_kernel(blocks, block_len, tree_dev, inv_root, n_in, *refs):
     plan_ref, gain_ref = refs[:2]
     tables = refs[2:6]
-    pieces = refs[6:6 + tree_dev]
-    q_t_ref, q_ref, grad_t_ref, grad_ref, delta_ref = refs[6 + tree_dev:11 + tree_dev]
-    half = tree_dev // 2
-    dq_ref, gain_part_ref = refs[11 + tree_dev:13 + tree_dev]
-    straight = refs[13 + tree_dev:13 + tree_dev + half]
-    crossed, raw, keys, keys_t, vals, shown, with_cos, with_sin, expo, mass, w_all, ds_all, found, spread, wide = refs[
-        13 + tree_dev + half:]
+    pieces = refs[6:6 + n_in]
+    q_t_ref, q_ref, grad_t_ref, grad_ref, delta_ref = refs[6 + n_in:11 + n_in]
+    dq_ref, gain_part_ref = refs[11 + n_in:13 + n_in]
+    parts = refs[13 + n_in:13 + n_in + tree_dev]
+    raw, keys, keys_t, vals, shown, with_cos, with_sin, expo, mass, w_all, ds_all, found, spread = refs[
+        13 + n_in + tree_dev:]
+    if n_in == 1:
+        raw, source_row = pieces[0], 4
+    else:
+        source_row = 0
+        for piece in range(tree_dev):
+            raw[piece] = pieces[piece][...]
     head_dim = gain_ref.shape[1]
     tokens = raw.shape[1]
     group = q_ref.shape[0] // tokens
-    count = plan_ref[4, 0]
+    count = plan_ref[5, 0]
     chunks = (count + blocks - 1) // blocks
     gain = gain_ref[...]
-    for piece in range(tree_dev):
-        raw[piece] = pieces[piece][...]
     query_block = lax.broadcasted_iota(jnp.int32, (1, tokens), 1) // block_len
 
     def rows_of(start):
@@ -136,7 +163,7 @@
     def load_chunk(c):
         for j in range(blocks):
             slot = jnp.minimum(c * blocks + j, tree_dev * blocks - 1)
-            piece = plan_ref[0, slot]
+            piece = plan_ref[source_row, slot]
             rows = rows_of(plan_ref[1, slot])
             cos, sin = block_tables(plan_ref[2, slot], tables)
             unit = raw[piece, rows, 0:head_dim].astype(F32)
@@ -171,10 +198,8 @@
         return pl.ds(g * tokens, tokens)
 
     def masses(c, first):
-        if staged:
-            wide[...] = dot_nn(keys[c], q_t_ref[...])
         for g in range(group):
-            scores = wide[:, cols_of(g)] if staged else dot_nn(keys[c], q_t_ref[:, cols_of(g)])
+            scores = dot_nn(keys[c], q_t_ref[:, cols_of(g)])
             e = exps(c, g, scores)
             if first:
                 e = jnp.where(key_row <= query_col, e, 0.0)
@@ -199,11 +224,9 @@
 
     @pl.loop(0, chunks)
     def _(c):
-        if staged:
-            wide[...] = dot_nn(vals[c], grad_t_ref[...])
         for g in range(group):
             cols = cols_of(g)
-            grad_prob = wide[:, cols] if staged else dot_nn(vals[c], grad_t_ref[:, cols])
+            grad_prob = dot_nn(vals[c], grad_t_ref[:, cols])
             weights = expo[c, g] * mass[g, 0:1, :]
             ds_all[:, cols] = (weights * (grad_prob - delta_ref[:, cols])).astype(BF16)
             w_all[:, cols] = weights.astype(BF16)
@@ -222,16 +245,8 @@
         rows = rows_of(lax.rem(slot, blocks))
         spread[plan_ref[0, slot], rows_of(plan_ref[1, slot]), :] = found[slot // blocks, rows, :]
 
-    for piece in range(half):
-        straight[piece][...] = spread[piece]
-        crossed[piece] = spread[half + piece]
-
-
-def merge_kernel(*refs):
-    parts, crossed_ref, outs = refs[:len(refs) // 2], refs[len(refs) // 2], refs[len(refs) // 2 + 1:]
-    outs[0][...] = (parts[0][...].astype(F32) + crossed_ref[0].astype(F32))
-    for i in range(1, len(parts)):
-        outs[i][...] = (parts[i][...].astype(F32) + crossed_ref[i].astype(F32)).astype(BF16)
+    for piece in range(tree_dev):
+        parts[piece][...] = spread[piece]
 
 
 def query_kernel(blocks, inv_root, depth_ref, t0, t1, t2, t3, gain_ref, q_ref, *refs):
@@ -241,19 +256,20 @@
     group = dq_refs[0].shape[1] // tokens
     cos, sin = own_tables(depth_ref, (t0, t1, t2, t3), blocks)
     gain = gain_ref[...]
-    part = jnp.zeros((8, head_dim), F32)
-    for head in range(group * len(dq_refs)):
-        cols = pl.ds(head * head_dim, head_dim)
-        rows = q_ref[:, cols].astype(F32)
-        recip = inverse_rms(rows)
-        normed = rows * recip
-        dq = jnp.transpose(dq_refs[head // group][:, pl.ds(head % group * tokens, tokens)])
-        scaled_grad = turned_back(dq, cos, sin) * inv_root
-        term = scaled_grad * normed
-        part = part + jnp.sum(term.reshape(tokens // 8, 8, head_dim), 0)
-        inner = jnp.mean(term * gain, -1, keepdims=True)
-        out_ref[:, cols] = (recip * (scaled_grad * gain - normed * inner)).astype(BF16)
-    part_ref[...] = part
+    part_ref[...] = jnp.zeros(part_ref.shape, F32)
+    for kv, dq_ref in enumerate(dq_refs):
+
+        @pl.loop(0, group)
+        def _(g):
+            cols = pl.ds(pl.multiple_of((kv * group + g) * head_dim, head_dim), head_dim)
+            rows = q_ref[:, cols].astype(F32)
+            recip = lax.rsqrt(row_means(rows * rows) + EPS)
+            normed = rows * recip
+            dq = jnp.transpose(dq_ref[:, pl.ds(pl.multiple_of(g * tokens, tokens), tokens)])
+            scaled_grad = turned_back(dq, cos, sin) * inv_root
+            term = scaled_grad * normed
+            part_ref[...] = part_ref[...] + jnp.sum(term.reshape(tokens // 8, 8, head_dim), 0)
+            out_ref[:, cols] = (recip * (scaled_grad * gain - normed * row_means(term * gain))).astype(BF16)
 
 
 def key_kernel(blocks, counts, depth_ref, t0, t1, t2, t3, gain_ref, k_ref, *refs):
@@ -306,16 +322,15 @@
                     pieces.append(self.send(own, there, lambda i: after(i, there(i))))
         return pieces
 
-    def across(self, crossed):
-        steps = range(0, self.size, 2)
-        return self.send(crossed, lambda i: i ^ 1, lambda i: any(self.after((i ^ 1) - step, i) for step in steps))
-
-    def back(self, merged):
+    def collect(self, parts):
         size, after = self.size, self.after
-        terms = []
-        for step, both in zip(range(2, size, 2), merged):
-            there = lambda i: (i - step) % size
-            terms.append(self.send(both, there, lambda i: after(there(i), i) or after(there(i), i ^ 1)))
+        terms = [parts[0]]
+        for odd in range(2):
+            for step in range(0, size, 2):
+                if odd or step:
+                    there = lambda i: ((i ^ odd) - step) % size
+                    part = parts[odd * size // 2 + step // 2]
+                    terms.append(self.send(part, there, lambda i: after(there(i), i)))
         return terms
 
 
@@ -347,10 +362,20 @@
     ]
     q_gain_row, k_gain_row = q_gain.reshape(1, head_dim), k_gain.reshape(1, head_dim)
 
+    groups = None
+    if cycle != tree_dev:
+        groups = [
+            [(start + 1 + tree.order(index)) % cycle for index in range(tree_dev)]
+            for start in range(0, cycle, tree_dev)
+        ]
     pieces = []
     for h in range(kv_heads):
         cols = slice(h * head_dim, (h + 1) * head_dim)
-        pieces.append(tree.gather(jnp.concatenate([k_raw[:, cols], values[:, cols]], 1)))
+        own = jnp.concatenate([k_raw[:, cols], values[:, cols]], 1)
+        if h == 0:
+            pieces.append(tree.gather(own))
+        else:
+            pieces.append([lax.all_gather(own, "ctx", axis_index_groups=groups)])
 
     params = pltpu.CompilerParams(vmem_limit_bytes=VMEM_LIMIT)
     smem = pl.BlockSpec(memory_space=pltpu.SMEM)
@@ -359,7 +384,7 @@
 
     plan = pl.pallas_call(
         lambda *refs: plan_kernel(blocks, tree_dev, *refs),
-        out_shape=sds((5, tree_blocks), jnp.int32),
+        out_shape=sds((6, tree_blocks), jnp.int32),
         in_specs=[smem, smem],
         out_specs=smem,
         name="plan",
@@ -384,19 +409,16 @@
         name="prep",
     )(depth, *tables, q_gain_row, q_raw, out_grad, saved_out)
 
-    half = tree_dev // 2
-
     def attend(h):
         return pl.pallas_call(
-            lambda *refs: main_kernel(blocks, block_len, tree_dev, inv_root, h > 0, *refs),
+            lambda *refs: main_kernel(blocks, block_len, tree_dev, inv_root, len(pieces[h]), *refs),
             out_shape=(
                 sds((head_dim, rows), F32),
                 sds((8, head_dim), F32),
-                *[sds((tokens, 2 * head_dim), BF16)] * half,
-                sds((half, tokens, 2 * head_dim), BF16),
+                *[sds((tokens, 2 * head_dim), BF16)] * tree_dev,
             ),
-            in_specs=[smem] + [vmem] * (10 + tree_dev),
-            out_specs=tuple([vmem] * (3 + half)),
+            in_specs=[smem] + [vmem] * (10 + len(pieces[h])),
+            out_specs=tuple([vmem] * (2 + tree_dev)),
             scratch_shapes=[
                 pltpu.VMEM((tree_dev, tokens, 2 * head_dim), BF16),
                 pltpu.VMEM((tree_dev + 1, tokens, head_dim), BF16),
@@ -411,7 +433,6 @@
                 pltpu.VMEM((tokens, rows), BF16),
                 pltpu.VMEM((tree_dev, tokens, 2 * head_dim), BF16),
                 pltpu.VMEM((tree_dev, tokens, 2 * head_dim), BF16),
-                pltpu.VMEM((tokens, rows), F32),
             ],
             compiler_params=params,
             cost_estimate=pl.CostEstimate(
@@ -424,20 +445,10 @@
 
     dq, terms, counts, k_gain_parts = [], [], [], []
     for h in range(kv_heads):
-        dq_here, k_gain_part, *parts, crossed = attend(h)
+        dq_here, k_gain_part, *parts = attend(h)
         dq.append(dq_here)
         k_gain_parts.append(k_gain_part)
-        own, *merged = pl.pallas_call(
-            merge_kernel,
-            out_shape=tuple(
-                sds((tokens, 2 * head_dim), F32 if i == 0 else BF16) for i in range(half)
-            ),
-            in_specs=[vmem] * (half + 1),
-            out_specs=tuple([vmem] * half),
-            compiler_params=params,
-            name="merge",
-        )(*parts, tree.across(crossed))
-        mine = [own, *tree.back(merged)]
+        mine = tree.collect(parts)
         terms.extend(mine)
         counts.append(len(mine))
 
@@ -451,7 +462,9 @@
     )(depth, *tables, q_gain_row, q_raw, *dq)
 
     gains = jnp.stack([jnp.sum(q_gain_part, 0), jnp.sum(sum(k_gain_parts), 0)])
-    gains = lax.all_gather(gains, ("ctx", "heads"))
+    everyone = cycle * lax.axis_size("heads")
+    gains = jnp.broadcast_to(gains[None], (everyone, *gains.shape))
+    gains = lax.all_to_all(gains, ("ctx", "heads"), 0, 0)
 
     dk_raw, dv, total = pl.pallas_call(
         lambda *refs: key_kernel(blocks, counts, *refs),

time: 166 us -> 134 us (0.81)
  blocking collectives: 46.2 us -> 9.63 us
  between operations: 1.28 us -> 14.8 us
  starting transfers between devices: 45 us -> 34.7 us
  Pallas kernels: 60.6 us -> 63 us
    all_gather x1 -> x0, blocking collectives: 46.2 us -> none  [on_device(): gains = lax.all_gather(gains, ('ctx', 'heads'))]
    ppermute x22 -> x21, starting transfers between devices: 45 us -> 34.6 us  [send(): return lax.ppermute(value, 'ctx', pairs)]
    all_to_all x0 -> x1, blocking collectives: none -> 9.63 us  [on_device(): gains = lax.all_to_all(gains, ('ctx', 'heads'), 0, 0)]
    pallas_call x2 -> x0, Pallas kernels: 4.36 us -> none  [on_device(): pl.pallas_call(merge_kernel, out_shape=tuple((sds((tokens, 2 * head_dim),...]
    pallas_call x1, Pallas kernels: 6.02 us -> 9.18 us  [on_device(): pl.pallas_call(lambda *refs: query_kernel(blocks, inv_root, *refs), out_s...]
    pallas_call x1, Pallas kernels: 7.48 us -> 9.54 us  [on_device(): pl.pallas_call(lambda *refs: prep_kernel(blocks, block_len, kv_heads, *re...]
    unnamed x56 -> x66, local copies, waits for them, and re-layouts: 3.84 us -> 2.84 us
    ppermute x22 -> x21, waiting for transfers between devices: 5.71 us -> 5.62 us  [send(): return lax.ppermute(value, 'ctx', pairs)]
  transfers between devices with their start and end apart: 22 -> 22, of which waited for: 3 -> 3; matrix products, arithmetic and copies ran while one was open for 1% -> 1% of each run, Pallas kernels for 35% -> 45%
where the time goes in v6:
time: 134 us; the launch traced here: 135 us
  Pallas kernels  63 us (47%)
  starting transfers between devices  34.7 us (26%)
  between operations  14.8 us (11%)
  blocking collectives  9.63 us (7%)
  waiting for transfers between devices  5.66 us (4%)
  local copies, waits for them, and re-layouts  4.32 us (3%)
  other arithmetic  2.64 us (2%)
    pallas_call x2, Pallas kernels, attend(): pl.pallas_call(lambda *refs: main_kernel(blocks, block_len, tree_dev, inv...  39.4 us
    ppermute x21, starting transfers between devices, send(): return lax.ppermute(value, 'ctx', pairs)  34.6 us
    all_to_all x1, blocking collectives, on_device(): gains = lax.all_to_all(gains, ('ctx', 'heads'), 0, 0)  9.63 us
    pallas_call x1, Pallas kernels, on_device(): pl.pallas_call(lambda *refs: prep_kernel(blocks, block_len, kv_heads, *re...  9.54 us
    pallas_call x1, Pallas kernels, on_device(): pl.pallas_call(lambda *refs: query_kernel(blocks, inv_root, *refs), out_s...  9.18 us
    ppermute x21, waiting for transfers between devices, send(): return lax.ppermute(value, 'ctx', pairs)  5.62 us
    pallas_call x1, Pallas kernels, on_device(): pl.pallas_call(lambda *refs: key_kernel(blocks, counts, *refs), out_shape...  2.88 us
    unnamed x66, local copies, waits for them, and re-layouts  2.84 us
  transfers between devices with their start and end apart: 22, of which 3 were waited for; matrix products, arithmetic and copies ran while one was open for 1% of the time, Pallas kernels for 45%

profile of v6, /device:TPU:0, one launch (start us, length us, event | category | flops | bytes accessed | tf_op | source)
XLA Modules:
  0.0 134.7 jit_solution(13621797687896321282)
XLA Ops:
  7.2 0.0 all-gather.3.cloned.1.call-start
  7.2 1.0 fusion.3
  8.2 0.7 pad_maximum_fusion.1
  8.8 0.0 all-gather.3.cloned.1.call-update
  8.9 1.3 collective-permute-start
  10.2 1.3 collective-permute-start.1
  11.5 1.3 collective-permute-start.2
  12.8 1.3 collective-permute-start.3
  14.1 1.3 collective-permute-start.4
  15.5 0.7 copy-done.17
  16.1 0.7 fusion.2
  16.8 2.0 %plan.1.refs_0_ = s32[6,32]{1,0:T(8,128)} custom-call(s32[1]{0:T(128)} %bitcast.1.refs_0_, s32[4,32]{1,0:T(4,128)} %get-tuple-element.79.refs_1_), custom_call_target="tpu_custom_call" | custom-call | tf_op jit(solution)/shard_map/plan/pallas_call | solution.py:385
  18.9 0.6 collective-permute-done.refs_7_
  19.5 1.3 collective-permute-start.5
  20.7 1.5 %collective-permute-done.1.refs_8_ = bf16[256,256]{1,0:T(8,128)(2,1)S(1)} collective-permute-done((bf16[256,256]{1,0:T(8,128)(2,1)S(1)}, bf16[256,256]{1,0:T(8,128)(2,1)S(1)}, u32[]{:S(2)}, u32[]{:S(2)}) %collective-permute-start.1) | collective-permute-done | bytes 131104 | tf_op jit(solution)/shard_map/ppermute | solution.py:310
  22.3 1.3 collective-permute-start.6
  23.6 0.5 broadcast_add_fusion.refs_0_
  24.1 9.5 %prep.1 = (bf16[128,2048]{1,0:T(8,128)(2,1)}, bf16[2048,128]{1,0:T(8,128)(2,1)}, bf16[128,2048]{1,0:T(8,128)(2,1)}, bf16[2048,128]{1,0:T(8,128)(2,1)}, f32[1,204...) custom-call(s32[4]{0:T(128)} %broadcast_add_fusion.refs_0_, ...), custom_call_target="tpu_custom_call" | custom-call | tf_op jit(solution)/shard_map/prep/pallas_call | solution.py:394
  33.7 3.5 %collective-permute-done.6.refs_13_ = bf16[256,256]{1,0:T(8,128)(2,1)S(1)} collective-permute-done((bf16[256,256]{1,0:T(8,128)(2,1)S(1)}, bf16[256,256]{1,0:T(8,128)(2,1)S(1)}, u32[]{:S(2)}, u32[]{:S(2)}) %collective-permute-start.6) | collective-permute-done | bytes 131104 | tf_op jit(solution)/shard_map/ppermute | solution.py:310
  37.2 0.6 copy-done.32
  37.9 19.8 %attend.2 = (f32[128,2048]{1,0:T(8,128)}, f32[8,128]{1,0:T(8,128)}, bf16[256,256]{1,0:T(8,128)(2,1)}, bf16[256,256]{1,0:T(8,128)(2,1)}, bf16[256,256]{1,0:T(8,12...) custom-call(s32[6,32]{1,0:T(8,128)} %plan.1.refs_0_, ...), custom_call_target="tpu_custom_call" | custom-call | flops 5368709120 | bytes 8388608 | tf_op jit(solution)/shard_map/attend/pallas_call | solution.py:413
  57.6 1.3 collective-permute-start.10
  58.9 8.7 %collective-permute-start.11 = (bf16[256,256]{1,0:T(8,128)(2,1)}, bf16[256,256]{1,0:T(8,128)(2,1)S(1)}, u32[]{:S(2)}, u32[]{:S(2)}) collective-permute-start(bf16[256,256]{1,0:T(8,128)(2,1)} %get-tuple-element.58), channel_id=1, source_target_pairs={{0,28},{8,4},{16,12},{20,8},{24,20},{28,16},{1,29},{9,5},{17,13},{... | collective-permute-start | bytes 393224 | tf_op jit(solution)/shard_map/ppermute | solution.py:310
  67.7 1.3 collective-permute-start.12
  69.0 1.3 collective-permute-start.13
  70.3 1.3 collective-permute-start.7
  71.6 0.0 all-gather.3.cloned.1.call-done
  71.6 19.6 %attend.3 = (f32[128,2048]{1,0:T(8,128)}, f32[8,128]{1,0:T(8,128)}, bf16[256,256]{1,0:T(8,128)(2,1)}, bf16[256,256]{1,0:T(8,128)(2,1)}, bf16[256,256]{1,0:T(8,12...) custom-call(s32[6,32]{1,0:T(8,128)} %plan.1.refs_0_, ...), custom_call_target="tpu_custom_call" | custom-call | flops 5368709120 | bytes 8388608 | tf_op jit(solution)/shard_map/attend/pallas_call | solution.py:413
  91.3 1.3 collective-permute-start.8
  92.6 1.3 collective-permute-start.9
  93.9 1.3 collective-permute-start.14
  95.2 1.3 collective-permute-start.15
  96.6 9.2 %query_back.1 = (bf16[256,2048]{1,0:T(8,128)(2,1)}, f32[8,128]{1,0:T(8,128)}) custom-call(s32[4]{0:T(128)} %broadcast_add_fusion.refs_0_, f32[32,128]{1,0:T(8,128)} %constant.66.clone.refs_1_.refs_2_, f32[32,128]{1,0:T(8,128)} %constant.67.clone.refs_2_.refs_3_, f32[64,128]{1,0:T(8,128)} %constant.68.clone.refs_3_.refs_4_, ...), custom_call_target="tpu_custom_call" | custom-call | tf_op jit(solution)/shard_map/query_back/pallas_call | solution.py:455
  105.8 0.7 reduce_sum.28
  106.6 1.3 collective-permute-start.16
  107.9 1.3 collective-permute-start.17
  109.3 1.3 collective-permute-start.18
  110.6 1.3 collective-permute-start.19
  111.9 1.3 collective-permute-start.20
  113.3 9.6 %all_to_all.5.refs_23_ = f32[32,2,128]{2,1,0:T(2,128)} all-to-all(f32[32,2,128]{2,1,0:T(2,128)S(1)} %broadcast_in_dim.11), channel_id=1, replica_groups=mesh['ctx'=8,'heads'=4] {'ctx','heads'}, dimensions={0} | all-to-all | bytes 65536 | tf_op jit(solution)/shard_map/all_to_all | solution.py:467
  123.0 0.5 copy-done.9
  123.6 0.1 copy-done.10
  123.6 0.1 copy-done.11
  123.7 0.0 copy-done.12
  123.7 0.1 copy-done.13
  123.8 2.9 %key_back.1 = (bf16[256,256]{1,0:T(8,128)(2,1)}, bf16[256,256]{1,0:T(8,128)(2,1)}, f32[2,128]{1,0:T(2,128)}) custom-call(s32[4]{0:T(128)} %broadcast_add_fusion.refs_0_, f32[32,128]{1,0:T(8,128)} %constant.66.clone.refs_1_.refs_2_, f32[32,128]{1,0:T(8,128)} %constant.67.clone.refs_2_.refs_3_, f32[64,128]{1,0:T(8,128)} %constant.68.clone.refs_3_.refs_4_, ...), custom_call_target="tpu_custom_call" | custom-call | tf_op jit(solution)/shard_map/key_back/pallas_call | solution.py:469
  126.7 0.6 copy-done.18
  127.3 0.5 slice_bitcast_fusion
  (80 shorter events, 0.2 us)
Async XLA Ops:
  7.2 64.4 %all-gather.3.cloned.1.call-start = ((), (), s32[]{:S(2)}) async-start(), calls=%async_computation.1 | async-start | bytes 1179648 | tf_op jit(solution)/shard_map/all_gather | solution.py:378
  8.9 24.7 %copy-start.14 = (bf16[256,256]{1,0:T(8,128)(2,1)}, bf16[256,256]{1,0:T(8,128)(2,1)S(1)}, u32[]{:S(2)}) copy-start(bf16[256,256]{1,0:T(8,128)(2,1)S(1)} %pad_maximum_fusion.refs_6_) | copy-start | bytes 393220
  8.9 10.5 %collective-permute-start = (bf16[256,256]{1,0:T(8,128)(2,1)S(1)}, bf16[256,256]{1,0:T(8,128)(2,1)S(1)}, u32[]{:S(2)}, u32[]{:S(2)}) collective-permute-start(bf16[256,256]{1,0:T(8,128)(2,1)S(1)} %pad_maximum_fusion.refs_6_), channel_id=1, source_target_pairs={{4,12},{8,16},{12,20},{16,24},{20,28},{24,0},{5,13},{9,17},{13,21}... | collective-permute-start | bytes 393224 | tf_op jit(solution)/shard_map/ppermute | solution.py:310
  10.2 12.1 %collective-permute-start.1 = (bf16[256,256]{1,0:T(8,128)(2,1)S(1)}, bf16[256,256]{1,0:T(8,128)(2,1)S(1)}, u32[]{:S(2)}, u32[]{:S(2)}) collective-permute-start(bf16[256,256]{1,0:T(8,128)(2,1)S(1)} %pad_maximum_fusion.refs_6_), channel_id=1, source_target_pairs={{4,20},{8,24},{12,28},{16,0},{5,21},{9,25},{13,29},{17,1},{6,22},{... | collective-permute-start | bytes 393224 | tf_op jit(solution)/shard_map/ppermute | solution.py:310
  11.5 22.1 %collective-permute-start.2 = (bf16[256,256]{1,0:T(8,128)(2,1)S(1)}, bf16[256,256]{1,0:T(8,128)(2,1)S(1)}, u32[]{:S(2)}, u32[]{:S(2)}) collective-permute-start(bf16[256,256]{1,0:T(8,128)(2,1)S(1)} %pad_maximum_fusion.refs_6_), channel_id=1, source_target_pairs={{4,28},{8,0},{5,29},{9,1},{6,30},{10,2},{7,31},{11,3}} | collective-permute-start | bytes 393224 | tf_op jit(solution)/shard_map/ppermute | solution.py:310
  12.8 20.8 %collective-permute-start.3 = (bf16[256,256]{1,0:T(8,128)(2,1)S(1)}, bf16[256,256]{1,0:T(8,128)(2,1)S(1)}, u32[]{:S(2)}, u32[]{:S(2)}) collective-permute-start(bf16[256,256]{1,0:T(8,128)(2,1)S(1)} %pad_maximum_fusion.refs_6_), channel_id=1, source_target_pairs={{4,0},{8,12},{16,20},{24,28},{5,1},{9,13},{17,21},{25,29},{6,2},{1... | collective-permute-start | bytes 393224 | tf_op jit(solution)/shard_map/ppermute | solution.py:310
  14.1 19.6 %collective-permute-start.4 = (bf16[256,256]{1,0:T(8,128)(2,1)S(1)}, bf16[256,256]{1,0:T(8,128)(2,1)S(1)}, u32[]{:S(2)}, u32[]{:S(2)}) collective-permute-start(bf16[256,256]{1,0:T(8,128)(2,1)S(1)} %pad_maximum_fusion.refs_6_), channel_id=1, source_target_pairs={{4,8},{8,20},{12,16},{16,28},{20,24},{28,0},{5,9},{9,21},{13,17},{... | collective-permute-start | bytes 393224 | tf_op jit(solution)/shard_map/ppermute | solution.py:310
  19.5 14.2 %copy-start.19 = (bf16[256,256]{1,0:T(8,128)(2,1)}, bf16[256,256]{1,0:T(8,128)(2,1)S(1)}, u32[]{:S(2)}) copy-start(bf16[256,256]{1,0:T(8,128)(2,1)S(1)} %collective-permute-done.refs_7_) | copy-start | bytes 393220
  19.5 14.2 %collective-permute-start.5 = (bf16[256,256]{1,0:T(8,128)(2,1)S(1)}, bf16[256,256]{1,0:T(8,128)(2,1)S(1)}, u32[]{:S(2)}, u32[]{:S(2)}) collective-permute-start(bf16[256,256]{1,0:T(8,128)(2,1)S(1)} %pad_maximum_fusion.refs_6_), channel_id=1, source_target_pairs={{4,16},{8,28},{12,24},{20,0},{5,17},{9,29},{13,25},{21,1},{6,18},{... | collective-permute-start | bytes 393224 | tf_op jit(solution)/shard_map/ppermute | solution.py:310
  22.3 11.4 %copy-start.20 = (bf16[256,256]{1,0:T(8,128)(2,1)}, bf16[256,256]{1,0:T(8,128)(2,1)S(1)}, u32[]{:S(2)}) copy-start(bf16[256,256]{1,0:T(8,128)(2,1)S(1)} %collective-permute-done.1.refs_8_) | copy-start | bytes 393220
  22.3 14.9 %collective-permute-start.6 = (bf16[256,256]{1,0:T(8,128)(2,1)S(1)}, bf16[256,256]{1,0:T(8,128)(2,1)S(1)}, u32[]{:S(2)}, u32[]{:S(2)}) collective-permute-start(bf16[256,256]{1,0:T(8,128)(2,1)S(1)} %pad_maximum_fusion.refs_6_), channel_id=1, source_target_pairs={{4,24},{12,0},{5,25},{13,1},{6,26},{14,2},{7,27},{15,3}} | collective-permute-start | bytes 393224 | tf_op jit(solution)/shard_map/ppermute | solution.py:310
  33.6 3.5 %copy-start.21 = (bf16[256,256]{1,0:T(8,128)(2,1)}, bf16[256,256]{1,0:T(8,128)(2,1)S(1)}, u32[]{:S(2)}) copy-start(bf16[256,256]{1,0:T(8,128)(2,1)S(1)} %collective-permute-done.2.refs_9_) | copy-start | bytes 393220
  33.7 3.5 %copy-start.22 = (bf16[256,256]{1,0:T(8,128)(2,1)}, bf16[256,256]{1,0:T(8,128)(2,1)S(1)}, u32[]{:S(2)}) copy-start(bf16[256,256]{1,0:T(8,128)(2,1)S(1)} %collective-permute-done.3.refs_10_) | copy-start | bytes 393220
  33.7 3.5 %copy-start.23 = (bf16[256,256]{1,0:T(8,128)(2,1)}, bf16[256,256]{1,0:T(8,128)(2,1)S(1)}, u32[]{:S(2)}) copy-start(bf16[256,256]{1,0:T(8,128)(2,1)S(1)} %collective-permute-done.4.refs_11_) | copy-start | bytes 393220
  33.7 3.5 %copy-start.31 = (bf16[256,256]{1,0:T(8,128)(2,1)}, bf16[256,256]{1,0:T(8,128)(2,1)S(1)}, u32[]{:S(2)}) copy-start(bf16[256,256]{1,0:T(8,128)(2,1)S(1)} %collective-permute-done.5.refs_12_) | copy-start | bytes 393220
  57.6 33.6 %collective-permute-start.10 = (bf16[256,256]{1,0:T(8,128)(2,1)}, bf16[256,256]{1,0:T(8,128)(2,1)S(1)}, u32[]{:S(2)}, u32[]{:S(2)}) collective-permute-start(bf16[256,256]{1,0:T(8,128)(2,1)} %get-tuple-element.57), channel_id=1, source_target_pairs={{0,4},{12,8},{20,16},{28,24},{1,5},{13,9},{21,17},{29,25},{2,6},{1... | collective-permute-start | bytes 393224 | tf_op jit(solution)/shard_map/ppermute | solution.py:310
  58.9 33.6 %collective-permute-start.11 = (bf16[256,256]{1,0:T(8,128)(2,1)}, bf16[256,256]{1,0:T(8,128)(2,1)S(1)}, u32[]{:S(2)}, u32[]{:S(2)}) collective-permute-start(bf16[256,256]{1,0:T(8,128)(2,1)} %get-tuple-element.58), channel_id=1, source_target_pairs={{0,28},{8,4},{16,12},{20,8},{24,20},{28,16},{1,29},{9,5},{17,13},{... | collective-permute-start | bytes 393224 | tf_op jit(solution)/shard_map/ppermute | solution.py:310
  67.7 26.2 %collective-permute-start.12 = (bf16[256,256]{1,0:T(8,128)(2,1)}, bf16[256,256]{1,0:T(8,128)(2,1)S(1)}, u32[]{:S(2)}, u32[]{:S(2)}) collective-permute-start(bf16[256,256]{1,0:T(8,128)(2,1)} %get-tuple-element.59), channel_id=1, source_target_pairs={{0,20},{16,4},{24,12},{28,8},{1,21},{17,5},{25,13},{29,9},{2,22},{... | collective-permute-start | bytes 393224 | tf_op jit(solution)/shard_map/ppermute | solution.py:310
  69.0 26.3 %collective-permute-start.13 = (bf16[256,256]{1,0:T(8,128)(2,1)}, bf16[256,256]{1,0:T(8,128)(2,1)S(1)}, u32[]{:S(2)}, u32[]{:S(2)}) collective-permute-start(bf16[256,256]{1,0:T(8,128)(2,1)} %get-tuple-element.60), channel_id=1, source_target_pairs={{0,12},{24,4},{1,13},{25,5},{2,14},{26,6},{3,15},{27,7}} | collective-permute-start | bytes 393224 | tf_op jit(solution)/shard_map/ppermute | solution.py:310
  70.3 36.3 %collective-permute-start.7 = (bf16[256,256]{1,0:T(8,128)(2,1)}, bf16[256,256]{1,0:T(8,128)(2,1)S(1)}, u32[]{:S(2)}, u32[]{:S(2)}) collective-permute-start(bf16[256,256]{1,0:T(8,128)(2,1)} %get-tuple-element.54), channel_id=1, source_target_pairs={{0,24},{12,4},{16,8},{20,12},{24,16},{28,20},{1,25},{13,5},{17,9},... | collective-permute-start | bytes 393224 | tf_op jit(solution)/shard_map/ppermute | solution.py:310
  71.6 19.6 %copy-start.27 = (bf16[256,256]{1,0:T(8,128)(2,1)S(1)}, bf16[256,256]{1,0:T(8,128)(2,1)}, u32[]{:S(2)}) copy-start(bf16[256,256]{1,0:T(8,128)(2,1)} %get-tuple-element.55) | copy-start | bytes 393220
  71.6 21.0 %copy-start.24 = (bf16[256,256]{1,0:T(8,128)(2,1)S(1)}, bf16[256,256]{1,0:T(8,128)(2,1)}, u32[]{:S(2)}) copy-start(bf16[256,256]{1,0:T(8,128)(2,1)} %get-tuple-element.56) | copy-start | bytes 393220
  91.2 14.5 %copy-start = (bf16[256,256]{1,0:T(8,128)(2,1)}, bf16[256,256]{1,0:T(8,128)(2,1)S(1)}, u32[]{:S(2)}) copy-start(bf16[256,256]{1,0:T(8,128)(2,1)S(1)} %collective-permute-done.10.refs_11_) | copy-start | bytes 393220
  91.3 16.6 %collective-permute-start.8 = (bf16[256,256]{1,0:T(8,128)(2,1)S(1)}, bf16[256,256]{1,0:T(8,128)(2,1)S(1)}, u32[]{:S(2)}, u32[]{:S(2)}) collective-permute-start(bf16[256,256]{1,0:T(8,128)(2,1)S(1)} %copy-done.27), channel_id=1, source_target_pairs={{0,16},{20,4},{24,8},{28,12},{1,17},{21,5},{25,9},{29,13},{2,18},{... | collective-permute-start | bytes 393224 | tf_op jit(solution)/shard_map/ppermute | solution.py:310
  92.6 13.2 %copy-start.1 = (bf16[256,256]{1,0:T(8,128)(2,1)}, bf16[256,256]{1,0:T(8,128)(2,1)S(1)}, u32[]{:S(2)}) copy-start(bf16[256,256]{1,0:T(8,128)(2,1)S(1)} %collective-permute-done.11.refs_12_) | copy-start | bytes 393220
  92.6 16.6 %collective-permute-start.9 = (bf16[256,256]{1,0:T(8,128)(2,1)S(1)}, bf16[256,256]{1,0:T(8,128)(2,1)S(1)}, u32[]{:S(2)}, u32[]{:S(2)}) collective-permute-start(bf16[256,256]{1,0:T(8,128)(2,1)S(1)} %copy-done.24), channel_id=1, source_target_pairs={{0,8},{28,4},{1,9},{29,5},{2,10},{30,6},{3,11},{31,7}} | collective-permute-start | bytes 393224 | tf_op jit(solution)/shard_map/ppermute | solution.py:310
  93.9 11.9 %copy-start.2 = (bf16[256,256]{1,0:T(8,128)(2,1)}, bf16[256,256]{1,0:T(8,128)(2,1)S(1)}, u32[]{:S(2)}) copy-start(bf16[256,256]{1,0:T(8,128)(2,1)S(1)} %collective-permute-done.12.refs_13_) | copy-start | bytes 393220
  93.9 16.6 %collective-permute-start.14 = (bf16[256,256]{1,0:T(8,128)(2,1)}, bf16[256,256]{1,0:T(8,128)(2,1)S(1)}, u32[]{:S(2)}, u32[]{:S(2)}) collective-permute-start(bf16[256,256]{1,0:T(8,128)(2,1)} %get-tuple-element.62), channel_id=1, source_target_pairs={{0,24},{12,4},{16,8},{20,12},{24,16},{28,20},{1,25},{13,5},{17,9},... | collective-permute-start | bytes 393224 | tf_op jit(solution)/shard_map/ppermute | solution.py:310
  95.2 10.6 %copy-start.3 = (bf16[256,256]{1,0:T(8,128)(2,1)}, bf16[256,256]{1,0:T(8,128)(2,1)S(1)}, u32[]{:S(2)}) copy-start(bf16[256,256]{1,0:T(8,128)(2,1)S(1)} %collective-permute-done.13.refs_14_) | copy-start | bytes 393220
  95.2 16.7 %collective-permute-start.15 = (bf16[256,256]{1,0:T(8,128)(2,1)}, bf16[256,256]{1,0:T(8,128)(2,1)S(1)}, u32[]{:S(2)}, u32[]{:S(2)}) collective-permute-start(bf16[256,256]{1,0:T(8,128)(2,1)} %get-tuple-element.63), channel_id=1, source_target_pairs={{0,16},{20,4},{24,8},{28,12},{1,17},{21,5},{25,9},{29,13},{2,18},{... | collective-permute-start | bytes 393224 | tf_op jit(solution)/shard_map/ppermute | solution.py:310
  96.5 10.0 %copy-start.30 = (bf16[256,256]{1,0:T(8,128)(2,1)S(1)}, bf16[256,256]{1,0:T(8,128)(2,1)}, u32[]{:S(2)}) copy-start(bf16[256,256]{1,0:T(8,128)(2,1)} %get-tuple-element.64) | copy-start | bytes 393220
  96.6 11.4 %copy-start.29 = (bf16[256,256]{1,0:T(8,128)(2,1)S(1)}, bf16[256,256]{1,0:T(8,128)(2,1)}, u32[]{:S(2)}) copy-start(bf16[256,256]{1,0:T(8,128)(2,1)} %get-tuple-element.65) | copy-start | bytes 393220
  96.6 12.7 %copy-start.28 = (bf16[256,256]{1,0:T(8,128)(2,1)S(1)}, bf16[256,256]{1,0:T(8,128)(2,1)}, u32[]{:S(2)}) copy-start(bf16[256,256]{1,0:T(8,128)(2,1)} %get-tuple-element.66) | copy-start | bytes 393220
  96.6 14.0 %copy-start.26 = (bf16[256,256]{1,0:T(8,128)(2,1)S(1)}, bf16[256,256]{1,0:T(8,128)(2,1)}, u32[]{:S(2)}) copy-start(bf16[256,256]{1,0:T(8,128)(2,1)} %get-tuple-element.67) | copy-start | bytes 393220
  96.6 15.3 %copy-start.25 = (bf16[256,256]{1,0:T(8,128)(2,1)S(1)}, bf16[256,256]{1,0:T(8,128)(2,1)}, u32[]{:S(2)}) copy-start(bf16[256,256]{1,0:T(8,128)(2,1)} %get-tuple-element.68) | copy-start | bytes 393220
  106.6 16.4 %copy-start.4 = (bf16[256,256]{1,0:T(8,128)(2,1)}, bf16[256,256]{1,0:T(8,128)(2,1)S(1)}, u32[]{:S(2)}) copy-start(bf16[256,256]{1,0:T(8,128)(2,1)S(1)} %collective-permute-done.7.refs_8_) | copy-start | bytes 393220
  106.6 16.3 %collective-permute-start.16 = (bf16[256,256]{1,0:T(8,128)(2,1)S(1)}, bf16[256,256]{1,0:T(8,128)(2,1)S(1)}, u32[]{:S(2)}, u32[]{:S(2)}) collective-permute-start(bf16[256,256]{1,0:T(8,128)(2,1)S(1)} %copy-done.30), channel_id=1, source_target_pairs={{0,8},{28,4},{1,9},{29,5},{2,10},{30,6},{3,11},{31,7}} | collective-permute-start | bytes 393224 | tf_op jit(solution)/shard_map/ppermute | solution.py:310
  107.9 15.1 %copy-start.5 = (bf16[256,256]{1,0:T(8,128)(2,1)}, bf16[256,256]{1,0:T(8,128)(2,1)S(1)}, u32[]{:S(2)}) copy-start(bf16[256,256]{1,0:T(8,128)(2,1)S(1)} %collective-permute-done.8.refs_9_) | copy-start | bytes 393220
  107.9 15.0 %collective-permute-start.17 = (bf16[256,256]{1,0:T(8,128)(2,1)S(1)}, bf16[256,256]{1,0:T(8,128)(2,1)S(1)}, u32[]{:S(2)}, u32[]{:S(2)}) collective-permute-start(bf16[256,256]{1,0:T(8,128)(2,1)S(1)} %copy-done.29), channel_id=1, source_target_pairs={{0,4},{12,8},{20,16},{28,24},{1,5},{13,9},{21,17},{29,25},{2,6},{1... | collective-permute-start | bytes 393224 | tf_op jit(solution)/shard_map/ppermute | solution.py:310
  109.2 13.8 %copy-start.6 = (bf16[256,256]{1,0:T(8,128)(2,1)}, bf16[256,256]{1,0:T(8,128)(2,1)S(1)}, u32[]{:S(2)}) copy-start(bf16[256,256]{1,0:T(8,128)(2,1)S(1)} %collective-permute-done.9.refs_10_) | copy-start | bytes 393220
  109.3 13.7 %collective-permute-start.18 = (bf16[256,256]{1,0:T(8,128)(2,1)S(1)}, bf16[256,256]{1,0:T(8,128)(2,1)S(1)}, u32[]{:S(2)}, u32[]{:S(2)}) collective-permute-start(bf16[256,256]{1,0:T(8,128)(2,1)S(1)} %copy-done.28), channel_id=1, source_target_pairs={{0,28},{8,4},{16,12},{20,8},{24,20},{28,16},{1,29},{9,5},{17,13},{... | collective-permute-start | bytes 393224 | tf_op jit(solution)/shard_map/ppermute | solution.py:310
  110.6 12.4 %copy-start.7 = (bf16[256,256]{1,0:T(8,128)(2,1)}, bf16[256,256]{1,0:T(8,128)(2,1)S(1)}, u32[]{:S(2)}) copy-start(bf16[256,256]{1,0:T(8,128)(2,1)S(1)} %collective-permute-done.14.refs_16_) | copy-start | bytes 393220
  110.6 12.4 %collective-permute-start.19 = (bf16[256,256]{1,0:T(8,128)(2,1)S(1)}, bf16[256,256]{1,0:T(8,128)(2,1)S(1)}, u32[]{:S(2)}, u32[]{:S(2)}) collective-permute-start(bf16[256,256]{1,0:T(8,128)(2,1)S(1)} %copy-done.26), channel_id=1, source_target_pairs={{0,20},{16,4},{24,12},{28,8},{1,21},{17,5},{25,13},{29,9},{2,22},{... | collective-permute-start | bytes 393224 | tf_op jit(solution)/shard_map/ppermute | solution.py:310
  111.9 11.1 %copy-start.8 = (bf16[256,256]{1,0:T(8,128)(2,1)}, bf16[256,256]{1,0:T(8,128)(2,1)S(1)}, u32[]{:S(2)}) copy-start(bf16[256,256]{1,0:T(8,128)(2,1)S(1)} %collective-permute-done.15.refs_17_) | copy-start | bytes 393220
  111.9 11.0 %collective-permute-start.20 = (bf16[256,256]{1,0:T(8,128)(2,1)S(1)}, bf16[256,256]{1,0:T(8,128)(2,1)S(1)}, u32[]{:S(2)}, u32[]{:S(2)}) collective-permute-start(bf16[256,256]{1,0:T(8,128)(2,1)S(1)} %copy-done.25), channel_id=1, source_target_pairs={{0,12},{24,4},{1,13},{25,5},{2,14},{26,6},{3,15},{27,7}} | collective-permute-start | bytes 393224 | tf_op jit(solution)/shard_map/ppermute | solution.py:310
  122.9 0.7 copy-start.11
  123.0 0.8 copy-start.12
  123.0 0.8 copy-start.13
  (7 other events, 4.8 us)
Sparse Core Ops, SparseCore 0:
  10.1 49.8 all-gather.2

commit v7 on v4

--- a/solution.py
+++ b/solution.py
@@ -100,34 +100,36 @@
         cols = pl.ds(head * head_dim, head_dim)
         here = pl.ds(g * tokens, tokens)
         rows = q_ref[:, cols].astype(F32)
-        rotated = turned(rows * inverse_rms(rows) * gain, cos, sin).astype(BF16)
-        q_rot_ref[here, :] = rotated
-        q_t_ref[:, here] = jnp.transpose(rotated)
+        rotated = turned(rows * inverse_rms(rows) * gain, cos, sin)
+        q_rot_ref[here, :] = rotated.astype(BF16)
+        q_t_ref[:, here] = jnp.transpose(rotated).astype(BF16)
         grad = grad_ref[:, cols]
         grad_heads_ref[here, :] = grad
-        grad_t_ref[:, here] = jnp.transpose(grad)
-        product = grad.astype(F32) * out_ref[:, cols].astype(F32)
-        delta_ref[:, here] = jnp.sum(jnp.transpose(product), 0, keepdims=True)
-
-
-def main_kernel(blocks, block_len, tree_dev, inv_root, staged, *refs):
+        grad_rows = jnp.transpose(grad.astype(F32))
+        grad_t_ref[:, here] = grad_rows.astype(BF16)
+        product = grad_rows * jnp.transpose(out_ref[:, cols].astype(F32))
+        delta_ref[:, here] = jnp.sum(product, 0, keepdims=True)
+
+
+def main_kernel(blocks, block_len, tree_dev, inv_root, head, *refs):
     plan_ref, gain_ref = refs[:2]
     tables = refs[2:6]
     pieces = refs[6:6 + tree_dev]
     q_t_ref, q_ref, grad_t_ref, grad_ref, delta_ref = refs[6 + tree_dev:11 + tree_dev]
-    half = tree_dev // 2
     dq_ref, gain_part_ref = refs[11 + tree_dev:13 + tree_dev]
-    straight = refs[13 + tree_dev:13 + tree_dev + half]
-    crossed, raw, keys, keys_t, vals, shown, with_cos, with_sin, expo, mass, w_all, ds_all, found, spread, wide = refs[
-        13 + tree_dev + half:]
+    parts = refs[13 + tree_dev:13 + 2 * tree_dev]
+    raw, keys, keys_t, vals, shown, with_cos, with_sin, expo, mass, w_all, ds_all, found, spread = refs[
+        13 + 2 * tree_dev:]
     head_dim = gain_ref.shape[1]
     tokens = raw.shape[1]
     group = q_ref.shape[0] // tokens
     count = plan_ref[4, 0]
     chunks = (count + blocks - 1) // blocks
     gain = gain_ref[...]
+    kv_heads = pieces[0].shape[1] // (2 * head_dim)
     for piece in range(tree_dev):
-        raw[piece] = pieces[piece][...]
+        raw[piece, :, 0:head_dim] = pieces[piece][:, head * head_dim:(head + 1) * head_dim]
+        raw[piece, :, head_dim:] = pieces[piece][:, (kv_heads + head) * head_dim:(kv_heads + head + 1) * head_dim]
     query_block = lax.broadcasted_iota(jnp.int32, (1, tokens), 1) // block_len
 
     def rows_of(start):
@@ -171,10 +173,8 @@
         return pl.ds(g * tokens, tokens)
 
     def masses(c, first):
-        if staged:
-            wide[...] = dot_nn(keys[c], q_t_ref[...])
         for g in range(group):
-            scores = wide[:, cols_of(g)] if staged else dot_nn(keys[c], q_t_ref[:, cols_of(g)])
+            scores = dot_nn(keys[c], q_t_ref[:, cols_of(g)])
             e = exps(c, g, scores)
             if first:
                 e = jnp.where(key_row <= query_col, e, 0.0)
@@ -199,11 +199,9 @@
 
     @pl.loop(0, chunks)
     def _(c):
-        if staged:
-            wide[...] = dot_nn(vals[c], grad_t_ref[...])
         for g in range(group):
             cols = cols_of(g)
-            grad_prob = wide[:, cols] if staged else dot_nn(vals[c], grad_t_ref[:, cols])
+            grad_prob = dot_nn(vals[c], grad_t_ref[:, cols])
             weights = expo[c, g] * mass[g, 0:1, :]
             ds_all[:, cols] = (weights * (grad_prob - delta_ref[:, cols])).astype(BF16)
             w_all[:, cols] = weights.astype(BF16)
@@ -222,16 +220,8 @@
         rows = rows_of(lax.rem(slot, blocks))
         spread[plan_ref[0, slot], rows_of(plan_ref[1, slot]), :] = found[slot // blocks, rows, :]
 
-    for piece in range(half):
-        straight[piece][...] = spread[piece]
-        crossed[piece] = spread[half + piece]
-
-
-def merge_kernel(*refs):
-    parts, crossed_ref, outs = refs[:len(refs) // 2], refs[len(refs) // 2], refs[len(refs) // 2 + 1:]
-    outs[0][...] = (parts[0][...].astype(F32) + crossed_ref[0].astype(F32))
-    for i in range(1, len(parts)):
-        outs[i][...] = (parts[i][...].astype(F32) + crossed_ref[i].astype(F32)).astype(BF16)
+    for piece in range(tree_dev):
+        parts[piece][...] = spread[piece]
 
 
 def query_kernel(blocks, inv_root, depth_ref, t0, t1, t2, t3, gain_ref, q_ref, *refs):
@@ -306,16 +296,15 @@
                     pieces.append(self.send(own, there, lambda i: after(i, there(i))))
         return pieces
 
-    def across(self, crossed):
-        steps = range(0, self.size, 2)
-        return self.send(crossed, lambda i: i ^ 1, lambda i: any(self.after((i ^ 1) - step, i) for step in steps))
-
-    def back(self, merged):
+    def collect(self, parts):
         size, after = self.size, self.after
-        terms = []
-        for step, both in zip(range(2, size, 2), merged):
-            there = lambda i: (i - step) % size
-            terms.append(self.send(both, there, lambda i: after(there(i), i) or after(there(i), i ^ 1)))
+        terms = [parts[0]]
+        for odd in range(2):
+            for step in range(0, size, 2):
+                if odd or step:
+                    there = lambda i: ((i ^ odd) - step) % size
+                    part = parts[odd * size // 2 + step // 2]
+                    terms.append(self.send(part, there, lambda i: after(there(i), i)))
         return terms
 
 
@@ -347,10 +336,7 @@
     ]
     q_gain_row, k_gain_row = q_gain.reshape(1, head_dim), k_gain.reshape(1, head_dim)
 
-    pieces = []
-    for h in range(kv_heads):
-        cols = slice(h * head_dim, (h + 1) * head_dim)
-        pieces.append(tree.gather(jnp.concatenate([k_raw[:, cols], values[:, cols]], 1)))
+    pieces = tree.gather(jnp.concatenate([k_raw, values], 1))
 
     params = pltpu.CompilerParams(vmem_limit_bytes=VMEM_LIMIT)
     smem = pl.BlockSpec(memory_space=pltpu.SMEM)
@@ -384,19 +370,16 @@
         name="prep",
     )(depth, *tables, q_gain_row, q_raw, out_grad, saved_out)
 
-    half = tree_dev // 2
-
     def attend(h):
         return pl.pallas_call(
-            lambda *refs: main_kernel(blocks, block_len, tree_dev, inv_root, h > 0, *refs),
+            lambda *refs: main_kernel(blocks, block_len, tree_dev, inv_root, h, *refs),
             out_shape=(
                 sds((head_dim, rows), F32),
                 sds((8, head_dim), F32),
-                *[sds((tokens, 2 * head_dim), BF16)] * half,
-                sds((half, tokens, 2 * head_dim), BF16),
+                *[sds((tokens, 2 * head_dim), BF16)] * tree_dev,
             ),
             in_specs=[smem] + [vmem] * (10 + tree_dev),
-            out_specs=tuple([vmem] * (3 + half)),
+            out_specs=tuple([vmem] * (2 + tree_dev)),
             scratch_shapes=[
                 pltpu.VMEM((tree_dev, tokens, 2 * head_dim), BF16),
                 pltpu.VMEM((tree_dev + 1, tokens, head_dim), BF16),
@@ -411,7 +394,6 @@
                 pltpu.VMEM((tokens, rows), BF16),
                 pltpu.VMEM((tree_dev, tokens, 2 * head_dim), BF16),
                 pltpu.VMEM((tree_dev, tokens, 2 * head_dim), BF16),
-                pltpu.VMEM((tokens, rows), F32),
             ],
             compiler_params=params,
             cost_estimate=pl.CostEstimate(
@@ -420,24 +402,14 @@
                 transcendentals=group * tokens * tree_dev * tokens,
             ),
             name="attend",
-        )(plan, k_gain_row, *tables, *pieces[h], *queries[5 * h:5 * h + 5])
+        )(plan, k_gain_row, *tables, *pieces, *queries[5 * h:5 * h + 5])
 
     dq, terms, counts, k_gain_parts = [], [], [], []
     for h in range(kv_heads):
-        dq_here, k_gain_part, *parts, crossed = attend(h)
+        dq_here, k_gain_part, *parts = attend(h)
         dq.append(dq_here)
         k_gain_parts.append(k_gain_part)
-        own, *merged = pl.pallas_call(
-            merge_kernel,
-            out_shape=tuple(
-                sds((tokens, 2 * head_dim), F32 if i == 0 else BF16) for i in range(half)
-            ),
-            in_specs=[vmem] * (half + 1),
-            out_specs=tuple([vmem] * half),
-            compiler_params=params,
-            name="merge",
-        )(*parts, tree.across(crossed))
-        mine = [own, *tree.back(merged)]
+        mine = tree.collect(parts)
         terms.extend(mine)
         counts.append(len(mine))
 
@@ -451,7 +423,9 @@
     )(depth, *tables, q_gain_row, q_raw, *dq)
 
     gains = jnp.stack([jnp.sum(q_gain_part, 0), jnp.sum(sum(k_gain_parts), 0)])
-    gains = lax.all_gather(gains, ("ctx", "heads"))
+    everyone = cycle * lax.axis_size("heads")
+    gains = jnp.broadcast_to(gains[None], (everyone, *gains.shape))
+    gains = lax.all_to_all(gains, ("ctx", "heads"), 0, 0)
 
     dk_raw, dv, total = pl.pallas_call(
         lambda *refs: key_kernel(blocks, counts, *refs),

time: 166 us -> 135 us (0.81)
  blocking collectives: 46.2 us -> 9.64 us
  waiting for transfers between devices: 5.71 us -> 19.5 us
  Pallas kernels: 60.6 us -> 54 us
    all_gather x1 -> x0, blocking collectives: 46.2 us -> none  [on_device(): gains = lax.all_gather(gains, ('ctx', 'heads'))]
    ppermute x22 -> x21, waiting for transfers between devices: 5.71 us -> 19.5 us  [send(): return lax.ppermute(value, 'ctx', pairs)]
    all_to_all x0 -> x1, blocking collectives: none -> 9.64 us  [on_device(): gains = lax.all_to_all(gains, ('ctx', 'heads'), 0, 0)]
    pallas_call x2 -> x0, Pallas kernels: 4.36 us -> none  [on_device(): pl.pallas_call(merge_kernel, out_shape=tuple((sds((tokens, 2 * head_dim),...]
    pallas_call x2, Pallas kernels: 38.2 us -> 36.3 us  [attend(): pl.pallas_call(lambda *refs: main_kernel(blocks, block_len, tree_dev, inv...]
    ppermute x22 -> x21, starting transfers between devices: 45 us -> 43.6 us  [send(): return lax.ppermute(value, 'ctx', pairs)]
    unnamed x56 -> x69, local copies, waits for them, and re-layouts: 3.84 us -> 3.22 us
  transfers between devices with their start and end apart: 22 -> 21, of which waited for: 3 -> 2; matrix products, arithmetic and copies ran while one was open for 1% -> 1% of each run, Pallas kernels for 35% -> 25%
where the time goes in v7:
time: 135 us; the launch traced here: 134 us
  Pallas kernels  54 us (40%)
  starting transfers between devices  43.6 us (32%)
  waiting for transfers between devices  19.5 us (14%)
  blocking collectives  9.64 us (7%)
  local copies, waits for them, and re-layouts  3.76 us (3%)
  other arithmetic  1.95 us (1%)
  between operations  1.41 us (1%)
    ppermute x21, starting transfers between devices, send(): return lax.ppermute(value, 'ctx', pairs)  43.6 us
    pallas_call x2, Pallas kernels, attend(): pl.pallas_call(lambda *refs: main_kernel(blocks, block_len, tree_dev, inv...  36.3 us
    ppermute x21, waiting for transfers between devices, send(): return lax.ppermute(value, 'ctx', pairs)  19.5 us
    all_to_all x1, blocking collectives, on_device(): gains = lax.all_to_all(gains, ('ctx', 'heads'), 0, 0)  9.64 us
    pallas_call x1, Pallas kernels, on_device(): pl.pallas_call(lambda *refs: prep_kernel(blocks, block_len, kv_heads, *re...  6.74 us
    pallas_call x1, Pallas kernels, on_device(): pl.pallas_call(lambda *refs: query_kernel(blocks, inv_root, *refs), out_s...  6.08 us
    unnamed x69, local copies, waits for them, and re-layouts  3.22 us
    pallas_call x1, Pallas kernels, on_device(): pl.pallas_call(lambda *refs: key_kernel(blocks, counts, *refs), out_shape...  2.88 us
  transfers between devices with their start and end apart: 21, of which 2 were waited for; matrix products, arithmetic and copies ran while one was open for 1% of the time, Pallas kernels for 25%

profile of v7, /device:TPU:0, one launch (start us, length us, event | category | flops | bytes accessed | tf_op | source)
XLA Modules:
  0.0 133.9 jit_solution(6502134505155612465)
XLA Ops:
  0.6 1.0 constant_dynamic-update-slice_fusion.1
  1.6 0.0 copy-done.14
  1.6 0.0 copy-start.18
  1.6 1.3 collective-permute-start.6
  2.9 1.3 collective-permute-start.5
  4.2 1.3 collective-permute-start.4
  5.5 1.3 collective-permute-start.3
  6.8 1.3 collective-permute-start.2
  8.1 16.4 %collective-permute-done.6.refs_13_ = bf16[256,512]{1,0:T(8,128)(2,1)S(1)} collective-permute-done((bf16[256,512]{1,0:T(8,128)(2,1)S(1)}, bf16[256,512]{1,0:T(8,128)(2,1)S(1)}, u32[]{:S(2)}, u32[]{:S(2)}) %collective-permute-start.6) | collective-permute-done | bytes 262176 | tf_op jit(solution)/shard_map/ppermute | solution.py:284
  24.5 1.3 collective-permute-start.1
  25.8 1.3 collective-permute-start
  27.1 0.7 fusion.2
  27.9 2.0 %plan.1.refs_0_ = s32[5,32]{1,0:T(8,128)} custom-call(s32[1]{0:T(128)} %bitcast.1.refs_0_, s32[4,32]{1,0:T(4,128)} %get-tuple-element.75.refs_1_), custom_call_target="tpu_custom_call" | custom-call | tf_op jit(solution)/shard_map/plan/pallas_call | solution.py:346
  29.9 0.5 broadcast_add_fusion.refs_0_
  30.4 6.7 %prep.1 = (bf16[128,2048]{1,0:T(8,128)(2,1)}, bf16[2048,128]{1,0:T(8,128)(2,1)}, bf16[128,2048]{1,0:T(8,128)(2,1)}, bf16[2048,128]{1,0:T(8,128)(2,1)}, f32[1,204...) custom-call(s32[4]{0:T(128)} %broadcast_add_fusion.refs_0_, ...), custom_call_target="tpu_custom_call" | custom-call | tf_op jit(solution)/shard_map/prep/pallas_call | solution.py:355
  37.2 0.0 collective-permute-done.4.refs_11_
  37.2 0.0 collective-permute-done.3.refs_10_
  37.2 3.1 %collective-permute-done.1.refs_8_ = bf16[256,512]{1,0:T(8,128)(2,1)S(1)} collective-permute-done((bf16[256,512]{1,0:T(8,128)(2,1)S(1)}, bf16[256,512]{1,0:T(8,128)(2,1)S(1)}, u32[]{:S(2)}, u32[]{:S(2)}) %collective-permute-start.1) | collective-permute-done | bytes 262176 | tf_op jit(solution)/shard_map/ppermute | solution.py:284
  40.4 0.7 copy-done.25
  41.1 0.1 copy-done.26
  41.2 18.1 %attend.2 = (f32[128,2048]{1,0:T(8,128)}, f32[8,128]{1,0:T(8,128)}, bf16[256,256]{1,0:T(8,128)(2,1)}, bf16[256,256]{1,0:T(8,128)(2,1)}, bf16[256,256]{1,0:T(8,12...) custom-call(s32[5,32]{1,0:T(8,128)} %plan.1.refs_0_, ...), custom_call_target="tpu_custom_call" | custom-call | flops 5368709120 | bytes 8388608 | tf_op jit(solution)/shard_map/attend/pallas_call | solution.py:374
  59.2 3.7 %collective-permute-start.7 = (bf16[256,256]{1,0:T(8,128)(2,1)}, bf16[256,256]{1,0:T(8,128)(2,1)S(1)}, u32[]{:S(2)}, u32[]{:S(2)}) collective-permute-start(bf16[256,256]{1,0:T(8,128)(2,1)} %get-tuple-element.54), channel_id=1, source_target_pairs={{0,24},{12,4},{16,8},{20,12},{24,16},{28,20},{1,25},{13,5},{17,9},... | collective-permute-start | bytes 393224 | tf_op jit(solution)/shard_map/ppermute | solution.py:284
  63.0 1.3 collective-permute-start.8
  64.3 1.3 collective-permute-start.9
  65.6 1.3 collective-permute-start.10
  66.9 15.0 %collective-permute-start.11 = (bf16[256,256]{1,0:T(8,128)(2,1)}, bf16[256,256]{1,0:T(8,128)(2,1)S(1)}, u32[]{:S(2)}, u32[]{:S(2)}) collective-permute-start(bf16[256,256]{1,0:T(8,128)(2,1)} %get-tuple-element.58), channel_id=1, source_target_pairs={{0,28},{8,4},{16,12},{20,8},{24,20},{28,16},{1,29},{9,5},{17,13},{... | collective-permute-start | bytes 393224 | tf_op jit(solution)/shard_map/ppermute | solution.py:284
  81.9 18.2 %attend.3 = (f32[128,2048]{1,0:T(8,128)}, f32[8,128]{1,0:T(8,128)}, bf16[256,256]{1,0:T(8,128)(2,1)}, bf16[256,256]{1,0:T(8,128)(2,1)}, bf16[256,256]{1,0:T(8,12...) custom-call(s32[5,32]{1,0:T(8,128)} %plan.1.refs_0_, ...), custom_call_target="tpu_custom_call" | custom-call | flops 5368709120 | bytes 8388608 | tf_op jit(solution)/shard_map/attend/pallas_call | solution.py:374
  100.1 0.0 collective-permute-done.7.refs_8_
  100.1 1.3 collective-permute-start.12
  101.5 1.3 collective-permute-start.13
  102.8 1.3 collective-permute-start.14
  104.1 1.5 %collective-permute-start.15 = (bf16[256,256]{1,0:T(8,128)(2,1)}, bf16[256,256]{1,0:T(8,128)(2,1)S(1)}, u32[]{:S(2)}, u32[]{:S(2)}) collective-permute-start(bf16[256,256]{1,0:T(8,128)(2,1)} %get-tuple-element.63), channel_id=1, source_target_pairs={{0,16},{20,4},{24,8},{28,12},{1,17},{21,5},{25,9},{29,13},{2,18},{... | collective-permute-start | bytes 393224 | tf_op jit(solution)/shard_map/ppermute | solution.py:284
  105.7 6.1 %query_back.1 = (bf16[256,2048]{1,0:T(8,128)(2,1)}, f32[8,128]{1,0:T(8,128)}) custom-call(s32[4]{0:T(128)} %broadcast_add_fusion.refs_0_, f32[32,128]{1,0:T(8,128)} %constant.66.clone.refs_1_.refs_2_, f32[32,128]{1,0:T(8,128)} %constant.67.clone.refs_2_.refs_3_, f32[64,128]{1,0:T(8,128)} %constant.68.clone.refs_3_.refs_4_, ...), custom_call_target="tpu_custom_call" | custom-call | tf_op jit(solution)/shard_map/query_back/pallas_call | solution.py:416
  111.8 0.7 reduce_sum.28
  112.5 1.3 collective-permute-start.16
  113.9 1.3 collective-permute-start.17
  115.2 1.4 %collective-permute-start.18 = (bf16[256,256]{1,0:T(8,128)(2,1)S(1)}, bf16[256,256]{1,0:T(8,128)(2,1)S(1)}, u32[]{:S(2)}, u32[]{:S(2)}) collective-permute-start(bf16[256,256]{1,0:T(8,128)(2,1)S(1)} %copy-done.29), channel_id=1, source_target_pairs={{0,28},{8,4},{16,12},{20,8},{24,20},{28,16},{1,29},{9,5},{17,13},{... | collective-permute-start | bytes 393224 | tf_op jit(solution)/shard_map/ppermute | solution.py:284
  116.7 1.3 collective-permute-start.19
  118.0 1.3 collective-permute-start.20
  119.3 9.6 %all_to_all.5.refs_23_ = f32[32,2,128]{2,1,0:T(2,128)} all-to-all(f32[32,2,128]{2,1,0:T(2,128)S(1)} %broadcast_in_dim.11), channel_id=1, replica_groups=mesh['ctx'=8,'heads'=4] {'ctx','heads'}, dimensions={0} | all-to-all | bytes 65536 | tf_op jit(solution)/shard_map/all_to_all | solution.py:428
  129.1 0.5 copy-done.9
  129.6 0.0 copy-done.10
  129.7 0.0 copy-done.11
  129.7 0.1 copy-done.12
  129.8 0.1 copy-done.13
  129.8 2.9 %key_back.1 = (bf16[256,256]{1,0:T(8,128)(2,1)}, bf16[256,256]{1,0:T(8,128)(2,1)}, f32[2,128]{1,0:T(2,128)}) custom-call(s32[4]{0:T(128)} %broadcast_add_fusion.refs_0_, f32[32,128]{1,0:T(8,128)} %constant.66.clone.refs_1_.refs_2_, f32[32,128]{1,0:T(8,128)} %constant.67.clone.refs_2_.refs_3_, f32[64,128]{1,0:T(8,128)} %constant.68.clone.refs_3_.refs_4_, ...), custom_call_target="tpu_custom_call" | custom-call | tf_op jit(solution)/shard_map/key_back/pallas_call | solution.py:430
  132.7 0.6 copy-done.19
  133.4 0.5 slice_bitcast_fusion
  (78 shorter events, 0.2 us)
Async XLA Ops:
  0.6 1.0 copy-start.14
  1.6 25.5 %copy-start.18 = (s32[4,32]{1,0:T(4,128)S(1)}, s32[4,32]{1,0:T(4,128)}, u32[]{:S(2)}) copy-start(s32[4,32]{1,0:T(4,128)} %param.19) | copy-start | bytes 1540
  1.6 35.5 %copy-start.15 = (bf16[256,512]{1,0:T(8,128)(2,1)}, bf16[256,512]{1,0:T(8,128)(2,1)S(1)}, u32[]{:S(2)}) copy-start(bf16[256,512]{1,0:T(8,128)(2,1)S(1)} %constant_dynamic-update-slice_fusion.refs_6_) | copy-start | bytes 786436
  1.6 22.9 %collective-permute-start.6 = (bf16[256,512]{1,0:T(8,128)(2,1)S(1)}, bf16[256,512]{1,0:T(8,128)(2,1)S(1)}, u32[]{:S(2)}, u32[]{:S(2)}) collective-permute-start(bf16[256,512]{1,0:T(8,128)(2,1)S(1)} %constant_dynamic-update-slice_fusion.refs_6_), channel_id=1, source_target_pairs={{4,24},{12,0},{5,25},{13,1},{6,26},{14,2},{7,27},{15,3}} | collective-permute-start | bytes 786440 | tf_op jit(solution)/shard_map/ppermute | solution.py:284
  2.9 22.9 %collective-permute-start.5 = (bf16[256,512]{1,0:T(8,128)(2,1)S(1)}, bf16[256,512]{1,0:T(8,128)(2,1)S(1)}, u32[]{:S(2)}, u32[]{:S(2)}) collective-permute-start(bf16[256,512]{1,0:T(8,128)(2,1)S(1)} %constant_dynamic-update-slice_fusion.refs_6_), channel_id=1, source_target_pairs={{4,16},{8,28},{12,24},{20,0},{5,17},{9,29},{13,25},{21,1},{6,18},{... | collective-permute-start | bytes 786440 | tf_op jit(solution)/shard_map/ppermute | solution.py:284
  4.2 32.9 %collective-permute-start.4 = (bf16[256,512]{1,0:T(8,128)(2,1)S(1)}, bf16[256,512]{1,0:T(8,128)(2,1)S(1)}, u32[]{:S(2)}, u32[]{:S(2)}) collective-permute-start(bf16[256,512]{1,0:T(8,128)(2,1)S(1)} %constant_dynamic-update-slice_fusion.refs_6_), channel_id=1, source_target_pairs={{4,8},{8,20},{12,16},{16,28},{20,24},{28,0},{5,9},{9,21},{13,17},{... | collective-permute-start | bytes 786440 | tf_op jit(solution)/shard_map/ppermute | solution.py:284
  5.5 31.6 %collective-permute-start.3 = (bf16[256,512]{1,0:T(8,128)(2,1)S(1)}, bf16[256,512]{1,0:T(8,128)(2,1)S(1)}, u32[]{:S(2)}, u32[]{:S(2)}) collective-permute-start(bf16[256,512]{1,0:T(8,128)(2,1)S(1)} %constant_dynamic-update-slice_fusion.refs_6_), channel_id=1, source_target_pairs={{4,0},{8,12},{16,20},{24,28},{5,1},{9,13},{17,21},{25,29},{6,2},{1... | collective-permute-start | bytes 786440 | tf_op jit(solution)/shard_map/ppermute | solution.py:284
  6.8 30.4 %collective-permute-start.2 = (bf16[256,512]{1,0:T(8,128)(2,1)S(1)}, bf16[256,512]{1,0:T(8,128)(2,1)S(1)}, u32[]{:S(2)}, u32[]{:S(2)}) collective-permute-start(bf16[256,512]{1,0:T(8,128)(2,1)S(1)} %constant_dynamic-update-slice_fusion.refs_6_), channel_id=1, source_target_pairs={{4,28},{8,0},{5,29},{9,1},{6,30},{10,2},{7,31},{11,3}} | collective-permute-start | bytes 786440 | tf_op jit(solution)/shard_map/ppermute | solution.py:284
  24.5 12.6 %copy-start.20 = (bf16[256,512]{1,0:T(8,128)(2,1)}, bf16[256,512]{1,0:T(8,128)(2,1)S(1)}, u32[]{:S(2)}) copy-start(bf16[256,512]{1,0:T(8,128)(2,1)S(1)} %collective-permute-done.6.refs_13_) | copy-start | bytes 786436
  24.5 15.8 %collective-permute-start.1 = (bf16[256,512]{1,0:T(8,128)(2,1)S(1)}, bf16[256,512]{1,0:T(8,128)(2,1)S(1)}, u32[]{:S(2)}, u32[]{:S(2)}) collective-permute-start(bf16[256,512]{1,0:T(8,128)(2,1)S(1)} %constant_dynamic-update-slice_fusion.refs_6_), channel_id=1, source_target_pairs={{4,20},{8,24},{12,28},{16,0},{5,21},{9,25},{13,29},{17,1},{6,22},{... | collective-permute-start | bytes 786440 | tf_op jit(solution)/shard_map/ppermute | solution.py:284
  25.8 11.3 %copy-start.21 = (bf16[256,512]{1,0:T(8,128)(2,1)}, bf16[256,512]{1,0:T(8,128)(2,1)S(1)}, u32[]{:S(2)}) copy-start(bf16[256,512]{1,0:T(8,128)(2,1)S(1)} %collective-permute-done.5.refs_12_) | copy-start | bytes 786436
  25.8 14.5 %collective-permute-start = (bf16[256,512]{1,0:T(8,128)(2,1)S(1)}, bf16[256,512]{1,0:T(8,128)(2,1)S(1)}, u32[]{:S(2)}, u32[]{:S(2)}) collective-permute-start(bf16[256,512]{1,0:T(8,128)(2,1)S(1)} %constant_dynamic-update-slice_fusion.refs_6_), channel_id=1, source_target_pairs={{4,12},{8,16},{12,20},{16,24},{20,28},{24,0},{5,13},{9,17},{13,21}... | collective-permute-start | bytes 786440 | tf_op jit(solution)/shard_map/ppermute | solution.py:284
  37.2 3.2 %copy-start.22 = (bf16[256,512]{1,0:T(8,128)(2,1)}, bf16[256,512]{1,0:T(8,128)(2,1)S(1)}, u32[]{:S(2)}) copy-start(bf16[256,512]{1,0:T(8,128)(2,1)S(1)} %collective-permute-done.4.refs_11_) | copy-start | bytes 786436
  37.2 3.2 %copy-start.23 = (bf16[256,512]{1,0:T(8,128)(2,1)}, bf16[256,512]{1,0:T(8,128)(2,1)S(1)}, u32[]{:S(2)}) copy-start(bf16[256,512]{1,0:T(8,128)(2,1)S(1)} %collective-permute-done.3.refs_10_) | copy-start | bytes 786436
  37.2 3.2 %copy-start.24 = (bf16[256,512]{1,0:T(8,128)(2,1)}, bf16[256,512]{1,0:T(8,128)(2,1)S(1)}, u32[]{:S(2)}) copy-start(bf16[256,512]{1,0:T(8,128)(2,1)S(1)} %collective-permute-done.2.refs_9_) | copy-start | bytes 786436
  40.4 0.8 copy-start.26
  59.2 40.9 %collective-permute-start.7 = (bf16[256,256]{1,0:T(8,128)(2,1)}, bf16[256,256]{1,0:T(8,128)(2,1)S(1)}, u32[]{:S(2)}, u32[]{:S(2)}) collective-permute-start(bf16[256,256]{1,0:T(8,128)(2,1)} %get-tuple-element.54), channel_id=1, source_target_pairs={{0,24},{12,4},{16,8},{20,12},{24,16},{28,20},{1,25},{13,5},{17,9},... | collective-permute-start | bytes 393224 | tf_op jit(solution)/shard_map/ppermute | solution.py:284
  63.0 38.5 %collective-permute-start.8 = (bf16[256,256]{1,0:T(8,128)(2,1)}, bf16[256,256]{1,0:T(8,128)(2,1)S(1)}, u32[]{:S(2)}, u32[]{:S(2)}) collective-permute-start(bf16[256,256]{1,0:T(8,128)(2,1)} %get-tuple-element.55), channel_id=1, source_target_pairs={{0,16},{20,4},{24,8},{28,12},{1,17},{21,5},{25,9},{29,13},{2,18},{... | collective-permute-start | bytes 393224 | tf_op jit(solution)/shard_map/ppermute | solution.py:284
  64.3 38.5 %collective-permute-start.9 = (bf16[256,256]{1,0:T(8,128)(2,1)}, bf16[256,256]{1,0:T(8,128)(2,1)S(1)}, u32[]{:S(2)}, u32[]{:S(2)}) collective-permute-start(bf16[256,256]{1,0:T(8,128)(2,1)} %get-tuple-element.56), channel_id=1, source_target_pairs={{0,8},{28,4},{1,9},{29,5},{2,10},{30,6},{3,11},{31,7}} | collective-permute-start | bytes 393224 | tf_op jit(solution)/shard_map/ppermute | solution.py:284
  65.6 38.5 %collective-permute-start.10 = (bf16[256,256]{1,0:T(8,128)(2,1)}, bf16[256,256]{1,0:T(8,128)(2,1)S(1)}, u32[]{:S(2)}, u32[]{:S(2)}) collective-permute-start(bf16[256,256]{1,0:T(8,128)(2,1)} %get-tuple-element.57), channel_id=1, source_target_pairs={{0,4},{12,8},{20,16},{28,24},{1,5},{13,9},{21,17},{29,25},{2,6},{1... | collective-permute-start | bytes 393224 | tf_op jit(solution)/shard_map/ppermute | solution.py:284
  66.9 45.6 %collective-permute-start.11 = (bf16[256,256]{1,0:T(8,128)(2,1)}, bf16[256,256]{1,0:T(8,128)(2,1)S(1)}, u32[]{:S(2)}, u32[]{:S(2)}) collective-permute-start(bf16[256,256]{1,0:T(8,128)(2,1)} %get-tuple-element.58), channel_id=1, source_target_pairs={{0,28},{8,4},{16,12},{20,8},{24,20},{28,16},{1,29},{9,5},{17,13},{... | collective-permute-start | bytes 393224 | tf_op jit(solution)/shard_map/ppermute | solution.py:284
  81.8 18.3 %copy-start.33 = (bf16[256,256]{1,0:T(8,128)(2,1)S(1)}, bf16[256,256]{1,0:T(8,128)(2,1)}, u32[]{:S(2)}) copy-start(bf16[256,256]{1,0:T(8,128)(2,1)} %get-tuple-element.59) | copy-start | bytes 393220
  81.9 19.6 %copy-start.31 = (bf16[256,256]{1,0:T(8,128)(2,1)S(1)}, bf16[256,256]{1,0:T(8,128)(2,1)}, u32[]{:S(2)}) copy-start(bf16[256,256]{1,0:T(8,128)(2,1)} %get-tuple-element.60) | copy-start | bytes 393220
  100.1 11.6 %copy-start = (bf16[256,256]{1,0:T(8,128)(2,1)}, bf16[256,256]{1,0:T(8,128)(2,1)S(1)}, u32[]{:S(2)}) copy-start(bf16[256,256]{1,0:T(8,128)(2,1)S(1)} %collective-permute-done.7.refs_8_) | copy-start | bytes 393220
  100.1 13.7 %collective-permute-start.12 = (bf16[256,256]{1,0:T(8,128)(2,1)S(1)}, bf16[256,256]{1,0:T(8,128)(2,1)S(1)}, u32[]{:S(2)}, u32[]{:S(2)}) collective-permute-start(bf16[256,256]{1,0:T(8,128)(2,1)S(1)} %copy-done.33), channel_id=1, source_target_pairs={{0,20},{16,4},{24,12},{28,8},{1,21},{17,5},{25,13},{29,9},{2,22},{... | collective-permute-start | bytes 393224 | tf_op jit(solution)/shard_map/ppermute | solution.py:284
  101.4 10.3 %copy-start.1 = (bf16[256,256]{1,0:T(8,128)(2,1)}, bf16[256,256]{1,0:T(8,128)(2,1)S(1)}, u32[]{:S(2)}) copy-start(bf16[256,256]{1,0:T(8,128)(2,1)S(1)} %collective-permute-done.8.refs_9_) | copy-start | bytes 393220
  101.5 13.7 %collective-permute-start.13 = (bf16[256,256]{1,0:T(8,128)(2,1)S(1)}, bf16[256,256]{1,0:T(8,128)(2,1)S(1)}, u32[]{:S(2)}, u32[]{:S(2)}) collective-permute-start(bf16[256,256]{1,0:T(8,128)(2,1)S(1)} %copy-done.31), channel_id=1, source_target_pairs={{0,12},{24,4},{1,13},{25,5},{2,14},{26,6},{3,15},{27,7}} | collective-permute-start | bytes 393224 | tf_op jit(solution)/shard_map/ppermute | solution.py:284
  102.8 9.0 %copy-start.2 = (bf16[256,256]{1,0:T(8,128)(2,1)}, bf16[256,256]{1,0:T(8,128)(2,1)S(1)}, u32[]{:S(2)}) copy-start(bf16[256,256]{1,0:T(8,128)(2,1)S(1)} %collective-permute-done.9.refs_10_) | copy-start | bytes 393220
  102.8 13.8 %collective-permute-start.14 = (bf16[256,256]{1,0:T(8,128)(2,1)}, bf16[256,256]{1,0:T(8,128)(2,1)S(1)}, u32[]{:S(2)}, u32[]{:S(2)}) collective-permute-start(bf16[256,256]{1,0:T(8,128)(2,1)} %get-tuple-element.62), channel_id=1, source_target_pairs={{0,24},{12,4},{16,8},{20,12},{24,16},{28,20},{1,25},{13,5},{17,9},... | collective-permute-start | bytes 393224 | tf_op jit(solution)/shard_map/ppermute | solution.py:284
  104.1 7.6 %copy-start.3 = (bf16[256,256]{1,0:T(8,128)(2,1)}, bf16[256,256]{1,0:T(8,128)(2,1)S(1)}, u32[]{:S(2)}) copy-start(bf16[256,256]{1,0:T(8,128)(2,1)S(1)} %collective-permute-done.10.refs_11_) | copy-start | bytes 393220
  104.1 13.8 %collective-permute-start.15 = (bf16[256,256]{1,0:T(8,128)(2,1)}, bf16[256,256]{1,0:T(8,128)(2,1)S(1)}, u32[]{:S(2)}, u32[]{:S(2)}) collective-permute-start(bf16[256,256]{1,0:T(8,128)(2,1)} %get-tuple-element.63), channel_id=1, source_target_pairs={{0,16},{20,4},{24,8},{28,12},{1,17},{21,5},{25,9},{29,13},{2,18},{... | collective-permute-start | bytes 393224 | tf_op jit(solution)/shard_map/ppermute | solution.py:284
  105.6 6.9 %copy-start.32 = (bf16[256,256]{1,0:T(8,128)(2,1)S(1)}, bf16[256,256]{1,0:T(8,128)(2,1)}, u32[]{:S(2)}) copy-start(bf16[256,256]{1,0:T(8,128)(2,1)} %get-tuple-element.64) | copy-start | bytes 393220
  105.6 8.3 %copy-start.30 = (bf16[256,256]{1,0:T(8,128)(2,1)S(1)}, bf16[256,256]{1,0:T(8,128)(2,1)}, u32[]{:S(2)}) copy-start(bf16[256,256]{1,0:T(8,128)(2,1)} %get-tuple-element.65) | copy-start | bytes 393220
  105.6 9.6 %copy-start.29 = (bf16[256,256]{1,0:T(8,128)(2,1)S(1)}, bf16[256,256]{1,0:T(8,128)(2,1)}, u32[]{:S(2)}) copy-start(bf16[256,256]{1,0:T(8,128)(2,1)} %get-tuple-element.66) | copy-start | bytes 393220
  105.6 11.0 %copy-start.28 = (bf16[256,256]{1,0:T(8,128)(2,1)S(1)}, bf16[256,256]{1,0:T(8,128)(2,1)}, u32[]{:S(2)}) copy-start(bf16[256,256]{1,0:T(8,128)(2,1)} %get-tuple-element.67) | copy-start | bytes 393220
  105.6 12.3 %copy-start.27 = (bf16[256,256]{1,0:T(8,128)(2,1)S(1)}, bf16[256,256]{1,0:T(8,128)(2,1)}, u32[]{:S(2)}) copy-start(bf16[256,256]{1,0:T(8,128)(2,1)} %get-tuple-element.68) | copy-start | bytes 393220
  112.5 16.5 %copy-start.4 = (bf16[256,256]{1,0:T(8,128)(2,1)}, bf16[256,256]{1,0:T(8,128)(2,1)S(1)}, u32[]{:S(2)}) copy-start(bf16[256,256]{1,0:T(8,128)(2,1)S(1)} %collective-permute-done.11.refs_12_) | copy-start | bytes 393220
  112.5 16.4 %collective-permute-start.16 = (bf16[256,256]{1,0:T(8,128)(2,1)S(1)}, bf16[256,256]{1,0:T(8,128)(2,1)S(1)}, u32[]{:S(2)}, u32[]{:S(2)}) collective-permute-start(bf16[256,256]{1,0:T(8,128)(2,1)S(1)} %copy-done.32), channel_id=1, source_target_pairs={{0,8},{28,4},{1,9},{29,5},{2,10},{30,6},{3,11},{31,7}} | collective-permute-start | bytes 393224 | tf_op jit(solution)/shard_map/ppermute | solution.py:284
  113.9 15.2 %copy-start.5 = (bf16[256,256]{1,0:T(8,128)(2,1)}, bf16[256,256]{1,0:T(8,128)(2,1)S(1)}, u32[]{:S(2)}) copy-start(bf16[256,256]{1,0:T(8,128)(2,1)S(1)} %collective-permute-done.12.refs_13_) | copy-start | bytes 393220
  113.9 15.1 %collective-permute-start.17 = (bf16[256,256]{1,0:T(8,128)(2,1)S(1)}, bf16[256,256]{1,0:T(8,128)(2,1)S(1)}, u32[]{:S(2)}, u32[]{:S(2)}) collective-permute-start(bf16[256,256]{1,0:T(8,128)(2,1)S(1)} %copy-done.30), channel_id=1, source_target_pairs={{0,4},{12,8},{20,16},{28,24},{1,5},{13,9},{21,17},{29,25},{2,6},{1... | collective-permute-start | bytes 393224 | tf_op jit(solution)/shard_map/ppermute | solution.py:284
  115.2 13.9 %copy-start.6 = (bf16[256,256]{1,0:T(8,128)(2,1)}, bf16[256,256]{1,0:T(8,128)(2,1)S(1)}, u32[]{:S(2)}) copy-start(bf16[256,256]{1,0:T(8,128)(2,1)S(1)} %collective-permute-done.13.refs_14_) | copy-start | bytes 393220
  115.2 13.8 %collective-permute-start.18 = (bf16[256,256]{1,0:T(8,128)(2,1)S(1)}, bf16[256,256]{1,0:T(8,128)(2,1)S(1)}, u32[]{:S(2)}, u32[]{:S(2)}) collective-permute-start(bf16[256,256]{1,0:T(8,128)(2,1)S(1)} %copy-done.29), channel_id=1, source_target_pairs={{0,28},{8,4},{16,12},{20,8},{24,20},{28,16},{1,29},{9,5},{17,13},{... | collective-permute-start | bytes 393224 | tf_op jit(solution)/shard_map/ppermute | solution.py:284
  116.6 12.5 %copy-start.7 = (bf16[256,256]{1,0:T(8,128)(2,1)}, bf16[256,256]{1,0:T(8,128)(2,1)S(1)}, u32[]{:S(2)}) copy-start(bf16[256,256]{1,0:T(8,128)(2,1)S(1)} %collective-permute-done.14.refs_16_) | copy-start | bytes 393220
  116.7 12.4 %collective-permute-start.19 = (bf16[256,256]{1,0:T(8,128)(2,1)S(1)}, bf16[256,256]{1,0:T(8,128)(2,1)S(1)}, u32[]{:S(2)}, u32[]{:S(2)}) collective-permute-start(bf16[256,256]{1,0:T(8,128)(2,1)S(1)} %copy-done.28), channel_id=1, source_target_pairs={{0,20},{16,4},{24,12},{28,8},{1,21},{17,5},{25,13},{29,9},{2,22},{... | collective-permute-start | bytes 393224 | tf_op jit(solution)/shard_map/ppermute | solution.py:284
  118.0 11.1 %copy-start.8 = (bf16[256,256]{1,0:T(8,128)(2,1)}, bf16[256,256]{1,0:T(8,128)(2,1)S(1)}, u32[]{:S(2)}) copy-start(bf16[256,256]{1,0:T(8,128)(2,1)S(1)} %collective-permute-done.15.refs_17_) | copy-start | bytes 393220
  118.0 11.0 %collective-permute-start.20 = (bf16[256,256]{1,0:T(8,128)(2,1)S(1)}, bf16[256,256]{1,0:T(8,128)(2,1)S(1)}, u32[]{:S(2)}, u32[]{:S(2)}) collective-permute-start(bf16[256,256]{1,0:T(8,128)(2,1)S(1)} %copy-done.27), channel_id=1, source_target_pairs={{0,12},{24,4},{1,13},{25,5},{2,14},{26,6},{3,15},{27,7}} | collective-permute-start | bytes 393224 | tf_op jit(solution)/shard_map/ppermute | solution.py:284
  129.0 0.7 copy-start.12
  129.0 0.8 copy-start.13
  (7 other events, 4.9 us)

commit v8 on v7

--- a/solution.py
+++ b/solution.py
@@ -111,15 +111,16 @@
         delta_ref[:, here] = jnp.sum(product, 0, keepdims=True)
 
 
-def main_kernel(blocks, block_len, tree_dev, inv_root, head, *refs):
+def main_kernel(blocks, block_len, tree_dev, inv_root, head, last, *refs):
     plan_ref, gain_ref = refs[:2]
     tables = refs[2:6]
-    pieces = refs[6:6 + tree_dev]
-    q_t_ref, q_ref, grad_t_ref, grad_ref, delta_ref = refs[6 + tree_dev:11 + tree_dev]
-    dq_ref, gain_part_ref = refs[11 + tree_dev:13 + tree_dev]
-    parts = refs[13 + tree_dev:13 + 2 * tree_dev]
-    raw, keys, keys_t, vals, shown, with_cos, with_sin, expo, mass, w_all, ds_all, found, spread = refs[
-        13 + 2 * tree_dev:]
+    half = tree_dev // 2
+    pieces, crossed_ref = refs[6:7 + half], refs[7 + half]
+    q_t_ref, q_ref, grad_t_ref, grad_ref, delta_ref = refs[8 + half:13 + half]
+    dq_ref, gain_part_ref = refs[13 + half:15 + half]
+    parts = refs[15 + half:15 + 2 * half + last]
+    crossed_part, raw, keys, keys_t, vals, shown, with_cos, with_sin, expo, mass, w_all, ds_all, found, spread = refs[
+        15 + 2 * half + last:]
     head_dim = gain_ref.shape[1]
     tokens = raw.shape[1]
     group = q_ref.shape[0] // tokens
@@ -127,9 +128,10 @@
     chunks = (count + blocks - 1) // blocks
     gain = gain_ref[...]
     kv_heads = pieces[0].shape[1] // (2 * head_dim)
-    for piece in range(tree_dev):
+    for piece in range(half + 1):
         raw[piece, :, 0:head_dim] = pieces[piece][:, head * head_dim:(head + 1) * head_dim]
         raw[piece, :, head_dim:] = pieces[piece][:, (kv_heads + head) * head_dim:(kv_heads + head + 1) * head_dim]
+    raw[half + 1:] = crossed_ref[...]
     query_block = lax.broadcasted_iota(jnp.int32, (1, tokens), 1) // block_len
 
     def rows_of(start):
@@ -220,12 +222,23 @@
         rows = rows_of(lax.rem(slot, blocks))
         spread[plan_ref[0, slot], rows_of(plan_ref[1, slot]), :] = found[slot // blocks, rows, :]
 
-    for piece in range(tree_dev):
+    for piece in range(half + last):
         parts[piece][...] = spread[piece]
-
-
-def query_kernel(blocks, inv_root, depth_ref, t0, t1, t2, t3, gain_ref, q_ref, *refs):
-    dq_refs, (out_ref, part_ref) = refs[:-2], refs[-2:]
+    crossed_part[...] = spread[half + last:]
+
+
+def join_kernel(*refs):
+    head_dim = refs[-1].shape[2] // 2
+    heads = refs[0].shape[1] // (2 * head_dim)
+    pieces, outs = refs[:-heads], refs[-heads:]
+    for head in range(heads):
+        for i, piece in enumerate(pieces):
+            outs[head][i, :, 0:head_dim] = piece[:, head * head_dim:(head + 1) * head_dim]
+            outs[head][i, :, head_dim:] = piece[:, (heads + head) * head_dim:(heads + head + 1) * head_dim]
+
+
+def query_kernel(blocks, inv_root, kv_heads, depth_ref, t0, t1, t2, t3, gain_ref, q_ref, *refs):
+    dq_refs, (k_part_refs, (out_ref, gains_ref)) = refs[:kv_heads], (refs[kv_heads:-2], refs[-2:])
     tokens = q_ref.shape[0]
     head_dim = gain_ref.shape[1]
     group = dq_refs[0].shape[1] // tokens
@@ -243,7 +256,9 @@
         part = part + jnp.sum(term.reshape(tokens // 8, 8, head_dim), 0)
         inner = jnp.mean(term * gain, -1, keepdims=True)
         out_ref[:, cols] = (recip * (scaled_grad * gain - normed * inner)).astype(BF16)
-    part_ref[...] = part
+    k_part = sum(ref[...] for ref in k_part_refs)
+    gains = jnp.concatenate([jnp.sum(part, 0, keepdims=True), jnp.sum(k_part, 0, keepdims=True)], 0)
+    gains_ref[...] = jnp.broadcast_to(gains[None], gains_ref.shape)
 
 
 def key_kernel(blocks, counts, depth_ref, t0, t1, t2, t3, gain_ref, k_ref, *refs):
@@ -288,24 +303,21 @@
 
     def gather(self, own):
         size, after = self.size, self.after
-        pieces = [own]
-        for odd in range(2):
-            for step in range(0, size, 2):
-                if odd or step:
-                    there = lambda i: (i + step) % size ^ odd
-                    pieces.append(self.send(own, there, lambda i: after(i, there(i))))
-        return pieces
-
-    def collect(self, parts):
-        size, after = self.size, self.after
-        terms = [parts[0]]
-        for odd in range(2):
-            for step in range(0, size, 2):
-                if odd or step:
-                    there = lambda i: ((i ^ odd) - step) % size
-                    part = parts[odd * size // 2 + step // 2]
-                    terms.append(self.send(part, there, lambda i: after(there(i), i)))
-        return terms
+        cross = self.send(own, lambda i: i ^ 1, lambda i: after(i, i ^ 1))
+        straight = []
+        for step in range(2, size, 2):
+            there = lambda i: (i + step) % size
+            straight.append(self.send(own, there, lambda i: after(i, there(i)) or after(i, there(i) ^ 1)))
+        return own, cross, straight
+
+    def across(self, value, steps, back=False):
+        if back:
+            return self.send(value, lambda i: i ^ 1, lambda i: any(self.after((i ^ 1) - step, i) for step in steps))
+        return self.send(value, lambda i: i ^ 1, lambda i: any(self.after(i - step, i ^ 1) for step in steps))
+
+    def home(self, value, step):
+        there = lambda i: (i - step) % self.size
+        return self.send(value, there, lambda i: self.after(there(i), i) or self.after(there(i), i ^ 1))
 
 
 def on_device(q_raw, k_raw, values, saved_out, out_grad, q_gain, k_gain, ancestors):
@@ -336,8 +348,8 @@
     ]
     q_gain_row, k_gain_row = q_gain.reshape(1, head_dim), k_gain.reshape(1, head_dim)
 
-    pieces = tree.gather(jnp.concatenate([k_raw, values], 1))
-
+    steps = range(2, tree_dev, 2)
+    own, cross, straight = tree.gather(jnp.concatenate([k_raw, values], 1))
     params = pltpu.CompilerParams(vmem_limit_bytes=VMEM_LIMIT)
     smem = pl.BlockSpec(memory_space=pltpu.SMEM)
     vmem = pl.BlockSpec(memory_space=pltpu.VMEM)
@@ -350,6 +362,16 @@
         out_specs=smem,
         name="plan",
     )(place, in_tree)
+
+    joined = pl.pallas_call(
+        join_kernel,
+        out_shape=tuple([sds((len(steps), tokens, 2 * head_dim), BF16)] * kv_heads),
+        in_specs=[vmem] * len(steps),
+        out_specs=tuple([vmem] * kv_heads),
+        compiler_params=params,
+        name="join",
+    )(*straight)
+    crossed = [tree.across(one, steps) for one in joined]
 
     rows = group * tokens
     queries = pl.pallas_call(
@@ -370,16 +392,20 @@
         name="prep",
     )(depth, *tables, q_gain_row, q_raw, out_grad, saved_out)
 
+    half = tree_dev // 2
+
     def attend(h):
+        last = h == kv_heads - 1
         return pl.pallas_call(
-            lambda *refs: main_kernel(blocks, block_len, tree_dev, inv_root, h, *refs),
+            lambda *refs: main_kernel(blocks, block_len, tree_dev, inv_root, h, last, *refs),
             out_shape=(
                 sds((head_dim, rows), F32),
                 sds((8, head_dim), F32),
-                *[sds((tokens, 2 * head_dim), BF16)] * tree_dev,
+                *[sds((tokens, 2 * head_dim), BF16)] * (half + last),
+                sds((half - last, tokens, 2 * head_dim), BF16),
             ),
-            in_specs=[smem] + [vmem] * (10 + tree_dev),
-            out_specs=tuple([vmem] * (2 + tree_dev)),
+            in_specs=[smem] + [vmem] * (12 + half),
+            out_specs=tuple([vmem] * (3 + half + last)),
             scratch_shapes=[
                 pltpu.VMEM((tree_dev, tokens, 2 * head_dim), BF16),
                 pltpu.VMEM((tree_dev + 1, tokens, head_dim), BF16),
@@ -402,29 +428,36 @@
                 transcendentals=group * tokens * tree_dev * tokens,
             ),
             name="attend",
-        )(plan, k_gain_row, *tables, *pieces, *queries[5 * h:5 * h + 5])
+        )(plan, k_gain_row, *tables, own, *straight, cross, crossed[h], *queries[5 * h:5 * h + 5])
 
     dq, terms, counts, k_gain_parts = [], [], [], []
     for h in range(kv_heads):
-        dq_here, k_gain_part, *parts = attend(h)
+        dq_here, k_gain_part, *parts, crossed_part = attend(h)
         dq.append(dq_here)
         k_gain_parts.append(k_gain_part)
-        mine = tree.collect(parts)
+        if len(parts) > half:
+            others = tree.across(crossed_part, steps, back=True)
+            mine = [parts[0], tree.across(parts[half], [0], back=True)]
+        else:
+            others = tree.across(crossed_part, [0, *steps], back=True)
+            mine = [parts[0], others[0]]
+            others = others[1:]
+        for i, step in enumerate(steps):
+            both = (parts[i + 1].astype(F32) + others[i].astype(F32)).astype(BF16)
+            mine.append(tree.home(both, step))
         terms.extend(mine)
         counts.append(len(mine))
 
-    dq_raw, q_gain_part = pl.pallas_call(
-        lambda *refs: query_kernel(blocks, inv_root, *refs),
-        out_shape=(sds((tokens, heads * head_dim), BF16), sds((8, head_dim), F32)),
-        in_specs=[smem] + [vmem] * (6 + kv_heads),
+    everyone = cycle * lax.axis_size("heads")
+    dq_raw, gains = pl.pallas_call(
+        lambda *refs: query_kernel(blocks, inv_root, kv_heads, *refs),
+        out_shape=(sds((tokens, heads * head_dim), BF16), sds((everyone, 2, head_dim), F32)),
+        in_specs=[smem] + [vmem] * (6 + 2 * kv_heads),
         out_specs=(vmem, vmem),
         compiler_params=params,
         name="query_back",
-    )(depth, *tables, q_gain_row, q_raw, *dq)
-
-    gains = jnp.stack([jnp.sum(q_gain_part, 0), jnp.sum(sum(k_gain_parts), 0)])
-    everyone = cycle * lax.axis_size("heads")
-    gains = jnp.broadcast_to(gains[None], (everyone, *gains.shape))
+    )(depth, *tables, q_gain_row, q_raw, *dq, *k_gain_parts)
+
     gains = lax.all_to_all(gains, ("ctx", "heads"), 0, 0)
 
     dk_raw, dv, total = pl.pallas_call(

time: 135 us -> 132 us (0.978)
  the two profiles are of different devices: /device:TPU:0 before, /device:TPU:11 now
where the time goes in v8:
time: 132 us; the launch traced here: 133 us
  starting transfers between devices  56.9 us (43%)
  Pallas kernels  39.5 us (30%)
  waiting for transfers between devices  28 us (21%)
  local copies, waits for them, and re-layouts  5.78 us (4%)
  other arithmetic  1.42 us (1%)
    ppermute x15, starting transfers between devices, send(): return lax.ppermute(value, 'ctx', pairs)  34.5 us
    ppermute x15, waiting for transfers between devices, send(): return lax.ppermute(value, 'ctx', pairs)  28 us
    all_to_all x1, starting transfers between devices, on_device(): gains = lax.all_to_all(gains, ('ctx', 'heads'), 0, 0)  22.3 us
    pallas_call x2, Pallas kernels, attend(): pl.pallas_call(lambda *refs: main_kernel(blocks, block_len, tree_dev, inv...  19.9 us
    pallas_call x1, Pallas kernels, on_device(): pl.pallas_call(lambda *refs: prep_kernel(blocks, block_len, kv_heads, *re...  6.81 us
    pallas_call x1, Pallas kernels, on_device(): pl.pallas_call(lambda *refs: query_kernel(blocks, inv_root, kv_heads, *re...  6.06 us
    unnamed x53, local copies, waits for them, and re-layouts  4.58 us
  transfers between devices with their start and end apart: 16, of which 4 were waited for; matrix products, arithmetic and copies ran while one was open for 2% of the time, Pallas kernels for 28%

profile of v8, /device:TPU:11, one launch (start us, length us, event | category | flops | bytes accessed | tf_op | source)
XLA Modules:
  0.0 132.7 jit_solution(2546423844789555485)
XLA Ops:
  0.6 1.0 constant_dynamic-update-slice_fusion.1
  1.6 0.0 copy-done.10
  1.6 2.1 %collective-permute-start.2 = (bf16[256,512]{1,0:T(8,128)(2,1)S(1)}, bf16[256,512]{1,0:T(8,128)(2,1)S(1)}, u32[]{:S(2)}, u32[]{:S(2)}) collective-permute-start(bf16[256,512]{1,0:T(8,128)(2,1)S(1)} %constant_dynamic-update-slice_fusion.refs_6_), channel_id=1, source_target_pairs={{4,28},{8,0},{12,4},{5,29},{9,1},{13,5},{6,30},{10,2},{14,6},{7,31... | collective-permute-start | bytes 786440 | tf_op jit(solution)/shard_map/ppermute | solution.py:299
  3.7 3.4 %collective-permute-start.1 = (bf16[256,512]{1,0:T(8,128)(2,1)S(1)}, bf16[256,512]{1,0:T(8,128)(2,1)S(1)}, u32[]{:S(2)}, u32[]{:S(2)}) collective-permute-start(bf16[256,512]{1,0:T(8,128)(2,1)S(1)} %constant_dynamic-update-slice_fusion.refs_6_), channel_id=1, source_target_pairs={{4,20},{8,24},{12,28},{16,0},{20,4},{5,21},{9,25},{13,29},{17,1},{... | collective-permute-start | bytes 786440 | tf_op jit(solution)/shard_map/ppermute | solution.py:299
  7.2 4.9 %collective-permute-start = (bf16[256,512]{1,0:T(8,128)(2,1)S(1)}, bf16[256,512]{1,0:T(8,128)(2,1)S(1)}, u32[]{:S(2)}, u32[]{:S(2)}) collective-permute-start(bf16[256,512]{1,0:T(8,128)(2,1)S(1)} %constant_dynamic-update-slice_fusion.refs_6_), channel_id=1, source_target_pairs={{4,12},{8,16},{12,20},{16,24},{20,28},{24,0},{28,4},{5,13},{9,17},... | collective-permute-start | bytes 786440 | tf_op jit(solution)/shard_map/ppermute | solution.py:299
  12.1 1.3 collective-permute-start.3
  13.4 0.0 collective-permute-done.2.refs_2_.refs_9_
  13.4 10.6 %collective-permute-done.1.refs_1_.refs_8_ = bf16[256,512]{1,0:T(8,128)(2,1)S(1)} collective-permute-done((bf16[256,512]{1,0:T(8,128)(2,1)S(1)}, bf16[256,512]{1,0:T(8,128)(2,1)S(1)}, u32[]{:S(2)}, u32[]{:S(2)}) %collective-permute-start.1) | collective-permute-done | bytes 262176 | tf_op jit(solution)/shard_map/ppermute | solution.py:299
  24.0 5.6 %collective-permute-done.refs_0_.refs_7_ = bf16[256,512]{1,0:T(8,128)(2,1)S(1)} collective-permute-done((bf16[256,512]{1,0:T(8,128)(2,1)S(1)}, bf16[256,512]{1,0:T(8,128)(2,1)S(1)}, u32[]{:S(2)}, u32[]{:S(2)}) %collective-permute-start) | collective-permute-done | bytes 262176 | tf_op jit(solution)/shard_map/ppermute | solution.py:299
  29.6 0.7 copy-done.2
  30.3 2.2 %join.1 = (bf16[3,256,256]{2,1,0:T(8,128)(2,1)}, bf16[3,256,256]{2,1,0:T(8,128)(2,1)}) custom-call(bf16[256,512]{1,0:T(8,128)(2,1)} %copy-done.2, bf16[256,512]{1,0:T(8,128)(2,1)} %copy-done.1, bf16[256,512]{1,0:T(8,128)(2,1)} %copy-done), custom_call_target="tpu_custom_call" | custom-call | tf_op jit(solution)/shard_map/join/pallas_call | solution.py:366
  32.5 1.3 collective-permute-start.5
  33.8 0.7 fusion.8
  34.5 2.0 %plan.1.refs_0_ = s32[5,32]{1,0:T(8,128)} custom-call(s32[1]{0:T(128)} %bitcast.1.refs_0_, s32[4,32]{1,0:T(4,128)} %get-tuple-element.75.refs_1_), custom_call_target="tpu_custom_call" | custom-call | tf_op jit(solution)/shard_map/plan/pallas_call | solution.py:358
  36.6 0.5 broadcast_add_fusion.refs_0_
  37.1 6.8 %prep.1 = (bf16[128,2048]{1,0:T(8,128)(2,1)}, bf16[2048,128]{1,0:T(8,128)(2,1)}, bf16[128,2048]{1,0:T(8,128)(2,1)}, bf16[2048,128]{1,0:T(8,128)(2,1)}, f32[1,204...) custom-call(s32[4]{0:T(128)} %broadcast_add_fusion.refs_0_, ...), custom_call_target="tpu_custom_call" | custom-call | tf_op jit(solution)/shard_map/prep/pallas_call | solution.py:377
  43.9 1.3 collective-permute-start.4
  45.2 0.0 collective-permute-done.3.refs_10_
  45.2 0.0 collective-permute-done.5.refs_11_
  45.3 0.7 copy-done.24
  45.9 0.1 copy-done.22
  46.1 10.0 %attend.3 = (f32[128,2048]{1,0:T(8,128)}, f32[8,128]{1,0:T(8,128)}, bf16[256,256]{1,0:T(8,128)(2,1)}, bf16[256,256]{1,0:T(8,128)(2,1)}, bf16[256,256]{1,0:T(8,12...) custom-call(s32[5,32]{1,0:T(8,128)} %plan.1.refs_0_, ...), custom_call_target="tpu_custom_call" | custom-call | flops 5368709120 | bytes 8388608 | tf_op jit(solution)/shard_map/attend/pallas_call | solution.py:399
  56.1 1.3 collective-permute-start.11
  57.3 0.0 collective-permute-done.4.refs_11_
  57.4 0.7 copy-done.23
  58.1 10.0 %attend.2 = (f32[128,2048]{1,0:T(8,128)}, f32[8,128]{1,0:T(8,128)}, bf16[256,256]{1,0:T(8,128)(2,1)}, bf16[256,256]{1,0:T(8,128)(2,1)}, bf16[256,256]{1,0:T(8,12...) custom-call(s32[5,32]{1,0:T(8,128)} %plan.1.refs_0_, f32[1,128]{1,0:T(1,128)} %bitcast.42, ...), custom_call_target="tpu_custom_call" | custom-call | flops 5368709120 | bytes 8388608 | tf_op jit(solution)/shard_map/attend/pallas_call | solution.py:399
  68.1 2.2 %collective-permute-start.6 = (bf16[4,256,256]{2,1,0:T(8,128)(2,1)}, bf16[4,256,256]{2,1,0:T(8,128)(2,1)S(1)}, u32[]{:S(2)}, u32[]{:S(2)}) collective-permute-start(bf16[4,256,256]{2,1,0:T(8,128)(2,1)} %get-tuple-element.55), channel_id=1, source_target_pairs={{0,4},{8,12},{12,8},{16,20},{20,16},{24,28},{28,24},{1,5},{9,13},{... | collective-permute-start | bytes 1572872 | tf_op jit(solution)/shard_map/ppermute | solution.py:299
  70.3 6.1 %query_back.1 = (bf16[256,2048]{1,0:T(8,128)(2,1)}, f32[32,2,128]{2,1,0:T(2,128)}) custom-call(s32[4]{0:T(128)} %broadcast_add_fusion.refs_0_, f32[32,128]{1,0:T(8,128)} %constant.64.clone.refs_1_.refs_2_, f32[32,128]{1,0:T(8,128)} %constant.65.clone.refs_2_.refs_3_, f32[64,128]{1,0:T(8,128)} %constant.66.clone.refs_3_.refs_4_, ...), custom_call_target="tpu_custom_call" | custom-call | tf_op jit(solution)/shard_map/query_back/pallas_call | solution.py:452
  76.4 22.3 %all-to-all-start = ((f32[32,2,128]{2,1,0:T(2,128)}), f32[32,2,128]{2,1,0:T(2,128)S(1)}, u32[]{:S(2)}, u32[]{:S(2)}) async-start(f32[32,2,128]{2,1,0:T(2,128)} %get-tuple-element.65), calls=%async_computation | async-start | bytes 65536 | tf_op jit(solution)/shard_map/all_to_all | solution.py:461
  98.7 2.2 %collective-permute-start.10 = (bf16[256,256]{1,0:T(8,128)(2,1)S(1)}, bf16[256,256]{1,0:T(8,128)(2,1)S(1)}, u32[]{:S(2)}, u32[]{:S(2)}) collective-permute-start(bf16[256,256]{1,0:T(8,128)(2,1)S(1)} %copy-done.25), channel_id=1, source_target_pairs={{0,4},{12,8},{20,16},{28,24},{1,5},{13,9},{21,17},{29,25},{2,6},{1... | collective-permute-start | bytes 393224 | tf_op jit(solution)/shard_map/ppermute | solution.py:299
  100.9 0.0 collective-permute-done.11
  101.0 0.0 copy-start.3
  101.0 0.0 copy-start.4
  101.0 0.1 fusion
  101.1 1.4 %collective-permute-start.14 = (bf16[256,256]{1,0:T(8,128)(2,1)S(1)}, bf16[256,256]{1,0:T(8,128)(2,1)S(1)}, u32[]{:S(2)}, u32[]{:S(2)}) collective-permute-start(bf16[256,256]{1,0:T(8,128)(2,1)S(1)} %get-tuple-element.72), channel_id=1, source_target_pairs={{0,8},{4,12},{28,4},{1,9},{5,13},{29,5},{2,10},{6,14},{30,6},{3,11... | collective-permute-start | bytes 393224 | tf_op jit(solution)/shard_map/ppermute | solution.py:299
  102.5 1.3 collective-permute-start.13
  103.8 4.6 %collective-permute-start.12 = (bf16[256,256]{1,0:T(8,128)(2,1)S(1)}, bf16[256,256]{1,0:T(8,128)(2,1)S(1)}, u32[]{:S(2)}, u32[]{:S(2)}) collective-permute-start(bf16[256,256]{1,0:T(8,128)(2,1)S(1)} %get-tuple-element.74), channel_id=1, source_target_pairs={{0,24},{4,28},{12,4},{16,8},{20,12},{24,16},{28,20},{1,25},{5,29},... | collective-permute-start | bytes 393224 | tf_op jit(solution)/shard_map/ppermute | solution.py:299
  108.5 0.1 fusion.3
  108.6 1.3 collective-permute-start.9
  109.9 1.3 collective-permute-start.8
  111.2 4.6 %collective-permute-start.7 = (bf16[256,256]{1,0:T(8,128)(2,1)S(1)}, bf16[256,256]{1,0:T(8,128)(2,1)S(1)}, u32[]{:S(2)}, u32[]{:S(2)}) collective-permute-start(bf16[256,256]{1,0:T(8,128)(2,1)S(1)} %get-tuple-element.71), channel_id=1, source_target_pairs={{0,24},{4,28},{12,4},{16,8},{20,12},{24,16},{28,20},{1,25},{5,29},... | collective-permute-start | bytes 393224 | tf_op jit(solution)/shard_map/ppermute | solution.py:299
  115.9 0.7 slice_bitcast_fusion.6.refs_8_
  116.6 6.1 %collective-permute-done.12.refs_14_ = bf16[256,256]{1,0:T(8,128)(2,1)S(1)} collective-permute-done((bf16[256,256]{1,0:T(8,128)(2,1)S(1)}, bf16[256,256]{1,0:T(8,128)(2,1)S(1)}, u32[]{:S(2)}, u32[]{:S(2)}) %collective-permute-start.12) | collective-permute-done | bytes 131104 | tf_op jit(solution)/shard_map/ppermute | solution.py:299
  122.7 5.6 %collective-permute-done.7.refs_9_ = bf16[256,256]{1,0:T(8,128)(2,1)S(1)} collective-permute-done((bf16[256,256]{1,0:T(8,128)(2,1)S(1)}, bf16[256,256]{1,0:T(8,128)(2,1)S(1)}, u32[]{:S(2)}, u32[]{:S(2)}) %collective-permute-start.7) | collective-permute-done | bytes 131104 | tf_op jit(solution)/shard_map/ppermute | solution.py:299
  128.3 0.6 copy-done.17
  129.0 2.5 %key_back.1 = (bf16[256,256]{1,0:T(8,128)(2,1)}, bf16[256,256]{1,0:T(8,128)(2,1)}, f32[2,128]{1,0:T(2,128)}) custom-call(s32[4]{0:T(128)} %broadcast_add_fusion.refs_0_, f32[32,128]{1,0:T(8,128)} %constant.64.clone.refs_1_.refs_2_, f32[32,128]{1,0:T(8,128)} %constant.65.clone.refs_2_.refs_3_, f32[64,128]{1,0:T(8,128)} %constant.66.clone.refs_3_.refs_4_, ...), custom_call_target="tpu_custom_call" | custom-call | tf_op jit(solution)/shard_map/key_back/pallas_call | solution.py:463
  131.5 0.6 copy-done.20
  132.2 0.5 slice_bitcast_fusion.7
  (51 shorter events, 0.1 us)
Async XLA Ops:
  0.6 1.0 copy-start.10
  1.6 42.3 %copy-start.18 = (bf16[256,512]{1,0:T(8,128)(2,1)}, bf16[256,512]{1,0:T(8,128)(2,1)S(1)}, u32[]{:S(2)}) copy-start(bf16[256,512]{1,0:T(8,128)(2,1)S(1)} %constant_dynamic-update-slice_fusion.refs_6_) | copy-start | bytes 786436
  1.6 11.7 %collective-permute-start.2 = (bf16[256,512]{1,0:T(8,128)(2,1)S(1)}, bf16[256,512]{1,0:T(8,128)(2,1)S(1)}, u32[]{:S(2)}, u32[]{:S(2)}) collective-permute-start(bf16[256,512]{1,0:T(8,128)(2,1)S(1)} %constant_dynamic-update-slice_fusion.refs_6_), channel_id=1, source_target_pairs={{4,28},{8,0},{12,4},{5,29},{9,1},{13,5},{6,30},{10,2},{14,6},{7,31... | collective-permute-start | bytes 786440 | tf_op jit(solution)/shard_map/ppermute | solution.py:299
  3.7 20.3 %collective-permute-start.1 = (bf16[256,512]{1,0:T(8,128)(2,1)S(1)}, bf16[256,512]{1,0:T(8,128)(2,1)S(1)}, u32[]{:S(2)}, u32[]{:S(2)}) collective-permute-start(bf16[256,512]{1,0:T(8,128)(2,1)S(1)} %constant_dynamic-update-slice_fusion.refs_6_), channel_id=1, source_target_pairs={{4,20},{8,24},{12,28},{16,0},{20,4},{5,21},{9,25},{13,29},{17,1},{... | collective-permute-start | bytes 786440 | tf_op jit(solution)/shard_map/ppermute | solution.py:299
  7.2 22.4 %collective-permute-start = (bf16[256,512]{1,0:T(8,128)(2,1)S(1)}, bf16[256,512]{1,0:T(8,128)(2,1)S(1)}, u32[]{:S(2)}, u32[]{:S(2)}) collective-permute-start(bf16[256,512]{1,0:T(8,128)(2,1)S(1)} %constant_dynamic-update-slice_fusion.refs_6_), channel_id=1, source_target_pairs={{4,12},{8,16},{12,20},{16,24},{20,28},{24,0},{28,4},{5,13},{9,17},... | collective-permute-start | bytes 786440 | tf_op jit(solution)/shard_map/ppermute | solution.py:299
  12.1 33.2 %collective-permute-start.3 = (bf16[256,512]{1,0:T(8,128)(2,1)S(1)}, bf16[256,512]{1,0:T(8,128)(2,1)S(1)}, u32[]{:S(2)}, u32[]{:S(2)}) collective-permute-start(bf16[256,512]{1,0:T(8,128)(2,1)S(1)} %constant_dynamic-update-slice_fusion.refs_6_), channel_id=1, source_target_pairs={{4,0},{8,12},{16,20},{24,28},{5,1},{9,13},{17,21},{25,29},{6,2},{1... | collective-permute-start | bytes 786440 | tf_op jit(solution)/shard_map/ppermute | solution.py:299
  13.4 16.3 %copy-start = (bf16[256,512]{1,0:T(8,128)(2,1)}, bf16[256,512]{1,0:T(8,128)(2,1)S(1)}, u32[]{:S(2)}) copy-start(bf16[256,512]{1,0:T(8,128)(2,1)S(1)} %collective-permute-done.2.refs_2_.refs_9_) | copy-start | bytes 786436
  24.0 5.6 %copy-start.1 = (bf16[256,512]{1,0:T(8,128)(2,1)}, bf16[256,512]{1,0:T(8,128)(2,1)S(1)}, u32[]{:S(2)}) copy-start(bf16[256,512]{1,0:T(8,128)(2,1)S(1)} %collective-permute-done.1.refs_1_.refs_8_) | copy-start | bytes 786436
  29.6 0.7 copy-start.2
  30.3 3.5 %copy-start.19 = (s32[4,32]{1,0:T(4,128)S(1)}, s32[4,32]{1,0:T(4,128)}, u32[]{:S(2)}) copy-start(s32[4,32]{1,0:T(4,128)} %param.19) | copy-start | bytes 1540
  32.5 12.7 %collective-permute-start.5 = (bf16[3,256,256]{2,1,0:T(8,128)(2,1)}, bf16[3,256,256]{2,1,0:T(8,128)(2,1)S(1)}, u32[]{:S(2)}, u32[]{:S(2)}) collective-permute-start(bf16[3,256,256]{2,1,0:T(8,128)(2,1)} %get-tuple-element.44), channel_id=1, source_target_pairs={{4,0},{12,8},{16,20},{20,16},{24,28},{28,24},{5,1},{13,9},{17,21},... | collective-permute-start | bytes 1179656 | tf_op jit(solution)/shard_map/ppermute | solution.py:299
  37.1 6.8 %copy-start.21 = (bf16[3,256,256]{2,1,0:T(8,128)(2,1)S(1)}, bf16[3,256,256]{2,1,0:T(8,128)(2,1)}, u32[]{:S(2)}) copy-start(bf16[3,256,256]{2,1,0:T(8,128)(2,1)} %get-tuple-element.37) | copy-start | bytes 1179652
  43.9 13.5 %collective-permute-start.4 = (bf16[3,256,256]{2,1,0:T(8,128)(2,1)S(1)}, bf16[3,256,256]{2,1,0:T(8,128)(2,1)S(1)}, u32[]{:S(2)}, u32[]{:S(2)}) collective-permute-start(bf16[3,256,256]{2,1,0:T(8,128)(2,1)S(1)} %copy-done.21), channel_id=1, source_target_pairs={{4,0},{12,8},{16,20},{20,16},{24,28},{28,24},{5,1},{13,9},{17,21},... | collective-permute-start | bytes 1179656 | tf_op jit(solution)/shard_map/ppermute | solution.py:299
  45.2 0.7 copy-start.24
  45.2 0.8 copy-start.22
  56.1 44.9 %collective-permute-start.11 = (bf16[3,256,256]{2,1,0:T(8,128)(2,1)}, bf16[3,256,256]{2,1,0:T(8,128)(2,1)S(1)}, u32[]{:S(2)}, u32[]{:S(2)}) collective-permute-start(bf16[3,256,256]{2,1,0:T(8,128)(2,1)} %get-tuple-element.62), channel_id=1, source_target_pairs={{0,4},{8,12},{16,20},{20,16},{24,28},{28,24},{1,5},{9,13},{17,21},... | collective-permute-start | bytes 1179656 | tf_op jit(solution)/shard_map/ppermute | solution.py:299
  57.4 0.8 copy-start.23
  68.1 40.4 %collective-permute-start.6 = (bf16[4,256,256]{2,1,0:T(8,128)(2,1)}, bf16[4,256,256]{2,1,0:T(8,128)(2,1)S(1)}, u32[]{:S(2)}, u32[]{:S(2)}) collective-permute-start(bf16[4,256,256]{2,1,0:T(8,128)(2,1)} %get-tuple-element.55), channel_id=1, source_target_pairs={{0,4},{8,12},{12,8},{16,20},{20,16},{24,28},{28,24},{1,5},{9,13},{... | collective-permute-start | bytes 1572872 | tf_op jit(solution)/shard_map/ppermute | solution.py:299
  70.3 28.5 %copy-start.25 = (bf16[256,256]{1,0:T(8,128)(2,1)S(1)}, bf16[256,256]{1,0:T(8,128)(2,1)}, u32[]{:S(2)}) copy-start(bf16[256,256]{1,0:T(8,128)(2,1)} %get-tuple-element.60) | copy-start | bytes 393220
  70.3 30.7 %copy-start.6 = (bf16[256,256]{1,0:T(8,128)(2,1)S(1)}, bf16[256,256]{1,0:T(8,128)(2,1)}, u32[]{:S(2)}) copy-start(bf16[256,256]{1,0:T(8,128)(2,1)} %get-tuple-element.61) | copy-start | bytes 393220
  70.3 30.7 %copy-start.7 = (bf16[256,256]{1,0:T(8,128)(2,1)S(1)}, bf16[256,256]{1,0:T(8,128)(2,1)}, u32[]{:S(2)}) copy-start(bf16[256,256]{1,0:T(8,128)(2,1)} %get-tuple-element.63) | copy-start | bytes 393220
  70.3 30.7 %copy-start.8 = (bf16[256,256]{1,0:T(8,128)(2,1)S(1)}, bf16[256,256]{1,0:T(8,128)(2,1)}, u32[]{:S(2)}) copy-start(bf16[256,256]{1,0:T(8,128)(2,1)} %get-tuple-element.64) | copy-start | bytes 393220
  76.4 40.2 %all-to-all-start = ((f32[32,2,128]{2,1,0:T(2,128)}), f32[32,2,128]{2,1,0:T(2,128)S(1)}, u32[]{:S(2)}, u32[]{:S(2)}) async-start(f32[32,2,128]{2,1,0:T(2,128)} %get-tuple-element.65), calls=%async_computation | async-start | bytes 65536 | tf_op jit(solution)/shard_map/all_to_all | solution.py:461
  98.7 11.2 %collective-permute-start.10 = (bf16[256,256]{1,0:T(8,128)(2,1)S(1)}, bf16[256,256]{1,0:T(8,128)(2,1)S(1)}, u32[]{:S(2)}, u32[]{:S(2)}) collective-permute-start(bf16[256,256]{1,0:T(8,128)(2,1)S(1)} %copy-done.25), channel_id=1, source_target_pairs={{0,4},{12,8},{20,16},{28,24},{1,5},{13,9},{21,17},{29,25},{2,6},{1... | collective-permute-start | bytes 393224 | tf_op jit(solution)/shard_map/ppermute | solution.py:299
  101.0 7.5 %copy-start.3 = (bf16[256,256]{1,0:T(8,128)(2,1)S(1)}, bf16[256,256]{1,0:T(8,128)(2,1)}, u32[]{:S(2)}) copy-start(bf16[256,256]{1,0:T(8,128)(2,1)} %get-tuple-element.56) | copy-start | bytes 393220
  101.0 7.5 %copy-start.4 = (bf16[256,256]{1,0:T(8,128)(2,1)S(1)}, bf16[256,256]{1,0:T(8,128)(2,1)}, u32[]{:S(2)}) copy-start(bf16[256,256]{1,0:T(8,128)(2,1)} %get-tuple-element.57) | copy-start | bytes 393220
  101.0 7.5 %copy-start.5 = (bf16[256,256]{1,0:T(8,128)(2,1)S(1)}, bf16[256,256]{1,0:T(8,128)(2,1)}, u32[]{:S(2)}) copy-start(bf16[256,256]{1,0:T(8,128)(2,1)} %get-tuple-element.58) | copy-start | bytes 393220
  101.1 10.1 %collective-permute-start.14 = (bf16[256,256]{1,0:T(8,128)(2,1)S(1)}, bf16[256,256]{1,0:T(8,128)(2,1)S(1)}, u32[]{:S(2)}, u32[]{:S(2)}) collective-permute-start(bf16[256,256]{1,0:T(8,128)(2,1)S(1)} %get-tuple-element.72), channel_id=1, source_target_pairs={{0,8},{4,12},{28,4},{1,9},{5,13},{29,5},{2,10},{6,14},{30,6},{3,11... | collective-permute-start | bytes 393224 | tf_op jit(solution)/shard_map/ppermute | solution.py:299
  102.5 14.0 %collective-permute-start.13 = (bf16[256,256]{1,0:T(8,128)(2,1)S(1)}, bf16[256,256]{1,0:T(8,128)(2,1)S(1)}, u32[]{:S(2)}, u32[]{:S(2)}) collective-permute-start(bf16[256,256]{1,0:T(8,128)(2,1)S(1)} %get-tuple-element.73), channel_id=1, source_target_pairs={{0,16},{4,20},{20,4},{24,8},{28,12},{1,17},{5,21},{21,5},{25,9},{2... | collective-permute-start | bytes 393224 | tf_op jit(solution)/shard_map/ppermute | solution.py:299
  103.8 18.9 %collective-permute-start.12 = (bf16[256,256]{1,0:T(8,128)(2,1)S(1)}, bf16[256,256]{1,0:T(8,128)(2,1)S(1)}, u32[]{:S(2)}, u32[]{:S(2)}) collective-permute-start(bf16[256,256]{1,0:T(8,128)(2,1)S(1)} %get-tuple-element.74), channel_id=1, source_target_pairs={{0,24},{4,28},{12,4},{16,8},{20,12},{24,16},{28,20},{1,25},{5,29},... | collective-permute-start | bytes 393224 | tf_op jit(solution)/shard_map/ppermute | solution.py:299
  108.6 14.1 %collective-permute-start.9 = (bf16[256,256]{1,0:T(8,128)(2,1)S(1)}, bf16[256,256]{1,0:T(8,128)(2,1)S(1)}, u32[]{:S(2)}, u32[]{:S(2)}) collective-permute-start(bf16[256,256]{1,0:T(8,128)(2,1)S(1)} %get-tuple-element.69), channel_id=1, source_target_pairs={{0,8},{4,12},{28,4},{1,9},{5,13},{29,5},{2,10},{6,14},{30,6},{3,11... | collective-permute-start | bytes 393224 | tf_op jit(solution)/shard_map/ppermute | solution.py:299
  109.9 6.6 %copy-start.11 = (bf16[256,256]{1,0:T(8,128)(2,1)}, bf16[256,256]{1,0:T(8,128)(2,1)S(1)}, u32[]{:S(2)}) copy-start(bf16[256,256]{1,0:T(8,128)(2,1)S(1)} %collective-permute-done.10.refs_13_) | copy-start | bytes 393220
  109.9 12.8 %collective-permute-start.8 = (bf16[256,256]{1,0:T(8,128)(2,1)S(1)}, bf16[256,256]{1,0:T(8,128)(2,1)S(1)}, u32[]{:S(2)}, u32[]{:S(2)}) collective-permute-start(bf16[256,256]{1,0:T(8,128)(2,1)S(1)} %get-tuple-element.70), channel_id=1, source_target_pairs={{0,16},{4,20},{20,4},{24,8},{28,12},{1,17},{5,21},{21,5},{25,9},{2... | collective-permute-start | bytes 393224 | tf_op jit(solution)/shard_map/ppermute | solution.py:299
  111.2 5.3 %copy-start.12 = (bf16[256,256]{1,0:T(8,128)(2,1)}, bf16[256,256]{1,0:T(8,128)(2,1)S(1)}, u32[]{:S(2)}) copy-start(bf16[256,256]{1,0:T(8,128)(2,1)S(1)} %collective-permute-done.14.refs_16_) | copy-start | bytes 393220
  111.2 17.1 %collective-permute-start.7 = (bf16[256,256]{1,0:T(8,128)(2,1)S(1)}, bf16[256,256]{1,0:T(8,128)(2,1)S(1)}, u32[]{:S(2)}, u32[]{:S(2)}) collective-permute-start(bf16[256,256]{1,0:T(8,128)(2,1)S(1)} %get-tuple-element.71), channel_id=1, source_target_pairs={{0,24},{4,28},{12,4},{16,8},{20,12},{24,16},{28,20},{1,25},{5,29},... | collective-permute-start | bytes 393224 | tf_op jit(solution)/shard_map/ppermute | solution.py:299
  116.6 11.7 %copy-start.9 = (f32[32,2,128]{2,1,0:T(2,128)}, f32[32,2,128]{2,1,0:T(2,128)S(1)}, u32[]{:S(2)}) copy-start(f32[32,2,128]{2,1,0:T(2,128)S(1)} %all-to-all-done.refs_17_) | copy-start | bytes 98308
  116.6 11.7 %copy-start.13 = (bf16[256,256]{1,0:T(8,128)(2,1)}, bf16[256,256]{1,0:T(8,128)(2,1)S(1)}, u32[]{:S(2)}) copy-start(bf16[256,256]{1,0:T(8,128)(2,1)S(1)} %collective-permute-done.13.refs_15_) | copy-start | bytes 393220
  122.7 5.6 %copy-start.14 = (bf16[256,256]{1,0:T(8,128)(2,1)}, bf16[256,256]{1,0:T(8,128)(2,1)S(1)}, u32[]{:S(2)}) copy-start(bf16[256,256]{1,0:T(8,128)(2,1)S(1)} %collective-permute-done.12.refs_14_) | copy-start | bytes 393220
  122.7 5.6 %copy-start.15 = (bf16[256,256]{1,0:T(8,128)(2,1)}, bf16[256,256]{1,0:T(8,128)(2,1)S(1)}, u32[]{:S(2)}) copy-start(bf16[256,256]{1,0:T(8,128)(2,1)S(1)} %collective-permute-done.9.refs_11_) | copy-start | bytes 393220
  122.7 5.6 %copy-start.16 = (bf16[256,256]{1,0:T(8,128)(2,1)}, bf16[256,256]{1,0:T(8,128)(2,1)S(1)}, u32[]{:S(2)}) copy-start(bf16[256,256]{1,0:T(8,128)(2,1)S(1)} %collective-permute-done.8.refs_10_) | copy-start | bytes 393220
  128.3 0.7 copy-start.17
  131.5 0.6 copy-start.20

commit v9 on v8

--- a/solution.py
+++ b/solution.py
@@ -111,27 +111,25 @@
         delta_ref[:, here] = jnp.sum(product, 0, keepdims=True)
 
 
-def main_kernel(blocks, block_len, tree_dev, inv_root, head, last, *refs):
+def main_kernel(blocks, block_len, tree_dev, inv_root, n_in, last, *refs):
     plan_ref, gain_ref = refs[:2]
     tables = refs[2:6]
     half = tree_dev // 2
-    pieces, crossed_ref = refs[6:7 + half], refs[7 + half]
-    q_t_ref, q_ref, grad_t_ref, grad_ref, delta_ref = refs[8 + half:13 + half]
-    dq_ref, gain_part_ref = refs[13 + half:15 + half]
-    parts = refs[15 + half:15 + 2 * half + last]
+    pieces, crossed_ref = refs[6:5 + n_in], refs[5 + n_in]
+    q_t_ref, q_ref, grad_t_ref, grad_ref, delta_ref = refs[6 + n_in:11 + n_in]
+    dq_ref, gain_part_ref = refs[11 + n_in:13 + n_in]
+    parts = refs[13 + n_in:13 + n_in + half + last]
     crossed_part, raw, keys, keys_t, vals, shown, with_cos, with_sin, expo, mass, w_all, ds_all, found, spread = refs[
-        15 + 2 * half + last:]
+        13 + n_in + half + last:]
     head_dim = gain_ref.shape[1]
     tokens = raw.shape[1]
     group = q_ref.shape[0] // tokens
     count = plan_ref[4, 0]
     chunks = (count + blocks - 1) // blocks
     gain = gain_ref[...]
-    kv_heads = pieces[0].shape[1] // (2 * head_dim)
-    for piece in range(half + 1):
-        raw[piece, :, 0:head_dim] = pieces[piece][:, head * head_dim:(head + 1) * head_dim]
-        raw[piece, :, head_dim:] = pieces[piece][:, (kv_heads + head) * head_dim:(kv_heads + head + 1) * head_dim]
-    raw[half + 1:] = crossed_ref[...]
+    for i, piece in enumerate(pieces):
+        raw[i] = piece[...]
+    raw[len(pieces):] = crossed_ref[...]
     query_block = lax.broadcasted_iota(jnp.int32, (1, tokens), 1) // block_len
 
     def rows_of(start):
@@ -228,13 +226,12 @@
 
 
 def join_kernel(*refs):
-    head_dim = refs[-1].shape[2] // 2
-    heads = refs[0].shape[1] // (2 * head_dim)
-    pieces, outs = refs[:-heads], refs[-heads:]
-    for head in range(heads):
-        for i, piece in enumerate(pieces):
-            outs[head][i, :, 0:head_dim] = piece[:, head * head_dim:(head + 1) * head_dim]
-            outs[head][i, :, head_dim:] = piece[:, (heads + head) * head_dim:(heads + head + 1) * head_dim]
+    arrays, joined, sems = refs[:-2], refs[-2], refs[-1]
+    copies = [pltpu.make_async_copy(ref, joined.at[i], sems.at[i]) for i, ref in enumerate(arrays)]
+    for copy in copies:
+        copy.start()
+    for copy in copies:
+        copy.wait()
 
 
 def query_kernel(blocks, inv_root, kv_heads, depth_ref, t0, t1, t2, t3, gain_ref, q_ref, *refs):
@@ -301,14 +298,12 @@
     def after(self, *pair):
         return self.order(pair[1] % self.size) > self.order(pair[0] % self.size)
 
-    def gather(self, own):
-        size, after = self.size, self.after
-        cross = self.send(own, lambda i: i ^ 1, lambda i: after(i, i ^ 1))
-        straight = []
-        for step in range(2, size, 2):
-            there = lambda i: (i + step) % size
-            straight.append(self.send(own, there, lambda i: after(i, there(i)) or after(i, there(i) ^ 1)))
-        return own, cross, straight
+    def along(self, own):
+        pieces = []
+        for step in range(2, self.size, 2):
+            there = lambda i: (i + step) % self.size
+            pieces.append(self.send(own, there, lambda i: self.after(i, there(i)) or self.after(i, there(i) ^ 1)))
+        return pieces
 
     def across(self, value, steps, back=False):
         if back:
@@ -349,7 +344,11 @@
     q_gain_row, k_gain_row = q_gain.reshape(1, head_dim), k_gain.reshape(1, head_dim)
 
     steps = range(2, tree_dev, 2)
-    own, cross, straight = tree.gather(jnp.concatenate([k_raw, values], 1))
+    own = []
+    for h in range(kv_heads):
+        cols = slice(h * head_dim, (h + 1) * head_dim)
+        own.append(jnp.concatenate([k_raw[:, cols], values[:, cols]], 1))
+
     params = pltpu.CompilerParams(vmem_limit_bytes=VMEM_LIMIT)
     smem = pl.BlockSpec(memory_space=pltpu.SMEM)
     vmem = pl.BlockSpec(memory_space=pltpu.VMEM)
@@ -363,15 +362,27 @@
         name="plan",
     )(place, in_tree)
 
-    joined = pl.pallas_call(
-        join_kernel,
-        out_shape=tuple([sds((len(steps), tokens, 2 * head_dim), BF16)] * kv_heads),
-        in_specs=[vmem] * len(steps),
-        out_specs=tuple([vmem] * kv_heads),
-        compiler_params=params,
-        name="join",
-    )(*straight)
-    crossed = [tree.across(one, steps) for one in joined]
+    def join(arrays):
+        count = len(arrays)
+        return pl.pallas_call(
+            join_kernel,
+            out_shape=sds((count, tokens, 2 * head_dim), BF16),
+            in_specs=[pl.BlockSpec(memory_space=pl.ANY)] * count,
+            out_specs=pl.BlockSpec(memory_space=pl.ANY),
+            scratch_shapes=[pltpu.SemaphoreType.DMA((count,))],
+            name="join",
+        )(*arrays)
+
+    pieces = []
+    for h in range(kv_heads):
+        straight = tree.along(own[h])
+        if h == 0:
+            cross = [tree.across(own[h], [0])]
+            crossed = tree.across(join(straight), steps)
+        else:
+            cross = []
+            crossed = tree.across(join([own[h], *straight]), [0, *steps])
+        pieces.append([own[h], *straight, *cross, crossed])
 
     rows = group * tokens
     queries = pl.pallas_call(
@@ -397,14 +408,14 @@
     def attend(h):
         last = h == kv_heads - 1
         return pl.pallas_call(
-            lambda *refs: main_kernel(blocks, block_len, tree_dev, inv_root, h, last, *refs),
+            lambda *refs: main_kernel(blocks, block_len, tree_dev, inv_root, len(pieces[h]), last, *refs),
             out_shape=(
                 sds((head_dim, rows), F32),
                 sds((8, head_dim), F32),
                 *[sds((tokens, 2 * head_dim), BF16)] * (half + last),
                 sds((half - last, tokens, 2 * head_dim), BF16),
             ),
-            in_specs=[smem] + [vmem] * (12 + half),
+            in_specs=[smem] + [vmem] * (10 + len(pieces[h])),
             out_specs=tuple([vmem] * (3 + half + last)),
             scratch_shapes=[
                 pltpu.VMEM((tree_dev, tokens, 2 * head_dim), BF16),
@@ -428,25 +439,14 @@
                 transcendentals=group * tokens * tree_dev * tokens,
             ),
             name="attend",
-        )(plan, k_gain_row, *tables, own, *straight, cross, crossed[h], *queries[5 * h:5 * h + 5])
-
-    dq, terms, counts, k_gain_parts = [], [], [], []
+        )(plan, k_gain_row, *tables, *pieces[h], *queries[5 * h:5 * h + 5])
+
+    dq, attended, k_gain_parts = [], [], []
     for h in range(kv_heads):
         dq_here, k_gain_part, *parts, crossed_part = attend(h)
         dq.append(dq_here)
         k_gain_parts.append(k_gain_part)
-        if len(parts) > half:
-            others = tree.across(crossed_part, steps, back=True)
-            mine = [parts[0], tree.across(parts[half], [0], back=True)]
-        else:
-            others = tree.across(crossed_part, [0, *steps], back=True)
-            mine = [parts[0], others[0]]
-            others = others[1:]
-        for i, step in enumerate(steps):
-            both = (parts[i + 1].astype(F32) + others[i].astype(F32)).astype(BF16)
-            mine.append(tree.home(both, step))
-        terms.extend(mine)
-        counts.append(len(mine))
+        attended.append((parts, crossed_part))
 
     everyone = cycle * lax.axis_size("heads")
     dq_raw, gains = pl.pallas_call(
@@ -458,6 +458,24 @@
         name="query_back",
     )(depth, *tables, q_gain_row, q_raw, *dq, *k_gain_parts)
 
+    terms, counts = [], []
+    for parts, crossed_part in attended:
+        if len(parts) > half:
+            others = tree.across(crossed_part, steps, back=True)
+            mine = [parts[0], tree.across(parts[half], [0], back=True)]
+        else:
+            others = tree.across(crossed_part, [0, *steps], back=True)
+            mine = [parts[0], others[0]]
+            others = others[1:]
+        merged = [
+            (parts[i + 1].astype(F32) + others[i].astype(F32)).astype(BF16) for i in range(len(steps))
+        ]
+        if len(parts) > half:
+            gains, *merged = lax.optimization_barrier((gains, *merged))
+        mine.extend(tree.home(both, step) for both, step in zip(merged, steps))
+        terms.extend(mine)
+        counts.append(len(mine))
+
     gains = lax.all_to_all(gains, ("ctx", "heads"), 0, 0)
 
     dk_raw, dv, total = pl.pallas_call(

time: 132 us -> 163 us (1.23)
  the two profiles are of different devices: /device:TPU:11 before, /device:TPU:3 now
where the time goes in v9:
time: 163 us
  starting transfers between devices  79.5 us (49%)
  Pallas kernels  59 us (36%)
  waiting for transfers between devices  13.7 us (8%)
  local copies, waits for them, and re-layouts  7.74 us (5%)
    ppermute x18, starting transfers between devices, send(): return lax.ppermute(value, 'ctx', pairs)  70.4 us
    pallas_call x2, Pallas kernels, join(): pl.pallas_call(join_kernel, out_shape=sds((count, tokens, 2 * head_dim),...  30.1 us
    ppermute x18, waiting for transfers between devices, send(): return lax.ppermute(value, 'ctx', pairs)  13.7 us
    pallas_call x2, Pallas kernels, attend(): pl.pallas_call(lambda *refs: main_kernel(blocks, block_len, tree_dev, inv...  11.6 us
    all_to_all x1, starting transfers between devices, on_device(): gains = lax.all_to_all(gains, ('ctx', 'heads'), 0, 0)  9.11 us
    pallas_call x1, Pallas kernels, on_device(): pl.pallas_call(lambda *refs: prep_kernel(blocks, block_len, kv_heads, *re...  6.74 us
    pallas_call x1, Pallas kernels, on_device(): pl.pallas_call(lambda *refs: query_kernel(blocks, inv_root, kv_heads, *re...  6.06 us
    unnamed x56, local copies, waits for them, and re-layouts  5.6 us
  transfers between devices with their start and end apart: 19, of which 4 were waited for; matrix products, arithmetic and copies ran while one was open for 1% of the time, Pallas kernels for 24%

profile of v9, /device:TPU:3, one launch (start us, length us, event | category | flops | bytes accessed | tf_op | source)
XLA Modules:
  0.0 162.6 jit_solution(8716226399646215672)
XLA Ops:
  0.6 1.0 fusion.9
  1.6 3.2 %collective-permute-start.5 = (bf16[256,256]{1,0:T(8,128)(2,1)S(1)}, bf16[256,256]{1,0:T(8,128)(2,1)S(1)}, u32[]{:S(2)}, u32[]{:S(2)}) collective-permute-start(bf16[256,256]{1,0:T(8,128)(2,1)S(1)} %pad_maximum_fusion.1.refs_0_.refs_6_), channel_id=1, source_target_pairs={{4,12},{8,16},{12,20},{16,24},{20,28},{24,0},{28,4},{5,13},{9,17},... | collective-permute-start | bytes 393224 | tf_op jit(solution)/shard_map/ppermute | solution.py:296
  4.8 4.2 %collective-permute-start.6 = (bf16[256,256]{1,0:T(8,128)(2,1)S(1)}, bf16[256,256]{1,0:T(8,128)(2,1)S(1)}, u32[]{:S(2)}, u32[]{:S(2)}) collective-permute-start(bf16[256,256]{1,0:T(8,128)(2,1)S(1)} %pad_maximum_fusion.1.refs_0_.refs_6_), channel_id=1, source_target_pairs={{4,20},{8,24},{12,28},{16,0},{20,4},{5,21},{9,25},{13,29},{17,1},{... | collective-permute-start | bytes 393224 | tf_op jit(solution)/shard_map/ppermute | solution.py:296
  9.1 1.9 %collective-permute-start.7 = (bf16[256,256]{1,0:T(8,128)(2,1)S(1)}, bf16[256,256]{1,0:T(8,128)(2,1)S(1)}, u32[]{:S(2)}, u32[]{:S(2)}) collective-permute-start(bf16[256,256]{1,0:T(8,128)(2,1)S(1)} %pad_maximum_fusion.1.refs_0_.refs_6_), channel_id=1, source_target_pairs={{4,28},{8,0},{12,4},{5,29},{9,1},{13,5},{6,30},{10,2},{14,6},{7,31... | collective-permute-start | bytes 393224 | tf_op jit(solution)/shard_map/ppermute | solution.py:296
  11.0 1.8 %collective-permute-done.6.refs_2_.refs_8_ = bf16[256,256]{1,0:T(8,128)(2,1)S(1)} collective-permute-done((bf16[256,256]{1,0:T(8,128)(2,1)S(1)}, bf16[256,256]{1,0:T(8,128)(2,1)S(1)}, u32[]{:S(2)}, u32[]{:S(2)}) %collective-permute-start.6) | collective-permute-done | bytes 131104 | tf_op jit(solution)/shard_map/ppermute | solution.py:296
  12.8 2.0 %collective-permute-done.7.refs_3_.refs_9_ = bf16[256,256]{1,0:T(8,128)(2,1)S(1)} collective-permute-done((bf16[256,256]{1,0:T(8,128)(2,1)S(1)}, bf16[256,256]{1,0:T(8,128)(2,1)S(1)}, u32[]{:S(2)}, u32[]{:S(2)}) %collective-permute-start.7) | collective-permute-done | bytes 131104 | tf_op jit(solution)/shard_map/ppermute | solution.py:296
  14.8 0.7 copy-done.14
  15.5 17.0 %join.3 = bf16[4,256,256]{2,1,0:T(8,128)(2,1)} custom-call(bf16[256,256]{1,0:T(8,128)(2,1)} %copy-done, bf16[256,256]{1,0:T(8,128)(2,1)} %copy-done.12, bf16[256,256]{1,0:T(8,128)(2,1)} %copy-done.13, bf16[256,256]{1,0:T(8,128)(2,1)} %copy-done.14), custom_call_target="tpu_custom_call" | custom-call | tf_op jit(solution)/shard_map/join/pallas_call | solution.py:367
  32.5 3.8 %collective-permute-start.8 = (bf16[4,256,256]{2,1,0:T(8,128)(2,1)}, bf16[4,256,256]{2,1,0:T(8,128)(2,1)S(1)}, u32[]{:S(2)}, u32[]{:S(2)}) collective-permute-start(bf16[4,256,256]{2,1,0:T(8,128)(2,1)} %join.3), channel_id=1, source_target_pairs={{4,0},{8,12},{12,8},{16,20},{20,16},{24,28},{28,24},{5,1},{9,13},{... | collective-permute-start | bytes 1572872 | tf_op jit(solution)/shard_map/ppermute | solution.py:296
  36.4 1.9 %collective-permute-start = (bf16[256,256]{1,0:T(8,128)(2,1)S(1)}, bf16[256,256]{1,0:T(8,128)(2,1)S(1)}, u32[]{:S(2)}, u32[]{:S(2)}) collective-permute-start(bf16[256,256]{1,0:T(8,128)(2,1)S(1)} %pad_maximum_fusion.refs_6_), channel_id=1, source_target_pairs={{4,12},{8,16},{12,20},{16,24},{20,28},{24,0},{28,4},{5,13},{9,17},... | collective-permute-start | bytes 393224 | tf_op jit(solution)/shard_map/ppermute | solution.py:296
  38.3 5.6 %collective-permute-start.1 = (bf16[256,256]{1,0:T(8,128)(2,1)S(1)}, bf16[256,256]{1,0:T(8,128)(2,1)S(1)}, u32[]{:S(2)}, u32[]{:S(2)}) collective-permute-start(bf16[256,256]{1,0:T(8,128)(2,1)S(1)} %pad_maximum_fusion.refs_6_), channel_id=1, source_target_pairs={{4,20},{8,24},{12,28},{16,0},{20,4},{5,21},{9,25},{13,29},{17,1},{... | collective-permute-start | bytes 393224 | tf_op jit(solution)/shard_map/ppermute | solution.py:296
  43.9 1.9 %collective-permute-start.2 = (bf16[256,256]{1,0:T(8,128)(2,1)S(1)}, bf16[256,256]{1,0:T(8,128)(2,1)S(1)}, u32[]{:S(2)}, u32[]{:S(2)}) collective-permute-start(bf16[256,256]{1,0:T(8,128)(2,1)S(1)} %pad_maximum_fusion.refs_6_), channel_id=1, source_target_pairs={{4,28},{8,0},{12,4},{5,29},{9,1},{13,5},{6,30},{10,2},{14,6},{7,31... | collective-permute-start | bytes 393224 | tf_op jit(solution)/shard_map/ppermute | solution.py:296
  45.8 1.3 collective-permute-start.3
  47.2 0.7 copy-done.22
  47.9 0.7 fusion.8
  48.6 2.0 %plan.1.refs_0_ = s32[5,32]{1,0:T(8,128)} custom-call(s32[1]{0:T(128)} %bitcast.1.refs_0_, s32[4,32]{1,0:T(4,128)} %get-tuple-element.83.refs_1_), custom_call_target="tpu_custom_call" | custom-call | tf_op jit(solution)/shard_map/plan/pallas_call | solution.py:357
  50.6 0.5 broadcast_add_fusion.refs_0_
  51.1 6.7 %prep.1 = (bf16[128,2048]{1,0:T(8,128)(2,1)}, bf16[2048,128]{1,0:T(8,128)(2,1)}, bf16[128,2048]{1,0:T(8,128)(2,1)}, bf16[2048,128]{1,0:T(8,128)(2,1)}, f32[1,204...) custom-call(s32[4]{0:T(128)} %broadcast_add_fusion.refs_0_, ...), custom_call_target="tpu_custom_call" | custom-call | tf_op jit(solution)/shard_map/prep/pallas_call | solution.py:388
  57.9 0.6 copy-done.9
  58.5 0.0 copy-done.10
  58.5 0.6 copy-done.11
  59.2 13.0 %join.2 = bf16[3,256,256]{2,1,0:T(8,128)(2,1)} custom-call(bf16[256,256]{1,0:T(8,128)(2,1)} %copy-done.9, bf16[256,256]{1,0:T(8,128)(2,1)} %copy-done.10, bf16[256,256]{1,0:T(8,128)(2,1)} %copy-done.11), custom_call_target="tpu_custom_call" | custom-call | tf_op jit(solution)/shard_map/join/pallas_call | solution.py:367
  72.2 1.3 collective-permute-start.4
  73.6 0.8 copy-done.24
  74.4 5.8 %attend.3 = (f32[128,2048]{1,0:T(8,128)}, f32[8,128]{1,0:T(8,128)}, bf16[256,256]{1,0:T(8,128)(2,1)}, bf16[256,256]{1,0:T(8,128)(2,1)}, bf16[256,256]{1,0:T(8,12...) custom-call(s32[5,32]{1,0:T(8,128)} %plan.1.refs_0_, ...), custom_call_target="tpu_custom_call" | custom-call | flops 5368709120 | bytes 8388608 | tf_op jit(solution)/shard_map/attend/pallas_call | solution.py:410
  80.1 1.3 collective-permute-start.14
  81.5 0.6 copy-done.26
  82.1 0.1 copy-done.25
  82.2 5.8 %attend.2 = (f32[128,2048]{1,0:T(8,128)}, f32[8,128]{1,0:T(8,128)}, bf16[256,256]{1,0:T(8,128)(2,1)}, bf16[256,256]{1,0:T(8,128)(2,1)}, bf16[256,256]{1,0:T(8,12...) custom-call(s32[5,32]{1,0:T(8,128)} %plan.1.refs_0_, f32[1,128]{1,0:T(1,128)} %bitcast.42, ...), custom_call_target="tpu_custom_call" | custom-call | flops 5368709120 | bytes 8388608 | tf_op jit(solution)/shard_map/attend/pallas_call | solution.py:410
  88.0 1.3 collective-permute-start.9
  89.3 1.5 collective-permute-start.13
  90.8 6.1 %query_back.1 = (bf16[256,2048]{1,0:T(8,128)(2,1)}, f32[32,2,128]{2,1,0:T(2,128)}) custom-call(s32[4]{0:T(128)} %broadcast_add_fusion.refs_0_, f32[32,128]{1,0:T(8,128)} %constant.64.clone.refs_1_.refs_2_, f32[32,128]{1,0:T(8,128)} %constant.65.clone.refs_2_.refs_3_, f32[64,128]{1,0:T(8,128)} %constant.66.clone.refs_3_.refs_4_, ...), custom_call_target="tpu_custom_call" | custom-call | tf_op jit(solution)/shard_map/query_back/pallas_call | solution.py:452
  96.9 1.9 %collective-permute-done.14 = bf16[3,256,256]{2,1,0:T(8,128)(2,1)S(1)} collective-permute-done((bf16[3,256,256]{2,1,0:T(8,128)(2,1)}, bf16[3,256,256]{2,1,0:T(8,128)(2,1)S(1)}, u32[]{:S(2)}, u32[]{:S(2)}) %collective-permute-start.14) | collective-permute-done | bytes 393248 | tf_op jit(solution)/shard_map/ppermute | solution.py:296
  98.8 0.1 fusion
  98.9 28.5 %collective-permute-start.15 = (bf16[256,256]{1,0:T(8,128)(2,1)S(1)}, bf16[256,256]{1,0:T(8,128)(2,1)S(1)}, u32[]{:S(2)}, u32[]{:S(2)}) collective-permute-start(bf16[256,256]{1,0:T(8,128)(2,1)S(1)} %get-tuple-element.66), channel_id=1, source_target_pairs={{0,24},{4,28},{12,4},{16,8},{20,12},{24,16},{28,20},{1,25},{5,29},... | collective-permute-start | bytes 393224 | tf_op jit(solution)/shard_map/ppermute | solution.py:296
  127.5 1.9 %collective-permute-start.16 = (bf16[256,256]{1,0:T(8,128)(2,1)S(1)}, bf16[256,256]{1,0:T(8,128)(2,1)S(1)}, u32[]{:S(2)}, u32[]{:S(2)}) collective-permute-start(bf16[256,256]{1,0:T(8,128)(2,1)S(1)} %get-tuple-element.67), channel_id=1, source_target_pairs={{0,16},{4,20},{20,4},{24,8},{28,12},{1,17},{5,21},{21,5},{25,9},{2... | collective-permute-start | bytes 393224 | tf_op jit(solution)/shard_map/ppermute | solution.py:296
  129.4 1.9 %collective-permute-start.17 = (bf16[256,256]{1,0:T(8,128)(2,1)S(1)}, bf16[256,256]{1,0:T(8,128)(2,1)S(1)}, u32[]{:S(2)}, u32[]{:S(2)}) collective-permute-start(bf16[256,256]{1,0:T(8,128)(2,1)S(1)} %get-tuple-element.68), channel_id=1, source_target_pairs={{0,8},{4,12},{28,4},{1,9},{5,13},{29,5},{2,10},{6,14},{30,6},{3,11... | collective-permute-start | bytes 393224 | tf_op jit(solution)/shard_map/ppermute | solution.py:296
  131.3 9.1 %all-to-all-start = ((f32[32,2,128]{2,1,0:T(2,128)}), f32[32,2,128]{2,1,0:T(2,128)S(1)}, u32[]{:S(2)}, u32[]{:S(2)}) async-start(f32[32,2,128]{2,1,0:T(2,128)} %get-tuple-element.69), calls=%async_computation | async-start | bytes 65536 | tf_op jit(solution)/shard_map/all_to_all | solution.py:479
  140.5 0.1 fusion.3
  140.6 5.0 %collective-permute-start.10 = (bf16[256,256]{1,0:T(8,128)(2,1)S(1)}, bf16[256,256]{1,0:T(8,128)(2,1)S(1)}, u32[]{:S(2)}, u32[]{:S(2)}) collective-permute-start(bf16[256,256]{1,0:T(8,128)(2,1)S(1)} %get-tuple-element.75), channel_id=1, source_target_pairs={{0,24},{4,28},{12,4},{16,8},{20,12},{24,16},{28,20},{1,25},{5,29},... | collective-permute-start | bytes 393224 | tf_op jit(solution)/shard_map/ppermute | solution.py:296
  145.6 1.9 %collective-permute-start.11 = (bf16[256,256]{1,0:T(8,128)(2,1)S(1)}, bf16[256,256]{1,0:T(8,128)(2,1)S(1)}, u32[]{:S(2)}, u32[]{:S(2)}) collective-permute-start(bf16[256,256]{1,0:T(8,128)(2,1)S(1)} %get-tuple-element.74), channel_id=1, source_target_pairs={{0,16},{4,20},{20,4},{24,8},{28,12},{1,17},{5,21},{21,5},{25,9},{2... | collective-permute-start | bytes 393224 | tf_op jit(solution)/shard_map/ppermute | solution.py:296
  147.5 1.9 %collective-permute-start.12 = (bf16[256,256]{1,0:T(8,128)(2,1)S(1)}, bf16[256,256]{1,0:T(8,128)(2,1)S(1)}, u32[]{:S(2)}, u32[]{:S(2)}) collective-permute-start(bf16[256,256]{1,0:T(8,128)(2,1)S(1)} %get-tuple-element.73), channel_id=1, source_target_pairs={{0,8},{4,12},{28,4},{1,9},{5,13},{29,5},{2,10},{6,14},{30,6},{3,11... | collective-permute-start | bytes 393224 | tf_op jit(solution)/shard_map/ppermute | solution.py:296
  149.4 0.7 slice_bitcast_fusion.6.refs_8_
  150.2 7.9 %collective-permute-done.11.refs_10_ = bf16[256,256]{1,0:T(8,128)(2,1)S(1)} collective-permute-done((bf16[256,256]{1,0:T(8,128)(2,1)S(1)}, bf16[256,256]{1,0:T(8,128)(2,1)S(1)}, u32[]{:S(2)}, u32[]{:S(2)}) %collective-permute-start.11) | collective-permute-done | bytes 131104 | tf_op jit(solution)/shard_map/ppermute | solution.py:296
  158.2 0.6 copy-done.20
  158.8 2.5 %key_back.1 = (bf16[256,256]{1,0:T(8,128)(2,1)}, bf16[256,256]{1,0:T(8,128)(2,1)}, f32[2,128]{1,0:T(2,128)}) custom-call(s32[4]{0:T(128)} %broadcast_add_fusion.refs_0_, f32[32,128]{1,0:T(8,128)} %constant.64.clone.refs_1_.refs_2_, f32[32,128]{1,0:T(8,128)} %constant.65.clone.refs_2_.refs_3_, f32[64,128]{1,0:T(8,128)} %constant.66.clone.refs_3_.refs_4_, ...), custom_call_target="tpu_custom_call" | custom-call | tf_op jit(solution)/shard_map/key_back/pallas_call | solution.py:481
  161.4 0.7 copy-done.23
  162.0 0.5 slice_bitcast_fusion.7
  (63 shorter events, 0.2 us)
Async XLA Ops:
  1.6 13.2 %copy-start = (bf16[256,256]{1,0:T(8,128)(2,1)}, bf16[256,256]{1,0:T(8,128)(2,1)S(1)}, u32[]{:S(2)}) copy-start(bf16[256,256]{1,0:T(8,128)(2,1)S(1)} %pad_maximum_fusion.1.refs_0_.refs_6_) | copy-start | bytes 393220
  1.6 9.4 %collective-permute-start.5 = (bf16[256,256]{1,0:T(8,128)(2,1)S(1)}, bf16[256,256]{1,0:T(8,128)(2,1)S(1)}, u32[]{:S(2)}, u32[]{:S(2)}) collective-permute-start(bf16[256,256]{1,0:T(8,128)(2,1)S(1)} %pad_maximum_fusion.1.refs_0_.refs_6_), channel_id=1, source_target_pairs={{4,12},{8,16},{12,20},{16,24},{20,28},{24,0},{28,4},{5,13},{9,17},... | collective-permute-start | bytes 393224 | tf_op jit(solution)/shard_map/ppermute | solution.py:296
  4.8 8.0 %collective-permute-start.6 = (bf16[256,256]{1,0:T(8,128)(2,1)S(1)}, bf16[256,256]{1,0:T(8,128)(2,1)S(1)}, u32[]{:S(2)}, u32[]{:S(2)}) collective-permute-start(bf16[256,256]{1,0:T(8,128)(2,1)S(1)} %pad_maximum_fusion.1.refs_0_.refs_6_), channel_id=1, source_target_pairs={{4,20},{8,24},{12,28},{16,0},{20,4},{5,21},{9,25},{13,29},{17,1},{... | collective-permute-start | bytes 393224 | tf_op jit(solution)/shard_map/ppermute | solution.py:296
  9.1 5.8 %collective-permute-start.7 = (bf16[256,256]{1,0:T(8,128)(2,1)S(1)}, bf16[256,256]{1,0:T(8,128)(2,1)S(1)}, u32[]{:S(2)}, u32[]{:S(2)}) collective-permute-start(bf16[256,256]{1,0:T(8,128)(2,1)S(1)} %pad_maximum_fusion.1.refs_0_.refs_6_), channel_id=1, source_target_pairs={{4,28},{8,0},{12,4},{5,29},{9,1},{13,5},{6,30},{10,2},{14,6},{7,31... | collective-permute-start | bytes 393224 | tf_op jit(solution)/shard_map/ppermute | solution.py:296
  11.0 3.8 %copy-start.12 = (bf16[256,256]{1,0:T(8,128)(2,1)}, bf16[256,256]{1,0:T(8,128)(2,1)S(1)}, u32[]{:S(2)}) copy-start(bf16[256,256]{1,0:T(8,128)(2,1)S(1)} %collective-permute-done.5.refs_1_.refs_7_) | copy-start | bytes 393220
  12.8 2.0 %copy-start.13 = (bf16[256,256]{1,0:T(8,128)(2,1)}, bf16[256,256]{1,0:T(8,128)(2,1)S(1)}, u32[]{:S(2)}) copy-start(bf16[256,256]{1,0:T(8,128)(2,1)S(1)} %collective-permute-done.6.refs_2_.refs_8_) | copy-start | bytes 393220
  14.8 0.7 copy-start.14
  32.5 41.0 %collective-permute-start.8 = (bf16[4,256,256]{2,1,0:T(8,128)(2,1)}, bf16[4,256,256]{2,1,0:T(8,128)(2,1)S(1)}, u32[]{:S(2)}, u32[]{:S(2)}) collective-permute-start(bf16[4,256,256]{2,1,0:T(8,128)(2,1)} %join.3), channel_id=1, source_target_pairs={{4,0},{8,12},{12,8},{16,20},{20,16},{24,28},{28,24},{5,1},{9,13},{... | collective-permute-start | bytes 1572872 | tf_op jit(solution)/shard_map/ppermute | solution.py:296
  36.4 21.5 %copy-start.8 = (bf16[256,256]{1,0:T(8,128)(2,1)}, bf16[256,256]{1,0:T(8,128)(2,1)S(1)}, u32[]{:S(2)}) copy-start(bf16[256,256]{1,0:T(8,128)(2,1)S(1)} %pad_maximum_fusion.refs_6_) | copy-start | bytes 393220
  36.4 21.5 %collective-permute-start = (bf16[256,256]{1,0:T(8,128)(2,1)S(1)}, bf16[256,256]{1,0:T(8,128)(2,1)S(1)}, u32[]{:S(2)}, u32[]{:S(2)}) collective-permute-start(bf16[256,256]{1,0:T(8,128)(2,1)S(1)} %pad_maximum_fusion.refs_6_), channel_id=1, source_target_pairs={{4,12},{8,16},{12,20},{16,24},{20,28},{24,0},{28,4},{5,13},{9,17},... | collective-permute-start | bytes 393224 | tf_op jit(solution)/shard_map/ppermute | solution.py:296
  38.3 19.6 %collective-permute-start.1 = (bf16[256,256]{1,0:T(8,128)(2,1)S(1)}, bf16[256,256]{1,0:T(8,128)(2,1)S(1)}, u32[]{:S(2)}, u32[]{:S(2)}) collective-permute-start(bf16[256,256]{1,0:T(8,128)(2,1)S(1)} %pad_maximum_fusion.refs_6_), channel_id=1, source_target_pairs={{4,20},{8,24},{12,28},{16,0},{20,4},{5,21},{9,25},{13,29},{17,1},{... | collective-permute-start | bytes 393224 | tf_op jit(solution)/shard_map/ppermute | solution.py:296
  43.9 14.0 %collective-permute-start.2 = (bf16[256,256]{1,0:T(8,128)(2,1)S(1)}, bf16[256,256]{1,0:T(8,128)(2,1)S(1)}, u32[]{:S(2)}, u32[]{:S(2)}) collective-permute-start(bf16[256,256]{1,0:T(8,128)(2,1)S(1)} %pad_maximum_fusion.refs_6_), channel_id=1, source_target_pairs={{4,28},{8,0},{12,4},{5,29},{9,1},{13,5},{6,30},{10,2},{14,6},{7,31... | collective-permute-start | bytes 393224 | tf_op jit(solution)/shard_map/ppermute | solution.py:296
  45.8 35.6 %collective-permute-start.3 = (bf16[256,256]{1,0:T(8,128)(2,1)S(1)}, bf16[256,256]{1,0:T(8,128)(2,1)S(1)}, u32[]{:S(2)}, u32[]{:S(2)}) collective-permute-start(bf16[256,256]{1,0:T(8,128)(2,1)S(1)} %pad_maximum_fusion.refs_6_), channel_id=1, source_target_pairs={{4,0},{8,12},{16,20},{24,28},{5,1},{9,13},{17,21},{25,29},{6,2},{1... | collective-permute-start | bytes 393224 | tf_op jit(solution)/shard_map/ppermute | solution.py:296
  47.2 0.7 copy-start.22
  57.8 0.7 copy-start.9
  57.9 0.7 copy-start.10
  58.5 0.6 copy-start.11
  72.2 9.2 %collective-permute-start.4 = (bf16[3,256,256]{2,1,0:T(8,128)(2,1)}, bf16[3,256,256]{2,1,0:T(8,128)(2,1)S(1)}, u32[]{:S(2)}, u32[]{:S(2)}) collective-permute-start(bf16[3,256,256]{2,1,0:T(8,128)(2,1)} %join.2), channel_id=1, source_target_pairs={{4,0},{12,8},{16,20},{20,16},{24,28},{28,24},{5,1},{13,9},{17,21},... | collective-permute-start | bytes 1179656 | tf_op jit(solution)/shard_map/ppermute | solution.py:296
  73.6 0.8 copy-start.24
  80.1 18.6 %collective-permute-start.14 = (bf16[3,256,256]{2,1,0:T(8,128)(2,1)}, bf16[3,256,256]{2,1,0:T(8,128)(2,1)S(1)}, u32[]{:S(2)}, u32[]{:S(2)}) collective-permute-start(bf16[3,256,256]{2,1,0:T(8,128)(2,1)} %get-tuple-element.63), channel_id=1, source_target_pairs={{0,4},{8,12},{16,20},{20,16},{24,28},{28,24},{1,5},{9,13},{17,21},... | collective-permute-start | bytes 1179656 | tf_op jit(solution)/shard_map/ppermute | solution.py:296
  81.4 0.7 copy-start.26
  81.5 0.8 copy-start.25
  82.2 7.1 %copy-start.27 = (bf16[256,256]{1,0:T(8,128)(2,1)S(1)}, bf16[256,256]{1,0:T(8,128)(2,1)}, u32[]{:S(2)}) copy-start(bf16[256,256]{1,0:T(8,128)(2,1)} %get-tuple-element.60) | copy-start | bytes 393220
  88.0 52.4 %collective-permute-start.9 = (bf16[4,256,256]{2,1,0:T(8,128)(2,1)}, bf16[4,256,256]{2,1,0:T(8,128)(2,1)S(1)}, u32[]{:S(2)}, u32[]{:S(2)}) collective-permute-start(bf16[4,256,256]{2,1,0:T(8,128)(2,1)} %get-tuple-element.55), channel_id=1, source_target_pairs={{0,4},{8,12},{12,8},{16,20},{20,16},{24,28},{28,24},{1,5},{9,13},{... | collective-permute-start | bytes 1572872 | tf_op jit(solution)/shard_map/ppermute | solution.py:296
  89.3 56.2 %collective-permute-start.13 = (bf16[256,256]{1,0:T(8,128)(2,1)S(1)}, bf16[256,256]{1,0:T(8,128)(2,1)S(1)}, u32[]{:S(2)}, u32[]{:S(2)}) collective-permute-start(bf16[256,256]{1,0:T(8,128)(2,1)S(1)} %copy-done.27), channel_id=1, source_target_pairs={{0,4},{12,8},{20,16},{28,24},{1,5},{13,9},{21,17},{29,25},{2,6},{1... | collective-permute-start | bytes 393224 | tf_op jit(solution)/shard_map/ppermute | solution.py:296
  90.8 8.0 %copy-start.1 = (bf16[256,256]{1,0:T(8,128)(2,1)S(1)}, bf16[256,256]{1,0:T(8,128)(2,1)}, u32[]{:S(2)}) copy-start(bf16[256,256]{1,0:T(8,128)(2,1)} %get-tuple-element.62) | copy-start | bytes 393220
  90.8 8.0 %copy-start.2 = (bf16[256,256]{1,0:T(8,128)(2,1)S(1)}, bf16[256,256]{1,0:T(8,128)(2,1)}, u32[]{:S(2)}) copy-start(bf16[256,256]{1,0:T(8,128)(2,1)} %get-tuple-element.64) | copy-start | bytes 393220
  90.8 8.0 %copy-start.3 = (bf16[256,256]{1,0:T(8,128)(2,1)S(1)}, bf16[256,256]{1,0:T(8,128)(2,1)}, u32[]{:S(2)}) copy-start(bf16[256,256]{1,0:T(8,128)(2,1)} %get-tuple-element.65) | copy-start | bytes 393220
  98.8 41.7 %copy-start.4 = (bf16[256,256]{1,0:T(8,128)(2,1)S(1)}, bf16[256,256]{1,0:T(8,128)(2,1)}, u32[]{:S(2)}) copy-start(bf16[256,256]{1,0:T(8,128)(2,1)} %get-tuple-element.56) | copy-start | bytes 393220
  98.8 41.7 %copy-start.5 = (bf16[256,256]{1,0:T(8,128)(2,1)S(1)}, bf16[256,256]{1,0:T(8,128)(2,1)}, u32[]{:S(2)}) copy-start(bf16[256,256]{1,0:T(8,128)(2,1)} %get-tuple-element.57) | copy-start | bytes 393220
  98.8 41.7 %copy-start.6 = (bf16[256,256]{1,0:T(8,128)(2,1)S(1)}, bf16[256,256]{1,0:T(8,128)(2,1)}, u32[]{:S(2)}) copy-start(bf16[256,256]{1,0:T(8,128)(2,1)} %get-tuple-element.58) | copy-start | bytes 393220
  98.9 48.6 %collective-permute-start.15 = (bf16[256,256]{1,0:T(8,128)(2,1)S(1)}, bf16[256,256]{1,0:T(8,128)(2,1)S(1)}, u32[]{:S(2)}, u32[]{:S(2)}) collective-permute-start(bf16[256,256]{1,0:T(8,128)(2,1)S(1)} %get-tuple-element.66), channel_id=1, source_target_pairs={{0,24},{4,28},{12,4},{16,8},{20,12},{24,16},{28,20},{1,25},{5,29},... | collective-permute-start | bytes 393224 | tf_op jit(solution)/shard_map/ppermute | solution.py:296
  127.5 22.7 %collective-permute-start.16 = (bf16[256,256]{1,0:T(8,128)(2,1)S(1)}, bf16[256,256]{1,0:T(8,128)(2,1)S(1)}, u32[]{:S(2)}, u32[]{:S(2)}) collective-permute-start(bf16[256,256]{1,0:T(8,128)(2,1)S(1)} %get-tuple-element.67), channel_id=1, source_target_pairs={{0,16},{4,20},{20,4},{24,8},{28,12},{1,17},{5,21},{21,5},{25,9},{2... | collective-permute-start | bytes 393224 | tf_op jit(solution)/shard_map/ppermute | solution.py:296
  129.4 20.8 %collective-permute-start.17 = (bf16[256,256]{1,0:T(8,128)(2,1)S(1)}, bf16[256,256]{1,0:T(8,128)(2,1)S(1)}, u32[]{:S(2)}, u32[]{:S(2)}) collective-permute-start(bf16[256,256]{1,0:T(8,128)(2,1)S(1)} %get-tuple-element.68), channel_id=1, source_target_pairs={{0,8},{4,12},{28,4},{1,9},{5,13},{29,5},{2,10},{6,14},{30,6},{3,11... | collective-permute-start | bytes 393224 | tf_op jit(solution)/shard_map/ppermute | solution.py:296
  131.3 18.8 %all-to-all-start = ((f32[32,2,128]{2,1,0:T(2,128)}), f32[32,2,128]{2,1,0:T(2,128)S(1)}, u32[]{:S(2)}, u32[]{:S(2)}) async-start(f32[32,2,128]{2,1,0:T(2,128)} %get-tuple-element.69), calls=%async_computation | async-start | bytes 65536 | tf_op jit(solution)/shard_map/all_to_all | solution.py:479
  140.6 9.6 %collective-permute-start.10 = (bf16[256,256]{1,0:T(8,128)(2,1)S(1)}, bf16[256,256]{1,0:T(8,128)(2,1)S(1)}, u32[]{:S(2)}, u32[]{:S(2)}) collective-permute-start(bf16[256,256]{1,0:T(8,128)(2,1)S(1)} %get-tuple-element.75), channel_id=1, source_target_pairs={{0,24},{4,28},{12,4},{16,8},{20,12},{24,16},{28,20},{1,25},{5,29},... | collective-permute-start | bytes 393224 | tf_op jit(solution)/shard_map/ppermute | solution.py:296
  145.5 4.5 %copy-start.15 = (bf16[256,256]{1,0:T(8,128)(2,1)}, bf16[256,256]{1,0:T(8,128)(2,1)S(1)}, u32[]{:S(2)}) copy-start(bf16[256,256]{1,0:T(8,128)(2,1)S(1)} %collective-permute-done.13.refs_13_) | copy-start | bytes 393220
  145.6 12.6 %collective-permute-start.11 = (bf16[256,256]{1,0:T(8,128)(2,1)S(1)}, bf16[256,256]{1,0:T(8,128)(2,1)S(1)}, u32[]{:S(2)}, u32[]{:S(2)}) collective-permute-start(bf16[256,256]{1,0:T(8,128)(2,1)S(1)} %get-tuple-element.74), channel_id=1, source_target_pairs={{0,16},{4,20},{20,4},{24,8},{28,12},{1,17},{5,21},{21,5},{25,9},{2... | collective-permute-start | bytes 393224 | tf_op jit(solution)/shard_map/ppermute | solution.py:296
  147.5 2.6 %copy-start.16 = (bf16[256,256]{1,0:T(8,128)(2,1)}, bf16[256,256]{1,0:T(8,128)(2,1)S(1)}, u32[]{:S(2)}) copy-start(bf16[256,256]{1,0:T(8,128)(2,1)S(1)} %collective-permute-done.15.refs_14_) | copy-start | bytes 393220
  147.5 10.6 %collective-permute-start.12 = (bf16[256,256]{1,0:T(8,128)(2,1)S(1)}, bf16[256,256]{1,0:T(8,128)(2,1)S(1)}, u32[]{:S(2)}, u32[]{:S(2)}) collective-permute-start(bf16[256,256]{1,0:T(8,128)(2,1)S(1)} %get-tuple-element.73), channel_id=1, source_target_pairs={{0,8},{4,12},{28,4},{1,9},{5,13},{29,5},{2,10},{6,14},{30,6},{3,11... | collective-permute-start | bytes 393224 | tf_op jit(solution)/shard_map/ppermute | solution.py:296
  150.1 8.0 %copy-start.7 = (f32[32,2,128]{2,1,0:T(2,128)}, f32[32,2,128]{2,1,0:T(2,128)S(1)}, u32[]{:S(2)}) copy-start(f32[32,2,128]{2,1,0:T(2,128)S(1)} %all-to-all-done.refs_17_) | copy-start | bytes 98308
  150.1 8.0 %copy-start.17 = (bf16[256,256]{1,0:T(8,128)(2,1)}, bf16[256,256]{1,0:T(8,128)(2,1)S(1)}, u32[]{:S(2)}) copy-start(bf16[256,256]{1,0:T(8,128)(2,1)S(1)} %collective-permute-done.16.refs_15_) | copy-start | bytes 393220
  150.1 8.0 %copy-start.18 = (bf16[256,256]{1,0:T(8,128)(2,1)}, bf16[256,256]{1,0:T(8,128)(2,1)S(1)}, u32[]{:S(2)}) copy-start(bf16[256,256]{1,0:T(8,128)(2,1)S(1)} %collective-permute-done.17.refs_16_) | copy-start | bytes 393220
  150.2 8.0 %copy-start.19 = (bf16[256,256]{1,0:T(8,128)(2,1)}, bf16[256,256]{1,0:T(8,128)(2,1)S(1)}, u32[]{:S(2)}) copy-start(bf16[256,256]{1,0:T(8,128)(2,1)S(1)} %collective-permute-done.10.refs_9_) | copy-start | bytes 393220
  158.1 0.7 copy-start.20
  158.1 0.7 copy-start.21
  161.4 0.7 copy-start.23

commit v10 on v9

--- a/solution.py
+++ b/solution.py
@@ -226,12 +226,16 @@
 
 
 def join_kernel(*refs):
-    arrays, joined, sems = refs[:-2], refs[-2], refs[-1]
-    copies = [pltpu.make_async_copy(ref, joined.at[i], sems.at[i]) for i, ref in enumerate(arrays)]
-    for copy in copies:
-        copy.start()
-    for copy in copies:
-        copy.wait()
+    for i in range(refs[-1].shape[0]):
+        refs[-1][i] = refs[i][...]
+
+
+def merge_kernel(*refs):
+    count = (len(refs) - 4) // 2
+    others_ref, gains_ref = refs[count:count + 2]
+    for i in range(count):
+        refs[-1 - count + i][...] = (refs[i][...].astype(F32) + others_ref[i].astype(F32)).astype(BF16)
+    refs[-1][...] = gains_ref[...]
 
 
 def query_kernel(blocks, inv_root, kv_heads, depth_ref, t0, t1, t2, t3, gain_ref, q_ref, *refs):
@@ -353,36 +357,28 @@
     smem = pl.BlockSpec(memory_space=pltpu.SMEM)
     vmem = pl.BlockSpec(memory_space=pltpu.VMEM)
     sds = jax.ShapeDtypeStruct
+    quick = pl.CostEstimate(flops=1024, bytes_accessed=1024, transcendentals=0)
 
     plan = pl.pallas_call(
         lambda *refs: plan_kernel(blocks, tree_dev, *refs),
         out_shape=sds((5, tree_blocks), jnp.int32),
         in_specs=[smem, smem],
         out_specs=smem,
+        cost_estimate=pl.CostEstimate(flops=4 * 10**9, bytes_accessed=16 * 1024 * 1024, transcendentals=0),
         name="plan",
     )(place, in_tree)
 
-    def join(arrays):
+    def join(arrays, *after):
         count = len(arrays)
         return pl.pallas_call(
             join_kernel,
             out_shape=sds((count, tokens, 2 * head_dim), BF16),
-            in_specs=[pl.BlockSpec(memory_space=pl.ANY)] * count,
-            out_specs=pl.BlockSpec(memory_space=pl.ANY),
-            scratch_shapes=[pltpu.SemaphoreType.DMA((count,))],
+            in_specs=[vmem] * count + [pl.BlockSpec(memory_space=pl.ANY)] * len(after),
+            out_specs=vmem,
+            compiler_params=params,
+            cost_estimate=quick,
             name="join",
-        )(*arrays)
-
-    pieces = []
-    for h in range(kv_heads):
-        straight = tree.along(own[h])
-        if h == 0:
-            cross = [tree.across(own[h], [0])]
-            crossed = tree.across(join(straight), steps)
-        else:
-            cross = []
-            crossed = tree.across(join([own[h], *straight]), [0, *steps])
-        pieces.append([own[h], *straight, *cross, crossed])
+        )(*arrays, *after)
 
     rows = group * tokens
     queries = pl.pallas_call(
@@ -400,8 +396,20 @@
         in_specs=[smem] + [vmem] * 8,
         out_specs=tuple([vmem] * (5 * kv_heads)),
         compiler_params=params,
+        cost_estimate=quick,
         name="prep",
     )(depth, *tables, q_gain_row, q_raw, out_grad, saved_out)
+
+    pieces = []
+    for h in range(kv_heads):
+        straight = tree.along(own[h])
+        if h == 0:
+            cross = [tree.across(own[h], [0])]
+            crossed = tree.across(join(straight, queries[4], queries[-1]), steps)
+        else:
+            cross = []
+            crossed = tree.across(join([own[h], *straight]), [0, *steps])
+        pieces.append([own[h], *straight, *cross, crossed])
 
     half = tree_dev // 2
 
@@ -467,11 +475,19 @@
             others = tree.across(crossed_part, [0, *steps], back=True)
             mine = [parts[0], others[0]]
             others = others[1:]
-        merged = [
-            (parts[i + 1].astype(F32) + others[i].astype(F32)).astype(BF16) for i in range(len(steps))
-        ]
         if len(parts) > half:
-            gains, *merged = lax.optimization_barrier((gains, *merged))
+            *merged, gains = pl.pallas_call(
+                merge_kernel,
+                out_shape=(*[sds((tokens, 2 * head_dim), BF16)] * len(steps), sds(gains.shape, F32)),
+                in_specs=[vmem] * (len(steps) + 2) + [pl.BlockSpec(memory_space=pl.ANY)],
+                out_specs=tuple([vmem] * (len(steps) + 1)),
+                compiler_params=params,
+                name="merge",
+            )(*parts[1:half], others, gains, merged[-1])
+        else:
+            merged = [
+                (parts[i + 1].astype(F32) + others[i].astype(F32)).astype(BF16) for i in range(len(steps))
+            ]
         mine.extend(tree.home(both, step) for both, step in zip(merged, steps))
         terms.extend(mine)
         counts.append(len(mine))

time: 163 us -> 137 us (0.84)
  starting transfers between devices: 79.5 us -> 54.5 us
  Pallas kernels: 59 us -> 34.6 us
  waiting for transfers between devices: 13.7 us -> 36.2 us
    ppermute x18, starting transfers between devices: 70.4 us -> 41.6 us  [send(): return lax.ppermute(value, 'ctx', pairs)]
    pallas_call x2, Pallas kernels: 30.1 us -> 3.74 us  [join(): pl.pallas_call(join_kernel, out_shape=sds((count, tokens, 2 * head_dim),...]
    ppermute x18, waiting for transfers between devices: 13.7 us -> 36.2 us  [send(): return lax.ppermute(value, 'ctx', pairs)]
    all_to_all x1, starting transfers between devices: 9.11 us -> 12.8 us  [on_device(): gains = lax.all_to_all(gains, ('ctx', 'heads'), 0, 0)]
    pallas_call x0 -> x1, Pallas kernels: none -> 1.98 us  [on_device(): pl.pallas_call(merge_kernel, out_shape=(*[sds((tokens, 2 * head_dim), BF1...]
    unnamed x56 -> x52, local copies, waits for them, and re-layouts: 5.6 us -> 5.74 us
  transfers between devices with their start and end apart: 19 -> 19, of which waited for: 4 -> 5; matrix products, arithmetic and copies ran while one was open for 1% -> 2% of each run, Pallas kernels for 24% -> 24%
where the time goes in v10:
time: 137 us; the launch traced here: 136 us
  starting transfers between devices  54.5 us (40%)
  waiting for transfers between devices  36.2 us (26%)
  Pallas kernels  34.6 us (25%)
  local copies, waits for them, and re-layouts  7.87 us (6%)
  other arithmetic  1.99 us (1%)
    ppermute x18, starting transfers between devices, send(): return lax.ppermute(value, 'ctx', pairs)  41.6 us
    ppermute x18, waiting for transfers between devices, send(): return lax.ppermute(value, 'ctx', pairs)  36.2 us
    all_to_all x1, starting transfers between devices, on_device(): gains = lax.all_to_all(gains, ('ctx', 'heads'), 0, 0)  12.8 us
    pallas_call x2, Pallas kernels, attend(): pl.pallas_call(lambda *refs: main_kernel(blocks, block_len, tree_dev, inv...  11.6 us
    pallas_call x1, Pallas kernels, on_device(): pl.pallas_call(lambda *refs: prep_kernel(blocks, block_len, kv_heads, *re...  6.74 us
    pallas_call x1, Pallas kernels, on_device(): pl.pallas_call(lambda *refs: query_kernel(blocks, inv_root, kv_heads, *re...  6.06 us
    unnamed x52, local copies, waits for them, and re-layouts  5.74 us
    pallas_call x2, Pallas kernels, join(): pl.pallas_call(join_kernel, out_shape=sds((count, tokens, 2 * head_dim),...  3.74 us
  transfers between devices with their start and end apart: 19, of which 5 were waited for; matrix products, arithmetic and copies ran while one was open for 2% of the time, Pallas kernels for 24%

profile of v10, /device:TPU:3, one launch (start us, length us, event | category | flops | bytes accessed | tf_op | source)
XLA Modules:
  0.0 136.3 jit_solution(6602334970874879395)
XLA Ops:
  0.6 1.0 fusion.6
  1.6 3.2 %collective-permute-start = (bf16[256,256]{1,0:T(8,128)(2,1)S(1)}, bf16[256,256]{1,0:T(8,128)(2,1)S(1)}, u32[]{:S(2)}, u32[]{:S(2)}) collective-permute-start(bf16[256,256]{1,0:T(8,128)(2,1)S(1)} %pad_maximum_fusion.refs_6_), channel_id=1, source_target_pairs={{4,12},{8,16},{12,20},{16,24},{20,28},{24,0},{28,4},{5,13},{9,17},... | collective-permute-start | bytes 393224 | tf_op jit(solution)/shard_map/ppermute | solution.py:300
  4.8 4.2 %collective-permute-start.1 = (bf16[256,256]{1,0:T(8,128)(2,1)S(1)}, bf16[256,256]{1,0:T(8,128)(2,1)S(1)}, u32[]{:S(2)}, u32[]{:S(2)}) collective-permute-start(bf16[256,256]{1,0:T(8,128)(2,1)S(1)} %pad_maximum_fusion.refs_6_), channel_id=1, source_target_pairs={{4,20},{8,24},{12,28},{16,0},{20,4},{5,21},{9,25},{13,29},{17,1},{... | collective-permute-start | bytes 393224 | tf_op jit(solution)/shard_map/ppermute | solution.py:300
  9.1 1.9 %collective-permute-start.2 = (bf16[256,256]{1,0:T(8,128)(2,1)S(1)}, bf16[256,256]{1,0:T(8,128)(2,1)S(1)}, u32[]{:S(2)}, u32[]{:S(2)}) collective-permute-start(bf16[256,256]{1,0:T(8,128)(2,1)S(1)} %pad_maximum_fusion.refs_6_), channel_id=1, source_target_pairs={{4,28},{8,0},{12,4},{5,29},{9,1},{13,5},{6,30},{10,2},{14,6},{7,31... | collective-permute-start | bytes 393224 | tf_op jit(solution)/shard_map/ppermute | solution.py:300
  11.0 3.4 %collective-permute-start.5 = (bf16[256,256]{1,0:T(8,128)(2,1)S(1)}, bf16[256,256]{1,0:T(8,128)(2,1)S(1)}, u32[]{:S(2)}, u32[]{:S(2)}) collective-permute-start(bf16[256,256]{1,0:T(8,128)(2,1)S(1)} %pad_maximum_fusion.1.refs_0_.refs_6_), channel_id=1, source_target_pairs={{4,12},{8,16},{12,20},{16,24},{20,28},{24,0},{28,4},{5,13},{9,17},... | collective-permute-start | bytes 393224 | tf_op jit(solution)/shard_map/ppermute | solution.py:300
  14.4 1.9 %collective-permute-start.6 = (bf16[256,256]{1,0:T(8,128)(2,1)S(1)}, bf16[256,256]{1,0:T(8,128)(2,1)S(1)}, u32[]{:S(2)}, u32[]{:S(2)}) collective-permute-start(bf16[256,256]{1,0:T(8,128)(2,1)S(1)} %pad_maximum_fusion.1.refs_0_.refs_6_), channel_id=1, source_target_pairs={{4,20},{8,24},{12,28},{16,0},{20,4},{5,21},{9,25},{13,29},{17,1},{... | collective-permute-start | bytes 393224 | tf_op jit(solution)/shard_map/ppermute | solution.py:300
  16.4 0.7 fusion.5
  17.1 3.1 %collective-permute-start.7 = (bf16[256,256]{1,0:T(8,128)(2,1)S(1)}, bf16[256,256]{1,0:T(8,128)(2,1)S(1)}, u32[]{:S(2)}, u32[]{:S(2)}) collective-permute-start(bf16[256,256]{1,0:T(8,128)(2,1)S(1)} %pad_maximum_fusion.1.refs_0_.refs_6_), channel_id=1, source_target_pairs={{4,28},{8,0},{12,4},{5,29},{9,1},{13,5},{6,30},{10,2},{14,6},{7,31... | collective-permute-start | bytes 393224 | tf_op jit(solution)/shard_map/ppermute | solution.py:300
  20.2 0.5 broadcast_add_fusion.refs_0_
  20.7 6.7 %prep.1 = (bf16[128,2048]{1,0:T(8,128)(2,1)}, bf16[2048,128]{1,0:T(8,128)(2,1)}, bf16[128,2048]{1,0:T(8,128)(2,1)}, bf16[2048,128]{1,0:T(8,128)(2,1)}, f32[1,204...) custom-call(s32[4]{0:T(128)} %broadcast_add_fusion.refs_0_, ...), custom_call_target="tpu_custom_call" | custom-call | flops 1024 | bytes 1024 | tf_op jit(solution)/shard_map/prep/pallas_call | solution.py:384
  27.5 0.6 copy-done.4
  28.2 1.8 %join.2 = bf16[3,256,256]{2,1,0:T(8,128)(2,1)} custom-call(bf16[256,256]{1,0:T(8,128)(2,1)} %copy-done.3, bf16[256,256]{1,0:T(8,128)(2,1)} %copy-done.4, bf16[256,256]{1,0:T(8,128)(2,1)} %copy-done.5, f32[1,2048]{1,0:T(1,128)} %get-tuple-element.39.refs_3_.refs_16_, f32[1,2048]{1,0:T(1,128)} %get-tuple-element.40.refs_4_.refs_15_), custom_call_target="tpu_custom_call" | custom-call | flops 1024 | bytes 1024 | tf_op jit(solution)/shard_map/join/pallas_call | solution.py:373
  30.0 1.3 collective-permute-start.4
  31.3 1.3 collective-permute-start.3
  32.7 0.6 copy-done.11
  33.3 0.6 copy-done.13
  34.0 1.9 %join.3 = bf16[4,256,256]{2,1,0:T(8,128)(2,1)} custom-call(bf16[256,256]{1,0:T(8,128)(2,1)} %copy-done.1, bf16[256,256]{1,0:T(8,128)(2,1)} %copy-done.11, bf16[256,256]{1,0:T(8,128)(2,1)} %copy-done.12, bf16[256,256]{1,0:T(8,128)(2,1)} %copy-done.13), custom_call_target="tpu_custom_call" | custom-call | flops 1024 | bytes 1024 | tf_op jit(solution)/shard_map/join/pallas_call | solution.py:373
  35.9 1.3 collective-permute-start.8
  37.2 2.0 %plan.1.refs_0_ = s32[5,32]{1,0:T(8,128)} custom-call(s32[1]{0:T(128)} %bitcast.1.refs_0_, s32[4,32]{1,0:T(4,128)} %get-tuple-element.80.refs_1_), custom_call_target="tpu_custom_call" | custom-call | flops 4000000000 | bytes 16777216 | tf_op jit(solution)/shard_map/plan/pallas_call | solution.py:362
  39.2 1.9 %collective-permute-done.3.refs_10_ = bf16[256,256]{1,0:T(8,128)(2,1)S(1)} collective-permute-done((bf16[256,256]{1,0:T(8,128)(2,1)S(1)}, bf16[256,256]{1,0:T(8,128)(2,1)S(1)}, u32[]{:S(2)}, u32[]{:S(2)}) %collective-permute-start.3) | collective-permute-done | bytes 131104 | tf_op jit(solution)/shard_map/ppermute | solution.py:300
  41.1 0.7 copy-done.25
  41.8 0.1 copy-done.24
  41.9 5.8 %attend.2 = (f32[128,2048]{1,0:T(8,128)}, f32[8,128]{1,0:T(8,128)}, bf16[256,256]{1,0:T(8,128)(2,1)}, bf16[256,256]{1,0:T(8,128)(2,1)}, bf16[256,256]{1,0:T(8,12...) custom-call(s32[5,32]{1,0:T(8,128)} %plan.1.refs_0_, f32[1,128]{1,0:T(1,128)} %bitcast.26, ...), custom_call_target="tpu_custom_call" | custom-call | flops 5368709120 | bytes 8388608 | tf_op jit(solution)/shard_map/attend/pallas_call | solution.py:418
  47.7 1.3 collective-permute-start.9
  49.0 3.5 %collective-permute-done.8.refs_10_ = bf16[4,256,256]{2,1,0:T(8,128)(2,1)S(1)} collective-permute-done((bf16[4,256,256]{2,1,0:T(8,128)(2,1)}, bf16[4,256,256]{2,1,0:T(8,128)(2,1)S(1)}, u32[]{:S(2)}, u32[]{:S(2)}) %collective-permute-start.8) | collective-permute-done | bytes 524320 | tf_op jit(solution)/shard_map/ppermute | solution.py:300
  52.5 0.8 copy-done.23
  53.3 5.8 %attend.3 = (f32[128,2048]{1,0:T(8,128)}, f32[8,128]{1,0:T(8,128)}, bf16[256,256]{1,0:T(8,128)(2,1)}, bf16[256,256]{1,0:T(8,128)(2,1)}, bf16[256,256]{1,0:T(8,12...) custom-call(s32[5,32]{1,0:T(8,128)} %plan.1.refs_0_, ...), custom_call_target="tpu_custom_call" | custom-call | flops 5368709120 | bytes 8388608 | tf_op jit(solution)/shard_map/attend/pallas_call | solution.py:418
  59.0 1.3 collective-permute-start.14
  60.3 1.5 %collective-permute-start.13 = (bf16[256,256]{1,0:T(8,128)(2,1)}, bf16[256,256]{1,0:T(8,128)(2,1)S(1)}, u32[]{:S(2)}, u32[]{:S(2)}) collective-permute-start(bf16[256,256]{1,0:T(8,128)(2,1)} %get-tuple-element.60), channel_id=1, source_target_pairs={{0,4},{12,8},{20,16},{28,24},{1,5},{13,9},{21,17},{29,25},{2,6},{1... | collective-permute-start | bytes 393224 | tf_op jit(solution)/shard_map/ppermute | solution.py:300
  61.8 6.1 %query_back.1 = (bf16[256,2048]{1,0:T(8,128)(2,1)}, f32[32,2,128]{2,1,0:T(2,128)}) custom-call(s32[4]{0:T(128)} %broadcast_add_fusion.refs_0_, f32[32,128]{1,0:T(8,128)} %constant.64.clone.refs_1_.refs_2_, f32[32,128]{1,0:T(8,128)} %constant.65.clone.refs_2_.refs_3_, f32[64,128]{1,0:T(8,128)} %constant.66.clone.refs_3_.refs_4_, ...), custom_call_target="tpu_custom_call" | custom-call | tf_op jit(solution)/shard_map/query_back/pallas_call | solution.py:460
  67.9 5.3 %collective-permute-done.9 = bf16[4,256,256]{2,1,0:T(8,128)(2,1)S(1)} collective-permute-done((bf16[4,256,256]{2,1,0:T(8,128)(2,1)}, bf16[4,256,256]{2,1,0:T(8,128)(2,1)S(1)}, u32[]{:S(2)}, u32[]{:S(2)}) %collective-permute-start.9) | collective-permute-done | bytes 524320 | tf_op jit(solution)/shard_map/ppermute | solution.py:300
  73.2 0.7 fusion
  73.9 18.4 %collective-permute-done.14.refs_3_ = bf16[3,256,256]{2,1,0:T(8,128)(2,1)S(1)} collective-permute-done((bf16[3,256,256]{2,1,0:T(8,128)(2,1)}, bf16[3,256,256]{2,1,0:T(8,128)(2,1)S(1)}, u32[]{:S(2)}, u32[]{:S(2)}) %collective-permute-start.14) | collective-permute-done | bytes 393248 | tf_op jit(solution)/shard_map/ppermute | solution.py:300
  92.4 0.7 copy-done.2
  93.1 2.0 %merge.1 = (bf16[256,256]{1,0:T(8,128)(2,1)}, bf16[256,256]{1,0:T(8,128)(2,1)}, bf16[256,256]{1,0:T(8,128)(2,1)}, f32[32,2,128]{2,1,0:T(2,128)}) custom-call(bf16[256,256]{1,0:T(8,128)(2,1)} %get-tuple-element.61.refs_0_, bf16[256,256]{1,0:T(8,128)(2,1)} %get-tuple-element.62.refs_1_, bf16[256,256]{1,0:T(8,128)(2,1)} %get-tuple-element.63.refs_2_, ...), custom_call_target="tpu_custom_call" | custom-call | tf_op jit(solution)/shard_map/merge/pallas_call | solution.py:479
  95.1 1.9 %collective-permute-start.15 = (bf16[256,256]{1,0:T(8,128)(2,1)}, bf16[256,256]{1,0:T(8,128)(2,1)S(1)}, u32[]{:S(2)}, u32[]{:S(2)}) collective-permute-start(bf16[256,256]{1,0:T(8,128)(2,1)} %get-tuple-element.66), channel_id=1, source_target_pairs={{0,24},{4,28},{12,4},{16,8},{20,12},{24,16},{28,20},{1,25},{5,29},... | collective-permute-start | bytes 393224 | tf_op jit(solution)/shard_map/ppermute | solution.py:300
  97.0 3.4 %collective-permute-start.12 = (bf16[256,256]{1,0:T(8,128)(2,1)S(1)}, bf16[256,256]{1,0:T(8,128)(2,1)S(1)}, u32[]{:S(2)}, u32[]{:S(2)}) collective-permute-start(bf16[256,256]{1,0:T(8,128)(2,1)S(1)} %copy-done), channel_id=1, source_target_pairs={{0,8},{4,12},{28,4},{1,9},{5,13},{29,5},{2,10},{6,14},{30,6},{3,11... | collective-permute-start | bytes 393224 | tf_op jit(solution)/shard_map/ppermute | solution.py:300
  100.4 1.9 %collective-permute-start.16 = (bf16[256,256]{1,0:T(8,128)(2,1)}, bf16[256,256]{1,0:T(8,128)(2,1)S(1)}, u32[]{:S(2)}, u32[]{:S(2)}) collective-permute-start(bf16[256,256]{1,0:T(8,128)(2,1)} %get-tuple-element.67), channel_id=1, source_target_pairs={{0,16},{4,20},{20,4},{24,8},{28,12},{1,17},{5,21},{21,5},{25,9},{2... | collective-permute-start | bytes 393224 | tf_op jit(solution)/shard_map/ppermute | solution.py:300
  102.3 1.9 %collective-permute-start.17 = (bf16[256,256]{1,0:T(8,128)(2,1)}, bf16[256,256]{1,0:T(8,128)(2,1)S(1)}, u32[]{:S(2)}, u32[]{:S(2)}) collective-permute-start(bf16[256,256]{1,0:T(8,128)(2,1)} %get-tuple-element.68), channel_id=1, source_target_pairs={{0,8},{4,12},{28,4},{1,9},{5,13},{29,5},{2,10},{6,14},{30,6},{3,11... | collective-permute-start | bytes 393224 | tf_op jit(solution)/shard_map/ppermute | solution.py:300
  104.2 12.8 %all-to-all-start = ((f32[32,2,128]{2,1,0:T(2,128)}), f32[32,2,128]{2,1,0:T(2,128)S(1)}, u32[]{:S(2)}, u32[]{:S(2)}) async-start(f32[32,2,128]{2,1,0:T(2,128)} %get-tuple-element.69), calls=%async_computation | async-start | bytes 65536 | tf_op jit(solution)/shard_map/all_to_all | solution.py:495
  117.1 5.0 %collective-permute-start.10 = (bf16[256,256]{1,0:T(8,128)(2,1)S(1)}, bf16[256,256]{1,0:T(8,128)(2,1)S(1)}, u32[]{:S(2)}, u32[]{:S(2)}) collective-permute-start(bf16[256,256]{1,0:T(8,128)(2,1)S(1)} %get-tuple-element.75), channel_id=1, source_target_pairs={{0,24},{4,28},{12,4},{16,8},{20,12},{24,16},{28,20},{1,25},{5,29},... | collective-permute-start | bytes 393224 | tf_op jit(solution)/shard_map/ppermute | solution.py:300
  122.1 1.9 %collective-permute-start.11 = (bf16[256,256]{1,0:T(8,128)(2,1)S(1)}, bf16[256,256]{1,0:T(8,128)(2,1)S(1)}, u32[]{:S(2)}, u32[]{:S(2)}) collective-permute-start(bf16[256,256]{1,0:T(8,128)(2,1)S(1)} %get-tuple-element.74), channel_id=1, source_target_pairs={{0,16},{4,20},{20,4},{24,8},{28,12},{1,17},{5,21},{21,5},{25,9},{2... | collective-permute-start | bytes 393224 | tf_op jit(solution)/shard_map/ppermute | solution.py:300
  124.0 0.7 slice_bitcast_fusion.3.refs_8_
  124.8 7.1 %collective-permute-done.11.refs_10_ = bf16[256,256]{1,0:T(8,128)(2,1)S(1)} collective-permute-done((bf16[256,256]{1,0:T(8,128)(2,1)S(1)}, bf16[256,256]{1,0:T(8,128)(2,1)S(1)}, u32[]{:S(2)}, u32[]{:S(2)}) %collective-permute-start.11) | collective-permute-done | bytes 131104 | tf_op jit(solution)/shard_map/ppermute | solution.py:300
  131.9 0.6 copy-done.20
  132.6 2.5 %key_back.1 = (bf16[256,256]{1,0:T(8,128)(2,1)}, bf16[256,256]{1,0:T(8,128)(2,1)}, f32[2,128]{1,0:T(2,128)}) custom-call(s32[4]{0:T(128)} %broadcast_add_fusion.refs_0_, f32[32,128]{1,0:T(8,128)} %constant.64.clone.refs_1_.refs_2_, f32[32,128]{1,0:T(8,128)} %constant.65.clone.refs_2_.refs_3_, f32[64,128]{1,0:T(8,128)} %constant.66.clone.refs_3_.refs_4_, ...), custom_call_target="tpu_custom_call" | custom-call | tf_op jit(solution)/shard_map/key_back/pallas_call | solution.py:497
  135.1 0.7 copy-done.22
  135.8 0.5 slice_bitcast_fusion.4
  (59 shorter events, 0.3 us)
Async XLA Ops:
  1.6 29.7 %copy-start.10 = (bf16[256,256]{1,0:T(8,128)(2,1)}, bf16[256,256]{1,0:T(8,128)(2,1)S(1)}, u32[]{:S(2)}) copy-start(bf16[256,256]{1,0:T(8,128)(2,1)S(1)} %pad_maximum_fusion.refs_6_) | copy-start | bytes 393220
  1.6 15.4 %collective-permute-start = (bf16[256,256]{1,0:T(8,128)(2,1)S(1)}, bf16[256,256]{1,0:T(8,128)(2,1)S(1)}, u32[]{:S(2)}, u32[]{:S(2)}) collective-permute-start(bf16[256,256]{1,0:T(8,128)(2,1)S(1)} %pad_maximum_fusion.refs_6_), channel_id=1, source_target_pairs={{4,12},{8,16},{12,20},{16,24},{20,28},{24,0},{28,4},{5,13},{9,17},... | collective-permute-start | bytes 393224 | tf_op jit(solution)/shard_map/ppermute | solution.py:300
  4.8 22.6 %collective-permute-start.1 = (bf16[256,256]{1,0:T(8,128)(2,1)S(1)}, bf16[256,256]{1,0:T(8,128)(2,1)S(1)}, u32[]{:S(2)}, u32[]{:S(2)}) collective-permute-start(bf16[256,256]{1,0:T(8,128)(2,1)S(1)} %pad_maximum_fusion.refs_6_), channel_id=1, source_target_pairs={{4,20},{8,24},{12,28},{16,0},{20,4},{5,21},{9,25},{13,29},{17,1},{... | collective-permute-start | bytes 393224 | tf_op jit(solution)/shard_map/ppermute | solution.py:300
  9.1 18.4 %collective-permute-start.2 = (bf16[256,256]{1,0:T(8,128)(2,1)S(1)}, bf16[256,256]{1,0:T(8,128)(2,1)S(1)}, u32[]{:S(2)}, u32[]{:S(2)}) collective-permute-start(bf16[256,256]{1,0:T(8,128)(2,1)S(1)} %pad_maximum_fusion.refs_6_), channel_id=1, source_target_pairs={{4,28},{8,0},{12,4},{5,29},{9,1},{13,5},{6,30},{10,2},{14,6},{7,31... | collective-permute-start | bytes 393224 | tf_op jit(solution)/shard_map/ppermute | solution.py:300
  11.0 5.4 %copy-start.21 = (s32[4,32]{1,0:T(4,128)S(1)}, s32[4,32]{1,0:T(4,128)}, u32[]{:S(2)}) copy-start(s32[4,32]{1,0:T(4,128)} %param.19) | copy-start | bytes 1540
  11.0 16.4 %copy-start.1 = (bf16[256,256]{1,0:T(8,128)(2,1)}, bf16[256,256]{1,0:T(8,128)(2,1)S(1)}, u32[]{:S(2)}) copy-start(bf16[256,256]{1,0:T(8,128)(2,1)S(1)} %pad_maximum_fusion.1.refs_0_.refs_6_) | copy-start | bytes 393220
  11.0 21.6 %collective-permute-start.5 = (bf16[256,256]{1,0:T(8,128)(2,1)S(1)}, bf16[256,256]{1,0:T(8,128)(2,1)S(1)}, u32[]{:S(2)}, u32[]{:S(2)}) collective-permute-start(bf16[256,256]{1,0:T(8,128)(2,1)S(1)} %pad_maximum_fusion.1.refs_0_.refs_6_), channel_id=1, source_target_pairs={{4,12},{8,16},{12,20},{16,24},{20,28},{24,0},{28,4},{5,13},{9,17},... | collective-permute-start | bytes 393224 | tf_op jit(solution)/shard_map/ppermute | solution.py:300
  14.4 18.2 %collective-permute-start.6 = (bf16[256,256]{1,0:T(8,128)(2,1)S(1)}, bf16[256,256]{1,0:T(8,128)(2,1)S(1)}, u32[]{:S(2)}, u32[]{:S(2)}) collective-permute-start(bf16[256,256]{1,0:T(8,128)(2,1)S(1)} %pad_maximum_fusion.1.refs_0_.refs_6_), channel_id=1, source_target_pairs={{4,20},{8,24},{12,28},{16,0},{20,4},{5,21},{9,25},{13,29},{17,1},{... | collective-permute-start | bytes 393224 | tf_op jit(solution)/shard_map/ppermute | solution.py:300
  17.1 10.4 %copy-start.3 = (bf16[256,256]{1,0:T(8,128)(2,1)}, bf16[256,256]{1,0:T(8,128)(2,1)S(1)}, u32[]{:S(2)}) copy-start(bf16[256,256]{1,0:T(8,128)(2,1)S(1)} %collective-permute-done.refs_0_.refs_7_) | copy-start | bytes 393220
  17.1 15.6 %collective-permute-start.7 = (bf16[256,256]{1,0:T(8,128)(2,1)S(1)}, bf16[256,256]{1,0:T(8,128)(2,1)S(1)}, u32[]{:S(2)}, u32[]{:S(2)}) collective-permute-start(bf16[256,256]{1,0:T(8,128)(2,1)S(1)} %pad_maximum_fusion.1.refs_0_.refs_6_), channel_id=1, source_target_pairs={{4,28},{8,0},{12,4},{5,29},{9,1},{13,5},{6,30},{10,2},{14,6},{7,31... | collective-permute-start | bytes 393224 | tf_op jit(solution)/shard_map/ppermute | solution.py:300
  27.4 0.7 copy-start.4
  27.5 0.7 copy-start.5
  30.0 11.2 %collective-permute-start.4 = (bf16[3,256,256]{2,1,0:T(8,128)(2,1)}, bf16[3,256,256]{2,1,0:T(8,128)(2,1)S(1)}, u32[]{:S(2)}, u32[]{:S(2)}) collective-permute-start(bf16[3,256,256]{2,1,0:T(8,128)(2,1)} %join.2), channel_id=1, source_target_pairs={{4,0},{12,8},{16,20},{20,16},{24,28},{28,24},{5,1},{13,9},{17,21},... | collective-permute-start | bytes 1179656 | tf_op jit(solution)/shard_map/ppermute | solution.py:300
  31.3 9.9 %collective-permute-start.3 = (bf16[256,256]{1,0:T(8,128)(2,1)S(1)}, bf16[256,256]{1,0:T(8,128)(2,1)S(1)}, u32[]{:S(2)}, u32[]{:S(2)}) collective-permute-start(bf16[256,256]{1,0:T(8,128)(2,1)S(1)} %pad_maximum_fusion.refs_6_), channel_id=1, source_target_pairs={{4,0},{8,12},{16,20},{24,28},{5,1},{9,13},{17,21},{25,29},{6,2},{1... | collective-permute-start | bytes 393224 | tf_op jit(solution)/shard_map/ppermute | solution.py:300
  32.6 0.6 copy-start.11
  32.6 0.7 copy-start.12
  33.3 0.7 copy-start.13
  35.9 16.6 %collective-permute-start.8 = (bf16[4,256,256]{2,1,0:T(8,128)(2,1)}, bf16[4,256,256]{2,1,0:T(8,128)(2,1)S(1)}, u32[]{:S(2)}, u32[]{:S(2)}) collective-permute-start(bf16[4,256,256]{2,1,0:T(8,128)(2,1)} %join.3), channel_id=1, source_target_pairs={{4,0},{8,12},{12,8},{16,20},{20,16},{24,28},{28,24},{5,1},{9,13},{... | collective-permute-start | bytes 1572872 | tf_op jit(solution)/shard_map/ppermute | solution.py:300
  41.1 0.7 copy-start.25
  41.1 0.8 copy-start.24
  47.7 25.4 %collective-permute-start.9 = (bf16[4,256,256]{2,1,0:T(8,128)(2,1)}, bf16[4,256,256]{2,1,0:T(8,128)(2,1)S(1)}, u32[]{:S(2)}, u32[]{:S(2)}) collective-permute-start(bf16[4,256,256]{2,1,0:T(8,128)(2,1)} %get-tuple-element.55), channel_id=1, source_target_pairs={{0,4},{8,12},{12,8},{16,20},{20,16},{24,28},{28,24},{1,5},{9,13},{... | collective-permute-start | bytes 1572872 | tf_op jit(solution)/shard_map/ppermute | solution.py:300
  52.5 0.8 copy-start.23
  59.0 33.3 %collective-permute-start.14 = (bf16[3,256,256]{2,1,0:T(8,128)(2,1)}, bf16[3,256,256]{2,1,0:T(8,128)(2,1)S(1)}, u32[]{:S(2)}, u32[]{:S(2)}) collective-permute-start(bf16[3,256,256]{2,1,0:T(8,128)(2,1)} %get-tuple-element.64), channel_id=1, source_target_pairs={{0,4},{8,12},{16,20},{20,16},{24,28},{28,24},{1,5},{9,13},{17,21},... | collective-permute-start | bytes 1179656 | tf_op jit(solution)/shard_map/ppermute | solution.py:300
  60.3 56.8 %collective-permute-start.13 = (bf16[256,256]{1,0:T(8,128)(2,1)}, bf16[256,256]{1,0:T(8,128)(2,1)S(1)}, u32[]{:S(2)}, u32[]{:S(2)}) collective-permute-start(bf16[256,256]{1,0:T(8,128)(2,1)} %get-tuple-element.60), channel_id=1, source_target_pairs={{0,4},{12,8},{20,16},{28,24},{1,5},{13,9},{21,17},{29,25},{2,6},{1... | collective-permute-start | bytes 393224 | tf_op jit(solution)/shard_map/ppermute | solution.py:300
  61.8 11.4 %copy-start.6 = (bf16[256,256]{1,0:T(8,128)(2,1)S(1)}, bf16[256,256]{1,0:T(8,128)(2,1)}, u32[]{:S(2)}) copy-start(bf16[256,256]{1,0:T(8,128)(2,1)} %get-tuple-element.56) | copy-start | bytes 393220
  61.8 11.4 %copy-start.7 = (bf16[256,256]{1,0:T(8,128)(2,1)S(1)}, bf16[256,256]{1,0:T(8,128)(2,1)}, u32[]{:S(2)}) copy-start(bf16[256,256]{1,0:T(8,128)(2,1)} %get-tuple-element.57) | copy-start | bytes 393220
  61.8 11.4 %copy-start.8 = (bf16[256,256]{1,0:T(8,128)(2,1)S(1)}, bf16[256,256]{1,0:T(8,128)(2,1)}, u32[]{:S(2)}) copy-start(bf16[256,256]{1,0:T(8,128)(2,1)} %get-tuple-element.58) | copy-start | bytes 393220
  92.4 0.8 copy-start.2
  93.1 3.9 %copy-start = (bf16[256,256]{1,0:T(8,128)(2,1)S(1)}, bf16[256,256]{1,0:T(8,128)(2,1)}, u32[]{:S(2)}) copy-start(bf16[256,256]{1,0:T(8,128)(2,1)} %get-tuple-element.73.refs_5_) | copy-start | bytes 393220
  95.1 27.0 %collective-permute-start.15 = (bf16[256,256]{1,0:T(8,128)(2,1)}, bf16[256,256]{1,0:T(8,128)(2,1)S(1)}, u32[]{:S(2)}, u32[]{:S(2)}) collective-permute-start(bf16[256,256]{1,0:T(8,128)(2,1)} %get-tuple-element.66), channel_id=1, source_target_pairs={{0,24},{4,28},{12,4},{16,8},{20,12},{24,16},{28,20},{1,25},{5,29},... | collective-permute-start | bytes 393224 | tf_op jit(solution)/shard_map/ppermute | solution.py:300
  97.0 34.8 %collective-permute-start.12 = (bf16[256,256]{1,0:T(8,128)(2,1)S(1)}, bf16[256,256]{1,0:T(8,128)(2,1)S(1)}, u32[]{:S(2)}, u32[]{:S(2)}) collective-permute-start(bf16[256,256]{1,0:T(8,128)(2,1)S(1)} %copy-done), channel_id=1, source_target_pairs={{0,8},{4,12},{28,4},{1,9},{5,13},{29,5},{2,10},{6,14},{30,6},{3,11... | collective-permute-start | bytes 393224 | tf_op jit(solution)/shard_map/ppermute | solution.py:300
  100.4 24.3 %collective-permute-start.16 = (bf16[256,256]{1,0:T(8,128)(2,1)}, bf16[256,256]{1,0:T(8,128)(2,1)S(1)}, u32[]{:S(2)}, u32[]{:S(2)}) collective-permute-start(bf16[256,256]{1,0:T(8,128)(2,1)} %get-tuple-element.67), channel_id=1, source_target_pairs={{0,16},{4,20},{20,4},{24,8},{28,12},{1,17},{5,21},{21,5},{25,9},{2... | collective-permute-start | bytes 393224 | tf_op jit(solution)/shard_map/ppermute | solution.py:300
  102.3 22.4 %collective-permute-start.17 = (bf16[256,256]{1,0:T(8,128)(2,1)}, bf16[256,256]{1,0:T(8,128)(2,1)S(1)}, u32[]{:S(2)}, u32[]{:S(2)}) collective-permute-start(bf16[256,256]{1,0:T(8,128)(2,1)} %get-tuple-element.68), channel_id=1, source_target_pairs={{0,8},{4,12},{28,4},{1,9},{5,13},{29,5},{2,10},{6,14},{30,6},{3,11... | collective-permute-start | bytes 393224 | tf_op jit(solution)/shard_map/ppermute | solution.py:300
  104.2 20.4 %all-to-all-start = ((f32[32,2,128]{2,1,0:T(2,128)}), f32[32,2,128]{2,1,0:T(2,128)S(1)}, u32[]{:S(2)}, u32[]{:S(2)}) async-start(f32[32,2,128]{2,1,0:T(2,128)} %get-tuple-element.69), calls=%async_computation | async-start | bytes 65536 | tf_op jit(solution)/shard_map/all_to_all | solution.py:495
  117.1 7.6 %copy-start.14 = (bf16[256,256]{1,0:T(8,128)(2,1)}, bf16[256,256]{1,0:T(8,128)(2,1)S(1)}, u32[]{:S(2)}) copy-start(bf16[256,256]{1,0:T(8,128)(2,1)S(1)} %collective-permute-done.13.refs_13_) | copy-start | bytes 393220
  117.1 7.6 %collective-permute-start.10 = (bf16[256,256]{1,0:T(8,128)(2,1)S(1)}, bf16[256,256]{1,0:T(8,128)(2,1)S(1)}, u32[]{:S(2)}, u32[]{:S(2)}) collective-permute-start(bf16[256,256]{1,0:T(8,128)(2,1)S(1)} %get-tuple-element.75), channel_id=1, source_target_pairs={{0,24},{4,28},{12,4},{16,8},{20,12},{24,16},{28,20},{1,25},{5,29},... | collective-permute-start | bytes 393224 | tf_op jit(solution)/shard_map/ppermute | solution.py:300
  122.1 2.6 %copy-start.15 = (bf16[256,256]{1,0:T(8,128)(2,1)}, bf16[256,256]{1,0:T(8,128)(2,1)S(1)}, u32[]{:S(2)}) copy-start(bf16[256,256]{1,0:T(8,128)(2,1)S(1)} %collective-permute-done.15.refs_14_) | copy-start | bytes 393220
  122.1 9.7 %collective-permute-start.11 = (bf16[256,256]{1,0:T(8,128)(2,1)S(1)}, bf16[256,256]{1,0:T(8,128)(2,1)S(1)}, u32[]{:S(2)}, u32[]{:S(2)}) collective-permute-start(bf16[256,256]{1,0:T(8,128)(2,1)S(1)} %get-tuple-element.74), channel_id=1, source_target_pairs={{0,16},{4,20},{20,4},{24,8},{28,12},{1,17},{5,21},{21,5},{25,9},{2... | collective-permute-start | bytes 393224 | tf_op jit(solution)/shard_map/ppermute | solution.py:300
  124.7 7.2 %copy-start.9 = (f32[32,2,128]{2,1,0:T(2,128)}, f32[32,2,128]{2,1,0:T(2,128)S(1)}, u32[]{:S(2)}) copy-start(f32[32,2,128]{2,1,0:T(2,128)S(1)} %all-to-all-done.refs_17_) | copy-start | bytes 98308
  124.7 7.2 %copy-start.17 = (bf16[256,256]{1,0:T(8,128)(2,1)}, bf16[256,256]{1,0:T(8,128)(2,1)S(1)}, u32[]{:S(2)}) copy-start(bf16[256,256]{1,0:T(8,128)(2,1)S(1)} %collective-permute-done.16.refs_15_) | copy-start | bytes 393220
  124.7 7.1 %copy-start.18 = (bf16[256,256]{1,0:T(8,128)(2,1)}, bf16[256,256]{1,0:T(8,128)(2,1)S(1)}, u32[]{:S(2)}) copy-start(bf16[256,256]{1,0:T(8,128)(2,1)S(1)} %collective-permute-done.17.refs_16_) | copy-start | bytes 393220
  124.8 7.1 %copy-start.19 = (bf16[256,256]{1,0:T(8,128)(2,1)}, bf16[256,256]{1,0:T(8,128)(2,1)S(1)}, u32[]{:S(2)}) copy-start(bf16[256,256]{1,0:T(8,128)(2,1)S(1)} %collective-permute-done.10.refs_9_) | copy-start | bytes 393220
  131.9 0.7 copy-start.20
  131.9 0.7 copy-start.16
  135.1 0.7 copy-start.22

commit v11 on v10

--- a/solution.py
+++ b/solution.py
@@ -111,16 +111,16 @@
         delta_ref[:, here] = jnp.sum(product, 0, keepdims=True)
 
 
-def main_kernel(blocks, block_len, tree_dev, inv_root, n_in, last, *refs):
+def main_kernel(blocks, block_len, tree_dev, inv_root, n_in, *refs):
     plan_ref, gain_ref = refs[:2]
     tables = refs[2:6]
     half = tree_dev // 2
     pieces, crossed_ref = refs[6:5 + n_in], refs[5 + n_in]
     q_t_ref, q_ref, grad_t_ref, grad_ref, delta_ref = refs[6 + n_in:11 + n_in]
     dq_ref, gain_part_ref = refs[11 + n_in:13 + n_in]
-    parts = refs[13 + n_in:13 + n_in + half + last]
+    parts = refs[13 + n_in:13 + n_in + half]
     crossed_part, raw, keys, keys_t, vals, shown, with_cos, with_sin, expo, mass, w_all, ds_all, found, spread = refs[
-        13 + n_in + half + last:]
+        13 + n_in + half:]
     head_dim = gain_ref.shape[1]
     tokens = raw.shape[1]
     group = q_ref.shape[0] // tokens
@@ -220,9 +220,9 @@
         rows = rows_of(lax.rem(slot, blocks))
         spread[plan_ref[0, slot], rows_of(plan_ref[1, slot]), :] = found[slot // blocks, rows, :]
 
-    for piece in range(half + last):
+    for piece in range(half):
         parts[piece][...] = spread[piece]
-    crossed_part[...] = spread[half + last:]
+    crossed_part[...] = spread[half:]
 
 
 def join_kernel(*refs):
@@ -231,11 +231,18 @@
 
 
 def merge_kernel(*refs):
-    count = (len(refs) - 4) // 2
-    others_ref, gains_ref = refs[count:count + 2]
+    count = (len(refs) - 3) // 2
+    parts, others_ref, gains_ref, before_ref = refs[:count], *refs[count:count + 3]
+    outs, joined_ref, gains_out_ref = refs[count + 3:-2], *refs[-2:]
     for i in range(count):
-        refs[-1 - count + i][...] = (refs[i][...].astype(F32) + others_ref[i].astype(F32)).astype(BF16)
-    refs[-1][...] = gains_ref[...]
+        both = (parts[i][...].astype(F32) + others_ref[i + 1].astype(F32)).astype(BF16)
+        if i < count - 1:
+            outs[i][...] = both
+        else:
+            joined_ref[joined_ref.shape[0] - 1] = both
+    for head in range(joined_ref.shape[0] - 1):
+        joined_ref[head] = before_ref[head]
+    gains_out_ref[...] = gains_ref[...]
 
 
 def query_kernel(blocks, inv_root, kv_heads, depth_ref, t0, t1, t2, t3, gain_ref, q_ref, *refs):
@@ -262,21 +269,32 @@
     gains_ref[...] = jnp.broadcast_to(gains[None], gains_ref.shape)
 
 
-def key_kernel(blocks, counts, depth_ref, t0, t1, t2, t3, gain_ref, k_ref, *refs):
-    sums, (gains_ref, dk_out_ref, dv_out_ref, total_ref) = refs[:-4], refs[-4:]
+def summed_terms(refs, places):
+    total = 0.0
+    for ref, place in zip(refs, places):
+        total = total + (ref[...] if place is None else ref[place]).astype(F32)
+    return total
+
+
+def early_kernel(places, gains_ref, *refs):
+    terms, (sum_ref, gains_out_ref) = refs[:-2], refs[-2:]
+    sum_ref[...] = summed_terms(terms, places)
+    gains_out_ref[...] = gains_ref[...]
+
+
+def key_kernel(blocks, places, depth_ref, t0, t1, t2, t3, gain_ref, k_ref, gains_ref, *refs):
+    terms, (dk_out_ref, dv_out_ref, total_ref) = refs[:-3], refs[-3:]
     total_ref[...] = jnp.sum(gains_ref[...], 0)
     head_dim = gain_ref.shape[1]
     cos, sin = own_tables(depth_ref, (t0, t1, t2, t3), blocks)
     gain = gain_ref[...]
-    for head, each in enumerate(counts):
+    for head, mine in enumerate(places):
         cols = pl.ds(head * head_dim, head_dim)
         rows = k_ref[:, cols].astype(F32)
         recip = inverse_rms(rows)
         normed = rows * recip
-        mine = sums[sum(counts[:head]):][:each]
-        both = mine[0][...].astype(F32)
-        for other in mine[1:]:
-            both = both + other[...].astype(F32)
+        both = summed_terms(terms[:len(mine)], mine)
+        terms = terms[len(mine):]
         grad = turned_back(both[:, 0:head_dim], cos, sin) * gain
         inner = jnp.mean(grad * normed, -1, keepdims=True)
         dk_out_ref[:, cols] = (recip * (grad - normed * inner)).astype(BF16)
@@ -357,6 +375,7 @@
     smem = pl.BlockSpec(memory_space=pltpu.SMEM)
     vmem = pl.BlockSpec(memory_space=pltpu.VMEM)
     sds = jax.ShapeDtypeStruct
+    slow = pl.CostEstimate(flops=4 * 10**9, bytes_accessed=16 * 1024 * 1024, transcendentals=0)
     quick = pl.CostEstimate(flops=1024, bytes_accessed=1024, transcendentals=0)
 
     plan = pl.pallas_call(
@@ -364,7 +383,7 @@
         out_shape=sds((5, tree_blocks), jnp.int32),
         in_specs=[smem, smem],
         out_specs=smem,
-        cost_estimate=pl.CostEstimate(flops=4 * 10**9, bytes_accessed=16 * 1024 * 1024, transcendentals=0),
+        cost_estimate=slow,
         name="plan",
     )(place, in_tree)
 
@@ -405,7 +424,7 @@
         straight = tree.along(own[h])
         if h == 0:
             cross = [tree.across(own[h], [0])]
-            crossed = tree.across(join(straight, queries[4], queries[-1]), steps)
+            crossed = tree.across(join(straight, cross[0], queries[4], queries[-1]), steps)
         else:
             cross = []
             crossed = tree.across(join([own[h], *straight]), [0, *steps])
@@ -414,17 +433,16 @@
     half = tree_dev // 2
 
     def attend(h):
-        last = h == kv_heads - 1
         return pl.pallas_call(
-            lambda *refs: main_kernel(blocks, block_len, tree_dev, inv_root, len(pieces[h]), last, *refs),
+            lambda *refs: main_kernel(blocks, block_len, tree_dev, inv_root, len(pieces[h]), *refs),
             out_shape=(
                 sds((head_dim, rows), F32),
                 sds((8, head_dim), F32),
-                *[sds((tokens, 2 * head_dim), BF16)] * (half + last),
-                sds((half - last, tokens, 2 * head_dim), BF16),
+                *[sds((tokens, 2 * head_dim), BF16)] * half,
+                sds((half, tokens, 2 * head_dim), BF16),
             ),
             in_specs=[smem] + [vmem] * (10 + len(pieces[h])),
-            out_specs=tuple([vmem] * (3 + half + last)),
+            out_specs=tuple([vmem] * (3 + half)),
             scratch_shapes=[
                 pltpu.VMEM((tree_dev, tokens, 2 * head_dim), BF16),
                 pltpu.VMEM((tree_dev + 1, tokens, head_dim), BF16),
@@ -466,42 +484,56 @@
         name="query_back",
     )(depth, *tables, q_gain_row, q_raw, *dq, *k_gain_parts)
 
-    terms, counts = [], []
-    for parts, crossed_part in attended:
-        if len(parts) > half:
-            others = tree.across(crossed_part, steps, back=True)
-            mine = [parts[0], tree.across(parts[half], [0], back=True)]
+    terms, farthest = [], []
+    for h, (parts, crossed_part) in enumerate(attended):
+        others = tree.across(crossed_part, [0, *steps], back=True)
+        if h < kv_heads - 1:
+            merged = [
+                (parts[i + 1].astype(F32) + others[i + 1].astype(F32)).astype(BF16) for i in range(len(steps))
+            ]
+            farthest.append(merged.pop())
         else:
-            others = tree.across(crossed_part, [0, *steps], back=True)
-            mine = [parts[0], others[0]]
-            others = others[1:]
-        if len(parts) > half:
-            *merged, gains = pl.pallas_call(
+            *merged, joined, gains = pl.pallas_call(
                 merge_kernel,
-                out_shape=(*[sds((tokens, 2 * head_dim), BF16)] * len(steps), sds(gains.shape, F32)),
-                in_specs=[vmem] * (len(steps) + 2) + [pl.BlockSpec(memory_space=pl.ANY)],
+                out_shape=(
+                    *[sds((tokens, 2 * head_dim), BF16)] * (len(steps) - 1),
+                    sds((kv_heads, tokens, 2 * head_dim), BF16),
+                    sds(gains.shape, F32),
+                ),
+                in_specs=[vmem] * (len(steps) + 3),
                 out_specs=tuple([vmem] * (len(steps) + 1)),
                 compiler_params=params,
                 name="merge",
-            )(*parts[1:half], others, gains, merged[-1])
-        else:
-            merged = [
-                (parts[i + 1].astype(F32) + others[i].astype(F32)).astype(BF16) for i in range(len(steps))
-            ]
-        mine.extend(tree.home(both, step) for both, step in zip(merged, steps))
-        terms.extend(mine)
-        counts.append(len(mine))
-
+            )(*parts[1:], others, gains, jnp.stack(farthest))
+            joined = tree.home(joined, steps[-1])
+        mine = [(parts[0], None), (others, 0)]
+        terms.append(mine + [(tree.home(both, step), None) for both, step in zip(merged, steps)])
+    for h in range(kv_heads):
+        if h < kv_heads - 1:
+            arrays, places = zip(*terms[h])
+            early, gains = pl.pallas_call(
+                lambda *refs: early_kernel(places, *refs),
+                out_shape=(sds((tokens, 2 * head_dim), F32), sds(gains.shape, F32)),
+                in_specs=[vmem] * (1 + len(arrays)),
+                out_specs=(vmem, vmem),
+                compiler_params=params,
+                cost_estimate=slow,
+                name="early",
+            )(gains, *arrays)
+            terms[h] = [(early, None)]
+        terms[h].append((joined, h))
     gains = lax.all_to_all(gains, ("ctx", "heads"), 0, 0)
 
+    arrays = [array for mine in terms for array, _ in mine]
+    places = [[place for _, place in mine] for mine in terms]
     dk_raw, dv, total = pl.pallas_call(
-        lambda *refs: key_kernel(blocks, counts, *refs),
+        lambda *refs: key_kernel(blocks, places, *refs),
         out_shape=(sds(k_raw.shape, BF16), sds(k_raw.shape, BF16), sds(gains.shape[1:], F32)),
-        in_specs=[smem] + [vmem] * (7 + len(terms)),
+        in_specs=[smem] + [vmem] * (7 + len(arrays)),
         out_specs=(vmem, vmem, vmem),
         compiler_params=params,
         name="key_back",
-    )(depth, *tables, k_gain_row, k_raw, *terms, gains)
+    )(depth, *tables, k_gain_row, k_raw, gains, *arrays)
     return (dq_raw, dk_raw, dv, total[0], total[1])
 
 

time: 137 us -> 132 us (0.964)
  the two profiles are of different devices: /device:TPU:3 before, /device:TPU:0 now
where the time goes in v11:
time: 132 us; the launch traced here: 133 us
  Pallas kernels  56.7 us (43%)
  starting transfers between devices  28.4 us (22%)
  waiting for transfers between devices  19.1 us (14%)
  blocking collectives  17.3 us (13%)
  local copies, waits for them, and re-layouts  7.92 us (6%)
  other arithmetic  2.09 us (2%)
    pallas_call x2, Pallas kernels, attend(): pl.pallas_call(lambda *refs: main_kernel(blocks, block_len, tree_dev, inv...  31.5 us
    ppermute x16, starting transfers between devices, send(): return lax.ppermute(value, 'ctx', pairs)  28.4 us
    ppermute x16, waiting for transfers between devices, send(): return lax.ppermute(value, 'ctx', pairs)  19.1 us
    all_to_all x1, blocking collectives, on_device(): gains = lax.all_to_all(gains, ('ctx', 'heads'), 0, 0)  17.3 us
    pallas_call x1, Pallas kernels, on_device(): pl.pallas_call(lambda *refs: prep_kernel(blocks, block_len, kv_heads, *re...  6.76 us
    unnamed x46, local copies, waits for them, and re-layouts  6.44 us
    pallas_call x1, Pallas kernels, on_device(): pl.pallas_call(lambda *refs: query_kernel(blocks, inv_root, kv_heads, *re...  6.02 us
    pallas_call x2, Pallas kernels, join(): pl.pallas_call(join_kernel, out_shape=sds((count, tokens, 2 * head_dim),...  3.73 us
  transfers between devices with their start and end apart: 16, of which 3 were waited for; matrix products, arithmetic and copies ran while one was open for 2% of the time, Pallas kernels for 41%

profile of v11, /device:TPU:0, one launch (start us, length us, event | category | flops | bytes accessed | tf_op | source)
XLA Modules:
  0.0 132.6 jit_solution(3388150346161121179)
XLA Ops:
  0.6 1.0 fusion.7
  1.6 1.3 collective-permute-start
  2.9 1.3 collective-permute-start.1
  4.2 1.3 collective-permute-start.2
  5.5 1.3 collective-permute-start.3
  6.9 1.3 collective-permute-start.5
  8.2 0.7 fusion.6
  8.9 3.3 %collective-permute-done.refs_0_.refs_7_ = bf16[256,256]{1,0:T(8,128)(2,1)S(1)} collective-permute-done((bf16[256,256]{1,0:T(8,128)(2,1)S(1)}, bf16[256,256]{1,0:T(8,128)(2,1)S(1)}, u32[]{:S(2)}, u32[]{:S(2)}) %collective-permute-start) | collective-permute-done | bytes 131104 | tf_op jit(solution)/shard_map/ppermute | solution.py:318
  12.2 1.3 collective-permute-start.6
  13.5 1.5 %collective-permute-done.1.refs_1_.refs_8_ = bf16[256,256]{1,0:T(8,128)(2,1)S(1)} collective-permute-done((bf16[256,256]{1,0:T(8,128)(2,1)S(1)}, bf16[256,256]{1,0:T(8,128)(2,1)S(1)}, u32[]{:S(2)}, u32[]{:S(2)}) %collective-permute-start.1) | collective-permute-done | bytes 131104 | tf_op jit(solution)/shard_map/ppermute | solution.py:318
  15.0 1.3 collective-permute-start.7
  16.3 0.5 broadcast_add_fusion.refs_0_
  16.8 6.8 %prep.1 = (bf16[128,2048]{1,0:T(8,128)(2,1)}, bf16[2048,128]{1,0:T(8,128)(2,1)}, bf16[128,2048]{1,0:T(8,128)(2,1)}, bf16[2048,128]{1,0:T(8,128)(2,1)}, f32[1,204...) custom-call(s32[4]{0:T(128)} %broadcast_add_fusion.refs_0_, ...), custom_call_target="tpu_custom_call" | custom-call | flops 1024 | bytes 1024 | tf_op jit(solution)/shard_map/prep/pallas_call | solution.py:403
  23.6 0.6 copy-done.6
  24.2 0.1 copy-done.7
  24.3 1.8 %join.2 = bf16[3,256,256]{2,1,0:T(8,128)(2,1)} custom-call(bf16[256,256]{1,0:T(8,128)(2,1)} %copy-done.4, bf16[256,256]{1,0:T(8,128)(2,1)} %copy-done.5, bf16[256,256]{1,0:T(8,128)(2,1)} %copy-done.6, bf16[256,256]{1,0:T(8,128)(2,1)} %copy-done.7, f32[1,2048]{1,0:T(1,128)} %get-tuple-element.40.refs_4_.refs_16_, f32[1,2048]{1,0:T(1,128)} %get-tuple-element.41.refs_5_.refs_15_), custom_call_target="tpu_custom_call" | custom-call | flops 1024 | bytes 1024 | tf_op jit(solution)/shard_map/join/pallas_call | solution.py:392
  26.1 1.3 collective-permute-start.4
  27.5 0.6 copy-done.14
  28.1 0.1 copy-done.15
  28.1 0.6 copy-done.16
  28.8 1.9 %join.3 = bf16[4,256,256]{2,1,0:T(8,128)(2,1)} custom-call(bf16[256,256]{1,0:T(8,128)(2,1)} %copy-done.2, bf16[256,256]{1,0:T(8,128)(2,1)} %copy-done.14, bf16[256,256]{1,0:T(8,128)(2,1)} %copy-done.15, bf16[256,256]{1,0:T(8,128)(2,1)} %copy-done.16), custom_call_target="tpu_custom_call" | custom-call | flops 1024 | bytes 1024 | tf_op jit(solution)/shard_map/join/pallas_call | solution.py:392
  30.7 1.3 collective-permute-start.8
  32.0 2.0 %plan.1.refs_0_ = s32[5,32]{1,0:T(8,128)} custom-call(s32[1]{0:T(128)} %bitcast.1.refs_0_, s32[4,32]{1,0:T(4,128)} %get-tuple-element.82.refs_1_), custom_call_target="tpu_custom_call" | custom-call | flops 4000000000 | bytes 16777216 | tf_op jit(solution)/shard_map/plan/pallas_call | solution.py:381
  34.0 14.3 %collective-permute-done.4.refs_11_ = bf16[3,256,256]{2,1,0:T(8,128)(2,1)S(1)} collective-permute-done((bf16[3,256,256]{2,1,0:T(8,128)(2,1)}, bf16[3,256,256]{2,1,0:T(8,128)(2,1)S(1)}, u32[]{:S(2)}, u32[]{:S(2)}) %collective-permute-start.4) | collective-permute-done | bytes 393248 | tf_op jit(solution)/shard_map/ppermute | solution.py:318
  48.3 0.8 copy-done.20
  49.1 15.8 %attend.2 = (f32[128,2048]{1,0:T(8,128)}, f32[8,128]{1,0:T(8,128)}, bf16[256,256]{1,0:T(8,128)(2,1)}, bf16[256,256]{1,0:T(8,128)(2,1)}, bf16[256,256]{1,0:T(8,12...) custom-call(s32[5,32]{1,0:T(8,128)} %plan.1.refs_0_, f32[1,128]{1,0:T(1,128)} %bitcast.26, ...), custom_call_target="tpu_custom_call" | custom-call | flops 5368709120 | bytes 8388608 | tf_op jit(solution)/shard_map/attend/pallas_call | solution.py:436
  64.8 1.3 collective-permute-start.10
  66.2 0.8 copy-done.19
  67.0 15.8 %attend.3 = (f32[128,2048]{1,0:T(8,128)}, f32[8,128]{1,0:T(8,128)}, bf16[256,256]{1,0:T(8,128)(2,1)}, bf16[256,256]{1,0:T(8,128)(2,1)}, bf16[256,256]{1,0:T(8,12...) custom-call(s32[5,32]{1,0:T(8,128)} %plan.1.refs_0_, f32[1,128]{1,0:T(1,128)} %bitcast.27, ...), custom_call_target="tpu_custom_call" | custom-call | flops 5368709120 | bytes 8388608 | tf_op jit(solution)/shard_map/attend/pallas_call | solution.py:436
  82.7 1.3 collective-permute-start.9
  84.1 0.8 fusion
  84.9 8.8 %collective-permute-start.11 = (bf16[256,256]{1,0:T(8,128)(2,1)S(1)}, bf16[256,256]{1,0:T(8,128)(2,1)S(1)}, u32[]{:S(2)}, u32[]{:S(2)}) collective-permute-start(bf16[256,256]{1,0:T(8,128)(2,1)S(1)} %get-tuple-element.76), channel_id=1, source_target_pairs={{0,24},{4,28},{12,4},{16,8},{20,12},{24,16},{28,20},{1,25},{5,29},... | collective-permute-start | bytes 393224 | tf_op jit(solution)/shard_map/ppermute | solution.py:318
  93.7 1.5 %collective-permute-start.12 = (bf16[256,256]{1,0:T(8,128)(2,1)S(1)}, bf16[256,256]{1,0:T(8,128)(2,1)S(1)}, u32[]{:S(2)}, u32[]{:S(2)}) collective-permute-start(bf16[256,256]{1,0:T(8,128)(2,1)S(1)} %get-tuple-element.75), channel_id=1, source_target_pairs={{0,16},{4,20},{20,4},{24,8},{28,12},{1,17},{5,21},{21,5},{25,9},{2... | collective-permute-start | bytes 393224 | tf_op jit(solution)/shard_map/ppermute | solution.py:318
  95.2 6.0 %query_back.1 = (bf16[256,2048]{1,0:T(8,128)(2,1)}, f32[32,2,128]{2,1,0:T(2,128)}) custom-call(s32[4]{0:T(128)} %broadcast_add_fusion.refs_0_, f32[32,128]{1,0:T(8,128)} %constant.64.clone.refs_1_.refs_2_, f32[32,128]{1,0:T(8,128)} %constant.65.clone.refs_2_.refs_3_, f32[64,128]{1,0:T(8,128)} %constant.66.clone.refs_3_.refs_4_, ...), custom_call_target="tpu_custom_call" | custom-call | tf_op jit(solution)/shard_map/query_back/pallas_call | solution.py:478
  101.3 0.8 copy-done
  102.1 2.1 %merge.1 = (bf16[256,256]{1,0:T(8,128)(2,1)}, bf16[256,256]{1,0:T(8,128)(2,1)}, bf16[2,256,256]{2,1,0:T(8,128)(2,1)}, f32[32,2,128]{2,1,0:T(2,128)}) custom-call(bf16[256,256]{1,0:T(8,128)(2,1)} %get-tuple-element.55.refs_0_, bf16[256,256]{1,0:T(8,128)(2,1)} %get-tuple-element.56.refs_1_, bf16[256,256]{1,0:T(8,128)(2,1)} %get-tuple-element.57.refs_2_, ...), custom_call_target="tpu_custom_call" | custom-call | tf_op jit(solution)/shard_map/merge/pallas_call | solution.py:496
  104.1 1.3 collective-permute-start.13
  105.4 1.3 collective-permute-start.14
  106.8 1.3 collective-permute-start.15
  108.1 0.6 copy-done.21
  108.7 0.0 copy-done.22
  108.8 2.0 %early.1 = (f32[256,256]{1,0:T(8,128)}, f32[32,2,128]{2,1,0:T(2,128)}) custom-call(f32[32,2,128]{2,1,0:T(2,128)} %get-tuple-element.62.refs_0_, bf16[256,256]{1,0:T(8,128)(2,1)} %get-tuple-element.63.refs_1_, bf16[4,256,256]{2,1,0:T(8,128)(2,1)} %copy-done.3, bf16[256,256]{1,0:T(8,128)(2,1)} %copy-done.21, bf16[256,256]{1,0:T(8,128)(2,1)} %copy-done.22), custom_call_target="tpu_custom_call" | custom-call | flops 4000000000 | bytes 16777216 | tf_op jit(solution)/shard_map/early/pallas_call | solution.py:514
  110.7 17.3 %all_to_all.5.refs_7_ = f32[32,2,128]{2,1,0:T(2,128)} all-to-all(f32[32,2,128]{2,1,0:T(2,128)} %get-tuple-element.66), channel_id=1, replica_groups=mesh['ctx'=8,'heads'=4] {'ctx','heads'}, dimensions={0} | all-to-all | bytes 65536 | tf_op jit(solution)/shard_map/all_to_all | solution.py:525
  128.1 0.6 copy-done.11
  128.8 0.1 copy-done.1
  128.9 2.6 %key_back.1 = (bf16[256,256]{1,0:T(8,128)(2,1)}, bf16[256,256]{1,0:T(8,128)(2,1)}, f32[2,128]{1,0:T(2,128)}) custom-call(s32[4]{0:T(128)} %broadcast_add_fusion.refs_0_, f32[32,128]{1,0:T(8,128)} %constant.64.clone.refs_1_.refs_2_, f32[32,128]{1,0:T(8,128)} %constant.65.clone.refs_2_.refs_3_, f32[64,128]{1,0:T(8,128)} %constant.66.clone.refs_3_.refs_4_, ...), custom_call_target="tpu_custom_call" | custom-call | tf_op jit(solution)/shard_map/key_back/pallas_call | solution.py:529
  131.5 0.6 copy-done.18
  132.1 0.5 slice_bitcast_fusion.3
  (48 shorter events, 0.2 us)
Async XLA Ops:
  1.6 5.3 %copy-start.13 = (bf16[256,256]{1,0:T(8,128)(2,1)}, bf16[256,256]{1,0:T(8,128)(2,1)S(1)}, u32[]{:S(2)}) copy-start(bf16[256,256]{1,0:T(8,128)(2,1)S(1)} %pad_maximum_fusion.refs_6_) | copy-start | bytes 393220
  1.6 10.5 %collective-permute-start = (bf16[256,256]{1,0:T(8,128)(2,1)S(1)}, bf16[256,256]{1,0:T(8,128)(2,1)S(1)}, u32[]{:S(2)}, u32[]{:S(2)}) collective-permute-start(bf16[256,256]{1,0:T(8,128)(2,1)S(1)} %pad_maximum_fusion.refs_6_), channel_id=1, source_target_pairs={{4,12},{8,16},{12,20},{16,24},{20,28},{24,0},{28,4},{5,13},{9,17},... | collective-permute-start | bytes 393224 | tf_op jit(solution)/shard_map/ppermute | solution.py:318
  2.9 12.1 %collective-permute-start.1 = (bf16[256,256]{1,0:T(8,128)(2,1)S(1)}, bf16[256,256]{1,0:T(8,128)(2,1)S(1)}, u32[]{:S(2)}, u32[]{:S(2)}) collective-permute-start(bf16[256,256]{1,0:T(8,128)(2,1)S(1)} %pad_maximum_fusion.refs_6_), channel_id=1, source_target_pairs={{4,20},{8,24},{12,28},{16,0},{20,4},{5,21},{9,25},{13,29},{17,1},{... | collective-permute-start | bytes 393224 | tf_op jit(solution)/shard_map/ppermute | solution.py:318
  4.2 19.3 %collective-permute-start.2 = (bf16[256,256]{1,0:T(8,128)(2,1)S(1)}, bf16[256,256]{1,0:T(8,128)(2,1)S(1)}, u32[]{:S(2)}, u32[]{:S(2)}) collective-permute-start(bf16[256,256]{1,0:T(8,128)(2,1)S(1)} %pad_maximum_fusion.refs_6_), channel_id=1, source_target_pairs={{4,28},{8,0},{12,4},{5,29},{9,1},{13,5},{6,30},{10,2},{14,6},{7,31... | collective-permute-start | bytes 393224 | tf_op jit(solution)/shard_map/ppermute | solution.py:318
  5.5 18.1 %collective-permute-start.3 = (bf16[256,256]{1,0:T(8,128)(2,1)S(1)}, bf16[256,256]{1,0:T(8,128)(2,1)S(1)}, u32[]{:S(2)}, u32[]{:S(2)}) collective-permute-start(bf16[256,256]{1,0:T(8,128)(2,1)S(1)} %pad_maximum_fusion.refs_6_), channel_id=1, source_target_pairs={{4,0},{8,12},{16,20},{24,28},{5,1},{9,13},{17,21},{25,29},{6,2},{1... | collective-permute-start | bytes 393224 | tf_op jit(solution)/shard_map/ppermute | solution.py:318
  6.8 1.4 %copy-start.17 = (s32[4,32]{1,0:T(4,128)S(1)}, s32[4,32]{1,0:T(4,128)}, u32[]{:S(2)}) copy-start(s32[4,32]{1,0:T(4,128)} %param.19) | copy-start | bytes 1540
  6.9 16.7 %copy-start.2 = (bf16[256,256]{1,0:T(8,128)(2,1)}, bf16[256,256]{1,0:T(8,128)(2,1)S(1)}, u32[]{:S(2)}) copy-start(bf16[256,256]{1,0:T(8,128)(2,1)S(1)} %pad_maximum_fusion.1.refs_0_.refs_6_) | copy-start | bytes 393220
  6.9 20.5 %collective-permute-start.5 = (bf16[256,256]{1,0:T(8,128)(2,1)S(1)}, bf16[256,256]{1,0:T(8,128)(2,1)S(1)}, u32[]{:S(2)}, u32[]{:S(2)}) collective-permute-start(bf16[256,256]{1,0:T(8,128)(2,1)S(1)} %pad_maximum_fusion.1.refs_0_.refs_6_), channel_id=1, source_target_pairs={{4,12},{8,16},{12,20},{16,24},{20,28},{24,0},{28,4},{5,13},{9,17},... | collective-permute-start | bytes 393224 | tf_op jit(solution)/shard_map/ppermute | solution.py:318
  12.2 11.4 %copy-start.4 = (bf16[256,256]{1,0:T(8,128)(2,1)}, bf16[256,256]{1,0:T(8,128)(2,1)S(1)}, u32[]{:S(2)}) copy-start(bf16[256,256]{1,0:T(8,128)(2,1)S(1)} %collective-permute-done.refs_0_.refs_7_) | copy-start | bytes 393220
  12.2 15.3 %collective-permute-start.6 = (bf16[256,256]{1,0:T(8,128)(2,1)S(1)}, bf16[256,256]{1,0:T(8,128)(2,1)S(1)}, u32[]{:S(2)}, u32[]{:S(2)}) collective-permute-start(bf16[256,256]{1,0:T(8,128)(2,1)S(1)} %pad_maximum_fusion.1.refs_0_.refs_6_), channel_id=1, source_target_pairs={{4,20},{8,24},{12,28},{16,0},{20,4},{5,21},{9,25},{13,29},{17,1},{... | collective-permute-start | bytes 393224 | tf_op jit(solution)/shard_map/ppermute | solution.py:318
  15.0 8.6 %copy-start.5 = (bf16[256,256]{1,0:T(8,128)(2,1)}, bf16[256,256]{1,0:T(8,128)(2,1)S(1)}, u32[]{:S(2)}) copy-start(bf16[256,256]{1,0:T(8,128)(2,1)S(1)} %collective-permute-done.1.refs_1_.refs_8_) | copy-start | bytes 393220
  15.0 12.5 %collective-permute-start.7 = (bf16[256,256]{1,0:T(8,128)(2,1)S(1)}, bf16[256,256]{1,0:T(8,128)(2,1)S(1)}, u32[]{:S(2)}, u32[]{:S(2)}) collective-permute-start(bf16[256,256]{1,0:T(8,128)(2,1)S(1)} %pad_maximum_fusion.1.refs_0_.refs_6_), channel_id=1, source_target_pairs={{4,28},{8,0},{12,4},{5,29},{9,1},{13,5},{6,30},{10,2},{14,6},{7,31... | collective-permute-start | bytes 393224 | tf_op jit(solution)/shard_map/ppermute | solution.py:318
  23.6 0.6 copy-start.6
  23.6 0.7 copy-start.7
  26.1 22.2 %collective-permute-start.4 = (bf16[3,256,256]{2,1,0:T(8,128)(2,1)}, bf16[3,256,256]{2,1,0:T(8,128)(2,1)S(1)}, u32[]{:S(2)}, u32[]{:S(2)}) collective-permute-start(bf16[3,256,256]{2,1,0:T(8,128)(2,1)} %join.2), channel_id=1, source_target_pairs={{4,0},{12,8},{16,20},{20,16},{24,28},{28,24},{5,1},{13,9},{17,21},... | collective-permute-start | bytes 1179656 | tf_op jit(solution)/shard_map/ppermute | solution.py:318
  27.4 0.7 copy-start.14
  27.5 0.7 copy-start.15
  28.1 0.6 copy-start.16
  30.7 35.4 %collective-permute-start.8 = (bf16[4,256,256]{2,1,0:T(8,128)(2,1)}, bf16[4,256,256]{2,1,0:T(8,128)(2,1)S(1)}, u32[]{:S(2)}, u32[]{:S(2)}) collective-permute-start(bf16[4,256,256]{2,1,0:T(8,128)(2,1)} %join.3), channel_id=1, source_target_pairs={{4,0},{8,12},{12,8},{16,20},{20,16},{24,28},{28,24},{5,1},{9,13},{... | collective-permute-start | bytes 1572872 | tf_op jit(solution)/shard_map/ppermute | solution.py:318
  48.3 0.8 copy-start.20
  64.8 19.2 %collective-permute-start.10 = (bf16[4,256,256]{2,1,0:T(8,128)(2,1)}, bf16[4,256,256]{2,1,0:T(8,128)(2,1)S(1)}, u32[]{:S(2)}, u32[]{:S(2)}) collective-permute-start(bf16[4,256,256]{2,1,0:T(8,128)(2,1)} %get-tuple-element.61), channel_id=1, source_target_pairs={{0,4},{8,12},{12,8},{16,20},{20,16},{24,28},{28,24},{1,5},{9,13},{... | collective-permute-start | bytes 1572872 | tf_op jit(solution)/shard_map/ppermute | solution.py:318
  66.2 0.8 copy-start.19
  66.9 17.1 %copy-start.8 = (bf16[256,256]{1,0:T(8,128)(2,1)S(1)}, bf16[256,256]{1,0:T(8,128)(2,1)}, u32[]{:S(2)}) copy-start(bf16[256,256]{1,0:T(8,128)(2,1)} %get-tuple-element.64) | copy-start | bytes 393220
  67.0 17.1 %copy-start.9 = (bf16[256,256]{1,0:T(8,128)(2,1)S(1)}, bf16[256,256]{1,0:T(8,128)(2,1)}, u32[]{:S(2)}) copy-start(bf16[256,256]{1,0:T(8,128)(2,1)} %get-tuple-element.65) | copy-start | bytes 393220
  67.0 17.1 %copy-start.10 = (bf16[256,256]{1,0:T(8,128)(2,1)S(1)}, bf16[256,256]{1,0:T(8,128)(2,1)}, u32[]{:S(2)}) copy-start(bf16[256,256]{1,0:T(8,128)(2,1)} %get-tuple-element.60) | copy-start | bytes 393220
  82.7 18.5 %collective-permute-start.9 = (bf16[4,256,256]{2,1,0:T(8,128)(2,1)}, bf16[4,256,256]{2,1,0:T(8,128)(2,1)S(1)}, u32[]{:S(2)}, u32[]{:S(2)}) collective-permute-start(bf16[4,256,256]{2,1,0:T(8,128)(2,1)} %get-tuple-element.58), channel_id=1, source_target_pairs={{0,4},{8,12},{12,8},{16,20},{20,16},{24,28},{28,24},{1,5},{9,13},{... | collective-permute-start | bytes 1572872 | tf_op jit(solution)/shard_map/ppermute | solution.py:318
  84.1 0.9 copy-start.3
  84.9 23.1 %collective-permute-start.11 = (bf16[256,256]{1,0:T(8,128)(2,1)S(1)}, bf16[256,256]{1,0:T(8,128)(2,1)S(1)}, u32[]{:S(2)}, u32[]{:S(2)}) collective-permute-start(bf16[256,256]{1,0:T(8,128)(2,1)S(1)} %get-tuple-element.76), channel_id=1, source_target_pairs={{0,24},{4,28},{12,4},{16,8},{20,12},{24,16},{28,20},{1,25},{5,29},... | collective-permute-start | bytes 393224 | tf_op jit(solution)/shard_map/ppermute | solution.py:318
  93.7 14.3 %collective-permute-start.12 = (bf16[256,256]{1,0:T(8,128)(2,1)S(1)}, bf16[256,256]{1,0:T(8,128)(2,1)S(1)}, u32[]{:S(2)}, u32[]{:S(2)}) collective-permute-start(bf16[256,256]{1,0:T(8,128)(2,1)S(1)} %get-tuple-element.75), channel_id=1, source_target_pairs={{0,16},{4,20},{20,4},{24,8},{28,12},{1,17},{5,21},{21,5},{25,9},{2... | collective-permute-start | bytes 393224 | tf_op jit(solution)/shard_map/ppermute | solution.py:318
  101.3 0.8 copy-start
  104.1 24.0 %collective-permute-start.13 = (bf16[2,256,256]{2,1,0:T(8,128)(2,1)}, bf16[2,256,256]{2,1,0:T(8,128)(2,1)S(1)}, u32[]{:S(2)}, u32[]{:S(2)}) collective-permute-start(bf16[2,256,256]{2,1,0:T(8,128)(2,1)} %get-tuple-element.68), channel_id=1, source_target_pairs={{0,8},{4,12},{28,4},{1,9},{5,13},{29,5},{2,10},{6,14},{30,6},{3,11... | collective-permute-start | bytes 786440 | tf_op jit(solution)/shard_map/ppermute | solution.py:318
  105.4 22.6 %collective-permute-start.14 = (bf16[256,256]{1,0:T(8,128)(2,1)}, bf16[256,256]{1,0:T(8,128)(2,1)S(1)}, u32[]{:S(2)}, u32[]{:S(2)}) collective-permute-start(bf16[256,256]{1,0:T(8,128)(2,1)} %get-tuple-element.70), channel_id=1, source_target_pairs={{0,24},{4,28},{12,4},{16,8},{20,12},{24,16},{28,20},{1,25},{5,29},... | collective-permute-start | bytes 393224 | tf_op jit(solution)/shard_map/ppermute | solution.py:318
  106.8 21.3 %collective-permute-start.15 = (bf16[256,256]{1,0:T(8,128)(2,1)}, bf16[256,256]{1,0:T(8,128)(2,1)S(1)}, u32[]{:S(2)}, u32[]{:S(2)}) collective-permute-start(bf16[256,256]{1,0:T(8,128)(2,1)} %get-tuple-element.71), channel_id=1, source_target_pairs={{0,16},{4,20},{20,4},{24,8},{28,12},{1,17},{5,21},{21,5},{25,9},{2... | collective-permute-start | bytes 393224 | tf_op jit(solution)/shard_map/ppermute | solution.py:318
  108.1 0.7 copy-start.21
  108.1 0.7 copy-start.22
  128.1 0.7 copy-start.11
  128.1 0.7 copy-start.12
  128.1 0.8 copy-start.1
  131.5 0.6 copy-start.18
